TPU v7x, 32 devices: a whole 2x2x4 slice. The times are simulated.
32 devices in a mesh: group: 2 (over y), patch: 4 (over z), visit: 2 (over x), band: 2 (over core).
Axes of the slice: x: 2, y: 2, z: 4, core: 2. Of those that a mesh axis runs over, the one named last changes fastest.
Arguments:
- template: bfloat16 [4096, 512], P(('group', 'patch')), parts along dimension 0, may hold values from -6 to 6
- science: bfloat16 [4096, 4, 512], P(('group', 'patch'), ('visit', 'band')), parts along dimension 0, may hold values from -6 to 6
- offsets: int32 [8, 4], P(('group', 'patch'), ('visit', 'band')), parts along dimension 0, may hold values from 0 to 496
- live_flags: int32 [8, 4], P(('group', 'patch'), ('visit', 'band')), parts along dimension 0, may hold values 0 or 1
- bank: bfloat16 [16, 31], replicated, may hold values from -1 to 1
- basis_index: int32 [8, 15, 2], P(('group', 'visit', 'band')), parts along dimension 0, may hold values from 0 to 15, as said below
- coeff: float32 [8, 15], P(('group', 'visit', 'band')), parts along dimension 0, may hold values from -4 to 4
- psf_profile: bfloat16 [31], replicated, may hold values from -1 to 1
Outputs:
- difference: bfloat16 [4096, 4, 512], P(('group', 'patch'), ('visit', 'band')), parts along dimension 0
- detection: float32 [4096, 512], P(('group', 'patch', 'visit', 'band')), parts along dimension 0
There are 2 independent parts, one for each index of `group`. A program takes and returns all parts, laid end to end along the dimension named above; an argument that names none is the same for every part. Nothing has to cross between parts.
Inputs may be any that keep to these rules, and one draw needn't show every extreme that they name: For each visit w, the 15 row profile indices basis_index[w, :, 0] are distinct, and so are the 15 column profile indices basis_index[w, :, 1].
All inputs are finite; a program needn't handle non-finite values. No bound on the sum of `live_flags` on one device may be relied on, other than what follows from the above.
Results may differ from a plain program's by a relative error of at most 0.0056.
Values may be sent and summed in bfloat16 or wider, within the bound.
No kernel may reach another device: no remote copies, remote signals or barrier semaphores. Data moves between devices by JAX's collectives and lax.ppermute only.
A program may use at most 64 MiB of HBM per device.

v0:
```python
import jax
import jax.numpy as jnp
from jax import lax
from jax.sharding import PartitionSpec as P


def shifted(shard, axis, by):
    devices = lax.axis_size(axis)
    pairs = [(i, i + by) for i in range(devices) if 0 <= i + by < devices]
    return lax.ppermute(shard, axis, pairs)


def toeplitz(profile, count):
    width = profile.shape[-1]
    lead = profile.shape[:-1]
    padded = jnp.concatenate([profile, jnp.zeros(lead + (count,), profile.dtype)], axis=-1)
    tiled = jnp.tile(padded, (1,) * len(lead) + (count,))
    tiled = tiled[..., : count * (count + width - 1)]
    return tiled.reshape(lead + (count, count + width - 1))


def profiles(bank, basis_index, coeff):
    table = bank.astype(jnp.float32)
    labels = jnp.arange(table.shape[0], dtype=jnp.int32)
    pick_row = (basis_index[:, 0:1] == labels[None, :]).astype(jnp.float32)
    pick_col = (basis_index[:, 1:2] == labels[None, :]).astype(jnp.float32)
    row_raw = jnp.dot(pick_row, table, precision=lax.Precision.HIGHEST)
    col_raw = jnp.dot(pick_col, table, precision=lax.Precision.HIGHEST)
    rowprof = (coeff[:, None] * row_raw).astype(jnp.bfloat16)
    colprof = col_raw.astype(jnp.bfloat16)
    return (rowprof, colprof)


def last_blocks(padded, block, count, extra):
    pieces = [padded[..., j * block : j * block + block + extra] for j in range(count // block)]
    return jnp.stack(pieces, axis=-2)


def lead_blocks(padded, block, count, extra, axis):
    pieces = [
        lax.slice_in_dim(padded, j * block, j * block + block + extra, axis=axis)
        for j in range(count // block)
    ]
    return jnp.stack(pieces, axis=axis)


def match_tile(window, sci, rowprof, colprof, psf):
    tile_rows, tile_cols = sci.shape
    half = psf.shape[0] // 2
    extra = 2 * half
    col_block = min(128, tile_cols)
    row_block = min(128, tile_rows)
    padded = jnp.pad(window, ((0, 0), (half, half)))
    pieces = last_blocks(padded, col_block, tile_cols, extra)
    colmat = toeplitz(colprof, col_block)
    smoothed = jnp.einsum("rji,kci->krjc", pieces, colmat, preferred_element_type=jnp.float32)
    smoothed = smoothed.reshape(colprof.shape[0], window.shape[0], tile_cols).astype(jnp.bfloat16)
    stacked = lead_blocks(smoothed, row_block, tile_rows, extra, 1)
    rowmat = toeplitz(rowprof, row_block)
    matched = jnp.einsum(
        "kbi,kjic->jbc", rowmat, stacked, preferred_element_type=jnp.float32
    ).reshape(tile_rows, tile_cols)
    difference = (sci.astype(jnp.float32) - matched).astype(jnp.bfloat16)
    dpad = jnp.pad(difference, ((0, 0), (half, half)))
    dpieces = last_blocks(dpad, col_block, tile_cols, extra)
    pcol = toeplitz(psf, col_block)
    filtrow = (
        jnp.einsum("rji,ci->rjc", dpieces, pcol, preferred_element_type=jnp.float32)
        .reshape(tile_rows, tile_cols)
        .astype(jnp.bfloat16)
    )
    fpad = jnp.pad(filtrow, ((half, half), (0, 0)))
    fpieces = lead_blocks(fpad, row_block, tile_rows, extra, 0)
    prow = toeplitz(psf, row_block)
    filtered = jnp.einsum("bi,jic->jbc", prow, fpieces, preferred_element_type=jnp.float32).reshape(
        tile_rows, tile_cols
    )
    return (difference, filtered)


def split_rows(filtered, shift_rows, live):
    tile_rows = filtered.shape[0]
    rolled = jnp.roll(filtered, shift_rows, axis=0)
    rowid = jnp.arange(tile_rows, dtype=jnp.int32)
    mine = (rowid >= shift_rows).astype(jnp.float32) * live
    spilled = (rowid < shift_rows).astype(jnp.float32) * live
    return (rolled * mine[:, None], rolled * spilled[:, None], mine, spilled)


def on_device(template, science, offsets, live_flags, bank, basis_index, coeff, psf_profile):
    tile_rows = template.shape[0]
    half = bank.shape[1] // 2
    below = shifted(template, "patch", -1)
    above = shifted(template[tile_rows - half :], "patch", 1)
    stacked = jnp.concatenate([above, template, below], axis=0)
    shift_rows = offsets[0, 0]
    window = lax.dynamic_slice_in_dim(stacked, shift_rows, tile_rows + 2 * half, 0)
    rowprof, colprof = profiles(bank, basis_index[0], coeff[0])
    difference, filtered = match_tile(window, science[:, 0, :], rowprof, colprof, psf_profile)
    live = live_flags[0, 0].astype(jnp.float32)
    mine, spill, mine_cover, spill_cover = split_rows(filtered, shift_rows, live)
    spill_in, cover_in = (
        shifted(spill.astype(jnp.bfloat16), "patch", 1).astype(spill.dtype),
        shifted(spill_cover.astype(jnp.bfloat16), "patch", 1).astype(spill_cover.dtype),
    )
    accum, cover = (
        lax.psum_scatter(mine + spill_in, ("visit", "band"), scatter_dimension=0, tiled=True),
        lax.psum_scatter(mine_cover + cover_in, ("visit", "band"), scatter_dimension=0, tiled=True),
    )
    detection = accum * lax.rsqrt(jnp.maximum(cover, 1.0))[:, None]
    return (difference[:, None, :], detection)


def solution(mesh):
    return jax.shard_map(
        on_device,
        mesh=mesh,
        in_specs=(
            P(("group", "patch"), None),
            P(("group", "patch"), ("visit", "band"), None),
            P(("group", "patch"), ("visit", "band")),
            P(("group", "patch"), ("visit", "band")),
            P(),
            P(("group", "visit", "band"), None, None),
            P(("group", "visit", "band"), None),
            P(),
        ),
        out_specs=(
            P(("group", "patch"), ("visit", "band"), None),
            P(("group", "patch", "visit", "band"), None),
        ),
        check_vma=False,
    )
```

profile of v0, /device:TPU:0, one launch (start us, length us, event | category | flops | bytes accessed | tf_op | source)
XLA Modules:
  0.0 122.1 jit_solution(18085833876973116050)
XLA Ops:
  7.2 0.0 copy-start
  7.2 0.0 reduce-scatter.2.cloned.1.call-start
  7.2 1.3 %copy.36 = bf16[512,512]{0,1:T(8,128)(2,1)S(1)} copy(bf16[512,512]{1,0:T(8,128)(2,1)} %param.8) | data formatting | bytes 1048576 | tf_op args[0]
  8.5 1.3 %collective-permute-start.1 = (bf16[512,512]{0,1:T(8,128)(2,1)S(1)}, bf16[512,512]{0,1:T(8,128)(2,1)}, u32[]{:S(2)}, u32[]{:S(2)}) collective-permute-start(bf16[512,512]{0,1:T(8,128)(2,1)S(1)} %copy.36), channel_id=1, source_target_pairs={{4,0},{8,4},{12,8},{5,1},{9,5},{13,9},{6,2},{10,6},{14,10},{7,3},{... | collective-permute-start | bytes 1572872 | tf_op jit(solution)/shard_map/ppermute | solution.py:10
  9.8 0.7 slice.77
  10.5 0.2 copy.34
  10.7 5.6 %collective-permute-start = (bf16[15,512]{0,1:T(8,128)(2,1)S(1)}, bf16[15,512]{0,1:T(8,128)(2,1)S(1)}, u32[]{:S(2)}, u32[]{:S(2)}) collective-permute-start(bf16[15,512]{0,1:T(8,128)(2,1)S(1)} %copy.34), channel_id=1, source_target_pairs={{0,4},{4,8},{8,12},{1,5},{5,9},{9,13},{2,6},{6,10},{10,14},{3,7},{... | collective-permute-start | bytes 46088 | tf_op jit(solution)/shard_map/ppermute | solution.py:10
  16.9 0.8 slice_bitcast_fusion.6
  18.3 0.0 copy-done
  18.3 0.2 convolution_convert_fusion.1
  18.5 0.8 fusion.8
  19.4 0.1 tile.12
  19.4 1.5 %tile.13 = bf16[15,20352]{1,0:T(8,128)(2,1)S(1)} reshape(bf16[15,128,159]{2,1,0:T(8,128)(2,1)S(1)} %tile.12) | data formatting | bytes 1221120 | tf_op jit(solution)/shard_map/tile | solution.py:17
  21.0 2.9 %reshape.55 = bf16[15,128,158]{2,1,0:T(8,128)(2,1)S(1)} reshape(bf16[15,20224]{1,0:T(8,128)(2,1)S(1)} %slice.97) | data formatting | bytes 1213440 | tf_op jit(solution)/shard_map/reshape | solution.py:19
  23.8 0.1 tile.14
  23.9 0.0 copy-start.2
  23.9 1.5 %tile.15 = bf16[15,20352]{1,0:T(8,128)(2,1)S(1)} reshape(bf16[15,128,159]{2,1,0:T(8,128)(2,1)S(1)} %tile.14) | data formatting | bytes 1221120 | tf_op jit(solution)/shard_map/tile | solution.py:17
  25.5 3.8 %reshape.56 = bf16[15,128,158]{2,1,0:T(8,128)(2,1)} reshape(bf16[15,20224]{1,0:T(8,128)(2,1)S(1)} %slice.102) | data formatting | bytes 1213440 | tf_op jit(solution)/shard_map/reshape | solution.py:19
  29.3 1.3 %copy.33 = bf16[512,1,512]{0,2,1:T(8,128)(2,1)S(1)} copy(bf16[512,1,512]{2,0,1:T(8,128)(2,1)} %param.9) | data formatting | bytes 1048576 | tf_op args[1]
  30.5 0.0 copy-done.2
  30.6 0.3 tile.17
  30.9 0.2 reshape.59
  31.1 0.0 collective-permute-done
  31.1 0.0 collective-permute-done.1
  31.1 3.2 %concatenate.18 = bf16[1039,512]{0,1:T(8,128)(2,1)S(1)} concatenate(bf16[15,512]{0,1:T(8,128)(2,1)S(1)} %collective-permute-done, bf16[512,512]{0,1:T(8,128)(2,1)S(1)} %copy.36, bf16[512,512]{0,1:T(8,128)(2,1)} %collective-permute-done.1), dimensions={0} | concatenate | bytes 2127872 | tf_op jit(solution)/shard_map/concatenate | solution.py:95
  34.3 0.4 constant_dynamic-slice_fusion
  34.7 0.1 fusion.36
  34.8 0.2 dynamic-slice_bitcast_fusion.1
  35.1 3.0 %convert_bitcast_fusion = bf16[15,542,4,128]{3,1,2,0:T(8,128)(2,1)S(1)} fusion(bf16[15,128,158]{2,1,0:T(8,128)(2,1)S(1)} %reshape.55, bf16[542,1,158]{0,2,1:T(8,128)(2,1)S(1)} %get-tuple-element.15, bf16[542,1,158]{0,2,1:T(8,128)(2,1)S(1)} %get-tuple-element.13, bf16[542,1,158]{0,2,1:T(8,128)(2,1)S(1)} %get-tuple-element.12, ...), kind=kOutput, calls=%fused_computation.8 | convolution fusion | flops 1322271872 | bytes 9616928 | tf_op jit(solution)/shard_map/rji,kci->krjc/dot_general | solution.py:56
  38.1 9.8 %copy.38 = bf16[15,542,4,128]{3,2,1,0:T(4,128)(2,1)} copy(bf16[15,542,4,128]{3,1,2,0:T(8,128)(2,1)S(1)} %convert_bitcast_fusion) | data formatting | bytes 16650240 | tf_op jit(solution)/shard_map/convert_element_type | solution.py:57
  47.8 12.9 %convert_element_type.69 = bf16[15,542,512]{2,1,0:T(8,128)(2,1)} reshape(bf16[15,542,4,128]{3,2,1,0:T(4,128)(2,1)} %copy.38) | data formatting | bytes 16650240 | tf_op jit(solution)/shard_map/convert_element_type | solution.py:57
  60.7 4.3 %slice_bitcast_fusion.3 = (bf16[15,1,158,512]{3,2,0,1:T(8,128)(2,1)S(1)}, bf16[15,1,158,512]{3,2,0,1:T(8,128)(2,1)S(1)}, bf16[15,1,158,512]{3,2,0,1:T(8,128)(2,1)S(1)}, bf16[15,1,158,512]{3,2,0,1:T(8,128)(2,1)S(1)}) fusion(bf16[15,542,512]{2,1,0:T(8,128)(2,1)} %convert_element_type.69), kind=kLoop, calls=%fused_computation.12 | loop fusion | bytes 19415040 | tf_op jit(solution)/shard_map/stack | solution.py:44
  65.0 0.0 copy-done.1
  65.0 2.7 %fusion = f32[4,512,128,1]{1,2,3,0:T(8,128)S(1)} fusion(bf16[15,1,158,512]{3,2,0,1:T(8,128)(2,1)S(1)} %get-tuple-element.9, bf16[15,1,158,512]{3,2,0,1:T(8,128)(2,1)S(1)} %get-tuple-element.10, bf16[15,1,158,512]{3,2,0,1:T(8,128)(2,1)S(1)} %get-tuple-element.11, bf16[15,1,158,512]{3,2,0,1:T(8,128)(2,1)S(1)} %get-tuple-element.8, ...), kind=kOutput, calls=%fused_computation | convolution fusion | flops 1257123840 | bytes 11362816 | tf_op jit(solution)/shard_map/kbi,kjic->jbc/dot_general | solution.py:60
  67.8 0.3 copy.41
  68.1 0.2 fusion.11
  68.3 0.1 fusion.38
  68.4 0.5 convolution_convert_fusion
  68.9 0.2 copy.43
  69.2 0.1 fusion.54
  69.3 0.2 copy.44
  69.5 0.1 fusion.40
  69.6 0.1 copy.45
  69.7 0.1 stack.76
  69.7 0.1 copy.46
  69.8 0.1 stack.77
  69.9 0.3 fusion.28
  70.2 0.0 copy-start.3
  70.3 0.3 multiply_convert_fusion
  70.6 4.0 %collective-permute-start.2 = (bf16[512,512]{1,0:T(8,128)(2,1)S(1)}, bf16[512,512]{1,0:T(8,128)(2,1)S(1)}, u32[]{:S(2)}, u32[]{:S(2)}) collective-permute-start(bf16[512,512]{1,0:T(8,128)(2,1)S(1)} %multiply_convert_fusion), channel_id=1, source_target_pairs={{0,4},{4,8},{8,12},{1,5},{5,9},{9,13},{2,6},{6,10},{10,14},{3,7},{... | collective-permute-start | bytes 1572872 | tf_op jit(solution)/shard_map/ppermute | solution.py:10
  74.6 10.5 %collective-permute-done.2 = bf16[512,512]{1,0:T(8,128)(2,1)S(1)} collective-permute-done((bf16[512,512]{1,0:T(8,128)(2,1)S(1)}, bf16[512,512]{1,0:T(8,128)(2,1)S(1)}, u32[]{:S(2)}, u32[]{:S(2)}) %collective-permute-start.2) | collective-permute-done | bytes 524320 | tf_op jit(solution)/shard_map/ppermute | solution.py:10
  85.1 1.4 %convert_add_fusion = f32[512,512]{1,0:T(8,128)} fusion(bf16[512,512]{1,0:T(8,128)(2,1)S(1)} %collective-permute-done.2, f32[512]{0:T(512)S(1)} %fusion.46, s32[]{:T(128)S(6)} %select_n.18, f32[512,512]{1,0:T(8,128)S(1)} %bitcast.89), kind=kLoop, calls=%fused_computation.25 | loop fusion | flops 1048576 | bytes 2623492 | tf_op jit(solution)/shard_map/add | solution.py:107
  86.5 0.0 reduce-scatter.2.cloned.1.call-update
  86.5 4.4 %collective-permute-start.3 = (bf16[512]{0:T(512)(128)(2,1)S(1)}, bf16[512]{0:T(512)(128)(2,1)S(1)}, u32[]{:S(2)}, u32[]{:S(2)}) collective-permute-start(bf16[512]{0:T(512)(128)(2,1)S(1)} %fusion.49), channel_id=1, source_target_pairs={{0,4},{4,8},{8,12},{1,5},{5,9},{9,13},{2,6},{6,10},{10,14},{3,7},{... | collective-permute-start | bytes 3080 | tf_op jit(solution)/shard_map/ppermute | solution.py:10
  90.9 0.0 copy-done.3
  90.9 0.6 dynamic-slice
  92.2 0.0 collective-permute-done.3
  92.2 5.7 %all-reduce.6 = f32[512]{0:T(512)S(1)} all-reduce(f32[512]{0:T(512)S(1)} %convert_add_fusion.1), channel_id=3, replica_groups=mesh['group'=2,'patch'=4,'visit'=2,'band'=2] {'visit','band'}, use_global_device_ids=true, to_apply=%region_1.2.clone | all-reduce | flops 512 | bytes 4096
  97.9 0.1 fusion.48
  98.0 0.3 copy.40
  98.3 0.2 fusion.9
  98.5 1.0 copy.48
  99.5 14.0 %reduce-scatter.2.cloned.1.call-done = f32[128,512]{1,0:T(8,128)} async-done(((f32[512,512]{1,0:T(8,128)}), f32[128,512]{1,0:T(8,128)}) %reduce-scatter.2.cloned.1.call-update) | async-done | bytes 262160 | tf_op jit(solution)/shard_map/reduce_scatter | solution.py:107
  113.5 1.7 %broadcast_multiply_fusion = f32[128,512]{1,0:T(8,128)} fusion(f32[128,512]{1,0:T(8,128)} %reduce-scatter.2.cloned.1.call-done, f32[128]{0:T(128)S(1)} %fusion.48), kind=kLoop, calls=%fused_computation.67 | loop fusion | flops 65536 | bytes 524800 | tf_op jit(solution)/shard_map/mul | solution.py:110
  (11 shorter events, 0.1 us)
Async XLA Ops:
  7.2 11.1 %copy-start = (bf16[16,31]{1,0:T(8,128)(2,1)S(1)}, bf16[16,31]{1,0:T(8,128)(2,1)}, u32[]{:S(2)}) copy-start(bf16[16,31]{1,0:T(8,128)(2,1)} %param.12) | copy-start | bytes 2980
  7.2 106.3 %reduce-scatter.2.cloned.1.call-start = ((), (), s32[]{:S(2)}) async-start(), calls=%async_computation.1 | async-start | bytes 1310720 | tf_op jit(solution)/shard_map/reduce_scatter | solution.py:107
  8.5 22.7 %collective-permute-start.1 = (bf16[512,512]{0,1:T(8,128)(2,1)S(1)}, bf16[512,512]{0,1:T(8,128)(2,1)}, u32[]{:S(2)}, u32[]{:S(2)}) collective-permute-start(bf16[512,512]{0,1:T(8,128)(2,1)S(1)} %copy.36), channel_id=1, source_target_pairs={{4,0},{8,4},{12,8},{5,1},{9,5},{13,9},{6,2},{10,6},{14,10},{7,3},{... | collective-permute-start | bytes 1572872 | tf_op jit(solution)/shard_map/ppermute | solution.py:10
  10.7 20.5 %collective-permute-start = (bf16[15,512]{0,1:T(8,128)(2,1)S(1)}, bf16[15,512]{0,1:T(8,128)(2,1)S(1)}, u32[]{:S(2)}, u32[]{:S(2)}) collective-permute-start(bf16[15,512]{0,1:T(8,128)(2,1)S(1)} %copy.34), channel_id=1, source_target_pairs={{0,4},{4,8},{8,12},{1,5},{5,9},{9,13},{2,6},{6,10},{10,14},{3,7},{... | collective-permute-start | bytes 46088 | tf_op jit(solution)/shard_map/ppermute | solution.py:10
  23.9 6.6 %copy-start.2 = (bf16[31]{0:T(256)(128)(2,1)S(1)}, bf16[31]{0:T(256)(128)(2,1)}, u32[]{:S(2)}) copy-start(bf16[31]{0:T(256)(128)(2,1)} %param.15) | copy-start | bytes 190
  60.7 4.3 %copy-start.1 = (bf16[15,128,158]{2,1,0:T(8,128)(2,1)S(1)}, bf16[15,128,158]{2,1,0:T(8,128)(2,1)}, u32[]{:S(2)}) copy-start(bf16[15,128,158]{2,1,0:T(8,128)(2,1)} %reshape.56) | copy-start | bytes 1820164
  70.2 20.7 %copy-start.3 = (u32[32]{0:T(128)S(1)}, u32[32]{0:T(128)}, u32[]{:S(2)}) copy-start(u32[32]{0:T(128)} %constant.53) | copy-start | bytes 388
  70.6 14.5 %collective-permute-start.2 = (bf16[512,512]{1,0:T(8,128)(2,1)S(1)}, bf16[512,512]{1,0:T(8,128)(2,1)S(1)}, u32[]{:S(2)}, u32[]{:S(2)}) collective-permute-start(bf16[512,512]{1,0:T(8,128)(2,1)S(1)} %multiply_convert_fusion), channel_id=1, source_target_pairs={{0,4},{4,8},{8,12},{1,5},{5,9},{9,13},{2,6},{6,10},{10,14},{3,7},{... | collective-permute-start | bytes 1572872 | tf_op jit(solution)/shard_map/ppermute | solution.py:10
  86.5 5.7 %collective-permute-start.3 = (bf16[512]{0:T(512)(128)(2,1)S(1)}, bf16[512]{0:T(512)(128)(2,1)S(1)}, u32[]{:S(2)}, u32[]{:S(2)}) collective-permute-start(bf16[512]{0:T(512)(128)(2,1)S(1)} %fusion.49), channel_id=1, source_target_pairs={{0,4},{4,8},{8,12},{1,5},{5,9},{9,13},{2,6},{6,10},{10,14},{3,7},{... | collective-permute-start | bytes 3080 | tf_op jit(solution)/shard_map/ppermute | solution.py:10
Sparse Core Ops, SparseCore 0:
  86.6 26.8 reduce-scatter.1
where the time goes:
time: 123 us; the launch traced here: 122 us
  local copies, waits for them, and re-layouts  48.7 us (40%)
  waiting for transfers between devices  24.6 us (20%)
  between operations  16.4 us (13%)
  starting transfers between devices  15.2 us (12%)
  matrix products  7.6 us (6%)
  blocking collectives  5.67 us (5%)
  other arithmetic  3.87 us (3%)
    convert_element_type x2, local copies, waits for them, and re-layouts, match_tile(): smoothed.reshape(colprof.shape[0], window.shape[0], tile_cols)  22.6 us
    ppermute x4, starting transfers between devices, shifted(): return lax.ppermute(shard, axis, pairs)  15.2 us
    reduce_scatter x1, waiting for transfers between devices, on_device(): lax.psum_scatter(mine + spill_in, ('visit', 'band'), scatter_dimension=0,...  14 us
    ppermute x4, waiting for transfers between devices, shifted(): return lax.ppermute(shard, axis, pairs)  10.6 us
    reshape x3, local copies, waits for them, and re-layouts, toeplitz(): return tiled.reshape(lead + (count, count + width - 1))  6.9 us
    unnamed x1, blocking collectives  5.67 us
    another operation x4, local copies, waits for them, and re-layouts, lead_blocks(): return jnp.stack(pieces, axis=axis)  4.52 us
    unnamed x12, local copies, waits for them, and re-layouts  4.15 us
  transfers between devices with their start and end apart: 5, of which 2 were waited for; matrix products, arithmetic and copies ran while one was open for 14% of the time, Pallas kernels for 0%

commit v1 on v0

v1 whole, which is shorter than its diff:
```python
import functools

import jax
import jax.numpy as jnp
from jax import lax
from jax.experimental import pallas as pl
from jax.experimental.pallas import tpu as pltpu
from jax.sharding import PartitionSpec as P

B = 16
CH = B * B
LANES = 128
GROUPS = LANES // B
F32 = jnp.float32
BF16 = jnp.bfloat16


def shifted(shard, axis, by):
    devices = lax.axis_size(axis)
    pairs = [(i, i + by) for i in range(devices) if 0 <= i + by < devices]
    return lax.ppermute(shard, axis, pairs)


def iota(shape, dim):
    return lax.broadcasted_iota(jnp.int32, shape, dim)


def params():
    return pltpu.CompilerParams(vmem_limit_bytes=48 * 1024 * 1024)


VM = pl.BlockSpec(memory_space=pltpu.VMEM)
SM = pl.BlockSpec(memory_space=pltpu.SMEM)


def group_transpose(parts):
    parts = list(parts)
    group = iota(parts[0].shape, 1) // B
    for step in (1, 2, 4):
        low = (group & step) == 0
        for m in range(GROUPS):
            if m & step:
                continue
            x, y = parts[m], parts[m + step]
            parts[m] = jnp.where(low, x, pltpu.roll(y, step * B, 1))
            parts[m + step] = jnp.where(low, pltpu.roll(x, LANES - step * B, 1), y)
    return parts


def conv_blocks(src, count, w_ref, xs, rs, dst, dst_row, batch):
    chunks = src.shape[0]
    blocks = chunks * GROUPS
    for q in range(3):
        xs[q, 0] = jnp.zeros((count, CH), xs.dtype)
        xs[q, blocks + 1] = jnp.zeros((count, CH), xs.dtype)
    for c in range(chunks):
        for h in range(2):
            rows = [src[c, pl.ds(GROUPS * h + i, count, stride=B), :] for i in range(GROUPS)]
            cols = group_transpose(rows)
            for g in range(GROUPS):
                for q in range(3):
                    moved = cols[g] if q == 1 else pltpu.roll(cols[g], (1 - q) % count, 0)
                    xs[q, 1 + c * GROUPS + g, :, h * LANES : (h + 1) * LANES] = moved.astype(xs.dtype)
    for b in range(0, blocks, batch):
        pieces = [
            xs[qr, b + qc : b + qc + batch].reshape(batch * count, CH).astype(BF16)
            for qr in range(3)
            for qc in range(3)
        ]
        out = jnp.dot(jnp.concatenate(pieces, axis=1), w_ref[...], preferred_element_type=F32)
        rs[b : b + batch] = out.reshape(batch, count, CH)
    for c in range(chunks):
        for h in range(2):
            cols = [rs[c * GROUPS + g, :, h * LANES : (h + 1) * LANES] for g in range(GROUPS)]
            rows = group_transpose(cols)
            for i in range(GROUPS):
                dst[c, pl.ds(dst_row + GROUPS * h + i, count, stride=B), :] = rows[i]


def weights_kernel(bank_ref, index_ref, coeff_ref, psf_ref, w_ref, pcol_ref, prow_ref):
    kernels = index_ref.shape[1]
    profs, taps = bank_ref.shape
    half = taps // 2
    delta = B - half
    bank = bank_ref[...]
    index = index_ref[0]
    labels = iota((kernels, profs), 1)
    pick_row = (index[:, 0:1] == labels).astype(F32).astype(BF16)
    pick_col = (index[:, 1:2] == labels).astype(F32).astype(BF16)
    diag = iota((kernels, kernels), 0) == iota((kernels, kernels), 1)
    weight = jnp.sum(jnp.where(diag, coeff_ref[...], 0.0), axis=1, keepdims=True)
    rowprof = (weight * jnp.dot(pick_row, bank, preferred_element_type=F32)).astype(BF16)
    colprof = jnp.dot(pick_col, bank, preferred_element_type=F32).astype(BF16)
    span = 3 * B
    total = 4 * B * B
    place = (iota((span, taps), 0) - delta == iota((span, taps), 1)).astype(F32).astype(BF16)
    col_t = lax.dot_general(place, colprof, (((1,), (1,)), ((), ())), preferred_element_type=F32).astype(BF16)
    spread = (span - 1 - iota((taps, total), 1) // B - delta == iota((taps, total), 0)).astype(F32).astype(BF16)
    row_rep = jnp.dot(rowprof, spread, preferred_element_type=F32).astype(BF16)
    z = jnp.dot(col_t, row_rep, preferred_element_type=F32)
    lane = iota((span, total), 1)
    for bit in (1, 2, 4, 8):
        z = jnp.where((lane & bit) != 0, pltpu.roll(z, bit, 0), z)
    z = z.astype(BF16)
    for phase in range(GROUPS):
        zp = z if phase == 0 else pltpu.roll(z, total - phase * B, 1)
        for g in range(span):
            start = span - 1 - g
            if start % GROUPS != phase:
                continue
            at = (start // GROUPS) * LANES
            for qc in range(3):
                row = (g // B) * 3 * CH + qc * CH + (g % B) * B
                w_ref[row : row + B, :] = zp[qc * B : (qc + 1) * B, at : at + CH]
    psf = psf_ref[...].astype(F32)
    size = pcol_ref.shape[0]
    blank = jnp.zeros((LANES, LANES), F32)
    bands = {}
    for off in (-1, 0, 1):
        tap = iota((LANES, LANES), 0) + off * LANES - iota((LANES, LANES), 1) + half
        block = blank
        for t in range(taps):
            block = jnp.where(tap == t, psf[:, t : t + 1], block)
        bands[off] = block.astype(BF16)
    for i in range(size // LANES):
        for j in range(size // LANES):
            pcol_ref[i * LANES : (i + 1) * LANES, j * LANES : (j + 1) * LANES] = bands.get(i - j, blank.astype(BF16))
    shape = prow_ref.shape
    tap = iota(shape, 1) - iota(shape, 0) - delta
    block = jnp.zeros(shape, F32)
    for t in range(taps):
        block = jnp.where(tap == t, psf[:, t : t + 1], block)
    prow_ref[...] = block.astype(BF16)


def to_chunks(dst, dst_row, value):
    value = value.astype(F32)
    rows = value.shape[0]
    for c in range(dst.shape[0]):
        dst[c, dst_row : dst_row + rows, :] = value[:, c * LANES : (c + 1) * LANES]


def own_kernel(t_ref, w_ref, m_ref, src, xs, rs):
    to_chunks(src, 0, t_ref[...])
    conv_blocks(src, t_ref.shape[0] // B, w_ref, xs, rs, m_ref, 0, rs.shape[0] // 2)


def filter_kernel(
    off_ref, live_ref, t_ref, msg_ref, next_ref, sci_ref, m1_ref, w_ref, pcol_ref, prow_ref,
    out_ref, m_ref, src, xs, rs, strip, sa, sb, diff, filt,
):
    rows, cols = t_ref.shape
    ext = rows + 2 * B
    edge = 2 * B
    to_chunks(src, 0, msg_ref[0:edge, :])
    to_chunks(src, edge, t_ref[0:edge, :])
    to_chunks(src, 2 * edge, t_ref[rows - edge : rows, :])
    to_chunks(src, 3 * edge, next_ref[0:edge, :])
    conv_blocks(src, 8, w_ref, xs, rs, strip, 0, rs.shape[0])
    m_ref[:, 0:edge, :] = strip[:, B : B + edge, :]
    m_ref[:, edge : rows, :] = m1_ref[:, B : rows - B, :]
    m_ref[:, rows : rows + edge, :] = strip[:, 5 * B : 5 * B + edge, :]
    to_chunks(sa, rows, sci_ref[...])
    to_chunks(sb, 0, msg_ref[edge : edge + rows, :])
    notes = msg_ref[0:B, 0:LANES].astype(F32)
    off_a = off_ref[0, 0]
    live_a = live_ref[0, 0].astype(F32)
    off_b = (notes[0, 0] * B + notes[0, 1]).astype(jnp.int32)
    live_b = notes[0, 2]
    tile_row = iota((ext, LANES), 0) - B
    in_a = (tile_row >= off_a) & (tile_row < off_a + rows)
    in_b = tile_row < off_b
    for c in range(cols // LANES):
        part = slice(c * LANES, (c + 1) * LANES)
        m = m_ref[c]
        a = sa[c, pl.ds(rows - B - off_a, ext), :]
        b = sb[c, pl.ds(rows - B - off_b, ext), :]
        diff[0, :, part] = jnp.where(in_a, a - m, 0.0).astype(BF16)
        diff[1, :, part] = jnp.where(in_b, b - m, 0.0).astype(BF16)
    for s in range(2):
        filt[s, 0:ext, :] = jnp.dot(diff[s], pcol_ref[...], preferred_element_type=F32).astype(BF16)
        filt[s, ext:, :] = jnp.zeros((filt.shape[1] - ext, cols), BF16)
    share, depth = prow_ref.shape
    prow = prow_ref[...].astype(F32)
    out_row = iota((share, depth), 0)
    lane = iota((B, cols), 1)
    for q in range(out_ref.shape[0]):
        row = out_row + q * share
        left = jnp.where(row >= off_a, prow * live_a, 0.0).astype(BF16)
        right = jnp.where(row < off_b, prow * live_b, 0.0).astype(BF16)
        span = slice(q * share, q * share + depth)
        total = jnp.dot(left, filt[0, span, :], preferred_element_type=F32)
        total += jnp.dot(right, filt[1, span, :], preferred_element_type=F32)
        out_ref[q, 0:share, :] = total.astype(BF16)
        start = jnp.clip(off_a - q * share, 0, share).astype(F32)
        stop = jnp.clip(off_b - q * share, 0, share).astype(F32)
        note = jnp.where(lane == 0, start, jnp.where(lane == 1, live_a, jnp.where(lane == 2, stop, live_b)))
        out_ref[q, share : share + B, :] = note.astype(BF16)


def tile_kernel(off_ref, next_ref, sci_ref, m_ref, w_ref, out_ref, src, xs, rs, big):
    rows, cols = next_ref.shape
    to_chunks(src, 0, next_ref[...])
    conv_blocks(src, rows // B, w_ref, xs, rs, big, rows, rs.shape[0] // 2)
    big[:, 0 : rows + B, :] = m_ref[:, B : rows + 2 * B, :]
    off = off_ref[0, 0]
    for c in range(cols // LANES):
        part = slice(c * LANES, (c + 1) * LANES)
        out_ref[:, part] = (sci_ref[:, part].astype(F32) - big[c, pl.ds(off, rows), :]).astype(BF16)


def coadd_kernel(recv_ref, out_ref):
    count, padded, cols = recv_ref.shape
    share = padded - B
    row = iota((share, LANES), 0).astype(F32)
    accum = jnp.zeros((share, cols), F32)
    cover = jnp.zeros((share, LANES), F32)
    for n in range(count):
        accum += recv_ref[n, 0:share, :].astype(F32)
        note = recv_ref[n, share : share + B, 0:LANES].astype(F32)[0:1, :]
        cover += jnp.where(row >= note[:, 0:1], note[:, 1:2], 0.0)
        cover += jnp.where(row < note[:, 2:3], note[:, 3:4], 0.0)
    scale = lax.rsqrt(jnp.maximum(cover, 1.0))
    for c in range(cols // LANES):
        part = slice(c * LANES, (c + 1) * LANES)
        out_ref[:, part] = accum[:, part] * scale


def call(body, shapes, specs, scratch, flops, name):
    return pl.pallas_call(
        body,
        out_shape=shapes,
        in_specs=specs,
        out_specs=jax.tree.map(lambda _: VM, shapes),
        scratch_shapes=scratch,
        compiler_params=params(),
        cost_estimate=pl.CostEstimate(flops=flops, bytes_accessed=1 << 21, transcendentals=0),
        name=name,
    )


def on_device(template, science, offsets, live_flags, bank, basis_index, coeff, psf_profile):
    rows, cols = template.shape
    sharers = lax.axis_size("visit") * lax.axis_size("band")
    share = rows // sharers
    chunks, blocks = cols // LANES, cols // B
    ext = rows + 2 * B
    edge = 2 * B
    sci = science[:, 0, :]
    off = offsets[0, 0]
    lane = jnp.arange(cols, dtype=jnp.int32)
    note = jnp.where(lane == 0, off // B, jnp.where(lane == 1, off % B, live_flags[0, 0])).astype(BF16)
    msg = jnp.concatenate([note[None], template[rows - edge + 1 :], sci], axis=0)
    msg = shifted(msg, "patch", 1)
    following = shifted(template, "patch", -1)

    sds = jax.ShapeDtypeStruct
    deep = 9 * CH
    depth = -(-(share + edge) // LANES) * LANES
    w, pcol, prow = call(
        weights_kernel,
        (sds((deep, CH), BF16), sds((cols, cols), BF16), sds((share, depth), BF16)),
        [VM] * 4, [], 1 << 26, "weights",
    )(bank, basis_index, coeff, psf_profile[None])
    count = rows // B
    conv_scratch = [
        pltpu.VMEM((chunks, rows, LANES), F32),
        pltpu.VMEM((3, blocks + 2, count, CH), BF16),
        pltpu.VMEM((blocks, count, CH), F32),
    ]
    conv_flops = 2 * rows * cols * deep
    m1 = call(own_kernel, sds((chunks, rows, LANES), F32), [VM] * 2, conv_scratch, conv_flops, "own")(template, w)
    out, m = call(
        filter_kernel,
        (sds((sharers, share + B, cols), BF16), sds((chunks, ext, LANES), F32)),
        [SM, SM] + [VM] * 8,
        [
            pltpu.VMEM((chunks, 8 * B, LANES), F32),
            pltpu.VMEM((3, blocks + 2, 8, CH), F32),
            pltpu.VMEM((blocks, 8, CH), F32),
            pltpu.VMEM((chunks, 8 * B, LANES), F32),
            pltpu.VMEM((chunks, 2 * rows + B, LANES), F32),
            pltpu.VMEM((chunks, 2 * rows + B, LANES), F32),
            pltpu.VMEM((2, ext, cols), BF16),
            pltpu.VMEM((2, rows - share + depth, cols), BF16),
        ],
        1 << 30, "filter",
    )(offsets, live_flags, template, msg, following, sci, m1, w, pcol, prow)
    recv = lax.all_to_all(out, ("visit", "band"), 0, 0, tiled=True)
    difference = call(
        tile_kernel, sds((rows, cols), BF16), [SM] + [VM] * 4,
        conv_scratch + [pltpu.VMEM((chunks, 2 * rows, LANES), F32)], conv_flops, "tile",
    )(offsets, following, sci, m, w)
    detection = call(coadd_kernel, sds((share, cols), F32), [VM], [], 1 << 20, "coadd")(recv)
    return (difference[:, None, :], detection)


def solution(mesh):
    return jax.shard_map(
        on_device,
        mesh=mesh,
        in_specs=(
            P(("group", "patch"), None),
            P(("group", "patch"), ("visit", "band"), None),
            P(("group", "patch"), ("visit", "band")),
            P(("group", "patch"), ("visit", "band")),
            P(),
            P(("group", "visit", "band"), None, None),
            P(("group", "visit", "band"), None),
            P(),
        ),
        out_specs=(
            P(("group", "patch"), ("visit", "band"), None),
            P(("group", "patch", "visit", "band"), None),
        ),
        check_vma=False,
    )
```

time: 123 us -> 45.4 us (0.37)
  local copies, waits for them, and re-layouts: 48.7 us -> 3.12 us
  Pallas kernels: 0 us -> 14.3 us
  between operations: 16.4 us -> 2.16 us
  waiting for transfers between devices: 24.6 us -> 13.6 us
  matrix products: 7.6 us -> 0 us
  blocking collectives: 5.67 us -> 0 us
  starting transfers between devices: 15.2 us -> 9.85 us
  other arithmetic: 3.87 us -> 1.91 us
    convert_element_type x4 -> x0, local copies, waits for them, and re-layouts: 23.1 us -> none  [the longest x2 22.6 us: match_tile(): smoothed.reshape(colprof.shape[0], window.shape[0], tile_cols)]
    pallas_call x0 -> x5, Pallas kernels: none -> 14.3 us  [the longest x1 4.96 us: on_device(): call(filter_kernel, (sds((sharers, share + B, cols), BF16), sds((chunks,...]
    reduce_scatter x1 -> x0, waiting for transfers between devices: 14 us -> none  [on_device(): lax.psum_scatter(mine + spill_in, ('visit', 'band'), scatter_dimension=0,...]
    ppermute x4 -> x2, starting transfers between devices: 15.2 us -> 6.24 us  [shifted(): return lax.ppermute(shard, axis, pairs)]
    another operation x13 -> x0, local copies, waits for them, and re-layouts: 8.38 us -> none  [the longest x4 4.52 us: lead_blocks(): return jnp.stack(pieces, axis=axis)]
    dot_general x6 -> x0, matrix products: 7.6 us -> none  [the longest x1 2.99 us: match_tile(): jnp.einsum('rji,kci->krjc', pieces, colmat, preferred_element_type=jnp.fl...]
    reshape x5 -> x0, local copies, waits for them, and re-layouts: 7.56 us -> none  [the longest x3 6.9 us: toeplitz(): return tiled.reshape(lead + (count, count + width - 1))]
    unnamed x1 -> x0, blocking collectives: 5.67 us -> none
  transfers between devices with their start and end apart: 5 -> 3, of which waited for: 2 -> 2; matrix products, arithmetic and copies ran while one was open for 14% -> 0% of each run, Pallas kernels for 0% -> 19%
where the time goes in v1:
time: 45.4 us; the launch traced here: 45 us
  Pallas kernels  14.3 us (31%)
  waiting for transfers between devices  13.6 us (30%)
  starting transfers between devices  9.85 us (22%)
  local copies, waits for them, and re-layouts  3.12 us (7%)
  between operations  2.16 us (5%)
  other arithmetic  1.91 us (4%)
    ppermute x2, waiting for transfers between devices, shifted(): return lax.ppermute(shard, axis, pairs)  9.36 us
    ppermute x2, starting transfers between devices, shifted(): return lax.ppermute(shard, axis, pairs)  6.24 us
    pallas_call x1, Pallas kernels, on_device(): call(filter_kernel, (sds((sharers, share + B, cols), BF16), sds((chunks,...  4.96 us
    all_to_all x1, waiting for transfers between devices, on_device(): recv = lax.all_to_all(out, ('visit', 'band'), 0, 0, tiled=True)  4.26 us
    pallas_call x1, Pallas kernels, on_device(): call(tile_kernel, sds((rows, cols), BF16), [SM] + [VM] * 4, conv_scratch...  3.99 us
    all_to_all x1, starting transfers between devices, on_device(): recv = lax.all_to_all(out, ('visit', 'band'), 0, 0, tiled=True)  3.61 us
    pallas_call x1, Pallas kernels, on_device(): call(own_kernel, sds((chunks, rows, LANES), F32), [VM] * 2, conv_scratch,...  2.96 us
    unnamed x21, local copies, waits for them, and re-layouts  2.35 us
  transfers between devices with their start and end apart: 3, of which 2 were waited for; matrix products, arithmetic and copies ran while one was open for 0% of the time, Pallas kernels for 19%

profile of v1, /device:TPU:0, one launch (start us, length us, event | category | flops | bytes accessed | tf_op | source)
XLA Modules:
  0.0 45.0 jit_solution(15748636580100365083)
XLA Ops:
  0.6 0.0 copy-start.3
  0.6 0.0 copy-start.9
  0.7 0.0 copy-start.8
  0.7 0.0 copy-start.7
  0.7 0.0 copy-start.6
  2.0 0.8 %slice.3 = bf16[31,512]{1,0:T(8,128)(2,1)S(1)} slice(bf16[512,512]{1,0:T(8,128)(2,1)} %t_ref.3), slice={[481:512], [0:512]} | slice | bytes 63488 | tf_op jit(solution)/shard_map/slice | solution.py:253
  2.8 1.9 %pad_maximum_fusion = bf16[544,512]{1,0:T(8,128)(2,1)} fusion(bf16[512,512]{1,0:T(8,128)(2,1)} %bitcast.10, bf16[31,512]{1,0:T(8,128)(2,1)S(1)} %slice.3, bf16[1,512]{1,0:T(2,128)(2,1)S(1)} %fusion), kind=kLoop, calls=%fused_computation | loop fusion | flops 1671168 | bytes 1114112 | tf_op jit(solution)/shard_map/concatenate | solution.py:253
  4.8 5.0 %collective-permute-start.1 = (bf16[544,512]{1,0:T(8,128)(2,1)}, bf16[544,512]{1,0:T(8,128)(2,1)S(1)}, u32[]{:S(2)}, u32[]{:S(2)}) collective-permute-start(bf16[544,512]{1,0:T(8,128)(2,1)} %pad_maximum_fusion), channel_id=1, source_target_pairs={{0,4},{4,8},{8,12},{1,5},{5,9},{9,13},{2,6},{6,10},{10,14},{3,7},{... | collective-permute-start | bytes 1671176 | tf_op jit(solution)/shard_map/ppermute | solution.py:21
  9.7 0.0 copy-done.3
  9.7 1.3 %collective-permute-start = (bf16[512,512]{1,0:T(8,128)(2,1)S(1)}, bf16[512,512]{1,0:T(8,128)(2,1)S(1)}, u32[]{:S(2)}, u32[]{:S(2)}) collective-permute-start(bf16[512,512]{1,0:T(8,128)(2,1)S(1)} %copy-done.3), channel_id=1, source_target_pairs={{4,0},{8,4},{12,8},{5,1},{9,5},{13,9},{6,2},{10,6},{14,10},{7,3},{... | collective-permute-start | bytes 1572872 | tf_op jit(solution)/shard_map/ppermute | solution.py:21
  11.0 0.0 copy-done.9
  11.0 0.1 copy.10.index_ref
  11.1 0.0 copy-done.8
  11.1 0.0 copy-done.7
  11.1 0.0 copy-done.6
  11.1 1.5 %weights.1 = (bf16[2304,256]{1,0:T(8,128)(2,1)S(1)}, bf16[512,512]{1,0:T(8,128)(2,1)S(1)}, bf16[128,256]{1,0:T(8,128)(2,1)S(1)}) custom-call(bf16[16,31]{1,0:T(8,128)(2,1)S(1)} %copy-done.6, s32[1,15,2]{2,1,0:T(8,128)S(1)} %copy.10.index_ref, f32[1,15]{1,0:T(1,128)S(1)} %copy-done.7, bf16[1,31]{1,0:T(2,128)(2,1)S(1)} %bitcast.13), custom_call_target="tpu_custom_call" | custom-call | flops 67108864 | bytes 2097152 | tf_op jit(solution)/shard_map/weights/pallas_call | solution.py:260
  12.6 0.0 copy-start.1
  12.7 0.0 copy-start
  12.7 3.0 %own.1.m1_ref = f32[4,512,128]{2,1,0:T(8,128)S(1)} custom-call(bf16[512,512]{1,0:T(8,128)(2,1)S(1)} %copy-done.3, bf16[2304,256]{1,0:T(8,128)(2,1)S(1)} %get-tuple-element.7.w_ref), custom_call_target="tpu_custom_call" | custom-call | flops 1207959552 | bytes 2097152 | tf_op jit(solution)/shard_map/own/pallas_call | solution.py:272
  15.6 0.0 copy-done.1
  15.6 9.4 %collective-permute-done.next_ref = bf16[512,512]{1,0:T(8,128)(2,1)S(1)} collective-permute-done((bf16[512,512]{1,0:T(8,128)(2,1)S(1)}, bf16[512,512]{1,0:T(8,128)(2,1)S(1)}, u32[]{:S(2)}, u32[]{:S(2)}) %collective-permute-start) | collective-permute-done | bytes 524320 | tf_op jit(solution)/shard_map/ppermute | solution.py:21
  25.0 0.0 collective-permute-done.1.msg_ref
  25.0 0.0 copy-done
  25.0 5.0 %filter.1 = (bf16[4,144,512]{2,1,0:T(8,128)(2,1)}, f32[4,544,128]{2,1,0:T(8,128)S(1)}) custom-call(s32[1,1]{1,0:T(1,128)} %copy.11.off_ref, s32[1,1]{1,0:T(1,128)} %copy.12.live_ref, bf16[512,512]{1,0:T(8,128)(2,1)S(1)} %copy-done.3, bf16[544,512]{1,0:T(8,128)(2,1)S(1)} %collective-permute-done.1.msg_ref, ...), custom_call_target="tpu_custom_call" | custom-call | flops 1073741824 | bytes 2097152 | tf_op jit(solution)/shard_map/filter/pallas_call | solution.py:273
  30.0 0.0 copy-start.4
  30.0 1.0 %copy-done.4 = f32[4,544,128]{2,1,0:T(8,128)} copy-done((f32[4,544,128]{2,1,0:T(8,128)}, f32[4,544,128]{2,1,0:T(8,128)S(1)}, u32[]{:S(2)}) %copy-start.4) | copy-done | bytes 1114136
  31.0 0.0 copy-start.2
  31.0 3.6 %all-to-all-start = ((bf16[4,144,512]{2,1,0:T(8,128)(2,1)}), bf16[4,144,512]{2,1,0:T(8,128)(2,1)S(1)}, u32[]{:S(2)}, u32[]{:S(2)}) async-start(bf16[4,144,512]{2,1,0:T(8,128)(2,1)} %get-tuple-element.11), calls=%async_computation | async-start | bytes 1179648 | tf_op jit(solution)/shard_map/all_to_all | solution.py:289
  34.6 0.0 copy-done.2
  34.6 0.0 copy-start.5
  34.6 1.2 %copy-done.5 = f32[4,544,128]{2,1,0:T(8,128)S(1)} copy-done((f32[4,544,128]{2,1,0:T(8,128)S(1)}, f32[4,544,128]{2,1,0:T(8,128)}, u32[]{:S(2)}) %copy-start.5) | copy-done | bytes 1114136
  35.8 4.0 %tile.1 = bf16[512,512]{1,0:T(8,128)(2,1)} custom-call(s32[1,1]{1,0:T(1,128)} %copy.11.off_ref, bf16[512,512]{1,0:T(8,128)(2,1)S(1)} %collective-permute-done.next_ref, bf16[512,512]{1,0:T(8,128)(2,1)S(1)} %bitcast.12, f32[4,544,128]{2,1,0:T(8,128)S(1)} %copy-done.5, bf16[2304,256]{1,0:T(8,128)(2,1)S(1)} %copy-done.2), custom_call_target="tpu_custom_call" | custom-call | flops 1207959552 | bytes 2097152 | tf_op jit(solution)/shard_map/tile/pallas_call | solution.py:290
  39.8 4.3 %all-to-all-done.recv_ref = bf16[4,144,512]{2,1,0:T(8,128)(2,1)S(1)} async-done(((bf16[4,144,512]{2,1,0:T(8,128)(2,1)}), bf16[4,144,512]{2,1,0:T(8,128)(2,1)S(1)}, u32[]{:S(2)}, u32[]{:S(2)}) %all-to-all-start) | async-done | bytes 589856 | tf_op jit(solution)/shard_map/all_to_all | solution.py:289
  44.1 0.9 %coadd.1 = f32[128,512]{1,0:T(8,128)} custom-call(bf16[4,144,512]{2,1,0:T(8,128)(2,1)S(1)} %all-to-all-done.recv_ref), custom_call_target="tpu_custom_call" | custom-call | flops 1048576 | bytes 2097152 | tf_op jit(solution)/shard_map/coadd/pallas_call | solution.py:294
  (1 shorter events, 0.0 us)
Async XLA Ops:
  0.6 9.1 %copy-start.3 = (bf16[512,512]{1,0:T(8,128)(2,1)S(1)}, bf16[512,512]{1,0:T(8,128)(2,1)}, u32[]{:S(2)}) copy-start(bf16[512,512]{1,0:T(8,128)(2,1)} %t_ref.3) | copy-start | bytes 1572868
  0.6 10.4 %copy-start.9 = (s32[1,15,2]{1,2,0:T(2,128)S(1)}, s32[1,15,2]{1,2,0:T(2,128)}, u32[]{:S(2)}) copy-start(s32[1,15,2]{1,2,0:T(2,128)} %param.13) | copy-start | bytes 364
  0.7 10.5 %copy-start.8 = (bf16[31]{0:T(256)(128)(2,1)S(1)}, bf16[31]{0:T(256)(128)(2,1)}, u32[]{:S(2)}) copy-start(bf16[31]{0:T(256)(128)(2,1)} %param.15) | copy-start | bytes 190
  0.7 10.5 %copy-start.7 = (f32[1,15]{1,0:T(1,128)S(1)}, f32[1,15]{1,0:T(1,128)}, u32[]{:S(2)}) copy-start(f32[1,15]{1,0:T(1,128)} %coeff_ref.1) | copy-start | bytes 184
  0.7 10.5 %copy-start.6 = (bf16[16,31]{1,0:T(8,128)(2,1)S(1)}, bf16[16,31]{1,0:T(8,128)(2,1)}, u32[]{:S(2)}) copy-start(bf16[16,31]{1,0:T(8,128)(2,1)} %bank_ref.1) | copy-start | bytes 2980
  4.8 20.2 %collective-permute-start.1 = (bf16[544,512]{1,0:T(8,128)(2,1)}, bf16[544,512]{1,0:T(8,128)(2,1)S(1)}, u32[]{:S(2)}, u32[]{:S(2)}) collective-permute-start(bf16[544,512]{1,0:T(8,128)(2,1)} %pad_maximum_fusion), channel_id=1, source_target_pairs={{0,4},{4,8},{8,12},{1,5},{5,9},{9,13},{2,6},{6,10},{10,14},{3,7},{... | collective-permute-start | bytes 1671176 | tf_op jit(solution)/shard_map/ppermute | solution.py:21
  9.7 15.3 %collective-permute-start = (bf16[512,512]{1,0:T(8,128)(2,1)S(1)}, bf16[512,512]{1,0:T(8,128)(2,1)S(1)}, u32[]{:S(2)}, u32[]{:S(2)}) collective-permute-start(bf16[512,512]{1,0:T(8,128)(2,1)S(1)} %copy-done.3), channel_id=1, source_target_pairs={{4,0},{8,4},{12,8},{5,1},{9,5},{13,9},{6,2},{10,6},{14,10},{7,3},{... | collective-permute-start | bytes 1572872 | tf_op jit(solution)/shard_map/ppermute | solution.py:21
  12.6 3.0 %copy-start.1 = (bf16[2304,256]{1,0:T(8,128)(2,1)}, bf16[2304,256]{1,0:T(8,128)(2,1)S(1)}, u32[]{:S(2)}) copy-start(bf16[2304,256]{1,0:T(8,128)(2,1)S(1)} %get-tuple-element.7.w_ref) | copy-start | bytes 3538948
  12.7 12.4 %copy-start = (bf16[512,1,512]{2,0,1:T(8,128)(2,1)S(1)}, bf16[512,1,512]{2,0,1:T(8,128)(2,1)}, u32[]{:S(2)}) copy-start(bf16[512,1,512]{2,0,1:T(8,128)(2,1)} %param.9) | copy-start | bytes 1572868
  30.0 1.0 %copy-start.4 = (f32[4,544,128]{2,1,0:T(8,128)}, f32[4,544,128]{2,1,0:T(8,128)S(1)}, u32[]{:S(2)}) copy-start(f32[4,544,128]{2,1,0:T(8,128)S(1)} %get-tuple-element.10.m_ref) | copy-start | bytes 3342340
  31.0 3.6 %copy-start.2 = (bf16[2304,256]{1,0:T(8,128)(2,1)S(1)}, bf16[2304,256]{1,0:T(8,128)(2,1)}, u32[]{:S(2)}) copy-start(bf16[2304,256]{1,0:T(8,128)(2,1)} %copy-done.1) | copy-start | bytes 3538948
  31.0 13.1 %all-to-all-start = ((bf16[4,144,512]{2,1,0:T(8,128)(2,1)}), bf16[4,144,512]{2,1,0:T(8,128)(2,1)S(1)}, u32[]{:S(2)}, u32[]{:S(2)}) async-start(bf16[4,144,512]{2,1,0:T(8,128)(2,1)} %get-tuple-element.11), calls=%async_computation | async-start | bytes 1179648 | tf_op jit(solution)/shard_map/all_to_all | solution.py:289
  34.6 1.2 %copy-start.5 = (f32[4,544,128]{2,1,0:T(8,128)S(1)}, f32[4,544,128]{2,1,0:T(8,128)}, u32[]{:S(2)}) copy-start(f32[4,544,128]{2,1,0:T(8,128)} %copy-done.4) | copy-start | bytes 3342340

commit v2 on v1

--- a/solution.py
+++ b/solution.py
@@ -26,7 +26,7 @@
 
 
 def params():
-    return pltpu.CompilerParams(vmem_limit_bytes=48 * 1024 * 1024)
+    return pltpu.CompilerParams(vmem_limit_bytes=20 * 1024 * 1024)
 
 
 VM = pl.BlockSpec(memory_space=pltpu.VMEM)
@@ -77,7 +77,16 @@
                 dst[c, pl.ds(dst_row + GROUPS * h + i, count, stride=B), :] = rows[i]
 
 
-def weights_kernel(bank_ref, index_ref, coeff_ref, psf_ref, w_ref, pcol_ref, prow_ref):
+def weights_kernel(
+    off_ref, live_ref, t_ref, bank_ref, index_ref, coeff_ref, psf_ref, w_ref, pcol_ref, prow_ref, msg_ref
+):
+    edge = 2 * B
+    rows, cols = t_ref.shape
+    lane = iota((1, cols), 1)
+    off = off_ref[0, 0]
+    note = jnp.where(lane == 0, off // B, jnp.where(lane == 1, off % B, live_ref[0, 0]))
+    tail = t_ref[rows - edge : rows, :].astype(F32)
+    msg_ref[...] = jnp.where(iota((edge, cols), 0) == 0, note.astype(F32), tail).astype(BF16)
     kernels = index_ref.shape[1]
     profs, taps = bank_ref.shape
     half = taps // 2
@@ -140,46 +149,84 @@
         dst[c, dst_row : dst_row + rows, :] = value[:, c * LANES : (c + 1) * LANES]
 
 
-def own_kernel(t_ref, w_ref, m_ref, src, xs, rs):
+def tile_diff(sky, m, base, first, last):
+    row = iota(m.shape, 0) + (base - B)
+    return jnp.where((row >= first) & (row < last), sky - m, 0.0).astype(BF16)
+
+
+def filter_inner(sci, start, first, last, m_ref, pcol_ref, edge_ref, filt_ref, diff):
+    chunks, rows, _ = m_ref.shape
+    edge = 2 * B
+    for c in range(chunks):
+        part = slice(c * LANES, (c + 1) * LANES)
+        sky = sci[c, pl.ds(start, rows + edge), :]
+        edge_ref[c, 0:edge, :] = sky[0:edge]
+        edge_ref[c, edge:, :] = sky[rows:]
+        diff[:, part] = tile_diff(sky[edge:rows], m_ref[c, B : rows - B, :], edge, first, last)
+    filt_ref[...] = jnp.dot(diff[...], pcol_ref[...], preferred_element_type=F32).astype(BF16)
+
+
+def own_kernel(off_ref, t_ref, sci_ref, w_ref, pcol_ref, m_ref, edge_ref, filt_ref, src, xs, rs, sci, diff):
+    rows = t_ref.shape[0]
     to_chunks(src, 0, t_ref[...])
-    conv_blocks(src, t_ref.shape[0] // B, w_ref, xs, rs, m_ref, 0, rs.shape[0] // 2)
-
-
-def filter_kernel(
-    off_ref, live_ref, t_ref, msg_ref, next_ref, sci_ref, m1_ref, w_ref, pcol_ref, prow_ref,
-    out_ref, m_ref, src, xs, rs, strip, sa, sb, diff, filt,
+    conv_blocks(src, rows // B, w_ref, xs, rs, m_ref, 0, rs.shape[0] // 2)
+    off = off_ref[0, 0]
+    to_chunks(sci, rows, sci_ref[...])
+    filter_inner(sci, rows - B - off, off, off + rows, m_ref, pcol_ref, edge_ref, filt_ref, diff)
+
+
+def read_note(msg_ref):
+    note = msg_ref[0:B, 0:LANES].astype(F32)
+    return (note[0, 0] * B + note[0, 1]).astype(jnp.int32), note[0, 2]
+
+
+def before_kernel(msg_ref, sci_ref, m_ref, pcol_ref, edge_ref, filt_ref, sci, diff):
+    rows = sci_ref.shape[0]
+    off, _ = read_note(msg_ref)
+    to_chunks(sci, 0, sci_ref[...])
+    filter_inner(sci, rows - B - off, off - rows, off, m_ref, pcol_ref, edge_ref, filt_ref, diff)
+
+
+def join_kernel(
+    off_ref, live_ref, t_ref, msg_ref, next_ref, w_ref, pcol_ref, prow_ref, edge_a, edge_b, filt_a, filt_b,
+    out_ref, m_ref, src, xs, rs, strip, diff, sides,
 ):
     rows, cols = t_ref.shape
-    ext = rows + 2 * B
     edge = 2 * B
-    to_chunks(src, 0, msg_ref[0:edge, :])
+    to_chunks(src, 0, msg_ref[...])
     to_chunks(src, edge, t_ref[0:edge, :])
     to_chunks(src, 2 * edge, t_ref[rows - edge : rows, :])
     to_chunks(src, 3 * edge, next_ref[0:edge, :])
     conv_blocks(src, 8, w_ref, xs, rs, strip, 0, rs.shape[0])
     m_ref[:, 0:edge, :] = strip[:, B : B + edge, :]
-    m_ref[:, edge : rows, :] = m1_ref[:, B : rows - B, :]
-    m_ref[:, rows : rows + edge, :] = strip[:, 5 * B : 5 * B + edge, :]
-    to_chunks(sa, rows, sci_ref[...])
-    to_chunks(sb, 0, msg_ref[edge : edge + rows, :])
-    notes = msg_ref[0:B, 0:LANES].astype(F32)
+    m_ref[:, edge:, :] = strip[:, 5 * B : 5 * B + edge, :]
     off_a = off_ref[0, 0]
     live_a = live_ref[0, 0].astype(F32)
-    off_b = (notes[0, 0] * B + notes[0, 1]).astype(jnp.int32)
-    live_b = notes[0, 2]
-    tile_row = iota((ext, LANES), 0) - B
-    in_a = (tile_row >= off_a) & (tile_row < off_a + rows)
-    in_b = tile_row < off_b
-    for c in range(cols // LANES):
-        part = slice(c * LANES, (c + 1) * LANES)
-        m = m_ref[c]
-        a = sa[c, pl.ds(rows - B - off_a, ext), :]
-        b = sb[c, pl.ds(rows - B - off_b, ext), :]
-        diff[0, :, part] = jnp.where(in_a, a - m, 0.0).astype(BF16)
-        diff[1, :, part] = jnp.where(in_b, b - m, 0.0).astype(BF16)
-    for s in range(2):
-        filt[s, 0:ext, :] = jnp.dot(diff[s], pcol_ref[...], preferred_element_type=F32).astype(BF16)
-        filt[s, ext:, :] = jnp.zeros((filt.shape[1] - ext, cols), BF16)
+    off_b, live_b = read_note(msg_ref)
+    for s, (side, first, last) in enumerate(((edge_a, off_a, off_a + rows), (edge_b, off_b - rows, off_b))):
+        for c in range(cols // LANES):
+            part = slice(c * LANES, (c + 1) * LANES)
+            for k, base in enumerate((0, rows)):
+                span = slice(k * edge, (k + 1) * edge)
+                at = (2 * s + k) * edge
+                diff[at : at + edge, part] = tile_diff(side[c, span, :], m_ref[c, span, :], base, first, last)
+    sides[...] = jnp.dot(diff[...], pcol_ref[...], preferred_element_type=F32).astype(BF16)
+    inner = (filt_a, filt_b)
+
+    def rows_of(s, low, high):
+        pieces = []
+        for start, stop, ref, at in (
+            (0, edge, sides, 2 * s * edge),
+            (edge, rows, inner[s], 0),
+            (rows, rows + edge, sides, (2 * s + 1) * edge),
+        ):
+            a, b = max(low, start), min(high, stop)
+            if a < b:
+                pieces.append(ref[at + a - start : at + b - start, :])
+        if high > rows + edge:
+            pieces.append(jnp.zeros((high - max(low, rows + edge), cols), BF16))
+        return jnp.concatenate(pieces, axis=0)
+
     share, depth = prow_ref.shape
     prow = prow_ref[...].astype(F32)
     out_row = iota((share, depth), 0)
@@ -188,9 +235,8 @@
         row = out_row + q * share
         left = jnp.where(row >= off_a, prow * live_a, 0.0).astype(BF16)
         right = jnp.where(row < off_b, prow * live_b, 0.0).astype(BF16)
-        span = slice(q * share, q * share + depth)
-        total = jnp.dot(left, filt[0, span, :], preferred_element_type=F32)
-        total += jnp.dot(right, filt[1, span, :], preferred_element_type=F32)
+        total = jnp.dot(left, rows_of(0, q * share, q * share + depth), preferred_element_type=F32)
+        total += jnp.dot(right, rows_of(1, q * share, q * share + depth), preferred_element_type=F32)
         out_ref[q, 0:share, :] = total.astype(BF16)
         start = jnp.clip(off_a - q * share, 0, share).astype(F32)
         stop = jnp.clip(off_b - q * share, 0, share).astype(F32)
@@ -198,11 +244,13 @@
         out_ref[q, share : share + B, :] = note.astype(BF16)
 
 
-def tile_kernel(off_ref, next_ref, sci_ref, m_ref, w_ref, out_ref, src, xs, rs, big):
+def tile_kernel(off_ref, next_ref, sci_ref, m1_ref, edge_ref, w_ref, out_ref, src, xs, rs, big):
     rows, cols = next_ref.shape
     to_chunks(src, 0, next_ref[...])
     conv_blocks(src, rows // B, w_ref, xs, rs, big, rows, rs.shape[0] // 2)
-    big[:, 0 : rows + B, :] = m_ref[:, B : rows + 2 * B, :]
+    big[:, 0:B, :] = edge_ref[:, B : 2 * B, :]
+    big[:, B : rows - B, :] = m1_ref[:, B : rows - B, :]
+    big[:, rows - B : rows + B, :] = edge_ref[:, 2 * B : 4 * B, :]
     off = off_ref[0, 0]
     for c in range(cols // LANES):
         part = slice(c * LANES, (c + 1) * LANES)
@@ -244,24 +292,21 @@
     sharers = lax.axis_size("visit") * lax.axis_size("band")
     share = rows // sharers
     chunks, blocks = cols // LANES, cols // B
-    ext = rows + 2 * B
     edge = 2 * B
+    inner = rows - edge
     sci = science[:, 0, :]
-    off = offsets[0, 0]
-    lane = jnp.arange(cols, dtype=jnp.int32)
-    note = jnp.where(lane == 0, off // B, jnp.where(lane == 1, off % B, live_flags[0, 0])).astype(BF16)
-    msg = jnp.concatenate([note[None], template[rows - edge + 1 :], sci], axis=0)
-    msg = shifted(msg, "patch", 1)
+    before = shifted(science, "patch", 1)[:, 0, :]
     following = shifted(template, "patch", -1)
 
     sds = jax.ShapeDtypeStruct
     deep = 9 * CH
     depth = -(-(share + edge) // LANES) * LANES
-    w, pcol, prow = call(
+    w, pcol, prow, msg = call(
         weights_kernel,
-        (sds((deep, CH), BF16), sds((cols, cols), BF16), sds((share, depth), BF16)),
-        [VM] * 4, [], 1 << 26, "weights",
-    )(bank, basis_index, coeff, psf_profile[None])
+        (sds((deep, CH), BF16), sds((cols, cols), BF16), sds((share, depth), BF16), sds((edge, cols), BF16)),
+        [SM, SM] + [VM] * 5, [], 1 << 26, "weights",
+    )(offsets, live_flags, template, bank, basis_index, coeff, psf_profile[None])
+    msg = shifted(msg, "patch", 1)
     count = rows // B
     conv_scratch = [
         pltpu.VMEM((chunks, rows, LANES), F32),
@@ -269,28 +314,32 @@
         pltpu.VMEM((blocks, count, CH), F32),
     ]
     conv_flops = 2 * rows * cols * deep
-    m1 = call(own_kernel, sds((chunks, rows, LANES), F32), [VM] * 2, conv_scratch, conv_flops, "own")(template, w)
-    out, m = call(
-        filter_kernel,
-        (sds((sharers, share + B, cols), BF16), sds((chunks, ext, LANES), F32)),
-        [SM, SM] + [VM] * 8,
+    sky_scratch = [pltpu.VMEM((chunks, 2 * rows + B, LANES), F32), pltpu.VMEM((inner, cols), BF16)]
+    sides = (sds((chunks, 2 * edge, LANES), F32), sds((inner, cols), BF16))
+    m1, edge_a, filt_a = call(
+        own_kernel, (sds((chunks, rows, LANES), F32),) + sides, [SM] + [VM] * 4,
+        conv_scratch + sky_scratch, conv_flops, "own",
+    )(offsets, template, sci, w, pcol)
+    edge_b, filt_b = call(before_kernel, sides, [VM] * 4, sky_scratch, 1 << 28, "before")(msg, before, m1, pcol)
+    out, m_edge = call(
+        join_kernel,
+        (sds((sharers, share + B, cols), BF16), sds((chunks, 2 * edge, LANES), F32)),
+        [SM, SM] + [VM] * 10,
         [
             pltpu.VMEM((chunks, 8 * B, LANES), F32),
             pltpu.VMEM((3, blocks + 2, 8, CH), F32),
             pltpu.VMEM((blocks, 8, CH), F32),
             pltpu.VMEM((chunks, 8 * B, LANES), F32),
-            pltpu.VMEM((chunks, 2 * rows + B, LANES), F32),
-            pltpu.VMEM((chunks, 2 * rows + B, LANES), F32),
-            pltpu.VMEM((2, ext, cols), BF16),
-            pltpu.VMEM((2, rows - share + depth, cols), BF16),
+            pltpu.VMEM((4 * edge, cols), BF16),
+            pltpu.VMEM((4 * edge, cols), BF16),
         ],
-        1 << 30, "filter",
-    )(offsets, live_flags, template, msg, following, sci, m1, w, pcol, prow)
+        1 << 29, "join",
+    )(offsets, live_flags, template, msg, following, w, pcol, prow, edge_a, edge_b, filt_a, filt_b)
     recv = lax.all_to_all(out, ("visit", "band"), 0, 0, tiled=True)
     difference = call(
-        tile_kernel, sds((rows, cols), BF16), [SM] + [VM] * 4,
+        tile_kernel, sds((rows, cols), BF16), [SM] + [VM] * 5,
         conv_scratch + [pltpu.VMEM((chunks, 2 * rows, LANES), F32)], conv_flops, "tile",
-    )(offsets, following, sci, m, w)
+    )(offsets, following, sci, m1, m_edge, w)
     detection = call(coadd_kernel, sds((share, cols), F32), [VM], [], 1 << 20, "coadd")(recv)
     return (difference[:, None, :], detection)
 

time: 45.4 us -> 41 us (0.903)
  waiting for transfers between devices: 13.6 us -> 4.48 us
  starting transfers between devices: 9.85 us -> 14.3 us
  local copies, waits for them, and re-layouts: 3.12 us -> 6.3 us
  other arithmetic: 1.91 us -> 0 us
  Pallas kernels: 14.3 us -> 13.4 us
    ppermute x2 -> x3, waiting for transfers between devices: 9.36 us -> 0.01 us  [shifted(): return lax.ppermute(shard, axis, pairs)]
    ppermute x2 -> x3, starting transfers between devices: 6.24 us -> 10.8 us  [shifted(): return lax.ppermute(shard, axis, pairs)]
    unnamed x21 -> x15, local copies, waits for them, and re-layouts: 2.35 us -> 6.3 us
    concatenate x1 -> x0, other arithmetic: 1.9 us -> none  [on_device(): msg = jnp.concatenate([note[None], template[rows - edge + 1:], sci], axis=0)]
    pallas_call x3 -> x4, Pallas kernels: 11.9 us -> 11 us  [the longest x1 3.99 us: on_device(): call(tile_kernel, sds((rows, cols), BF16), [SM] + [VM] * 5, conv_scratch...]
    slice x1 -> x0, local copies, waits for them, and re-layouts: 0.77 us -> none  [on_device(): msg = jnp.concatenate([note[None], template[rows - edge + 1:], sci], axis=0)]
  transfers between devices with their start and end apart: 3 -> 4, of which waited for: 2 -> 1; matrix products, arithmetic and copies ran while one was open for 0% -> 2% of each run, Pallas kernels for 19% -> 23%
where the time goes in v2:
time: 41 us; the launch traced here: 40.5 us
  starting transfers between devices  14.3 us (35%)
  Pallas kernels  13.4 us (33%)
  local copies, waits for them, and re-layouts  6.3 us (15%)
  waiting for transfers between devices  4.48 us (11%)
  between operations  2.02 us (5%)
    ppermute x3, starting transfers between devices, shifted(): return lax.ppermute(shard, axis, pairs)  10.8 us
    unnamed x15, local copies, waits for them, and re-layouts  6.3 us
    all_to_all x1, waiting for transfers between devices, on_device(): recv = lax.all_to_all(out, ('visit', 'band'), 0, 0, tiled=True)  4.47 us
    pallas_call x1, Pallas kernels, on_device(): call(tile_kernel, sds((rows, cols), BF16), [SM] + [VM] * 5, conv_scratch...  3.99 us
    all_to_all x1, starting transfers between devices, on_device(): recv = lax.all_to_all(out, ('visit', 'band'), 0, 0, tiled=True)  3.48 us
    pallas_call x1, Pallas kernels, on_device(): call(own_kernel, (sds((chunks, rows, LANES), F32),) + sides, [SM] + [VM]...  3.41 us
    pallas_call x1, Pallas kernels, on_device(): call(join_kernel, (sds((sharers, share + B, cols), BF16), sds((chunks, 2...  2.97 us
    pallas_call x1, Pallas kernels, on_device(): call(weights_kernel, (sds((deep, CH), BF16), sds((cols, cols), BF16), sds...  1.5 us
  transfers between devices with their start and end apart: 4, of which 1 were waited for; matrix products, arithmetic and copies ran while one was open for 2% of the time, Pallas kernels for 23%

profile of v2, /device:TPU:0, one launch (start us, length us, event | category | flops | bytes accessed | tf_op | source)
XLA Modules:
  0.0 40.5 jit_solution(14718402011187826773)
XLA Ops:
  0.6 5.0 %collective-permute-start.2 = (bf16[512,1,512]{2,0,1:T(8,128)(2,1)}, bf16[512,1,512]{2,0,1:T(8,128)(2,1)S(1)}, u32[]{:S(2)}, u32[]{:S(2)}) collective-permute-start(bf16[512,1,512]{2,0,1:T(8,128)(2,1)} %param.9), channel_id=1, source_target_pairs={{0,4},{4,8},{8,12},{1,5},{5,9},{9,13},{2,6},{6,10},{10,14},{3,7},{... | collective-permute-start | bytes 1572872 | tf_op jit(solution)/shard_map/ppermute | solution.py:21
  5.6 1.3 %collective-permute-start = (bf16[512,512]{1,0:T(8,128)(2,1)}, bf16[512,512]{1,0:T(8,128)(2,1)S(1)}, u32[]{:S(2)}, u32[]{:S(2)}) collective-permute-start(bf16[512,512]{1,0:T(8,128)(2,1)} %t_ref.5), channel_id=1, source_target_pairs={{4,0},{8,4},{12,8},{5,1},{9,5},{13,9},{6,2},{10,6},{14,10},{7,3},{... | collective-permute-start | bytes 1572872 | tf_op jit(solution)/shard_map/ppermute | solution.py:21
  8.2 0.8 %copy.10.index_ref = s32[1,15,2]{2,1,0:T(8,128)S(1)} copy(s32[1,15,2]{1,2,0:T(2,128)} %param.13) | data formatting | bytes 240 | tf_op args[5]
  9.0 0.0 copy-start
  9.0 1.0 %copy-done = bf16[512,512]{1,0:T(8,128)(2,1)S(1)} copy-done((bf16[512,512]{1,0:T(8,128)(2,1)S(1)}, bf16[512,512]{1,0:T(8,128)(2,1)}, u32[]{:S(2)}) %copy-start) | copy-done | bytes 524312
  10.0 0.0 copy-start.2
  10.0 0.7 %copy-done.2 = bf16[16,31]{1,0:T(8,128)(2,1)S(1)} copy-done((bf16[16,31]{1,0:T(8,128)(2,1)S(1)}, bf16[16,31]{1,0:T(8,128)(2,1)}, u32[]{:S(2)}) %copy-start.2) | copy-done | bytes 1016
  10.7 0.0 copy-start.3
  10.7 0.7 %copy-done.3 = f32[1,15]{1,0:T(1,128)S(1)} copy-done((f32[1,15]{1,0:T(1,128)S(1)}, f32[1,15]{1,0:T(1,128)}, u32[]{:S(2)}) %copy-start.3) | copy-done | bytes 84
  11.3 0.0 copy-start.4
  11.3 0.7 %copy-done.4 = bf16[31]{0:T(256)(128)(2,1)S(1)} copy-done((bf16[31]{0:T(256)(128)(2,1)S(1)}, bf16[31]{0:T(256)(128)(2,1)}, u32[]{:S(2)}) %copy-start.4) | copy-done | bytes 86
  12.0 1.5 %weights.1 = (bf16[2304,256]{1,0:T(8,128)(2,1)S(1)}, bf16[512,512]{1,0:T(8,128)(2,1)S(1)}, bf16[128,256]{1,0:T(8,128)(2,1)S(1)}, bf16[32,512]{1,0:T(8,128)(2,1)S(1)}) custom-call(s32[1,1]{1,0:T(1,128)S(6)} %copy.11.off_ref, s32[1,1]{1,0:T(1,128)S(6)} %copy.12.live_ref, bf16[512,512]{1,0:T(8,128)(2,1)S(1)} %copy-done, bf16[16,31]{1,0:T(8,128)(2,1)S(1)} %copy-done.2, ...), custom_call_target="tpu_custom_call" | custom-call | flops 67108864 | bytes 2097152 | tf_op jit(solution)/shard_map/weights/pallas_call | solution.py:304
  13.5 4.6 %collective-permute-start.1 = (bf16[32,512]{1,0:T(8,128)(2,1)S(1)}, bf16[32,512]{1,0:T(8,128)(2,1)S(1)}, u32[]{:S(2)}, u32[]{:S(2)}) collective-permute-start(bf16[32,512]{1,0:T(8,128)(2,1)S(1)} %get-tuple-element.16), channel_id=1, source_target_pairs={{0,4},{4,8},{8,12},{1,5},{5,9},{9,13},{2,6},{6,10},{10,14},{3,7},{... | collective-permute-start | bytes 98312 | tf_op jit(solution)/shard_map/ppermute | solution.py:21
  18.1 0.0 copy-start.5
  18.1 1.0 %copy-done.5 = bf16[512,1,512]{2,0,1:T(8,128)(2,1)S(1)} copy-done((bf16[512,1,512]{2,0,1:T(8,128)(2,1)S(1)}, bf16[512,1,512]{2,0,1:T(8,128)(2,1)}, u32[]{:S(2)}) %copy-start.5) | copy-done | bytes 524312
  19.1 3.4 %own.1 = (f32[4,512,128]{2,1,0:T(8,128)S(1)}, f32[4,64,128]{2,1,0:T(8,128)S(1)}, bf16[480,512]{1,0:T(8,128)(2,1)S(1)}) custom-call(s32[1,1]{1,0:T(1,128)S(6)} %copy.11.off_ref, bf16[512,512]{1,0:T(8,128)(2,1)S(1)} %copy-done, bf16[512,512]{1,0:T(8,128)(2,1)S(1)} %bitcast.6, bf16[2304,256]{1,0:T(8,128)(2,1)S(1)} %get-tuple-element.13.w_ref, ...), custom_call_target="tpu_custom_call" | custom-call | flops 1207959552 | bytes 2097152 | tf_op jit(solution)/shard_map/own/pallas_call | solution.py:319
  22.5 0.0 copy-start.1
  22.5 0.0 collective-permute-done.1.msg_ref
  22.5 0.0 collective-permute-done.2
  22.6 0.6 %before.1 = (f32[4,64,128]{2,1,0:T(8,128)S(1)}, bf16[480,512]{1,0:T(8,128)(2,1)S(1)}) custom-call(bf16[32,512]{1,0:T(8,128)(2,1)S(1)} %collective-permute-done.1.msg_ref, bf16[512,512]{1,0:T(8,128)(2,1)S(1)} %bitcast.4, f32[4,512,128]{2,1,0:T(8,128)S(1)} %get-tuple-element.15.m_ref.m1_ref, bf16[512,512]{1,0:T(8,128)(2,1)S(1)} %get-tuple-element.14.pcol_ref), custom_call_target="tpu_custom_call" | custom-call | flops 268435456 | bytes 2097152 | tf_op jit(solution)/shard_map/before/pallas_call | solution.py:323
  23.1 0.0 collective-permute-done.next_ref
  23.2 0.4 %copy-done.1 = bf16[512,512]{1,0:T(8,128)(2,1)S(1)} copy-done((bf16[512,512]{1,0:T(8,128)(2,1)S(1)}, bf16[512,512]{1,0:T(8,128)(2,1)}, u32[]{:S(2)}) %copy-start.1) | copy-done | bytes 524312
  23.6 3.0 %join.1 = (bf16[4,144,512]{2,1,0:T(8,128)(2,1)}, f32[4,64,128]{2,1,0:T(8,128)S(1)}) custom-call(s32[1,1]{1,0:T(1,128)S(6)} %copy.11.off_ref, s32[1,1]{1,0:T(1,128)S(6)} %copy.12.live_ref, bf16[512,512]{1,0:T(8,128)(2,1)S(1)} %copy-done.1, bf16[32,512]{1,0:T(8,128)(2,1)S(1)} %collective-permute-done.1.msg_ref, ...), custom_call_target="tpu_custom_call" | custom-call | flops 536870912 | bytes 2097152 | tf_op jit(solution)/shard_map/join/pallas_call | solution.py:324
  26.5 3.5 %all-to-all-start = ((bf16[4,144,512]{2,1,0:T(8,128)(2,1)}), bf16[4,144,512]{2,1,0:T(8,128)(2,1)S(1)}, u32[]{:S(2)}, u32[]{:S(2)}) async-start(bf16[4,144,512]{2,1,0:T(8,128)(2,1)} %get-tuple-element.23), calls=%async_computation | async-start | bytes 1179648 | tf_op jit(solution)/shard_map/all_to_all | solution.py:338
  30.0 0.0 copy-start.6
  30.0 1.0 %copy-done.6 = bf16[512,1,512]{2,0,1:T(8,128)(2,1)S(1)} copy-done((bf16[512,1,512]{2,0,1:T(8,128)(2,1)S(1)}, bf16[512,1,512]{2,0,1:T(8,128)(2,1)}, u32[]{:S(2)}) %copy-start.6) | copy-done | bytes 524312
  31.1 4.0 %tile.1 = bf16[512,512]{1,0:T(8,128)(2,1)} custom-call(s32[1,1]{1,0:T(1,128)S(6)} %copy.11.off_ref, bf16[512,512]{1,0:T(8,128)(2,1)S(1)} %collective-permute-done.next_ref, bf16[512,512]{1,0:T(8,128)(2,1)S(1)} %bitcast.7, f32[4,512,128]{2,1,0:T(8,128)S(1)} %get-tuple-element.15.m_ref.m1_ref, f32[4,64,128]{2,1,0:T(8,128)S(1)} %get-tuple-element.22.edge_ref, ...), custom_call_target="tpu_custom_call" | custom-call | flops 1207959552 | bytes 2097152 | tf_op jit(solution)/shard_map/tile/pallas_call | solution.py:339
  35.1 4.5 %all-to-all-done.recv_ref = bf16[4,144,512]{2,1,0:T(8,128)(2,1)S(1)} async-done(((bf16[4,144,512]{2,1,0:T(8,128)(2,1)}), bf16[4,144,512]{2,1,0:T(8,128)(2,1)S(1)}, u32[]{:S(2)}, u32[]{:S(2)}) %all-to-all-start) | async-done | bytes 589856 | tf_op jit(solution)/shard_map/all_to_all | solution.py:338
  39.5 0.9 %coadd.1 = f32[128,512]{1,0:T(8,128)} custom-call(bf16[4,144,512]{2,1,0:T(8,128)(2,1)S(1)} %all-to-all-done.recv_ref), custom_call_target="tpu_custom_call" | custom-call | flops 1048576 | bytes 2097152 | tf_op jit(solution)/shard_map/coadd/pallas_call | solution.py:343
Async XLA Ops:
  0.6 21.9 %collective-permute-start.2 = (bf16[512,1,512]{2,0,1:T(8,128)(2,1)}, bf16[512,1,512]{2,0,1:T(8,128)(2,1)S(1)}, u32[]{:S(2)}, u32[]{:S(2)}) collective-permute-start(bf16[512,1,512]{2,0,1:T(8,128)(2,1)} %param.9), channel_id=1, source_target_pairs={{0,4},{4,8},{8,12},{1,5},{5,9},{9,13},{2,6},{6,10},{10,14},{3,7},{... | collective-permute-start | bytes 1572872 | tf_op jit(solution)/shard_map/ppermute | solution.py:21
  5.6 17.6 %collective-permute-start = (bf16[512,512]{1,0:T(8,128)(2,1)}, bf16[512,512]{1,0:T(8,128)(2,1)S(1)}, u32[]{:S(2)}, u32[]{:S(2)}) collective-permute-start(bf16[512,512]{1,0:T(8,128)(2,1)} %t_ref.5), channel_id=1, source_target_pairs={{4,0},{8,4},{12,8},{5,1},{9,5},{13,9},{6,2},{10,6},{14,10},{7,3},{... | collective-permute-start | bytes 1572872 | tf_op jit(solution)/shard_map/ppermute | solution.py:21
  9.0 1.0 %copy-start = (bf16[512,512]{1,0:T(8,128)(2,1)S(1)}, bf16[512,512]{1,0:T(8,128)(2,1)}, u32[]{:S(2)}) copy-start(bf16[512,512]{1,0:T(8,128)(2,1)} %t_ref.5) | copy-start | bytes 1572868
  10.0 0.7 %copy-start.2 = (bf16[16,31]{1,0:T(8,128)(2,1)S(1)}, bf16[16,31]{1,0:T(8,128)(2,1)}, u32[]{:S(2)}) copy-start(bf16[16,31]{1,0:T(8,128)(2,1)} %bank_ref.1) | copy-start | bytes 2980
  10.7 0.7 %copy-start.3 = (f32[1,15]{1,0:T(1,128)S(1)}, f32[1,15]{1,0:T(1,128)}, u32[]{:S(2)}) copy-start(f32[1,15]{1,0:T(1,128)} %coeff_ref.1) | copy-start | bytes 184
  11.3 0.7 %copy-start.4 = (bf16[31]{0:T(256)(128)(2,1)S(1)}, bf16[31]{0:T(256)(128)(2,1)}, u32[]{:S(2)}) copy-start(bf16[31]{0:T(256)(128)(2,1)} %param.15) | copy-start | bytes 190
  13.5 9.0 %collective-permute-start.1 = (bf16[32,512]{1,0:T(8,128)(2,1)S(1)}, bf16[32,512]{1,0:T(8,128)(2,1)S(1)}, u32[]{:S(2)}, u32[]{:S(2)}) collective-permute-start(bf16[32,512]{1,0:T(8,128)(2,1)S(1)} %get-tuple-element.16), channel_id=1, source_target_pairs={{0,4},{4,8},{8,12},{1,5},{5,9},{9,13},{2,6},{6,10},{10,14},{3,7},{... | collective-permute-start | bytes 98312 | tf_op jit(solution)/shard_map/ppermute | solution.py:21
  18.1 1.0 %copy-start.5 = (bf16[512,1,512]{2,0,1:T(8,128)(2,1)S(1)}, bf16[512,1,512]{2,0,1:T(8,128)(2,1)}, u32[]{:S(2)}) copy-start(bf16[512,1,512]{2,0,1:T(8,128)(2,1)} %param.9) | copy-start | bytes 1572868
  22.5 1.1 %copy-start.1 = (bf16[512,512]{1,0:T(8,128)(2,1)S(1)}, bf16[512,512]{1,0:T(8,128)(2,1)}, u32[]{:S(2)}) copy-start(bf16[512,512]{1,0:T(8,128)(2,1)} %t_ref.5) | copy-start | bytes 1572868
  26.5 13.0 %all-to-all-start = ((bf16[4,144,512]{2,1,0:T(8,128)(2,1)}), bf16[4,144,512]{2,1,0:T(8,128)(2,1)S(1)}, u32[]{:S(2)}, u32[]{:S(2)}) async-start(bf16[4,144,512]{2,1,0:T(8,128)(2,1)} %get-tuple-element.23), calls=%async_computation | async-start | bytes 1179648 | tf_op jit(solution)/shard_map/all_to_all | solution.py:338
  30.0 1.0 %copy-start.6 = (bf16[512,1,512]{2,0,1:T(8,128)(2,1)S(1)}, bf16[512,1,512]{2,0,1:T(8,128)(2,1)}, u32[]{:S(2)}) copy-start(bf16[512,1,512]{2,0,1:T(8,128)(2,1)} %param.9) | copy-start | bytes 1572868

commit v3 on v2

--- a/solution.py
+++ b/solution.py
@@ -25,12 +25,9 @@
     return lax.broadcasted_iota(jnp.int32, shape, dim)
 
 
-def params():
-    return pltpu.CompilerParams(vmem_limit_bytes=20 * 1024 * 1024)
-
-
+LIMIT = 58
 VM = pl.BlockSpec(memory_space=pltpu.VMEM)
-SM = pl.BlockSpec(memory_space=pltpu.SMEM)
+HBM = pl.BlockSpec(memory_space=pltpu.HBM)
 
 
 def group_transpose(parts):
@@ -77,27 +74,36 @@
                 dst[c, pl.ds(dst_row + GROUPS * h + i, count, stride=B), :] = rows[i]
 
 
-def weights_kernel(
-    off_ref, live_ref, t_ref, bank_ref, index_ref, coeff_ref, psf_ref, w_ref, pcol_ref, prow_ref, msg_ref
+def column(row):
+    size = row.shape[1]
+    diag = iota((size, size), 0) == iota((size, size), 1)
+    return jnp.sum(jnp.where(diag, row, jnp.zeros_like(row)), axis=1, keepdims=True)
+
+
+def first_kernel(
+    off_hbm, live_hbm, t_hbm, sci_hbm, bank_hbm, index_hbm, coeff_hbm, psf_hbm,
+    w_ref, pcol_ref, prow_ref, note_ref, ends_ref, m_ref, edge_ref, filt_ref,
+    off_ref, live_ref, t_ref, sci_ref, bank_ref, index_ref, coeff_ref, psf_ref, sems,
+    src, xs, rs, sci, diff,
 ):
-    edge = 2 * B
-    rows, cols = t_ref.shape
-    lane = iota((1, cols), 1)
-    off = off_ref[0, 0]
-    note = jnp.where(lane == 0, off // B, jnp.where(lane == 1, off % B, live_ref[0, 0]))
-    tail = t_ref[rows - edge : rows, :].astype(F32)
-    msg_ref[...] = jnp.where(iota((edge, cols), 0) == 0, note.astype(F32), tail).astype(BF16)
-    kernels = index_ref.shape[1]
+    pairs = (
+        (bank_hbm, bank_ref), (index_hbm, index_ref), (coeff_hbm, coeff_ref), (psf_hbm, psf_ref),
+        (off_hbm, off_ref), (live_hbm, live_ref), (t_hbm, t_ref), (sci_hbm, sci_ref),
+    )
+    copies = [pltpu.make_async_copy(a, b, sems.at[n]) for n, (a, b) in enumerate(pairs)]
+    for copy in copies:
+        copy.start()
+    for copy in copies[:4]:
+        copy.wait()
     profs, taps = bank_ref.shape
     half = taps // 2
     delta = B - half
     bank = bank_ref[...]
-    index = index_ref[0]
-    labels = iota((kernels, profs), 1)
-    pick_row = (index[:, 0:1] == labels).astype(F32).astype(BF16)
-    pick_col = (index[:, 1:2] == labels).astype(F32).astype(BF16)
-    diag = iota((kernels, kernels), 0) == iota((kernels, kernels), 1)
-    weight = jnp.sum(jnp.where(diag, coeff_ref[...], 0.0), axis=1, keepdims=True)
+    index = index_ref[0].astype(F32)
+    labels = iota((index.shape[1], profs), 1).astype(F32)
+    pick_row = (column(index[0:1]) == labels).astype(F32).astype(BF16)
+    pick_col = (column(index[1:2]) == labels).astype(F32).astype(BF16)
+    weight = column(coeff_ref[...])
     rowprof = (weight * jnp.dot(pick_row, bank, preferred_element_type=F32)).astype(BF16)
     colprof = jnp.dot(pick_col, bank, preferred_element_type=F32).astype(BF16)
     span = 3 * B
@@ -140,6 +146,21 @@
     for t in range(taps):
         block = jnp.where(tap == t, psf[:, t : t + 1], block)
     prow_ref[...] = block.astype(BF16)
+    for copy in copies[4:]:
+        copy.wait()
+    edge = 2 * B
+    rows, cols = t_ref.shape
+    lane = iota((1, cols), 1)
+    off = off_ref[0, 0]
+    note = jnp.where(lane == 0, off // B, jnp.where(lane == 1, off % B, live_ref[0, 0]))
+    tail = t_ref[rows - edge : rows, :].astype(F32)
+    note_ref[...] = jnp.where(iota((edge, cols), 0) == 0, note.astype(F32), tail).astype(BF16)
+    ends_ref[0:edge, :] = t_ref[0:edge, :]
+    ends_ref[edge:, :] = t_ref[rows - edge : rows, :]
+    to_chunks(src, 0, t_ref[...])
+    conv_blocks(src, rows // B, w_ref, xs, rs, m_ref, 0, rs.shape[0] // 2)
+    to_chunks(sci, rows, sci_ref[...])
+    filter_inner(sci, rows - B - off, off, off + rows, m_ref, pcol_ref, edge_ref, filt_ref, diff)
 
 
 def to_chunks(dst, dst_row, value):
@@ -166,15 +187,6 @@
     filt_ref[...] = jnp.dot(diff[...], pcol_ref[...], preferred_element_type=F32).astype(BF16)
 
 
-def own_kernel(off_ref, t_ref, sci_ref, w_ref, pcol_ref, m_ref, edge_ref, filt_ref, src, xs, rs, sci, diff):
-    rows = t_ref.shape[0]
-    to_chunks(src, 0, t_ref[...])
-    conv_blocks(src, rows // B, w_ref, xs, rs, m_ref, 0, rs.shape[0] // 2)
-    off = off_ref[0, 0]
-    to_chunks(sci, rows, sci_ref[...])
-    filter_inner(sci, rows - B - off, off, off + rows, m_ref, pcol_ref, edge_ref, filt_ref, diff)
-
-
 def read_note(msg_ref):
     note = msg_ref[0:B, 0:LANES].astype(F32)
     return (note[0, 0] * B + note[0, 1]).astype(jnp.int32), note[0, 2]
@@ -188,20 +200,18 @@
 
 
 def join_kernel(
-    off_ref, live_ref, t_ref, msg_ref, next_ref, w_ref, pcol_ref, prow_ref, edge_a, edge_b, filt_a, filt_b,
+    note_ref, ends_ref, msg_ref, next_ref, w_ref, pcol_ref, prow_ref, edge_a, edge_b, filt_a, filt_b,
     out_ref, m_ref, src, xs, rs, strip, diff, sides,
 ):
-    rows, cols = t_ref.shape
+    rows, cols = next_ref.shape
     edge = 2 * B
     to_chunks(src, 0, msg_ref[...])
-    to_chunks(src, edge, t_ref[0:edge, :])
-    to_chunks(src, 2 * edge, t_ref[rows - edge : rows, :])
+    to_chunks(src, edge, ends_ref[...])
     to_chunks(src, 3 * edge, next_ref[0:edge, :])
     conv_blocks(src, 8, w_ref, xs, rs, strip, 0, rs.shape[0])
     m_ref[:, 0:edge, :] = strip[:, B : B + edge, :]
     m_ref[:, edge:, :] = strip[:, 5 * B : 5 * B + edge, :]
-    off_a = off_ref[0, 0]
-    live_a = live_ref[0, 0].astype(F32)
+    off_a, live_a = read_note(note_ref)
     off_b, live_b = read_note(msg_ref)
     for s, (side, first, last) in enumerate(((edge_a, off_a, off_a + rows), (edge_b, off_b - rows, off_b))):
         for c in range(cols // LANES):
@@ -244,14 +254,14 @@
         out_ref[q, share : share + B, :] = note.astype(BF16)
 
 
-def tile_kernel(off_ref, next_ref, sci_ref, m1_ref, edge_ref, w_ref, out_ref, src, xs, rs, big):
+def tile_kernel(note_ref, next_ref, sci_ref, m1_ref, edge_ref, w_ref, out_ref, src, xs, rs, big):
     rows, cols = next_ref.shape
     to_chunks(src, 0, next_ref[...])
     conv_blocks(src, rows // B, w_ref, xs, rs, big, rows, rs.shape[0] // 2)
     big[:, 0:B, :] = edge_ref[:, B : 2 * B, :]
     big[:, B : rows - B, :] = m1_ref[:, B : rows - B, :]
     big[:, rows - B : rows + B, :] = edge_ref[:, 2 * B : 4 * B, :]
-    off = off_ref[0, 0]
+    off, _ = read_note(note_ref)
     for c in range(cols // LANES):
         part = slice(c * LANES, (c + 1) * LANES)
         out_ref[:, part] = (sci_ref[:, part].astype(F32) - big[c, pl.ds(off, rows), :]).astype(BF16)
@@ -274,14 +284,14 @@
         out_ref[:, part] = accum[:, part] * scale
 
 
-def call(body, shapes, specs, scratch, flops, name):
+def call(body, shapes, specs, scratch, flops, name, limit=20):
     return pl.pallas_call(
         body,
         out_shape=shapes,
         in_specs=specs,
         out_specs=jax.tree.map(lambda _: VM, shapes),
         scratch_shapes=scratch,
-        compiler_params=params(),
+        compiler_params=pltpu.CompilerParams(vmem_limit_bytes=limit * 1024 * 1024),
         cost_estimate=pl.CostEstimate(flops=flops, bytes_accessed=1 << 21, transcendentals=0),
         name=name,
     )
@@ -294,19 +304,15 @@
     chunks, blocks = cols // LANES, cols // B
     edge = 2 * B
     inner = rows - edge
-    sci = science[:, 0, :]
     before = shifted(science, "patch", 1)[:, 0, :]
     following = shifted(template, "patch", -1)
 
     sds = jax.ShapeDtypeStruct
     deep = 9 * CH
     depth = -(-(share + edge) // LANES) * LANES
-    w, pcol, prow, msg = call(
-        weights_kernel,
-        (sds((deep, CH), BF16), sds((cols, cols), BF16), sds((share, depth), BF16), sds((edge, cols), BF16)),
-        [SM, SM] + [VM] * 5, [], 1 << 26, "weights",
-    )(offsets, live_flags, template, bank, basis_index, coeff, psf_profile[None])
-    msg = shifted(msg, "patch", 1)
+    sci = science[:, 0, :]
+    taps = psf_profile.shape[0]
+    index = jnp.swapaxes(basis_index, 1, 2)
     count = rows // B
     conv_scratch = [
         pltpu.VMEM((chunks, rows, LANES), F32),
@@ -316,15 +322,26 @@
     conv_flops = 2 * rows * cols * deep
     sky_scratch = [pltpu.VMEM((chunks, 2 * rows + B, LANES), F32), pltpu.VMEM((inner, cols), BF16)]
     sides = (sds((chunks, 2 * edge, LANES), F32), sds((inner, cols), BF16))
-    m1, edge_a, filt_a = call(
-        own_kernel, (sds((chunks, rows, LANES), F32),) + sides, [SM] + [VM] * 4,
-        conv_scratch + sky_scratch, conv_flops, "own",
-    )(offsets, template, sci, w, pcol)
+    w, pcol, prow, note, ends, m1, edge_a, filt_a = call(
+        first_kernel,
+        (
+            sds((deep, CH), BF16), sds((cols, cols), BF16), sds((share, depth), BF16), sds((edge, cols), BF16),
+            sds((2 * edge, cols), BF16), sds((chunks, rows, LANES), F32),
+        ) + sides,
+        [HBM] * 8,
+        [
+            pltpu.SMEM((1, 1), jnp.int32), pltpu.SMEM((1, 1), jnp.int32), pltpu.VMEM((rows, cols), BF16),
+            pltpu.VMEM((rows, cols), BF16), pltpu.VMEM(bank.shape, BF16), pltpu.VMEM(index.shape, jnp.int32),
+            pltpu.VMEM(coeff.shape, F32), pltpu.VMEM((1, taps), BF16), pltpu.SemaphoreType.DMA((8,)),
+        ] + conv_scratch + sky_scratch,
+        conv_flops, "first", LIMIT,
+    )(offsets, live_flags, template, sci, bank, index, coeff, psf_profile[None])
+    msg = shifted(note, "patch", 1)
     edge_b, filt_b = call(before_kernel, sides, [VM] * 4, sky_scratch, 1 << 28, "before")(msg, before, m1, pcol)
     out, m_edge = call(
         join_kernel,
         (sds((sharers, share + B, cols), BF16), sds((chunks, 2 * edge, LANES), F32)),
-        [SM, SM] + [VM] * 10,
+        [VM] * 11,
         [
             pltpu.VMEM((chunks, 8 * B, LANES), F32),
             pltpu.VMEM((3, blocks + 2, 8, CH), F32),
@@ -334,12 +351,12 @@
             pltpu.VMEM((4 * edge, cols), BF16),
         ],
         1 << 29, "join",
-    )(offsets, live_flags, template, msg, following, w, pcol, prow, edge_a, edge_b, filt_a, filt_b)
+    )(note, ends, msg, following, w, pcol, prow, edge_a, edge_b, filt_a, filt_b)
     recv = lax.all_to_all(out, ("visit", "band"), 0, 0, tiled=True)
     difference = call(
-        tile_kernel, sds((rows, cols), BF16), [SM] + [VM] * 5,
+        tile_kernel, sds((rows, cols), BF16), [VM] * 6,
         conv_scratch + [pltpu.VMEM((chunks, 2 * rows, LANES), F32)], conv_flops, "tile",
-    )(offsets, following, sci, m1, m_edge, w)
+    )(note, following, sci, m1, m_edge, w)
     detection = call(coadd_kernel, sds((share, cols), F32), [VM], [], 1 << 20, "coadd")(recv)
     return (difference[:, None, :], detection)
 

time: 41 us -> 44.1 us (1.076)
  Pallas kernels: 13.4 us -> 15.6 us
  waiting for transfers between devices: 4.48 us -> 6.39 us
  local copies, waits for them, and re-layouts: 6.3 us -> 5.15 us
    pallas_call x3 -> x2, Pallas kernels: 8.91 us -> 11.1 us  [the longest x1 7.13 us: on_device(): call(first_kernel, (sds((deep, CH), BF16), sds((cols, cols), BF16), sds((...]
    ppermute x3, waiting for transfers between devices: 0.01 us -> 1.9 us  [shifted(): return lax.ppermute(shard, axis, pairs)]
    unnamed x15 -> x22, local copies, waits for them, and re-layouts: 6.3 us -> 5.15 us
  transfers between devices with their start and end apart: 4 -> 4, of which waited for: 1 -> 2; matrix products, arithmetic and copies ran while one was open for 2% -> 0% of each run, Pallas kernels for 23% -> 27%
where the time goes in v3:
time: 44.1 us; the launch traced here: 43.6 us
  Pallas kernels  15.6 us (35%)
  starting transfers between devices  14.4 us (33%)
  waiting for transfers between devices  6.39 us (14%)
  local copies, waits for them, and re-layouts  5.15 us (12%)
  between operations  2.03 us (5%)
    ppermute x3, starting transfers between devices, shifted(): return lax.ppermute(shard, axis, pairs)  10.8 us
    pallas_call x1, Pallas kernels, on_device(): call(first_kernel, (sds((deep, CH), BF16), sds((cols, cols), BF16), sds((...  7.13 us
    unnamed x22, local copies, waits for them, and re-layouts  5.15 us
    all_to_all x1, waiting for transfers between devices, on_device(): recv = lax.all_to_all(out, ('visit', 'band'), 0, 0, tiled=True)  4.49 us
    pallas_call x1, Pallas kernels, on_device(): call(tile_kernel, sds((rows, cols), BF16), [VM] * 6, conv_scratch + [pltp...  3.96 us
    all_to_all x1, starting transfers between devices, on_device(): recv = lax.all_to_all(out, ('visit', 'band'), 0, 0, tiled=True)  3.61 us
    pallas_call x1, Pallas kernels, on_device(): call(join_kernel, (sds((sharers, share + B, cols), BF16), sds((chunks, 2...  3 us
    ppermute x3, waiting for transfers between devices, shifted(): return lax.ppermute(shard, axis, pairs)  1.9 us
  transfers between devices with their start and end apart: 4, of which 2 were waited for; matrix products, arithmetic and copies ran while one was open for 0% of the time, Pallas kernels for 27%

profile of v3, /device:TPU:0, one launch (start us, length us, event | category | flops | bytes accessed | tf_op | source)
XLA Modules:
  0.0 43.6 jit_solution(6677752605930493039)
XLA Ops:
  0.6 5.0 %collective-permute-start.2 = (bf16[512,1,512]{2,0,1:T(8,128)(2,1)}, bf16[512,1,512]{2,0,1:T(8,128)(2,1)S(1)}, u32[]{:S(2)}, u32[]{:S(2)}) collective-permute-start(bf16[512,1,512]{2,0,1:T(8,128)(2,1)} %param.9), channel_id=1, source_target_pairs={{0,4},{4,8},{8,12},{1,5},{5,9},{9,13},{2,6},{6,10},{10,14},{3,7},{... | collective-permute-start | bytes 1572872 | tf_op jit(solution)/shard_map/ppermute | solution.py:21
  5.6 1.3 %collective-permute-start = (bf16[512,512]{1,0:T(8,128)(2,1)}, bf16[512,512]{1,0:T(8,128)(2,1)S(1)}, u32[]{:S(2)}, u32[]{:S(2)}) collective-permute-start(bf16[512,512]{1,0:T(8,128)(2,1)} %t_hbm.1), channel_id=1, source_target_pairs={{4,0},{8,4},{12,8},{5,1},{9,5},{13,9},{6,2},{10,6},{14,10},{7,3},{... | collective-permute-start | bytes 1572872 | tf_op jit(solution)/shard_map/ppermute | solution.py:21
  8.2 7.1 %first.1 = (bf16[2304,256]{1,0:T(8,128)(2,1)}, bf16[512,512]{1,0:T(8,128)(2,1)}, bf16[128,256]{1,0:T(8,128)(2,1)}, bf16[32,512]{1,0:T(8,128)(2,1)}, bf16[64,512]...) custom-call(s32[1,1]{1,0:T(1,128)S(6)} %copy.10.off_hbm, ...), custom_call_target="tpu_custom_call" | custom-call | flops 1207959552 | bytes 2097152 | tf_op jit(solution)/shard_map/first/pallas_call | solution.py:325
  15.3 4.6 %collective-permute-start.1 = (bf16[32,512]{1,0:T(8,128)(2,1)}, bf16[32,512]{1,0:T(8,128)(2,1)S(1)}, u32[]{:S(2)}, u32[]{:S(2)}) collective-permute-start(bf16[32,512]{1,0:T(8,128)(2,1)} %get-tuple-element.14.note_ref), channel_id=1, source_target_pairs={{0,4},{4,8},{8,12},{1,5},{5,9},{9,13},{2,6},{6,10},{10,14},{3,7},{... | collective-permute-start | bytes 98312 | tf_op jit(solution)/shard_map/ppermute | solution.py:21
  19.9 1.9 %collective-permute-done.1.msg_ref = bf16[32,512]{1,0:T(8,128)(2,1)S(1)} collective-permute-done((bf16[32,512]{1,0:T(8,128)(2,1)}, bf16[32,512]{1,0:T(8,128)(2,1)S(1)}, u32[]{:S(2)}, u32[]{:S(2)}) %collective-permute-start.1) | collective-permute-done | bytes 32800 | tf_op jit(solution)/shard_map/ppermute | solution.py:21
  21.8 0.0 collective-permute-done.2
  21.8 0.0 copy-start
  21.8 1.0 %copy-done = bf16[512,512]{1,0:T(8,128)(2,1)S(1)} copy-done((bf16[512,512]{1,0:T(8,128)(2,1)S(1)}, bf16[512,512]{1,0:T(8,128)(2,1)}, u32[]{:S(2)}) %copy-start) | copy-done | bytes 524312
  22.8 0.0 copy-start.3
  22.8 1.2 %copy-done.3 = f32[4,512,128]{2,1,0:T(8,128)S(1)} copy-done((f32[4,512,128]{2,1,0:T(8,128)S(1)}, f32[4,512,128]{2,1,0:T(8,128)}, u32[]{:S(2)}) %copy-start.3) | copy-done | bytes 1048600
  24.1 0.0 copy-start.1
  24.1 0.0 copy-start.2
  24.1 0.0 copy-start.6
  24.1 0.0 copy-start.7
  24.1 0.0 copy-start.8
  24.1 0.0 copy-start.9
  24.1 0.6 %before.1 = (f32[4,64,128]{2,1,0:T(8,128)S(1)}, bf16[480,512]{1,0:T(8,128)(2,1)S(1)}) custom-call(bf16[32,512]{1,0:T(8,128)(2,1)S(1)} %collective-permute-done.1.msg_ref, bf16[512,512]{1,0:T(8,128)(2,1)S(1)} %bitcast.5, f32[4,512,128]{2,1,0:T(8,128)S(1)} %copy-done.3, bf16[512,512]{1,0:T(8,128)(2,1)S(1)} %copy-done), custom_call_target="tpu_custom_call" | custom-call | flops 268435456 | bytes 2097152 | tf_op jit(solution)/shard_map/before/pallas_call | solution.py:340
  24.7 0.0 collective-permute-done.next_ref
  24.7 0.4 copy-done.1
  25.1 0.4 copy-done.2
  25.5 0.0 copy-done.6
  25.5 0.0 copy-done.7
  25.5 0.0 copy-done.8
  25.5 0.0 copy-done.9
  25.5 0.0 copy-start.5
  25.5 1.0 %copy-done.5 = bf16[480,512]{1,0:T(8,128)(2,1)S(1)} copy-done((bf16[480,512]{1,0:T(8,128)(2,1)S(1)}, bf16[480,512]{1,0:T(8,128)(2,1)}, u32[]{:S(2)}) %copy-start.5) | copy-done | bytes 491544
  26.5 3.0 %join.1 = (bf16[4,144,512]{2,1,0:T(8,128)(2,1)}, f32[4,64,128]{2,1,0:T(8,128)S(1)}) custom-call(bf16[32,512]{1,0:T(8,128)(2,1)S(1)} %copy-done.9, bf16[64,512]{1,0:T(8,128)(2,1)S(1)} %copy-done.8, bf16[32,512]{1,0:T(8,128)(2,1)S(1)} %collective-permute-done.1.msg_ref, bf16[512,512]{1,0:T(8,128)(2,1)S(1)} %collective-permute-done.next_ref, ...), custom_call_target="tpu_custom_call" | custom-call | flops 536870912 | bytes 2097152 | tf_op jit(solution)/shard_map/join/pallas_call | solution.py:341
  29.5 0.0 copy-start.4
  29.5 3.6 %all-to-all-start = ((bf16[4,144,512]{2,1,0:T(8,128)(2,1)}), bf16[4,144,512]{2,1,0:T(8,128)(2,1)S(1)}, u32[]{:S(2)}, u32[]{:S(2)}) async-start(bf16[4,144,512]{2,1,0:T(8,128)(2,1)} %get-tuple-element.25), calls=%async_computation | async-start | bytes 1179648 | tf_op jit(solution)/shard_map/all_to_all | solution.py:355
  33.2 0.0 copy-done.4
  33.2 0.0 copy-start.10
  33.2 1.0 %copy-done.10 = bf16[512,1,512]{2,0,1:T(8,128)(2,1)S(1)} copy-done((bf16[512,1,512]{2,0,1:T(8,128)(2,1)S(1)}, bf16[512,1,512]{2,0,1:T(8,128)(2,1)}, u32[]{:S(2)}) %copy-start.10) | copy-done | bytes 524312
  34.2 4.0 %tile.1 = bf16[512,512]{1,0:T(8,128)(2,1)} custom-call(bf16[32,512]{1,0:T(8,128)(2,1)S(1)} %copy-done.9, bf16[512,512]{1,0:T(8,128)(2,1)S(1)} %collective-permute-done.next_ref, bf16[512,512]{1,0:T(8,128)(2,1)S(1)} %bitcast.7, f32[4,512,128]{2,1,0:T(8,128)S(1)} %copy-done.4, f32[4,64,128]{2,1,0:T(8,128)S(1)} %get-tuple-element.24.edge_ref, ...), custom_call_target="tpu_custom_call" | custom-call | flops 1207959552 | bytes 2097152 | tf_op jit(solution)/shard_map/tile/pallas_call | solution.py:356
  38.2 4.5 %all-to-all-done.recv_ref = bf16[4,144,512]{2,1,0:T(8,128)(2,1)S(1)} async-done(((bf16[4,144,512]{2,1,0:T(8,128)(2,1)}), bf16[4,144,512]{2,1,0:T(8,128)(2,1)S(1)}, u32[]{:S(2)}, u32[]{:S(2)}) %all-to-all-start) | async-done | bytes 589856 | tf_op jit(solution)/shard_map/all_to_all | solution.py:355
  42.7 0.9 %coadd.1 = f32[128,512]{1,0:T(8,128)} custom-call(bf16[4,144,512]{2,1,0:T(8,128)(2,1)S(1)} %all-to-all-done.recv_ref), custom_call_target="tpu_custom_call" | custom-call | flops 1048576 | bytes 2097152 | tf_op jit(solution)/shard_map/coadd/pallas_call | solution.py:360
Async XLA Ops:
  0.6 21.2 %collective-permute-start.2 = (bf16[512,1,512]{2,0,1:T(8,128)(2,1)}, bf16[512,1,512]{2,0,1:T(8,128)(2,1)S(1)}, u32[]{:S(2)}, u32[]{:S(2)}) collective-permute-start(bf16[512,1,512]{2,0,1:T(8,128)(2,1)} %param.9), channel_id=1, source_target_pairs={{0,4},{4,8},{8,12},{1,5},{5,9},{9,13},{2,6},{6,10},{10,14},{3,7},{... | collective-permute-start | bytes 1572872 | tf_op jit(solution)/shard_map/ppermute | solution.py:21
  5.6 19.1 %collective-permute-start = (bf16[512,512]{1,0:T(8,128)(2,1)}, bf16[512,512]{1,0:T(8,128)(2,1)S(1)}, u32[]{:S(2)}, u32[]{:S(2)}) collective-permute-start(bf16[512,512]{1,0:T(8,128)(2,1)} %t_hbm.1), channel_id=1, source_target_pairs={{4,0},{8,4},{12,8},{5,1},{9,5},{13,9},{6,2},{10,6},{14,10},{7,3},{... | collective-permute-start | bytes 1572872 | tf_op jit(solution)/shard_map/ppermute | solution.py:21
  15.3 6.5 %collective-permute-start.1 = (bf16[32,512]{1,0:T(8,128)(2,1)}, bf16[32,512]{1,0:T(8,128)(2,1)S(1)}, u32[]{:S(2)}, u32[]{:S(2)}) collective-permute-start(bf16[32,512]{1,0:T(8,128)(2,1)} %get-tuple-element.14.note_ref), channel_id=1, source_target_pairs={{0,4},{4,8},{8,12},{1,5},{5,9},{9,13},{2,6},{6,10},{10,14},{3,7},{... | collective-permute-start | bytes 98312 | tf_op jit(solution)/shard_map/ppermute | solution.py:21
  21.8 1.0 %copy-start = (bf16[512,512]{1,0:T(8,128)(2,1)S(1)}, bf16[512,512]{1,0:T(8,128)(2,1)}, u32[]{:S(2)}) copy-start(bf16[512,512]{1,0:T(8,128)(2,1)} %get-tuple-element.18.pcol_ref) | copy-start | bytes 1572868
  22.8 1.2 %copy-start.3 = (f32[4,512,128]{2,1,0:T(8,128)S(1)}, f32[4,512,128]{2,1,0:T(8,128)}, u32[]{:S(2)}) copy-start(f32[4,512,128]{2,1,0:T(8,128)} %get-tuple-element.15.m_ref.m1_ref) | copy-start | bytes 3145732
  24.1 1.0 %copy-start.1 = (bf16[512,512]{1,0:T(8,128)(2,1)S(1)}, bf16[512,512]{1,0:T(8,128)(2,1)}, u32[]{:S(2)}) copy-start(bf16[512,512]{1,0:T(8,128)(2,1)} %get-tuple-element.18.pcol_ref) | copy-start | bytes 1572868
  24.1 1.4 %copy-start.2 = (bf16[2304,256]{1,0:T(8,128)(2,1)S(1)}, bf16[2304,256]{1,0:T(8,128)(2,1)}, u32[]{:S(2)}) copy-start(bf16[2304,256]{1,0:T(8,128)(2,1)} %get-tuple-element.17.w_ref) | copy-start | bytes 3538948
  24.1 1.4 %copy-start.6 = (f32[4,64,128]{2,1,0:T(8,128)S(1)}, f32[4,64,128]{2,1,0:T(8,128)}, u32[]{:S(2)}) copy-start(f32[4,64,128]{2,1,0:T(8,128)} %get-tuple-element.20.edge_a) | copy-start | bytes 393220
  24.1 1.4 %copy-start.7 = (bf16[128,256]{1,0:T(8,128)(2,1)S(1)}, bf16[128,256]{1,0:T(8,128)(2,1)}, u32[]{:S(2)}) copy-start(bf16[128,256]{1,0:T(8,128)(2,1)} %get-tuple-element.19.prow_ref) | copy-start | bytes 196612
  24.1 1.4 %copy-start.8 = (bf16[64,512]{1,0:T(8,128)(2,1)S(1)}, bf16[64,512]{1,0:T(8,128)(2,1)}, u32[]{:S(2)}) copy-start(bf16[64,512]{1,0:T(8,128)(2,1)} %get-tuple-element.16.ends_ref) | copy-start | bytes 196612
  24.1 1.4 %copy-start.9 = (bf16[32,512]{1,0:T(8,128)(2,1)S(1)}, bf16[32,512]{1,0:T(8,128)(2,1)}, u32[]{:S(2)}) copy-start(bf16[32,512]{1,0:T(8,128)(2,1)} %get-tuple-element.14.note_ref) | copy-start | bytes 98308
  25.5 1.0 %copy-start.5 = (bf16[480,512]{1,0:T(8,128)(2,1)S(1)}, bf16[480,512]{1,0:T(8,128)(2,1)}, u32[]{:S(2)}) copy-start(bf16[480,512]{1,0:T(8,128)(2,1)} %get-tuple-element.22.filt_a) | copy-start | bytes 1474564
  29.5 3.6 %copy-start.4 = (f32[4,512,128]{2,1,0:T(8,128)S(1)}, f32[4,512,128]{2,1,0:T(8,128)}, u32[]{:S(2)}) copy-start(f32[4,512,128]{2,1,0:T(8,128)} %get-tuple-element.15.m_ref.m1_ref) | copy-start | bytes 3145732
  29.5 13.1 %all-to-all-start = ((bf16[4,144,512]{2,1,0:T(8,128)(2,1)}), bf16[4,144,512]{2,1,0:T(8,128)(2,1)S(1)}, u32[]{:S(2)}, u32[]{:S(2)}) async-start(bf16[4,144,512]{2,1,0:T(8,128)(2,1)} %get-tuple-element.25), calls=%async_computation | async-start | bytes 1179648 | tf_op jit(solution)/shard_map/all_to_all | solution.py:355
  33.2 1.0 %copy-start.10 = (bf16[512,1,512]{2,0,1:T(8,128)(2,1)S(1)}, bf16[512,1,512]{2,0,1:T(8,128)(2,1)}, u32[]{:S(2)}) copy-start(bf16[512,1,512]{2,0,1:T(8,128)(2,1)} %param.9) | copy-start | bytes 1572868

commit v4 on v3

--- a/solution.py
+++ b/solution.py
@@ -25,7 +25,7 @@
     return lax.broadcasted_iota(jnp.int32, shape, dim)
 
 
-LIMIT = 58
+LIMIT = 20
 VM = pl.BlockSpec(memory_space=pltpu.VMEM)
 HBM = pl.BlockSpec(memory_space=pltpu.HBM)
 
@@ -254,13 +254,16 @@
         out_ref[q, share : share + B, :] = note.astype(BF16)
 
 
-def tile_kernel(note_ref, next_ref, sci_ref, m1_ref, edge_ref, w_ref, out_ref, src, xs, rs, big):
+def tile_kernel(sci_hbm, note_ref, next_ref, m1_ref, edge_ref, w_ref, out_ref, src, xs, rs, big, sci_ref, sem):
     rows, cols = next_ref.shape
+    copy = pltpu.make_async_copy(sci_hbm, sci_ref, sem)
+    copy.start()
     to_chunks(src, 0, next_ref[...])
     conv_blocks(src, rows // B, w_ref, xs, rs, big, rows, rs.shape[0] // 2)
     big[:, 0:B, :] = edge_ref[:, B : 2 * B, :]
     big[:, B : rows - B, :] = m1_ref[:, B : rows - B, :]
     big[:, rows - B : rows + B, :] = edge_ref[:, 2 * B : 4 * B, :]
+    copy.wait()
     off, _ = read_note(note_ref)
     for c in range(cols // LANES):
         part = slice(c * LANES, (c + 1) * LANES)
@@ -284,7 +287,11 @@
         out_ref[:, part] = accum[:, part] * scale
 
 
-def call(body, shapes, specs, scratch, flops, name, limit=20):
+def in_hbm(*arrays):
+    return [pltpu.with_memory_space_constraint(x, pltpu.HBM) for x in arrays]
+
+
+def call(body, shapes, specs, scratch, flops, name, limit=LIMIT):
     return pl.pallas_call(
         body,
         out_shape=shapes,
@@ -334,8 +341,8 @@
             pltpu.VMEM((rows, cols), BF16), pltpu.VMEM(bank.shape, BF16), pltpu.VMEM(index.shape, jnp.int32),
             pltpu.VMEM(coeff.shape, F32), pltpu.VMEM((1, taps), BF16), pltpu.SemaphoreType.DMA((8,)),
         ] + conv_scratch + sky_scratch,
-        conv_flops, "first", LIMIT,
-    )(offsets, live_flags, template, sci, bank, index, coeff, psf_profile[None])
+        conv_flops, "first",
+    )(offsets, live_flags, *in_hbm(template, sci, bank, index, coeff, psf_profile[None]))
     msg = shifted(note, "patch", 1)
     edge_b, filt_b = call(before_kernel, sides, [VM] * 4, sky_scratch, 1 << 28, "before")(msg, before, m1, pcol)
     out, m_edge = call(
@@ -354,9 +361,12 @@
     )(note, ends, msg, following, w, pcol, prow, edge_a, edge_b, filt_a, filt_b)
     recv = lax.all_to_all(out, ("visit", "band"), 0, 0, tiled=True)
     difference = call(
-        tile_kernel, sds((rows, cols), BF16), [VM] * 6,
-        conv_scratch + [pltpu.VMEM((chunks, 2 * rows, LANES), F32)], conv_flops, "tile",
-    )(note, following, sci, m1, m_edge, w)
+        tile_kernel, sds((rows, cols), BF16), [HBM] + [VM] * 5,
+        conv_scratch + [
+            pltpu.VMEM((chunks, 2 * rows, LANES), F32), pltpu.VMEM((rows, cols), BF16), pltpu.SemaphoreType.DMA,
+        ],
+        conv_flops, "tile",
+    )(*in_hbm(sci), note, following, m1, m_edge, w)
     detection = call(coadd_kernel, sds((share, cols), F32), [VM], [], 1 << 20, "coadd")(recv)
     return (difference[:, None, :], detection)
 

time: 44.1 us -> 38.3 us (0.87)
  local copies, waits for them, and re-layouts: 5.15 us -> 0 us
    unnamed x22 -> x0, local copies, waits for them, and re-layouts: 5.15 us -> none
    pallas_call x1, Pallas kernels: 7.13 us -> 5.79 us  [on_device(): call(first_kernel, (sds((deep, CH), BF16), sds((cols, cols), BF16), sds((...]
    pallas_call x1, Pallas kernels: 3.96 us -> 4.98 us  [on_device(): call(tile_kernel, sds((rows, cols), BF16), [HBM] + [VM] * 5, conv_scratch...]
  transfers between devices with their start and end apart: 4 -> 4, of which waited for: 2 -> 3; matrix products, arithmetic and copies ran while one was open for 0% -> 0% of each run, Pallas kernels for 27% -> 30%
where the time goes in v4:
time: 38.3 us; the launch traced here: 38 us
  Pallas kernels  15.3 us (40%)
  starting transfers between devices  14.2 us (37%)
  waiting for transfers between devices  6.53 us (17%)
  between operations  1.98 us (5%)
    ppermute x3, starting transfers between devices, shifted(): return lax.ppermute(shard, axis, pairs)  10.8 us
    pallas_call x1, Pallas kernels, on_device(): call(first_kernel, (sds((deep, CH), BF16), sds((cols, cols), BF16), sds((...  5.79 us
    pallas_call x1, Pallas kernels, on_device(): call(tile_kernel, sds((rows, cols), BF16), [HBM] + [VM] * 5, conv_scratch...  4.98 us
    all_to_all x1, waiting for transfers between devices, on_device(): recv = lax.all_to_all(out, ('visit', 'band'), 0, 0, tiled=True)  4.53 us
    all_to_all x1, starting transfers between devices, on_device(): recv = lax.all_to_all(out, ('visit', 'band'), 0, 0, tiled=True)  3.48 us
    pallas_call x1, Pallas kernels, on_device(): call(join_kernel, (sds((sharers, share + B, cols), BF16), sds((chunks, 2...  2.98 us
    ppermute x3, waiting for transfers between devices, shifted(): return lax.ppermute(shard, axis, pairs)  2 us
    pallas_call x1, Pallas kernels, on_device(): call(coadd_kernel, sds((share, cols), F32), [VM], [], 1 << 20, 'coadd')  0.93 us
  transfers between devices with their start and end apart: 4, of which 3 were waited for; matrix products, arithmetic and copies ran while one was open for 0% of the time, Pallas kernels for 30%

profile of v4, /device:TPU:0, one launch (start us, length us, event | category | flops | bytes accessed | tf_op | source)
XLA Modules:
  0.0 38.0 jit_solution(16528260057514506795)
XLA Ops:
  0.6 5.0 %collective-permute-start.2 = (bf16[512,1,512]{2,0,1:T(8,128)(2,1)}, bf16[512,1,512]{2,0,1:T(8,128)(2,1)S(1)}, u32[]{:S(2)}, u32[]{:S(2)}) collective-permute-start(bf16[512,1,512]{2,0,1:T(8,128)(2,1)} %param.9), channel_id=1, source_target_pairs={{0,4},{4,8},{8,12},{1,5},{5,9},{9,13},{2,6},{6,10},{10,14},{3,7},{... | collective-permute-start | bytes 1572872 | tf_op jit(solution)/shard_map/ppermute | solution.py:21
  5.6 1.3 %collective-permute-start = (bf16[512,512]{1,0:T(8,128)(2,1)}, bf16[512,512]{1,0:T(8,128)(2,1)S(1)}, u32[]{:S(2)}, u32[]{:S(2)}) collective-permute-start(bf16[512,512]{1,0:T(8,128)(2,1)} %t_hbm.1), channel_id=1, source_target_pairs={{4,0},{8,4},{12,8},{5,1},{9,5},{13,9},{6,2},{10,6},{14,10},{7,3},{... | collective-permute-start | bytes 1572872 | tf_op jit(solution)/shard_map/ppermute | solution.py:21
  8.2 5.8 %first.1 = (bf16[2304,256]{1,0:T(8,128)(2,1)S(1)}, bf16[512,512]{1,0:T(8,128)(2,1)S(1)}, bf16[128,256]{1,0:T(8,128)(2,1)S(1)}, bf16[32,512]{1,0:T(8,128)(2,1)S(1...) custom-call(s32[1,1]{1,0:T(1,128)S(6)} %copy.10.off_hbm, ...), custom_call_target="tpu_custom_call" | custom-call | flops 1207959552 | bytes 2097152 | tf_op jit(solution)/shard_map/first/pallas_call | solution.py:332
  14.0 4.5 %collective-permute-start.1 = (bf16[32,512]{1,0:T(8,128)(2,1)S(1)}, bf16[32,512]{1,0:T(8,128)(2,1)S(1)}, u32[]{:S(2)}, u32[]{:S(2)}) collective-permute-start(bf16[32,512]{1,0:T(8,128)(2,1)S(1)} %get-tuple-element.14.note_ref), channel_id=1, source_target_pairs={{0,4},{4,8},{8,12},{1,5},{5,9},{9,13},{2,6},{6,10},{10,14},{3,7},{... | collective-permute-start | bytes 98312 | tf_op jit(solution)/shard_map/ppermute | solution.py:21
  18.5 1.6 %collective-permute-done.1.msg_ref = bf16[32,512]{1,0:T(8,128)(2,1)S(1)} collective-permute-done((bf16[32,512]{1,0:T(8,128)(2,1)S(1)}, bf16[32,512]{1,0:T(8,128)(2,1)S(1)}, u32[]{:S(2)}, u32[]{:S(2)}) %collective-permute-start.1) | collective-permute-done | bytes 32800 | tf_op jit(solution)/shard_map/ppermute | solution.py:21
  20.1 0.0 collective-permute-done.2
  20.1 0.6 %before.1 = (f32[4,64,128]{2,1,0:T(8,128)S(1)}, bf16[480,512]{1,0:T(8,128)(2,1)S(1)}) custom-call(bf16[32,512]{1,0:T(8,128)(2,1)S(1)} %collective-permute-done.1.msg_ref, bf16[512,512]{1,0:T(8,128)(2,1)S(1)} %bitcast.5, f32[4,512,128]{2,1,0:T(8,128)S(1)} %get-tuple-element.15.m_ref.m1_ref, bf16[512,512]{1,0:T(8,128)(2,1)S(1)} %get-tuple-element.18.pcol_ref), custom_call_target="tpu_custom_call" | custom-call | flops 268435456 | bytes 2097152 | tf_op jit(solution)/shard_map/before/pallas_call | solution.py:347
  20.7 0.4 %collective-permute-done.next_ref = bf16[512,512]{1,0:T(8,128)(2,1)S(1)} collective-permute-done((bf16[512,512]{1,0:T(8,128)(2,1)}, bf16[512,512]{1,0:T(8,128)(2,1)S(1)}, u32[]{:S(2)}, u32[]{:S(2)}) %collective-permute-start) | collective-permute-done | bytes 524320 | tf_op jit(solution)/shard_map/ppermute | solution.py:21
  21.1 3.0 %join.1 = (bf16[4,144,512]{2,1,0:T(8,128)(2,1)}, f32[4,64,128]{2,1,0:T(8,128)S(1)}) custom-call(bf16[32,512]{1,0:T(8,128)(2,1)S(1)} %get-tuple-element.14.note_ref, bf16[64,512]{1,0:T(8,128)(2,1)S(1)} %get-tuple-element.16.ends_ref, bf16[32,512]{1,0:T(8,128)(2,1)S(1)} %collective-permute-done.1.msg_ref, bf16[512,512]{1,0:T(8,128)(2,1)S(1)} %collective-permute-done.next_ref, ...), custom_call_target="tpu_custom_call" | custom-call | flops 536870912 | bytes 2097152 | tf_op jit(solution)/shard_map/join/pallas_call | solution.py:348
  24.1 3.5 %all-to-all-start = ((bf16[4,144,512]{2,1,0:T(8,128)(2,1)}), bf16[4,144,512]{2,1,0:T(8,128)(2,1)S(1)}, u32[]{:S(2)}, u32[]{:S(2)}) async-start(bf16[4,144,512]{2,1,0:T(8,128)(2,1)} %get-tuple-element.25), calls=%async_computation | async-start | bytes 1179648 | tf_op jit(solution)/shard_map/all_to_all | solution.py:362
  27.6 5.0 %tile.1 = bf16[512,512]{1,0:T(8,128)(2,1)} custom-call(bf16[512,512]{1,0:T(8,128)(2,1)} %bitcast.7, bf16[32,512]{1,0:T(8,128)(2,1)S(1)} %get-tuple-element.14.note_ref, bf16[512,512]{1,0:T(8,128)(2,1)S(1)} %collective-permute-done.next_ref, f32[4,512,128]{2,1,0:T(8,128)S(1)} %get-tuple-element.15.m_ref.m1_ref, f32[4,64,128]{2,1,0:T(8,128)S(1)} %get-tuple-element.24.edge_ref, ...), custom_call_target="tpu_custom_call" | custom-call | flops 1207959552 | bytes 2097152 | tf_op jit(solution)/shard_map/tile/pallas_call | solution.py:363
  32.5 4.5 %all-to-all-done.recv_ref = bf16[4,144,512]{2,1,0:T(8,128)(2,1)S(1)} async-done(((bf16[4,144,512]{2,1,0:T(8,128)(2,1)}), bf16[4,144,512]{2,1,0:T(8,128)(2,1)S(1)}, u32[]{:S(2)}, u32[]{:S(2)}) %all-to-all-start) | async-done | bytes 589856 | tf_op jit(solution)/shard_map/all_to_all | solution.py:362
  37.1 0.9 %coadd.1 = f32[128,512]{1,0:T(8,128)} custom-call(bf16[4,144,512]{2,1,0:T(8,128)(2,1)S(1)} %all-to-all-done.recv_ref), custom_call_target="tpu_custom_call" | custom-call | flops 1048576 | bytes 2097152 | tf_op jit(solution)/shard_map/coadd/pallas_call | solution.py:370
Async XLA Ops:
  0.6 19.4 %collective-permute-start.2 = (bf16[512,1,512]{2,0,1:T(8,128)(2,1)}, bf16[512,1,512]{2,0,1:T(8,128)(2,1)S(1)}, u32[]{:S(2)}, u32[]{:S(2)}) collective-permute-start(bf16[512,1,512]{2,0,1:T(8,128)(2,1)} %param.9), channel_id=1, source_target_pairs={{0,4},{4,8},{8,12},{1,5},{5,9},{9,13},{2,6},{6,10},{10,14},{3,7},{... | collective-permute-start | bytes 1572872 | tf_op jit(solution)/shard_map/ppermute | solution.py:21
  5.6 15.5 %collective-permute-start = (bf16[512,512]{1,0:T(8,128)(2,1)}, bf16[512,512]{1,0:T(8,128)(2,1)S(1)}, u32[]{:S(2)}, u32[]{:S(2)}) collective-permute-start(bf16[512,512]{1,0:T(8,128)(2,1)} %t_hbm.1), channel_id=1, source_target_pairs={{4,0},{8,4},{12,8},{5,1},{9,5},{13,9},{6,2},{10,6},{14,10},{7,3},{... | collective-permute-start | bytes 1572872 | tf_op jit(solution)/shard_map/ppermute | solution.py:21
  14.0 6.1 %collective-permute-start.1 = (bf16[32,512]{1,0:T(8,128)(2,1)S(1)}, bf16[32,512]{1,0:T(8,128)(2,1)S(1)}, u32[]{:S(2)}, u32[]{:S(2)}) collective-permute-start(bf16[32,512]{1,0:T(8,128)(2,1)S(1)} %get-tuple-element.14.note_ref), channel_id=1, source_target_pairs={{0,4},{4,8},{8,12},{1,5},{5,9},{9,13},{2,6},{6,10},{10,14},{3,7},{... | collective-permute-start | bytes 98312 | tf_op jit(solution)/shard_map/ppermute | solution.py:21
  24.1 13.0 %all-to-all-start = ((bf16[4,144,512]{2,1,0:T(8,128)(2,1)}), bf16[4,144,512]{2,1,0:T(8,128)(2,1)S(1)}, u32[]{:S(2)}, u32[]{:S(2)}) async-start(bf16[4,144,512]{2,1,0:T(8,128)(2,1)} %get-tuple-element.25), calls=%async_computation | async-start | bytes 1179648 | tf_op jit(solution)/shard_map/all_to_all | solution.py:362

commit v5 on v4

--- a/solution.py
+++ b/solution.py
@@ -44,34 +44,54 @@
     return parts
 
 
-def conv_blocks(src, count, w_ref, xs, rs, dst, dst_row, batch):
+def conv_blocks(src, count, w_ref, xs, dst, dst_row):
     chunks = src.shape[0]
     blocks = chunks * GROUPS
-    for q in range(3):
-        xs[q, 0] = jnp.zeros((count, CH), xs.dtype)
-        xs[q, blocks + 1] = jnp.zeros((count, CH), xs.dtype)
-    for c in range(chunks):
+    wide = count // 8
+
+    def load(c):
         for h in range(2):
-            rows = [src[c, pl.ds(GROUPS * h + i, count, stride=B), :] for i in range(GROUPS)]
-            cols = group_transpose(rows)
-            for g in range(GROUPS):
-                for q in range(3):
-                    moved = cols[g] if q == 1 else pltpu.roll(cols[g], (1 - q) % count, 0)
-                    xs[q, 1 + c * GROUPS + g, :, h * LANES : (h + 1) * LANES] = moved.astype(xs.dtype)
-    for b in range(0, blocks, batch):
+            rows = [
+                jnp.concatenate(
+                    [src[c, pl.ds(B * v + GROUPS * h + i, 8, stride=B * wide), :] for v in range(wide)], axis=0
+                )
+                for i in range(GROUPS)
+            ]
+            part = slice(h * LANES, (h + 1) * LANES)
+            for g, here in enumerate(group_transpose(rows)):
+                at = 1 + c * GROUPS + g
+                after = pltpu.roll(here[0:8], 7, 0)
+                prior = pltpu.roll(here[count - 8 :], 1, 0)
+                if wide > 1:
+                    after = jnp.concatenate([here[8:], after], axis=0)
+                    prior = jnp.concatenate([prior, here[: count - 8]], axis=0)
+                xs[0, at, :, part] = prior.astype(xs.dtype)
+                xs[1, at, :, part] = here.astype(xs.dtype)
+                xs[2, at, :, part] = after.astype(xs.dtype)
+
+    def solve(c):
+        b = c * GROUPS
         pieces = [
-            xs[qr, b + qc : b + qc + batch].reshape(batch * count, CH).astype(BF16)
+            xs[qr, b + qc : b + qc + GROUPS].reshape(GROUPS * count, CH).astype(BF16)
             for qr in range(3)
             for qc in range(3)
         ]
         out = jnp.dot(jnp.concatenate(pieces, axis=1), w_ref[...], preferred_element_type=F32)
-        rs[b : b + batch] = out.reshape(batch, count, CH)
+        for h in range(2):
+            part = slice(h * LANES, (h + 1) * LANES)
+            rows = group_transpose([out[g * count : (g + 1) * count, part] for g in range(GROUPS)])
+            for i in range(GROUPS):
+                for v in range(wide):
+                    dst[c, pl.ds(dst_row + B * v + GROUPS * h + i, 8, stride=B * wide), :] = rows[i][8 * v : 8 * v + 8]
+
+    for q in range(3):
+        xs[q, 0] = jnp.zeros((count, CH), xs.dtype)
+        xs[q, blocks + 1] = jnp.zeros((count, CH), xs.dtype)
+    load(0)
     for c in range(chunks):
-        for h in range(2):
-            cols = [rs[c * GROUPS + g, :, h * LANES : (h + 1) * LANES] for g in range(GROUPS)]
-            rows = group_transpose(cols)
-            for i in range(GROUPS):
-                dst[c, pl.ds(dst_row + GROUPS * h + i, count, stride=B), :] = rows[i]
+        if c + 1 < chunks:
+            load(c + 1)
+        solve(c)
 
 
 def column(row):
@@ -82,9 +102,9 @@
 
 def first_kernel(
     off_hbm, live_hbm, t_hbm, sci_hbm, bank_hbm, index_hbm, coeff_hbm, psf_hbm,
-    w_ref, pcol_ref, prow_ref, note_ref, ends_ref, m_ref, edge_ref, filt_ref,
-    off_ref, live_ref, t_ref, sci_ref, bank_ref, index_ref, coeff_ref, psf_ref, sems,
-    src, xs, rs, sci, diff,
+    w_ref, pcol_ref, prow_ref, note_ref, ends_ref, sci_ref, m_ref, edge_ref, filt_ref,
+    off_ref, live_ref, t_ref, bank_ref, index_ref, coeff_ref, psf_ref, sems,
+    src, xs, sci, diff,
 ):
     pairs = (
         (bank_hbm, bank_ref), (index_hbm, index_ref), (coeff_hbm, coeff_ref), (psf_hbm, psf_ref),
@@ -158,7 +178,7 @@
     ends_ref[0:edge, :] = t_ref[0:edge, :]
     ends_ref[edge:, :] = t_ref[rows - edge : rows, :]
     to_chunks(src, 0, t_ref[...])
-    conv_blocks(src, rows // B, w_ref, xs, rs, m_ref, 0, rs.shape[0] // 2)
+    conv_blocks(src, rows // B, w_ref, xs, m_ref, 0)
     to_chunks(sci, rows, sci_ref[...])
     filter_inner(sci, rows - B - off, off, off + rows, m_ref, pcol_ref, edge_ref, filt_ref, diff)
 
@@ -201,14 +221,14 @@
 
 def join_kernel(
     note_ref, ends_ref, msg_ref, next_ref, w_ref, pcol_ref, prow_ref, edge_a, edge_b, filt_a, filt_b,
-    out_ref, m_ref, src, xs, rs, strip, diff, sides,
+    out_ref, m_ref, src, xs, strip, diff, sides,
 ):
     rows, cols = next_ref.shape
     edge = 2 * B
     to_chunks(src, 0, msg_ref[...])
     to_chunks(src, edge, ends_ref[...])
     to_chunks(src, 3 * edge, next_ref[0:edge, :])
-    conv_blocks(src, 8, w_ref, xs, rs, strip, 0, rs.shape[0])
+    conv_blocks(src, 8, w_ref, xs, strip, 0)
     m_ref[:, 0:edge, :] = strip[:, B : B + edge, :]
     m_ref[:, edge:, :] = strip[:, 5 * B : 5 * B + edge, :]
     off_a, live_a = read_note(note_ref)
@@ -254,16 +274,13 @@
         out_ref[q, share : share + B, :] = note.astype(BF16)
 
 
-def tile_kernel(sci_hbm, note_ref, next_ref, m1_ref, edge_ref, w_ref, out_ref, src, xs, rs, big, sci_ref, sem):
+def tile_kernel(sci_ref, note_ref, next_ref, m1_ref, edge_ref, w_ref, out_ref, src, xs, big):
     rows, cols = next_ref.shape
-    copy = pltpu.make_async_copy(sci_hbm, sci_ref, sem)
-    copy.start()
     to_chunks(src, 0, next_ref[...])
-    conv_blocks(src, rows // B, w_ref, xs, rs, big, rows, rs.shape[0] // 2)
+    conv_blocks(src, rows // B, w_ref, xs, big, rows)
     big[:, 0:B, :] = edge_ref[:, B : 2 * B, :]
     big[:, B : rows - B, :] = m1_ref[:, B : rows - B, :]
     big[:, rows - B : rows + B, :] = edge_ref[:, 2 * B : 4 * B, :]
-    copy.wait()
     off, _ = read_note(note_ref)
     for c in range(cols // LANES):
         part = slice(c * LANES, (c + 1) * LANES)
@@ -324,21 +341,20 @@
     conv_scratch = [
         pltpu.VMEM((chunks, rows, LANES), F32),
         pltpu.VMEM((3, blocks + 2, count, CH), BF16),
-        pltpu.VMEM((blocks, count, CH), F32),
     ]
     conv_flops = 2 * rows * cols * deep
     sky_scratch = [pltpu.VMEM((chunks, 2 * rows + B, LANES), F32), pltpu.VMEM((inner, cols), BF16)]
     sides = (sds((chunks, 2 * edge, LANES), F32), sds((inner, cols), BF16))
-    w, pcol, prow, note, ends, m1, edge_a, filt_a = call(
+    w, pcol, prow, note, ends, tile, m1, edge_a, filt_a = call(
         first_kernel,
         (
             sds((deep, CH), BF16), sds((cols, cols), BF16), sds((share, depth), BF16), sds((edge, cols), BF16),
-            sds((2 * edge, cols), BF16), sds((chunks, rows, LANES), F32),
+            sds((2 * edge, cols), BF16), sds((rows, cols), BF16), sds((chunks, rows, LANES), F32),
         ) + sides,
         [HBM] * 8,
         [
             pltpu.SMEM((1, 1), jnp.int32), pltpu.SMEM((1, 1), jnp.int32), pltpu.VMEM((rows, cols), BF16),
-            pltpu.VMEM((rows, cols), BF16), pltpu.VMEM(bank.shape, BF16), pltpu.VMEM(index.shape, jnp.int32),
+            pltpu.VMEM(bank.shape, BF16), pltpu.VMEM(index.shape, jnp.int32),
             pltpu.VMEM(coeff.shape, F32), pltpu.VMEM((1, taps), BF16), pltpu.SemaphoreType.DMA((8,)),
         ] + conv_scratch + sky_scratch,
         conv_flops, "first",
@@ -352,7 +368,6 @@
         [
             pltpu.VMEM((chunks, 8 * B, LANES), F32),
             pltpu.VMEM((3, blocks + 2, 8, CH), F32),
-            pltpu.VMEM((blocks, 8, CH), F32),
             pltpu.VMEM((chunks, 8 * B, LANES), F32),
             pltpu.VMEM((4 * edge, cols), BF16),
             pltpu.VMEM((4 * edge, cols), BF16),
@@ -361,12 +376,9 @@
     )(note, ends, msg, following, w, pcol, prow, edge_a, edge_b, filt_a, filt_b)
     recv = lax.all_to_all(out, ("visit", "band"), 0, 0, tiled=True)
     difference = call(
-        tile_kernel, sds((rows, cols), BF16), [HBM] + [VM] * 5,
-        conv_scratch + [
-            pltpu.VMEM((chunks, 2 * rows, LANES), F32), pltpu.VMEM((rows, cols), BF16), pltpu.SemaphoreType.DMA,
-        ],
-        conv_flops, "tile",
-    )(*in_hbm(sci), note, following, m1, m_edge, w)
+        tile_kernel, sds((rows, cols), BF16), [VM] * 6,
+        conv_scratch + [pltpu.VMEM((chunks, 2 * rows, LANES), F32)], conv_flops, "tile",
+    )(tile, note, following, m1, m_edge, w)
     detection = call(coadd_kernel, sds((share, cols), F32), [VM], [], 1 << 20, "coadd")(recv)
     return (difference[:, None, :], detection)
 

time: 38.3 us -> 38.1 us (level)
  Pallas kernels: 15.3 us -> 13.7 us
  local copies, waits for them, and re-layouts: 0 us -> 1.04 us
    pallas_call x1, Pallas kernels: 4.98 us -> 3.89 us  [on_device(): call(tile_kernel, sds((rows, cols), BF16), [VM] * 6, conv_scratch + [pltp...]
    unnamed x0 -> x4, local copies, waits for them, and re-layouts: none -> 1.04 us
  transfers between devices with their start and end apart: 4 -> 4, of which waited for: 3 -> 3; matrix products, arithmetic and copies ran while one was open for 0% -> 0% of each run, Pallas kernels for 30% -> 27%
where the time goes in v5:
time: 38.1 us; the launch traced here: 37.8 us
  starting transfers between devices  14.2 us (37%)
  Pallas kernels  13.7 us (36%)
  waiting for transfers between devices  6.76 us (18%)
  between operations  1.99 us (5%)
  local copies, waits for them, and re-layouts  1.04 us (3%)
    ppermute x3, starting transfers between devices, shifted(): return lax.ppermute(shard, axis, pairs)  10.8 us
    pallas_call x1, Pallas kernels, on_device(): call(first_kernel, (sds((deep, CH), BF16), sds((cols, cols), BF16), sds((...  5.58 us
    all_to_all x1, waiting for transfers between devices, on_device(): recv = lax.all_to_all(out, ('visit', 'band'), 0, 0, tiled=True)  4.58 us
    pallas_call x1, Pallas kernels, on_device(): call(tile_kernel, sds((rows, cols), BF16), [VM] * 6, conv_scratch + [pltp...  3.89 us
    all_to_all x1, starting transfers between devices, on_device(): recv = lax.all_to_all(out, ('visit', 'band'), 0, 0, tiled=True)  3.48 us
    pallas_call x1, Pallas kernels, on_device(): call(join_kernel, (sds((sharers, share + B, cols), BF16), sds((chunks, 2...  2.74 us
    ppermute x3, waiting for transfers between devices, shifted(): return lax.ppermute(shard, axis, pairs)  2.18 us
    unnamed x4, local copies, waits for them, and re-layouts  1.04 us
  transfers between devices with their start and end apart: 4, of which 3 were waited for; matrix products, arithmetic and copies ran while one was open for 0% of the time, Pallas kernels for 27%

profile of v5, /device:TPU:0, one launch (start us, length us, event | category | flops | bytes accessed | tf_op | source)
XLA Modules:
  0.0 37.8 jit_solution(9582345616907185676)
XLA Ops:
  0.6 5.0 %collective-permute-start.2 = (bf16[512,1,512]{2,0,1:T(8,128)(2,1)}, bf16[512,1,512]{2,0,1:T(8,128)(2,1)S(1)}, u32[]{:S(2)}, u32[]{:S(2)}) collective-permute-start(bf16[512,1,512]{2,0,1:T(8,128)(2,1)} %param.9), channel_id=1, source_target_pairs={{0,4},{4,8},{8,12},{1,5},{5,9},{9,13},{2,6},{6,10},{10,14},{3,7},{... | collective-permute-start | bytes 1572872 | tf_op jit(solution)/shard_map/ppermute | solution.py:21
  5.6 1.3 %collective-permute-start = (bf16[512,512]{1,0:T(8,128)(2,1)}, bf16[512,512]{1,0:T(8,128)(2,1)S(1)}, u32[]{:S(2)}, u32[]{:S(2)}) collective-permute-start(bf16[512,512]{1,0:T(8,128)(2,1)} %t_hbm.1), channel_id=1, source_target_pairs={{4,0},{8,4},{12,8},{5,1},{9,5},{13,9},{6,2},{10,6},{14,10},{7,3},{... | collective-permute-start | bytes 1572872 | tf_op jit(solution)/shard_map/ppermute | solution.py:21
  8.2 5.6 %first.1 = (bf16[2304,256]{1,0:T(8,128)(2,1)S(1)}, bf16[512,512]{1,0:T(8,128)(2,1)S(1)}, bf16[128,256]{1,0:T(8,128)(2,1)S(1)}, bf16[32,512]{1,0:T(8,128)(2,1)S(1...) custom-call(s32[1,1]{1,0:T(1,128)S(6)} %copy.10.off_hbm, ...), custom_call_target="tpu_custom_call" | custom-call | flops 1207959552 | bytes 2097152 | tf_op jit(solution)/shard_map/first/pallas_call | solution.py:348
  13.8 0.0 copy-start
  13.8 4.5 %collective-permute-start.1 = (bf16[32,512]{1,0:T(8,128)(2,1)S(1)}, bf16[32,512]{1,0:T(8,128)(2,1)S(1)}, u32[]{:S(2)}, u32[]{:S(2)}) collective-permute-start(bf16[32,512]{1,0:T(8,128)(2,1)S(1)} %get-tuple-element.16.note_ref), channel_id=1, source_target_pairs={{0,4},{4,8},{8,12},{1,5},{5,9},{9,13},{2,6},{6,10},{10,14},{3,7},{... | collective-permute-start | bytes 98312 | tf_op jit(solution)/shard_map/ppermute | solution.py:21
  18.3 1.6 %collective-permute-done.1.msg_ref = bf16[32,512]{1,0:T(8,128)(2,1)S(1)} collective-permute-done((bf16[32,512]{1,0:T(8,128)(2,1)S(1)}, bf16[32,512]{1,0:T(8,128)(2,1)S(1)}, u32[]{:S(2)}, u32[]{:S(2)}) %collective-permute-start.1) | collective-permute-done | bytes 32800 | tf_op jit(solution)/shard_map/ppermute | solution.py:21
  19.9 0.0 collective-permute-done.2
  19.9 0.6 %before.1 = (f32[4,64,128]{2,1,0:T(8,128)S(1)}, bf16[480,512]{1,0:T(8,128)(2,1)S(1)}) custom-call(bf16[32,512]{1,0:T(8,128)(2,1)S(1)} %collective-permute-done.1.msg_ref, bf16[512,512]{1,0:T(8,128)(2,1)S(1)} %bitcast.5, f32[4,512,128]{2,1,0:T(8,128)S(1)} %get-tuple-element.17.m_ref.m1_ref, bf16[512,512]{1,0:T(8,128)(2,1)S(1)} %get-tuple-element.20.pcol_ref), custom_call_target="tpu_custom_call" | custom-call | flops 268435456 | bytes 2097152 | tf_op jit(solution)/shard_map/before/pallas_call | solution.py:363
  20.5 0.6 %collective-permute-done.next_ref = bf16[512,512]{1,0:T(8,128)(2,1)S(1)} collective-permute-done((bf16[512,512]{1,0:T(8,128)(2,1)}, bf16[512,512]{1,0:T(8,128)(2,1)S(1)}, u32[]{:S(2)}, u32[]{:S(2)}) %collective-permute-start) | collective-permute-done | bytes 524320 | tf_op jit(solution)/shard_map/ppermute | solution.py:21
  21.1 2.7 %join.1 = (bf16[4,144,512]{2,1,0:T(8,128)(2,1)}, f32[4,64,128]{2,1,0:T(8,128)S(1)}) custom-call(bf16[32,512]{1,0:T(8,128)(2,1)S(1)} %get-tuple-element.16.note_ref, bf16[64,512]{1,0:T(8,128)(2,1)S(1)} %get-tuple-element.18.ends_ref, bf16[32,512]{1,0:T(8,128)(2,1)S(1)} %collective-permute-done.1.msg_ref, bf16[512,512]{1,0:T(8,128)(2,1)S(1)} %collective-permute-done.next_ref, ...), custom_call_target="tpu_custom_call" | custom-call | flops 536870912 | bytes 2097152 | tf_op jit(solution)/shard_map/join/pallas_call | solution.py:364
  23.8 0.0 copy-done
  23.8 3.5 %all-to-all-start = ((bf16[4,144,512]{2,1,0:T(8,128)(2,1)}), bf16[4,144,512]{2,1,0:T(8,128)(2,1)S(1)}, u32[]{:S(2)}, u32[]{:S(2)}) async-start(bf16[4,144,512]{2,1,0:T(8,128)(2,1)} %get-tuple-element.27), calls=%async_computation | async-start | bytes 1179648 | tf_op jit(solution)/shard_map/all_to_all | solution.py:377
  27.3 0.0 copy-start.1
  27.3 1.0 %copy-done.1 = bf16[512,512]{1,0:T(8,128)(2,1)S(1)} copy-done((bf16[512,512]{1,0:T(8,128)(2,1)S(1)}, bf16[512,512]{1,0:T(8,128)(2,1)}, u32[]{:S(2)}) %copy-start.1) | copy-done | bytes 524312
  28.4 3.9 %tile.1 = bf16[512,512]{1,0:T(8,128)(2,1)} custom-call(bf16[512,512]{1,0:T(8,128)(2,1)S(1)} %copy-done.1, bf16[32,512]{1,0:T(8,128)(2,1)S(1)} %get-tuple-element.16.note_ref, bf16[512,512]{1,0:T(8,128)(2,1)S(1)} %collective-permute-done.next_ref, f32[4,512,128]{2,1,0:T(8,128)S(1)} %get-tuple-element.17.m_ref.m1_ref, ...), custom_call_target="tpu_custom_call" | custom-call | flops 1207959552 | bytes 2097152 | tf_op jit(solution)/shard_map/tile/pallas_call | solution.py:378
  32.3 4.6 %all-to-all-done.recv_ref = bf16[4,144,512]{2,1,0:T(8,128)(2,1)S(1)} async-done(((bf16[4,144,512]{2,1,0:T(8,128)(2,1)}), bf16[4,144,512]{2,1,0:T(8,128)(2,1)S(1)}, u32[]{:S(2)}, u32[]{:S(2)}) %all-to-all-start) | async-done | bytes 589856 | tf_op jit(solution)/shard_map/all_to_all | solution.py:377
  36.8 0.9 %coadd.1 = f32[128,512]{1,0:T(8,128)} custom-call(bf16[4,144,512]{2,1,0:T(8,128)(2,1)S(1)} %all-to-all-done.recv_ref), custom_call_target="tpu_custom_call" | custom-call | flops 1048576 | bytes 2097152 | tf_op jit(solution)/shard_map/coadd/pallas_call | solution.py:382
Async XLA Ops:
  0.6 19.3 %collective-permute-start.2 = (bf16[512,1,512]{2,0,1:T(8,128)(2,1)}, bf16[512,1,512]{2,0,1:T(8,128)(2,1)S(1)}, u32[]{:S(2)}, u32[]{:S(2)}) collective-permute-start(bf16[512,1,512]{2,0,1:T(8,128)(2,1)} %param.9), channel_id=1, source_target_pairs={{0,4},{4,8},{8,12},{1,5},{5,9},{9,13},{2,6},{6,10},{10,14},{3,7},{... | collective-permute-start | bytes 1572872 | tf_op jit(solution)/shard_map/ppermute | solution.py:21
  5.6 15.5 %collective-permute-start = (bf16[512,512]{1,0:T(8,128)(2,1)}, bf16[512,512]{1,0:T(8,128)(2,1)S(1)}, u32[]{:S(2)}, u32[]{:S(2)}) collective-permute-start(bf16[512,512]{1,0:T(8,128)(2,1)} %t_hbm.1), channel_id=1, source_target_pairs={{4,0},{8,4},{12,8},{5,1},{9,5},{13,9},{6,2},{10,6},{14,10},{7,3},{... | collective-permute-start | bytes 1572872 | tf_op jit(solution)/shard_map/ppermute | solution.py:21
  13.8 10.1 %copy-start = (bf16[512,512]{1,0:T(8,128)(2,1)}, bf16[512,512]{1,0:T(8,128)(2,1)S(1)}, u32[]{:S(2)}) copy-start(bf16[512,512]{1,0:T(8,128)(2,1)S(1)} %get-tuple-element.15.sci_ref) | copy-start | bytes 1572868
  13.8 6.1 %collective-permute-start.1 = (bf16[32,512]{1,0:T(8,128)(2,1)S(1)}, bf16[32,512]{1,0:T(8,128)(2,1)S(1)}, u32[]{:S(2)}, u32[]{:S(2)}) collective-permute-start(bf16[32,512]{1,0:T(8,128)(2,1)S(1)} %get-tuple-element.16.note_ref), channel_id=1, source_target_pairs={{0,4},{4,8},{8,12},{1,5},{5,9},{9,13},{2,6},{6,10},{10,14},{3,7},{... | collective-permute-start | bytes 98312 | tf_op jit(solution)/shard_map/ppermute | solution.py:21
  23.8 13.0 %all-to-all-start = ((bf16[4,144,512]{2,1,0:T(8,128)(2,1)}), bf16[4,144,512]{2,1,0:T(8,128)(2,1)S(1)}, u32[]{:S(2)}, u32[]{:S(2)}) async-start(bf16[4,144,512]{2,1,0:T(8,128)(2,1)} %get-tuple-element.27), calls=%async_computation | async-start | bytes 1179648 | tf_op jit(solution)/shard_map/all_to_all | solution.py:377
  27.3 1.0 %copy-start.1 = (bf16[512,512]{1,0:T(8,128)(2,1)S(1)}, bf16[512,512]{1,0:T(8,128)(2,1)}, u32[]{:S(2)}) copy-start(bf16[512,512]{1,0:T(8,128)(2,1)} %copy-done) | copy-start | bytes 1572868

commit v6 on v5

--- a/solution.py
+++ b/solution.py
@@ -21,11 +21,15 @@
     return lax.ppermute(shard, axis, pairs)
 
 
+def partner(me, k, count):
+    return me ^ k if count & (count - 1) == 0 else (me + k) % count
+
+
 def iota(shape, dim):
     return lax.broadcasted_iota(jnp.int32, shape, dim)
 
 
-LIMIT = 20
+LIMIT = 10
 VM = pl.BlockSpec(memory_space=pltpu.VMEM)
 HBM = pl.BlockSpec(memory_space=pltpu.HBM)
 
@@ -221,8 +225,9 @@
 
 def join_kernel(
     note_ref, ends_ref, msg_ref, next_ref, w_ref, pcol_ref, prow_ref, edge_a, edge_b, filt_a, filt_b,
-    out_ref, m_ref, src, xs, strip, diff, sides,
+    *rest,
 ):
+    *outs, m_ref, src, xs, strip, diff, filt = rest
     rows, cols = next_ref.shape
     edge = 2 * B
     to_chunks(src, 0, msg_ref[...])
@@ -240,38 +245,30 @@
                 span = slice(k * edge, (k + 1) * edge)
                 at = (2 * s + k) * edge
                 diff[at : at + edge, part] = tile_diff(side[c, span, :], m_ref[c, span, :], base, first, last)
-    sides[...] = jnp.dot(diff[...], pcol_ref[...], preferred_element_type=F32).astype(BF16)
-    inner = (filt_a, filt_b)
-
-    def rows_of(s, low, high):
-        pieces = []
-        for start, stop, ref, at in (
-            (0, edge, sides, 2 * s * edge),
-            (edge, rows, inner[s], 0),
-            (rows, rows + edge, sides, (2 * s + 1) * edge),
-        ):
-            a, b = max(low, start), min(high, stop)
-            if a < b:
-                pieces.append(ref[at + a - start : at + b - start, :])
-        if high > rows + edge:
-            pieces.append(jnp.zeros((high - max(low, rows + edge), cols), BF16))
-        return jnp.concatenate(pieces, axis=0)
-
+    sides = jnp.dot(diff[...], pcol_ref[...], preferred_element_type=F32).astype(BF16)
+    for s, inner in enumerate((filt_a, filt_b)):
+        filt[s, 0:edge, :] = sides[2 * s * edge : (2 * s + 1) * edge]
+        filt[s, edge:rows, :] = inner[...]
+        filt[s, rows : rows + edge, :] = sides[(2 * s + 1) * edge : (2 * s + 2) * edge]
+        filt[s, rows + edge :, :] = jnp.zeros((filt.shape[1] - rows - edge, cols), BF16)
     share, depth = prow_ref.shape
     prow = prow_ref[...].astype(F32)
     out_row = iota((share, depth), 0)
     lane = iota((B, cols), 1)
-    for q in range(out_ref.shape[0]):
-        row = out_row + q * share
+    me = lax.axis_index("visit") * lax.axis_size("band") + lax.axis_index("band")
+    for k, out_ref in enumerate(outs):
+        base = partner(me, k, len(outs)) * share
+        row = out_row + base
         left = jnp.where(row >= off_a, prow * live_a, 0.0).astype(BF16)
         right = jnp.where(row < off_b, prow * live_b, 0.0).astype(BF16)
-        total = jnp.dot(left, rows_of(0, q * share, q * share + depth), preferred_element_type=F32)
-        total += jnp.dot(right, rows_of(1, q * share, q * share + depth), preferred_element_type=F32)
-        out_ref[q, 0:share, :] = total.astype(BF16)
-        start = jnp.clip(off_a - q * share, 0, share).astype(F32)
-        stop = jnp.clip(off_b - q * share, 0, share).astype(F32)
+        span = pl.ds(pl.multiple_of(base, B), depth)
+        total = jnp.dot(left, filt[0, span, :], preferred_element_type=F32)
+        total += jnp.dot(right, filt[1, span, :], preferred_element_type=F32)
+        out_ref[0:share, :] = total.astype(BF16)
+        start = jnp.clip(off_a - base, 0, share).astype(F32)
+        stop = jnp.clip(off_b - base, 0, share).astype(F32)
         note = jnp.where(lane == 0, start, jnp.where(lane == 1, live_a, jnp.where(lane == 2, stop, live_b)))
-        out_ref[q, share : share + B, :] = note.astype(BF16)
+        out_ref[share : share + B, :] = note.astype(BF16)
 
 
 def tile_kernel(sci_ref, note_ref, next_ref, m1_ref, edge_ref, w_ref, out_ref, src, xs, big):
@@ -287,15 +284,15 @@
         out_ref[:, part] = (sci_ref[:, part].astype(F32) - big[c, pl.ds(off, rows), :]).astype(BF16)
 
 
-def coadd_kernel(recv_ref, out_ref):
-    count, padded, cols = recv_ref.shape
-    share = padded - B
+def coadd_kernel(*refs):
+    *parts, out_ref = refs
+    share, cols = out_ref.shape
     row = iota((share, LANES), 0).astype(F32)
     accum = jnp.zeros((share, cols), F32)
     cover = jnp.zeros((share, LANES), F32)
-    for n in range(count):
-        accum += recv_ref[n, 0:share, :].astype(F32)
-        note = recv_ref[n, share : share + B, 0:LANES].astype(F32)[0:1, :]
+    for part in parts:
+        accum += part[0:share, :].astype(F32)
+        note = part[share : share + B, 0:LANES].astype(F32)[0:1, :]
         cover += jnp.where(row >= note[:, 0:1], note[:, 1:2], 0.0)
         cover += jnp.where(row < note[:, 2:3], note[:, 3:4], 0.0)
     scale = lax.rsqrt(jnp.maximum(cover, 1.0))
@@ -361,25 +358,27 @@
     )(offsets, live_flags, *in_hbm(template, sci, bank, index, coeff, psf_profile[None]))
     msg = shifted(note, "patch", 1)
     edge_b, filt_b = call(before_kernel, sides, [VM] * 4, sky_scratch, 1 << 28, "before")(msg, before, m1, pcol)
-    out, m_edge = call(
+    *parts, m_edge = call(
         join_kernel,
-        (sds((sharers, share + B, cols), BF16), sds((chunks, 2 * edge, LANES), F32)),
+        (sds((share + B, cols), BF16),) * sharers + (sds((chunks, 2 * edge, LANES), F32),),
         [VM] * 11,
         [
             pltpu.VMEM((chunks, 8 * B, LANES), F32),
             pltpu.VMEM((3, blocks + 2, 8, CH), F32),
             pltpu.VMEM((chunks, 8 * B, LANES), F32),
             pltpu.VMEM((4 * edge, cols), BF16),
-            pltpu.VMEM((4 * edge, cols), BF16),
+            pltpu.VMEM((2, rows - share + depth, cols), BF16),
         ],
         1 << 29, "join",
     )(note, ends, msg, following, w, pcol, prow, edge_a, edge_b, filt_a, filt_b)
-    recv = lax.all_to_all(out, ("visit", "band"), 0, 0, tiled=True)
+    for k in reversed(range(1, sharers)):
+        pairs = [(i, partner(i, k, sharers)) for i in range(sharers)]
+        parts[k] = lax.ppermute(parts[k], ("visit", "band"), pairs)
     difference = call(
         tile_kernel, sds((rows, cols), BF16), [VM] * 6,
         conv_scratch + [pltpu.VMEM((chunks, 2 * rows, LANES), F32)], conv_flops, "tile",
     )(tile, note, following, m1, m_edge, w)
-    detection = call(coadd_kernel, sds((share, cols), F32), [VM], [], 1 << 20, "coadd")(recv)
+    detection = call(coadd_kernel, sds((share, cols), F32), [VM] * sharers, [], 1 << 20, "coadd")(parts[0], *parts[:0:-1])
     return (difference[:, None, :], detection)
 
 

time: 38.1 us -> 33.6 us (0.88)
  starting transfers between devices: 14.2 us -> 12.7 us
  waiting for transfers between devices: 6.76 us -> 5.71 us
  local copies, waits for them, and re-layouts: 1.04 us -> 0 us
  Pallas kernels: 13.7 us -> 12.9 us
    all_to_all x1 -> x0, waiting for transfers between devices: 4.58 us -> none  [on_device(): recv = lax.all_to_all(out, ('visit', 'band'), 0, 0, tiled=True)]
    ppermute x0 -> x3, waiting for transfers between devices: none -> 3.56 us  [on_device(): parts[k] = lax.ppermute(parts[k], ('visit', 'band'), pairs)]
    all_to_all x1 -> x0, starting transfers between devices: 3.48 us -> none  [on_device(): recv = lax.all_to_all(out, ('visit', 'band'), 0, 0, tiled=True)]
    ppermute x0 -> x3, starting transfers between devices: none -> 1.92 us  [on_device(): parts[k] = lax.ppermute(parts[k], ('visit', 'band'), pairs)]
    unnamed x4 -> x0, local copies, waits for them, and re-layouts: 1.04 us -> none
    pallas_call x2, Pallas kernels: 3.67 us -> 2.88 us  [the longest x1 1.95 us: on_device(): call(join_kernel, (sds((share + B, cols), BF16),) * sharers + (sds((chunk...]
  transfers between devices with their start and end apart: 4 -> 6, of which waited for: 3 -> 4; matrix products, arithmetic and copies ran while one was open for 0% -> 0% of each run, Pallas kernels for 27% -> 30%
where the time goes in v6:
time: 33.6 us; the launch traced here: 33.4 us
  Pallas kernels  12.9 us (38%)
  starting transfers between devices  12.7 us (38%)
  waiting for transfers between devices  5.71 us (17%)
  between operations  1.98 us (6%)
    ppermute x3, starting transfers between devices, shifted(): return lax.ppermute(shard, axis, pairs)  10.8 us
    pallas_call x1, Pallas kernels, on_device(): call(first_kernel, (sds((deep, CH), BF16), sds((cols, cols), BF16), sds((...  5.59 us
    pallas_call x1, Pallas kernels, on_device(): call(tile_kernel, sds((rows, cols), BF16), [VM] * 6, conv_scratch + [pltp...  3.89 us
    ppermute x3, waiting for transfers between devices, on_device(): parts[k] = lax.ppermute(parts[k], ('visit', 'band'), pairs)  3.56 us
    ppermute x3, waiting for transfers between devices, shifted(): return lax.ppermute(shard, axis, pairs)  2.16 us
    pallas_call x1, Pallas kernels, on_device(): call(join_kernel, (sds((share + B, cols), BF16),) * sharers + (sds((chunk...  1.95 us
    ppermute x3, starting transfers between devices, on_device(): parts[k] = lax.ppermute(parts[k], ('visit', 'band'), pairs)  1.92 us
    pallas_call x1, Pallas kernels, on_device(): call(coadd_kernel, sds((share, cols), F32), [VM] * sharers, [], 1 << 20,...  0.93 us
  transfers between devices with their start and end apart: 6, of which 4 were waited for; matrix products, arithmetic and copies ran while one was open for 0% of the time, Pallas kernels for 30%

profile of v6, /device:TPU:0, one launch (start us, length us, event | category | flops | bytes accessed | tf_op | source)
XLA Modules:
  0.0 33.4 jit_solution(10710123293795930295)
XLA Ops:
  0.6 5.0 %collective-permute-start.2 = (bf16[512,1,512]{2,0,1:T(8,128)(2,1)}, bf16[512,1,512]{2,0,1:T(8,128)(2,1)S(1)}, u32[]{:S(2)}, u32[]{:S(2)}) collective-permute-start(bf16[512,1,512]{2,0,1:T(8,128)(2,1)} %param.9), channel_id=1, source_target_pairs={{0,4},{4,8},{8,12},{1,5},{5,9},{9,13},{2,6},{6,10},{10,14},{3,7},{... | collective-permute-start | bytes 1572872 | tf_op jit(solution)/shard_map/ppermute | solution.py:21
  5.6 1.3 %collective-permute-start = (bf16[512,512]{1,0:T(8,128)(2,1)}, bf16[512,512]{1,0:T(8,128)(2,1)S(1)}, u32[]{:S(2)}, u32[]{:S(2)}) collective-permute-start(bf16[512,512]{1,0:T(8,128)(2,1)} %t_hbm.1), channel_id=1, source_target_pairs={{4,0},{8,4},{12,8},{5,1},{9,5},{13,9},{6,2},{10,6},{14,10},{7,3},{... | collective-permute-start | bytes 1572872 | tf_op jit(solution)/shard_map/ppermute | solution.py:21
  8.2 5.6 %first.1 = (bf16[2304,256]{1,0:T(8,128)(2,1)S(1)}, bf16[512,512]{1,0:T(8,128)(2,1)S(1)}, bf16[128,256]{1,0:T(8,128)(2,1)S(1)}, bf16[32,512]{1,0:T(8,128)(2,1)S(1...) custom-call(s32[1,1]{1,0:T(1,128)S(6)} %copy.10.off_hbm, ...), custom_call_target="tpu_custom_call" | custom-call | flops 1207959552 | bytes 2097152 | tf_op jit(solution)/shard_map/first/pallas_call | solution.py:345
  13.8 4.5 %collective-permute-start.1 = (bf16[32,512]{1,0:T(8,128)(2,1)S(1)}, bf16[32,512]{1,0:T(8,128)(2,1)S(1)}, u32[]{:S(2)}, u32[]{:S(2)}) collective-permute-start(bf16[32,512]{1,0:T(8,128)(2,1)S(1)} %get-tuple-element.19.note_ref), channel_id=1, source_target_pairs={{0,4},{4,8},{8,12},{1,5},{5,9},{9,13},{2,6},{6,10},{10,14},{3,7},{... | collective-permute-start | bytes 98312 | tf_op jit(solution)/shard_map/ppermute | solution.py:21
  18.3 1.6 %collective-permute-done.1.msg_ref = bf16[32,512]{1,0:T(8,128)(2,1)S(1)} collective-permute-done((bf16[32,512]{1,0:T(8,128)(2,1)S(1)}, bf16[32,512]{1,0:T(8,128)(2,1)S(1)}, u32[]{:S(2)}, u32[]{:S(2)}) %collective-permute-start.1) | collective-permute-done | bytes 32800 | tf_op jit(solution)/shard_map/ppermute | solution.py:21
  19.9 0.0 collective-permute-done.2
  19.9 0.6 %before.1 = (f32[4,64,128]{2,1,0:T(8,128)S(1)}, bf16[480,512]{1,0:T(8,128)(2,1)S(1)}) custom-call(bf16[32,512]{1,0:T(8,128)(2,1)S(1)} %collective-permute-done.1.msg_ref, bf16[512,512]{1,0:T(8,128)(2,1)S(1)} %bitcast.5, f32[4,512,128]{2,1,0:T(8,128)S(1)} %get-tuple-element.20.m_ref.m1_ref, bf16[512,512]{1,0:T(8,128)(2,1)S(1)} %get-tuple-element.23.pcol_ref), custom_call_target="tpu_custom_call" | custom-call | flops 268435456 | bytes 2097152 | tf_op jit(solution)/shard_map/before/pallas_call | solution.py:360
  20.5 0.6 %collective-permute-done.next_ref = bf16[512,512]{1,0:T(8,128)(2,1)S(1)} collective-permute-done((bf16[512,512]{1,0:T(8,128)(2,1)}, bf16[512,512]{1,0:T(8,128)(2,1)S(1)}, u32[]{:S(2)}, u32[]{:S(2)}) %collective-permute-start) | collective-permute-done | bytes 524320 | tf_op jit(solution)/shard_map/ppermute | solution.py:21
  21.1 2.0 %join.1 = (bf16[144,512]{1,0:T(8,128)(2,1)S(1)}, bf16[144,512]{1,0:T(8,128)(2,1)S(1)}, bf16[144,512]{1,0:T(8,128)(2,1)S(1)}, bf16[144,512]{1,0:T(8,128)(2,1)S(1)}, f32[4,64,128]{2,1,0:T(8,128)S(1)}) custom-call(bf16[32,512]{1,0:T(8,128)(2,1)S(1)} %get-tuple-element.19.note_ref, bf16[64,512]{1,0:T(8,128)(2,1)S(1)} %get-tuple-element.21.ends_ref, ...), custom_call_target="tpu_custom_call" | custom-call | flops 536870912 | bytes 2097152 | tf_op jit(solution)/shard_map/join/pallas_call | solution.py:361
  23.0 0.1 collective-permute-start.3
  23.1 1.6 %collective-permute-start.4 = (bf16[144,512]{1,0:T(8,128)(2,1)S(1)}, bf16[144,512]{1,0:T(8,128)(2,1)S(1)}, u32[]{:S(2)}, u32[]{:S(2)}) collective-permute-start(bf16[144,512]{1,0:T(8,128)(2,1)S(1)} %get-tuple-element.32), channel_id=1, source_target_pairs={{0,2},{1,3},{2,0},{3,1},{4,6},{5,7},{6,4},{7,5},{8,10},{9,11},{10,... | collective-permute-start | bytes 442376 | tf_op jit(solution)/shard_map/ppermute | solution.py:376
  24.7 0.3 collective-permute-start.5
  25.0 3.9 %tile.1 = bf16[512,512]{1,0:T(8,128)(2,1)} custom-call(bf16[512,512]{1,0:T(8,128)(2,1)S(1)} %get-tuple-element.18.sci_ref, bf16[32,512]{1,0:T(8,128)(2,1)S(1)} %get-tuple-element.19.note_ref, bf16[512,512]{1,0:T(8,128)(2,1)S(1)} %collective-permute-done.next_ref, f32[4,512,128]{2,1,0:T(8,128)S(1)} %get-tuple-element.20.m_ref.m1_ref, ...), custom_call_target="tpu_custom_call" | custom-call | flops 1207959552 | bytes 2097152 | tf_op jit(solution)/shard_map/tile/pallas_call | solution.py:377
  28.9 0.3 %collective-permute-done.3.refs_1_ = bf16[144,512]{1,0:T(8,128)(2,1)S(1)} collective-permute-done((bf16[144,512]{1,0:T(8,128)(2,1)S(1)}, bf16[144,512]{1,0:T(8,128)(2,1)S(1)}, u32[]{:S(2)}, u32[]{:S(2)}) %collective-permute-start.3) | collective-permute-done | bytes 147488 | tf_op jit(solution)/shard_map/ppermute | solution.py:376
  29.2 3.2 %collective-permute-done.4.refs_2_ = bf16[144,512]{1,0:T(8,128)(2,1)S(1)} collective-permute-done((bf16[144,512]{1,0:T(8,128)(2,1)S(1)}, bf16[144,512]{1,0:T(8,128)(2,1)S(1)}, u32[]{:S(2)}, u32[]{:S(2)}) %collective-permute-start.4) | collective-permute-done | bytes 147488 | tf_op jit(solution)/shard_map/ppermute | solution.py:376
  32.4 0.0 collective-permute-done.5.refs_3_
  32.4 0.9 %coadd.1 = f32[128,512]{1,0:T(8,128)} custom-call(bf16[144,512]{1,0:T(8,128)(2,1)S(1)} %get-tuple-element.30.refs_0_, bf16[144,512]{1,0:T(8,128)(2,1)S(1)} %collective-permute-done.3.refs_1_, bf16[144,512]{1,0:T(8,128)(2,1)S(1)} %collective-permute-done.4.refs_2_, bf16[144,512]{1,0:T(8,128)(2,1)S(1)} %collective-permute-done.5.refs_3_), custom_call_target="tpu_custom_call" | custom-call | flops 1048576 | bytes 2097152 | tf_op jit(solution)/shard_map/coadd/pallas_call | solution.py:381
Async XLA Ops:
  0.6 19.3 %collective-permute-start.2 = (bf16[512,1,512]{2,0,1:T(8,128)(2,1)}, bf16[512,1,512]{2,0,1:T(8,128)(2,1)S(1)}, u32[]{:S(2)}, u32[]{:S(2)}) collective-permute-start(bf16[512,1,512]{2,0,1:T(8,128)(2,1)} %param.9), channel_id=1, source_target_pairs={{0,4},{4,8},{8,12},{1,5},{5,9},{9,13},{2,6},{6,10},{10,14},{3,7},{... | collective-permute-start | bytes 1572872 | tf_op jit(solution)/shard_map/ppermute | solution.py:21
  5.6 15.5 %collective-permute-start = (bf16[512,512]{1,0:T(8,128)(2,1)}, bf16[512,512]{1,0:T(8,128)(2,1)S(1)}, u32[]{:S(2)}, u32[]{:S(2)}) collective-permute-start(bf16[512,512]{1,0:T(8,128)(2,1)} %t_hbm.1), channel_id=1, source_target_pairs={{4,0},{8,4},{12,8},{5,1},{9,5},{13,9},{6,2},{10,6},{14,10},{7,3},{... | collective-permute-start | bytes 1572872 | tf_op jit(solution)/shard_map/ppermute | solution.py:21
  13.8 6.1 %collective-permute-start.1 = (bf16[32,512]{1,0:T(8,128)(2,1)S(1)}, bf16[32,512]{1,0:T(8,128)(2,1)S(1)}, u32[]{:S(2)}, u32[]{:S(2)}) collective-permute-start(bf16[32,512]{1,0:T(8,128)(2,1)S(1)} %get-tuple-element.19.note_ref), channel_id=1, source_target_pairs={{0,4},{4,8},{8,12},{1,5},{5,9},{9,13},{2,6},{6,10},{10,14},{3,7},{... | collective-permute-start | bytes 98312 | tf_op jit(solution)/shard_map/ppermute | solution.py:21
  23.0 6.2 %collective-permute-start.3 = (bf16[144,512]{1,0:T(8,128)(2,1)S(1)}, bf16[144,512]{1,0:T(8,128)(2,1)S(1)}, u32[]{:S(2)}, u32[]{:S(2)}) collective-permute-start(bf16[144,512]{1,0:T(8,128)(2,1)S(1)} %get-tuple-element.31), channel_id=1, source_target_pairs={{0,3},{1,2},{2,1},{3,0},{4,7},{5,6},{6,5},{7,4},{8,11},{9,10},{10,... | collective-permute-start | bytes 442376 | tf_op jit(solution)/shard_map/ppermute | solution.py:376
  23.1 9.3 %collective-permute-start.4 = (bf16[144,512]{1,0:T(8,128)(2,1)S(1)}, bf16[144,512]{1,0:T(8,128)(2,1)S(1)}, u32[]{:S(2)}, u32[]{:S(2)}) collective-permute-start(bf16[144,512]{1,0:T(8,128)(2,1)S(1)} %get-tuple-element.32), channel_id=1, source_target_pairs={{0,2},{1,3},{2,0},{3,1},{4,6},{5,7},{6,4},{7,5},{8,10},{9,11},{10,... | collective-permute-start | bytes 442376 | tf_op jit(solution)/shard_map/ppermute | solution.py:376
  24.7 7.7 %collective-permute-start.5 = (bf16[144,512]{1,0:T(8,128)(2,1)S(1)}, bf16[144,512]{1,0:T(8,128)(2,1)S(1)}, u32[]{:S(2)}, u32[]{:S(2)}) collective-permute-start(bf16[144,512]{1,0:T(8,128)(2,1)S(1)} %get-tuple-element.33), channel_id=1, source_target_pairs={{0,1},{1,0},{2,3},{3,2},{4,5},{5,4},{6,7},{7,6},{8,9},{9,8},{10,11... | collective-permute-start | bytes 442376 | tf_op jit(solution)/shard_map/ppermute | solution.py:376

commit v7 on v6

--- a/solution.py
+++ b/solution.py
@@ -15,10 +15,19 @@
 BF16 = jnp.bfloat16
 
 
-def shifted(shard, axis, by):
-    devices = lax.axis_size(axis)
-    pairs = [(i, i + by) for i in range(devices) if 0 <= i + by < devices]
-    return lax.ppermute(shard, axis, pairs)
+def swap_partner(p, parity, count):
+    other = p + 1 if p % 2 == parity else p - 1
+    return other if 0 <= other < count else p
+
+
+def place():
+    p = lax.axis_index("patch")
+    return p % 2 == 0, p > 0, p < lax.axis_size("patch") - 1
+
+
+def pick(flag, valid, yes, no):
+    value = jnp.where(flag, yes.astype(F32), no.astype(F32))
+    return jnp.where(valid, value, 0.0)
 
 
 def partner(me, k, count):
@@ -104,15 +113,52 @@
     return jnp.sum(jnp.where(diag, row, jnp.zeros_like(row)), axis=1, keepdims=True)
 
 
+def pack_kernel(
+    off_hbm, live_hbm, t_hbm, sci_hbm, msg1_ref, msg2_ref, note_ref, off_ref, live_ref, tail_ref, sems
+):
+    rows, cols = t_hbm.shape
+    edge = 2 * B
+    even, _, _ = place()
+
+    def send(one, two):
+        pltpu.make_async_copy(one, msg1_ref.at[pl.ds(edge, rows)], sems.at[0]).start()
+        pltpu.make_async_copy(two, msg2_ref.at[pl.ds(edge, rows)], sems.at[1]).start()
+
+    def finish(one, two):
+        pltpu.make_async_copy(one, msg1_ref.at[pl.ds(edge, rows)], sems.at[0]).wait()
+        pltpu.make_async_copy(two, msg2_ref.at[pl.ds(edge, rows)], sems.at[1]).wait()
+
+    small = [
+        pltpu.make_async_copy(off_hbm, off_ref, sems.at[2]),
+        pltpu.make_async_copy(live_hbm, live_ref, sems.at[3]),
+        pltpu.make_async_copy(t_hbm.at[pl.ds(rows - edge, edge)], tail_ref, sems.at[4]),
+    ]
+    for copy in small:
+        copy.start()
+    pl.when(even)(lambda: send(sci_hbm, t_hbm))
+    pl.when(jnp.logical_not(even))(lambda: send(t_hbm, sci_hbm))
+    for copy in small:
+        copy.wait()
+    lane = iota((1, cols), 1)
+    off = off_ref[0, 0]
+    note = jnp.where(lane == 0, off // B, jnp.where(lane == 1, off % B, live_ref[0, 0]))
+    head = jnp.where(iota((edge, cols), 0) == 0, note.astype(F32), tail_ref[...].astype(F32)).astype(BF16)
+    note_ref[...] = head
+    msg1_ref[0:edge, :] = head
+    msg2_ref[0:edge, :] = head
+    pl.when(even)(lambda: finish(sci_hbm, t_hbm))
+    pl.when(jnp.logical_not(even))(lambda: finish(t_hbm, sci_hbm))
+
+
 def first_kernel(
-    off_hbm, live_hbm, t_hbm, sci_hbm, bank_hbm, index_hbm, coeff_hbm, psf_hbm,
-    w_ref, pcol_ref, prow_ref, note_ref, ends_ref, sci_ref, m_ref, edge_ref, filt_ref,
-    off_ref, live_ref, t_ref, bank_ref, index_ref, coeff_ref, psf_ref, sems,
+    note_ref, t_hbm, sci_hbm, bank_hbm, index_hbm, coeff_hbm, psf_hbm,
+    w_ref, pcol_ref, prow_ref, ends_ref, sci_ref, m_ref, edge_ref, filt_ref,
+    t_ref, bank_ref, index_ref, coeff_ref, psf_ref, sems,
     src, xs, sci, diff,
 ):
     pairs = (
         (bank_hbm, bank_ref), (index_hbm, index_ref), (coeff_hbm, coeff_ref), (psf_hbm, psf_ref),
-        (off_hbm, off_ref), (live_hbm, live_ref), (t_hbm, t_ref), (sci_hbm, sci_ref),
+        (t_hbm, t_ref), (sci_hbm, sci_ref),
     )
     copies = [pltpu.make_async_copy(a, b, sems.at[n]) for n, (a, b) in enumerate(pairs)]
     for copy in copies:
@@ -174,11 +220,7 @@
         copy.wait()
     edge = 2 * B
     rows, cols = t_ref.shape
-    lane = iota((1, cols), 1)
-    off = off_ref[0, 0]
-    note = jnp.where(lane == 0, off // B, jnp.where(lane == 1, off % B, live_ref[0, 0]))
-    tail = t_ref[rows - edge : rows, :].astype(F32)
-    note_ref[...] = jnp.where(iota((edge, cols), 0) == 0, note.astype(F32), tail).astype(BF16)
+    off, _ = read_note(note_ref)
     ends_ref[0:edge, :] = t_ref[0:edge, :]
     ends_ref[edge:, :] = t_ref[rows - edge : rows, :]
     to_chunks(src, 0, t_ref[...])
@@ -212,32 +254,43 @@
 
 
 def read_note(msg_ref):
-    note = msg_ref[0:B, 0:LANES].astype(F32)
+    return decode(msg_ref[0:B, 0:LANES].astype(F32))
+
+
+def decode(note):
     return (note[0, 0] * B + note[0, 1]).astype(jnp.int32), note[0, 2]
 
 
-def before_kernel(msg_ref, sci_ref, m_ref, pcol_ref, edge_ref, filt_ref, sci, diff):
-    rows = sci_ref.shape[0]
-    off, _ = read_note(msg_ref)
-    to_chunks(sci, 0, sci_ref[...])
+def note_before(got1_ref, got2_ref):
+    even, has_before, _ = place()
+    return decode(pick(even, has_before, got2_ref[0:B, 0:LANES], got1_ref[0:B, 0:LANES]))
+
+
+def before_kernel(got1_ref, got2_ref, m_ref, pcol_ref, edge_ref, filt_ref, sci, diff):
+    edge = 2 * B
+    rows = got1_ref.shape[0] - edge
+    even, has_before, _ = place()
+    off, _ = note_before(got1_ref, got2_ref)
+    to_chunks(sci, 0, pick(even, has_before, got2_ref[edge:, :], got1_ref[edge:, :]))
     filter_inner(sci, rows - B - off, off - rows, off, m_ref, pcol_ref, edge_ref, filt_ref, diff)
 
 
 def join_kernel(
-    note_ref, ends_ref, msg_ref, next_ref, w_ref, pcol_ref, prow_ref, edge_a, edge_b, filt_a, filt_b,
+    note_ref, ends_ref, got1_ref, got2_ref, w_ref, pcol_ref, prow_ref, edge_a, edge_b, filt_a, filt_b,
     *rest,
 ):
     *outs, m_ref, src, xs, strip, diff, filt = rest
-    rows, cols = next_ref.shape
-    edge = 2 * B
-    to_chunks(src, 0, msg_ref[...])
+    edge = 2 * B
+    rows, cols = got1_ref.shape[0] - edge, got1_ref.shape[1]
+    even, has_before, has_next = place()
+    to_chunks(src, 0, pick(even, has_before, got2_ref[0:edge, :], got1_ref[0:edge, :]))
     to_chunks(src, edge, ends_ref[...])
-    to_chunks(src, 3 * edge, next_ref[0:edge, :])
+    to_chunks(src, 3 * edge, pick(even, has_next, got1_ref[edge : 2 * edge, :], got2_ref[edge : 2 * edge, :]))
     conv_blocks(src, 8, w_ref, xs, strip, 0)
     m_ref[:, 0:edge, :] = strip[:, B : B + edge, :]
     m_ref[:, edge:, :] = strip[:, 5 * B : 5 * B + edge, :]
     off_a, live_a = read_note(note_ref)
-    off_b, live_b = read_note(msg_ref)
+    off_b, live_b = note_before(got1_ref, got2_ref)
     for s, (side, first, last) in enumerate(((edge_a, off_a, off_a + rows), (edge_b, off_b - rows, off_b))):
         for c in range(cols // LANES):
             part = slice(c * LANES, (c + 1) * LANES)
@@ -271,9 +324,10 @@
         out_ref[share : share + B, :] = note.astype(BF16)
 
 
-def tile_kernel(sci_ref, note_ref, next_ref, m1_ref, edge_ref, w_ref, out_ref, src, xs, big):
-    rows, cols = next_ref.shape
-    to_chunks(src, 0, next_ref[...])
+def tile_kernel(sci_ref, note_ref, got1_ref, got2_ref, m1_ref, edge_ref, w_ref, out_ref, src, xs, big):
+    rows, cols = sci_ref.shape
+    even, _, has_next = place()
+    to_chunks(src, 0, pick(even, has_next, got1_ref[2 * B :, :], got2_ref[2 * B :, :]))
     conv_blocks(src, rows // B, w_ref, xs, big, rows)
     big[:, 0:B, :] = edge_ref[:, B : 2 * B, :]
     big[:, B : rows - B, :] = m1_ref[:, B : rows - B, :]
@@ -325,14 +379,27 @@
     chunks, blocks = cols // LANES, cols // B
     edge = 2 * B
     inner = rows - edge
-    before = shifted(science, "patch", 1)[:, 0, :]
-    following = shifted(template, "patch", -1)
-
     sds = jax.ShapeDtypeStruct
     deep = 9 * CH
     depth = -(-(share + edge) // LANES) * LANES
     sci = science[:, 0, :]
     taps = psf_profile.shape[0]
+    held = in_hbm(template, sci)
+    msg1, msg2, note = call(
+        pack_kernel,
+        (sds((edge + rows, cols), BF16), sds((edge + rows, cols), BF16), sds((edge, cols), BF16)),
+        [HBM] * 4,
+        [
+            pltpu.SMEM((1, 1), jnp.int32), pltpu.SMEM((1, 1), jnp.int32), pltpu.VMEM((edge, cols), BF16),
+            pltpu.SemaphoreType.DMA((5,)),
+        ],
+        1 << 20, "pack",
+    )(offsets, live_flags, *held)
+    panels = lax.axis_size("patch")
+    got1, got2 = (
+        lax.ppermute(msg, "patch", [(p, swap_partner(p, parity, panels)) for p in range(panels)])
+        for parity, msg in enumerate((msg1, msg2))
+    )
     index = jnp.swapaxes(basis_index, 1, 2)
     count = rows // B
     conv_scratch = [
@@ -342,22 +409,20 @@
     conv_flops = 2 * rows * cols * deep
     sky_scratch = [pltpu.VMEM((chunks, 2 * rows + B, LANES), F32), pltpu.VMEM((inner, cols), BF16)]
     sides = (sds((chunks, 2 * edge, LANES), F32), sds((inner, cols), BF16))
-    w, pcol, prow, note, ends, tile, m1, edge_a, filt_a = call(
+    w, pcol, prow, ends, tile, m1, edge_a, filt_a = call(
         first_kernel,
         (
-            sds((deep, CH), BF16), sds((cols, cols), BF16), sds((share, depth), BF16), sds((edge, cols), BF16),
-            sds((2 * edge, cols), BF16), sds((rows, cols), BF16), sds((chunks, rows, LANES), F32),
+            sds((deep, CH), BF16), sds((cols, cols), BF16), sds((share, depth), BF16), sds((2 * edge, cols), BF16),
+             sds((rows, cols), BF16), sds((chunks, rows, LANES), F32),
         ) + sides,
-        [HBM] * 8,
+        [VM] + [HBM] * 6,
         [
-            pltpu.SMEM((1, 1), jnp.int32), pltpu.SMEM((1, 1), jnp.int32), pltpu.VMEM((rows, cols), BF16),
-            pltpu.VMEM(bank.shape, BF16), pltpu.VMEM(index.shape, jnp.int32),
-            pltpu.VMEM(coeff.shape, F32), pltpu.VMEM((1, taps), BF16), pltpu.SemaphoreType.DMA((8,)),
+            pltpu.VMEM((rows, cols), BF16), pltpu.VMEM(bank.shape, BF16), pltpu.VMEM(index.shape, jnp.int32),
+            pltpu.VMEM(coeff.shape, F32), pltpu.VMEM((1, taps), BF16), pltpu.SemaphoreType.DMA((6,)),
         ] + conv_scratch + sky_scratch,
         conv_flops, "first",
-    )(offsets, live_flags, *in_hbm(template, sci, bank, index, coeff, psf_profile[None]))
-    msg = shifted(note, "patch", 1)
-    edge_b, filt_b = call(before_kernel, sides, [VM] * 4, sky_scratch, 1 << 28, "before")(msg, before, m1, pcol)
+    )(note, *held, *in_hbm(bank, index, coeff, psf_profile[None]))
+    edge_b, filt_b = call(before_kernel, sides, [VM] * 4, sky_scratch, 1 << 28, "before")(got1, got2, m1, pcol)
     *parts, m_edge = call(
         join_kernel,
         (sds((share + B, cols), BF16),) * sharers + (sds((chunks, 2 * edge, LANES), F32),),
@@ -370,14 +435,14 @@
             pltpu.VMEM((2, rows - share + depth, cols), BF16),
         ],
         1 << 29, "join",
-    )(note, ends, msg, following, w, pcol, prow, edge_a, edge_b, filt_a, filt_b)
+    )(note, ends, got1, got2, w, pcol, prow, edge_a, edge_b, filt_a, filt_b)
     for k in reversed(range(1, sharers)):
         pairs = [(i, partner(i, k, sharers)) for i in range(sharers)]
         parts[k] = lax.ppermute(parts[k], ("visit", "band"), pairs)
     difference = call(
-        tile_kernel, sds((rows, cols), BF16), [VM] * 6,
+        tile_kernel, sds((rows, cols), BF16), [VM] * 7,
         conv_scratch + [pltpu.VMEM((chunks, 2 * rows, LANES), F32)], conv_flops, "tile",
-    )(tile, note, following, m1, m_edge, w)
+    )(tile, note, got1, got2, m1, m_edge, w)
     detection = call(coadd_kernel, sds((share, cols), F32), [VM] * sharers, [], 1 << 20, "coadd")(parts[0], *parts[:0:-1])
     return (difference[:, None, :], detection)
 

time: 33.6 us -> 34.3 us (1.021)
  the two profiles are of different devices: /device:TPU:0 before, /device:TPU:17 now
where the time goes in v7:
time: 34.3 us; the launch traced here: 34.1 us
  Pallas kernels  14.5 us (42%)
  waiting for transfers between devices  10.9 us (32%)
  starting transfers between devices  6.76 us (20%)
  between operations  1.96 us (6%)
    ppermute x2, waiting for transfers between devices, on_device(): lax.ppermute(msg, 'patch', [(p, swap_partner(p, parity, panels)) for p in...  7.57 us
    pallas_call x1, Pallas kernels, on_device(): call(first_kernel, (sds((deep, CH), BF16), sds((cols, cols), BF16), sds((...  5.56 us
    pallas_call x1, Pallas kernels, on_device(): call(tile_kernel, sds((rows, cols), BF16), [VM] * 7, conv_scratch + [pltp...  4.02 us
    ppermute x3, starting transfers between devices, on_device(): parts[k] = lax.ppermute(parts[k], ('visit', 'band'), pairs)  3.49 us
    ppermute x3, waiting for transfers between devices, on_device(): parts[k] = lax.ppermute(parts[k], ('visit', 'band'), pairs)  3.3 us
    ppermute x2, starting transfers between devices, on_device(): lax.ppermute(msg, 'patch', [(p, swap_partner(p, parity, panels)) for p in...  3.27 us
    pallas_call x1, Pallas kernels, on_device(): call(join_kernel, (sds((share + B, cols), BF16),) * sharers + (sds((chunk...  1.97 us
    pallas_call x1, Pallas kernels, on_device(): call(pack_kernel, (sds((edge + rows, cols), BF16), sds((edge + rows, cols...  1.27 us
  transfers between devices with their start and end apart: 5, of which 4 were waited for; matrix products, arithmetic and copies ran while one was open for 0% of the time, Pallas kernels for 28%

profile of v7, /device:TPU:17, one launch (start us, length us, event | category | flops | bytes accessed | tf_op | source)
XLA Modules:
  0.0 34.1 jit_solution(14604901587452671817)
XLA Ops:
  1.9 1.3 %pack.1 = (bf16[544,512]{1,0:T(8,128)(2,1)S(1)}, bf16[544,512]{1,0:T(8,128)(2,1)S(1)}, bf16[32,512]{1,0:T(8,128)(2,1)S(1)}) custom-call(s32[1,1]{1,0:T(1,128)S(6)} %copy.10.off_hbm, s32[1,1]{1,0:T(1,128)S(6)} %copy.11.live_hbm, bf16[512,512]{1,0:T(8,128)(2,1)} %t_hbm.3, bf16[512,512]{1,0:T(8,128)(2,1)} %bitcast.5), custom_call_target="tpu_custom_call" | custom-call | flops 1048576 | bytes 2097152 | tf_op jit(solution)/shard_map/pack/pallas_call | solution.py:388
  3.2 1.4 %collective-permute-start = (bf16[544,512]{1,0:T(8,128)(2,1)S(1)}, bf16[544,512]{1,0:T(8,128)(2,1)S(1)}, u32[]{:S(2)}, u32[]{:S(2)}) collective-permute-start(bf16[544,512]{1,0:T(8,128)(2,1)S(1)} %get-tuple-element.22), channel_id=1, source_target_pairs={{0,4},{4,0},{8,12},{12,8},{1,5},{5,1},{9,13},{13,9},{2,6},{6,2},{1... | collective-permute-start | bytes 1671176 | tf_op jit(solution)/shard_map/ppermute | solution.py:400
  4.6 1.9 %collective-permute-start.1 = (bf16[544,512]{1,0:T(8,128)(2,1)S(1)}, bf16[544,512]{1,0:T(8,128)(2,1)S(1)}, u32[]{:S(2)}, u32[]{:S(2)}) collective-permute-start(bf16[544,512]{1,0:T(8,128)(2,1)S(1)} %get-tuple-element.23), channel_id=1, source_target_pairs={{0,0},{4,8},{8,4},{12,12},{1,1},{5,9},{9,5},{13,13},{2,2},{6,10},{... | collective-permute-start | bytes 1671176 | tf_op jit(solution)/shard_map/ppermute | solution.py:400
  6.5 5.6 %first.1 = (bf16[2304,256]{1,0:T(8,128)(2,1)S(1)}, bf16[512,512]{1,0:T(8,128)(2,1)S(1)}, bf16[128,256]{1,0:T(8,128)(2,1)S(1)}, bf16[64,512]{1,0:T(8,128)(2,1)S(1...) custom-call(bf16[32,512]{1,0:T(8,128)(2,1)S(1)} %get-tuple-element.2, ...), custom_call_target="tpu_custom_call" | custom-call | flops 1207959552 | bytes 2097152 | tf_op jit(solution)/shard_map/first/pallas_call | solution.py:412
  12.0 4.7 %collective-permute-done.got1_ref = bf16[544,512]{1,0:T(8,128)(2,1)S(1)} collective-permute-done((bf16[544,512]{1,0:T(8,128)(2,1)S(1)}, bf16[544,512]{1,0:T(8,128)(2,1)S(1)}, u32[]{:S(2)}, u32[]{:S(2)}) %collective-permute-start) | collective-permute-done | bytes 557088 | tf_op jit(solution)/shard_map/ppermute | solution.py:400
  16.8 2.9 %collective-permute-done.1.got2_ref = bf16[544,512]{1,0:T(8,128)(2,1)S(1)} collective-permute-done((bf16[544,512]{1,0:T(8,128)(2,1)S(1)}, bf16[544,512]{1,0:T(8,128)(2,1)S(1)}, u32[]{:S(2)}, u32[]{:S(2)}) %collective-permute-start.1) | collective-permute-done | bytes 557088 | tf_op jit(solution)/shard_map/ppermute | solution.py:400
  19.6 0.7 %before.1 = (f32[4,64,128]{2,1,0:T(8,128)S(1)}, bf16[480,512]{1,0:T(8,128)(2,1)S(1)}) custom-call(bf16[544,512]{1,0:T(8,128)(2,1)S(1)} %collective-permute-done.got1_ref, bf16[544,512]{1,0:T(8,128)(2,1)S(1)} %collective-permute-done.1.got2_ref, f32[4,512,128]{2,1,0:T(8,128)S(1)} %get-tuple-element.24.m_ref.m1_ref, ...), custom_call_target="tpu_custom_call" | custom-call | flops 268435456 | bytes 2097152 | tf_op jit(solution)/shard_map/before/pallas_call | solution.py:425
  20.4 2.0 %join.1 = (bf16[144,512]{1,0:T(8,128)(2,1)S(1)}, bf16[144,512]{1,0:T(8,128)(2,1)S(1)}, bf16[144,512]{1,0:T(8,128)(2,1)S(1)}, bf16[144,512]{1,0:T(8,128)(2,1)S(1)}, f32[4,64,128]{2,1,0:T(8,128)S(1)}) custom-call(bf16[32,512]{1,0:T(8,128)(2,1)S(1)} %get-tuple-element.20.note_ref, bf16[64,512]{1,0:T(8,128)(2,1)S(1)} %get-tuple-element.25.ends_ref, ...), custom_call_target="tpu_custom_call" | custom-call | flops 536870912 | bytes 2097152 | tf_op jit(solution)/shard_map/join/pallas_call | solution.py:426
  22.3 3.0 %collective-permute-start.2 = (bf16[144,512]{1,0:T(8,128)(2,1)S(1)}, bf16[144,512]{1,0:T(8,128)(2,1)S(1)}, u32[]{:S(2)}, u32[]{:S(2)}) collective-permute-start(bf16[144,512]{1,0:T(8,128)(2,1)S(1)} %get-tuple-element.35), channel_id=1, source_target_pairs={{0,3},{1,2},{2,1},{3,0},{4,7},{5,6},{6,5},{7,4},{8,11},{9,10},{10,... | collective-permute-start | bytes 442376 | tf_op jit(solution)/shard_map/ppermute | solution.py:441
  25.4 0.3 collective-permute-start.3
  25.6 0.2 collective-permute-start.4
  25.8 4.0 %tile.1 = bf16[512,512]{1,0:T(8,128)(2,1)} custom-call(bf16[512,512]{1,0:T(8,128)(2,1)S(1)} %get-tuple-element.21.sci_ref, bf16[32,512]{1,0:T(8,128)(2,1)S(1)} %get-tuple-element.20.note_ref, bf16[544,512]{1,0:T(8,128)(2,1)S(1)} %collective-permute-done.got1_ref, bf16[544,512]{1,0:T(8,128)(2,1)S(1)} %collective-permute-done.1.got2_ref, ...), custom_call_target="tpu_custom_call" | custom-call | flops 1207959552 | bytes 2097152 | tf_op jit(solution)/shard_map/tile/pallas_call | solution.py:442
  29.8 0.1 collective-permute-done.2.refs_1_
  30.0 3.2 %collective-permute-done.3.refs_2_ = bf16[144,512]{1,0:T(8,128)(2,1)S(1)} collective-permute-done((bf16[144,512]{1,0:T(8,128)(2,1)S(1)}, bf16[144,512]{1,0:T(8,128)(2,1)S(1)}, u32[]{:S(2)}, u32[]{:S(2)}) %collective-permute-start.3) | collective-permute-done | bytes 147488 | tf_op jit(solution)/shard_map/ppermute | solution.py:441
  33.1 0.0 collective-permute-done.4.refs_3_
  33.1 0.9 %coadd.1 = f32[128,512]{1,0:T(8,128)} custom-call(bf16[144,512]{1,0:T(8,128)(2,1)S(1)} %get-tuple-element.34.refs_0_, bf16[144,512]{1,0:T(8,128)(2,1)S(1)} %collective-permute-done.2.refs_1_, bf16[144,512]{1,0:T(8,128)(2,1)S(1)} %collective-permute-done.3.refs_2_, bf16[144,512]{1,0:T(8,128)(2,1)S(1)} %collective-permute-done.4.refs_3_), custom_call_target="tpu_custom_call" | custom-call | flops 1048576 | bytes 2097152 | tf_op jit(solution)/shard_map/coadd/pallas_call | solution.py:446
Async XLA Ops:
  3.2 13.6 %collective-permute-start = (bf16[544,512]{1,0:T(8,128)(2,1)S(1)}, bf16[544,512]{1,0:T(8,128)(2,1)S(1)}, u32[]{:S(2)}, u32[]{:S(2)}) collective-permute-start(bf16[544,512]{1,0:T(8,128)(2,1)S(1)} %get-tuple-element.22), channel_id=1, source_target_pairs={{0,4},{4,0},{8,12},{12,8},{1,5},{5,1},{9,13},{13,9},{2,6},{6,2},{1... | collective-permute-start | bytes 1671176 | tf_op jit(solution)/shard_map/ppermute | solution.py:400
  4.6 15.1 %collective-permute-start.1 = (bf16[544,512]{1,0:T(8,128)(2,1)S(1)}, bf16[544,512]{1,0:T(8,128)(2,1)S(1)}, u32[]{:S(2)}, u32[]{:S(2)}) collective-permute-start(bf16[544,512]{1,0:T(8,128)(2,1)S(1)} %get-tuple-element.23), channel_id=1, source_target_pairs={{0,0},{4,8},{8,4},{12,12},{1,1},{5,9},{9,5},{13,13},{2,2},{6,10},{... | collective-permute-start | bytes 1671176 | tf_op jit(solution)/shard_map/ppermute | solution.py:400
  22.3 7.6 %collective-permute-start.2 = (bf16[144,512]{1,0:T(8,128)(2,1)S(1)}, bf16[144,512]{1,0:T(8,128)(2,1)S(1)}, u32[]{:S(2)}, u32[]{:S(2)}) collective-permute-start(bf16[144,512]{1,0:T(8,128)(2,1)S(1)} %get-tuple-element.35), channel_id=1, source_target_pairs={{0,3},{1,2},{2,1},{3,0},{4,7},{5,6},{6,5},{7,4},{8,11},{9,10},{10,... | collective-permute-start | bytes 442376 | tf_op jit(solution)/shard_map/ppermute | solution.py:441
  25.4 7.8 %collective-permute-start.3 = (bf16[144,512]{1,0:T(8,128)(2,1)S(1)}, bf16[144,512]{1,0:T(8,128)(2,1)S(1)}, u32[]{:S(2)}, u32[]{:S(2)}) collective-permute-start(bf16[144,512]{1,0:T(8,128)(2,1)S(1)} %get-tuple-element.36), channel_id=1, source_target_pairs={{0,2},{1,3},{2,0},{3,1},{4,6},{5,7},{6,4},{7,5},{8,10},{9,11},{10,... | collective-permute-start | bytes 442376 | tf_op jit(solution)/shard_map/ppermute | solution.py:441
  25.6 7.5 %collective-permute-start.4 = (bf16[144,512]{1,0:T(8,128)(2,1)S(1)}, bf16[144,512]{1,0:T(8,128)(2,1)S(1)}, u32[]{:S(2)}, u32[]{:S(2)}) collective-permute-start(bf16[144,512]{1,0:T(8,128)(2,1)S(1)} %get-tuple-element.37), channel_id=1, source_target_pairs={{0,1},{1,0},{2,3},{3,2},{4,5},{5,4},{6,7},{7,6},{8,9},{9,8},{10,11... | collective-permute-start | bytes 442376 | tf_op jit(solution)/shard_map/ppermute | solution.py:441

commit v8 on v7

--- a/solution.py
+++ b/solution.py
@@ -11,8 +11,15 @@
 CH = B * B
 LANES = 128
 GROUPS = LANES // B
+PITCH = B + 1
 F32 = jnp.float32
 BF16 = jnp.bfloat16
+
+
+def shifted(shard, axis, by):
+    devices = lax.axis_size(axis)
+    pairs = [(i, i + by) for i in range(devices) if 0 <= i + by < devices]
+    return lax.ppermute(shard, axis, pairs)
 
 
 def swap_partner(p, parity, count):
@@ -57,30 +64,27 @@
     return parts
 
 
-def conv_blocks(src, count, w_ref, xs, dst, dst_row):
+def to_blocks(dst, block, value):
+    value = value.astype(F32)
+    for a in range(value.shape[0] // B):
+        at = (block + a) * PITCH
+        for c in range(dst.shape[0]):
+            dst[c, at : at + B, :] = value[a * B : (a + 1) * B, c * LANES : (c + 1) * LANES]
+
+
+def conv_blocks(src, count, w_ref, xs, dst):
     chunks = src.shape[0]
     blocks = chunks * GROUPS
-    wide = count // 8
 
     def load(c):
         for h in range(2):
-            rows = [
-                jnp.concatenate(
-                    [src[c, pl.ds(B * v + GROUPS * h + i, 8, stride=B * wide), :] for v in range(wide)], axis=0
-                )
-                for i in range(GROUPS)
-            ]
+            rows = [src[c, pl.ds(GROUPS * h + i, count, stride=PITCH), :] for i in range(GROUPS)]
             part = slice(h * LANES, (h + 1) * LANES)
             for g, here in enumerate(group_transpose(rows)):
                 at = 1 + c * GROUPS + g
-                after = pltpu.roll(here[0:8], 7, 0)
-                prior = pltpu.roll(here[count - 8 :], 1, 0)
-                if wide > 1:
-                    after = jnp.concatenate([here[8:], after], axis=0)
-                    prior = jnp.concatenate([prior, here[: count - 8]], axis=0)
-                xs[0, at, :, part] = prior.astype(xs.dtype)
+                xs[0, at, :, part] = pltpu.roll(here, 1, 0).astype(xs.dtype)
                 xs[1, at, :, part] = here.astype(xs.dtype)
-                xs[2, at, :, part] = after.astype(xs.dtype)
+                xs[2, at, :, part] = pltpu.roll(here, count - 1, 0).astype(xs.dtype)
 
     def solve(c):
         b = c * GROUPS
@@ -94,8 +98,7 @@
             part = slice(h * LANES, (h + 1) * LANES)
             rows = group_transpose([out[g * count : (g + 1) * count, part] for g in range(GROUPS)])
             for i in range(GROUPS):
-                for v in range(wide):
-                    dst[c, pl.ds(dst_row + B * v + GROUPS * h + i, 8, stride=B * wide), :] = rows[i][8 * v : 8 * v + 8]
+                dst[c, pl.ds(GROUPS * h + i, count, stride=PITCH), :] = rows[i]
 
     for q in range(3):
         xs[q, 0] = jnp.zeros((count, CH), xs.dtype)
@@ -113,48 +116,31 @@
     return jnp.sum(jnp.where(diag, row, jnp.zeros_like(row)), axis=1, keepdims=True)
 
 
-def pack_kernel(
-    off_hbm, live_hbm, t_hbm, sci_hbm, msg1_ref, msg2_ref, note_ref, off_ref, live_ref, tail_ref, sems
-):
+def pack_kernel(off_hbm, live_hbm, t_hbm, msg_ref, off_ref, live_ref, sems):
     rows, cols = t_hbm.shape
     edge = 2 * B
-    even, _, _ = place()
-
-    def send(one, two):
-        pltpu.make_async_copy(one, msg1_ref.at[pl.ds(edge, rows)], sems.at[0]).start()
-        pltpu.make_async_copy(two, msg2_ref.at[pl.ds(edge, rows)], sems.at[1]).start()
-
-    def finish(one, two):
-        pltpu.make_async_copy(one, msg1_ref.at[pl.ds(edge, rows)], sems.at[0]).wait()
-        pltpu.make_async_copy(two, msg2_ref.at[pl.ds(edge, rows)], sems.at[1]).wait()
-
-    small = [
+    copies = [
+        pltpu.make_async_copy(t_hbm.at[pl.ds(rows - edge, edge)], msg_ref.at[pl.ds(0, edge)], sems.at[0]),
+        pltpu.make_async_copy(t_hbm.at[pl.ds(0, edge)], msg_ref.at[pl.ds(edge, edge)], sems.at[1]),
         pltpu.make_async_copy(off_hbm, off_ref, sems.at[2]),
         pltpu.make_async_copy(live_hbm, live_ref, sems.at[3]),
-        pltpu.make_async_copy(t_hbm.at[pl.ds(rows - edge, edge)], tail_ref, sems.at[4]),
     ]
-    for copy in small:
+    for copy in copies:
         copy.start()
-    pl.when(even)(lambda: send(sci_hbm, t_hbm))
-    pl.when(jnp.logical_not(even))(lambda: send(t_hbm, sci_hbm))
-    for copy in small:
+    for copy in copies:
         copy.wait()
     lane = iota((1, cols), 1)
     off = off_ref[0, 0]
-    note = jnp.where(lane == 0, off // B, jnp.where(lane == 1, off % B, live_ref[0, 0]))
-    head = jnp.where(iota((edge, cols), 0) == 0, note.astype(F32), tail_ref[...].astype(F32)).astype(BF16)
-    note_ref[...] = head
-    msg1_ref[0:edge, :] = head
-    msg2_ref[0:edge, :] = head
-    pl.when(even)(lambda: finish(sci_hbm, t_hbm))
-    pl.when(jnp.logical_not(even))(lambda: finish(t_hbm, sci_hbm))
+    note = jnp.where(lane == 0, off // B, jnp.where(lane == 1, off % B, live_ref[0, 0])).astype(F32)
+    block = msg_ref[0:B, :].astype(F32)
+    msg_ref[0:B, :] = jnp.where(iota((B, cols), 0) == 0, note, block).astype(BF16)
 
 
 def first_kernel(
     note_ref, t_hbm, sci_hbm, bank_hbm, index_hbm, coeff_hbm, psf_hbm,
-    w_ref, pcol_ref, prow_ref, ends_ref, sci_ref, m_ref, edge_ref, filt_ref,
+    w_ref, pcol_ref, prow_ref, sci_ref, m_ref, edge_ref, filt_ref,
     t_ref, bank_ref, index_ref, coeff_ref, psf_ref, sems,
-    src, xs, sci, diff,
+    src, xs, res, sci, diff,
 ):
     pairs = (
         (bank_hbm, bank_ref), (index_hbm, index_ref), (coeff_hbm, coeff_ref), (psf_hbm, psf_ref),
@@ -221,10 +207,10 @@
     edge = 2 * B
     rows, cols = t_ref.shape
     off, _ = read_note(note_ref)
-    ends_ref[0:edge, :] = t_ref[0:edge, :]
-    ends_ref[edge:, :] = t_ref[rows - edge : rows, :]
-    to_chunks(src, 0, t_ref[...])
-    conv_blocks(src, rows // B, w_ref, xs, m_ref, 0)
+    to_blocks(src, 0, t_ref[...])
+    conv_blocks(src, rows // B, w_ref, xs, res)
+    for a in range(1, rows // B - 1):
+        m_ref[:, B * a : B * (a + 1), :] = res[:, PITCH * a : PITCH * a + B, :]
     to_chunks(sci, rows, sci_ref[...])
     filter_inner(sci, rows - B - off, off, off + rows, m_ref, pcol_ref, edge_ref, filt_ref, diff)
 
@@ -266,29 +252,28 @@
     return decode(pick(even, has_before, got2_ref[0:B, 0:LANES], got1_ref[0:B, 0:LANES]))
 
 
-def before_kernel(got1_ref, got2_ref, m_ref, pcol_ref, edge_ref, filt_ref, sci, diff):
-    edge = 2 * B
-    rows = got1_ref.shape[0] - edge
-    even, has_before, _ = place()
+def before_kernel(got1_ref, got2_ref, sci_ref, m_ref, pcol_ref, edge_ref, filt_ref, sci, diff):
+    rows = sci_ref.shape[0]
     off, _ = note_before(got1_ref, got2_ref)
-    to_chunks(sci, 0, pick(even, has_before, got2_ref[edge:, :], got1_ref[edge:, :]))
+    to_chunks(sci, 0, sci_ref[...])
     filter_inner(sci, rows - B - off, off - rows, off, m_ref, pcol_ref, edge_ref, filt_ref, diff)
 
 
 def join_kernel(
-    note_ref, ends_ref, got1_ref, got2_ref, w_ref, pcol_ref, prow_ref, edge_a, edge_b, filt_a, filt_b,
+    note_ref, got1_ref, got2_ref, w_ref, pcol_ref, prow_ref, edge_a, edge_b, filt_a, filt_b,
     *rest,
 ):
     *outs, m_ref, src, xs, strip, diff, filt = rest
     edge = 2 * B
-    rows, cols = got1_ref.shape[0] - edge, got1_ref.shape[1]
+    rows, cols = filt_a.shape[0] + edge, filt_a.shape[1]
     even, has_before, has_next = place()
-    to_chunks(src, 0, pick(even, has_before, got2_ref[0:edge, :], got1_ref[0:edge, :]))
-    to_chunks(src, edge, ends_ref[...])
-    to_chunks(src, 3 * edge, pick(even, has_next, got1_ref[edge : 2 * edge, :], got2_ref[edge : 2 * edge, :]))
-    conv_blocks(src, 8, w_ref, xs, strip, 0)
-    m_ref[:, 0:edge, :] = strip[:, B : B + edge, :]
-    m_ref[:, edge:, :] = strip[:, 5 * B : 5 * B + edge, :]
+    to_blocks(src, 0, pick(even, has_before, got2_ref[0:edge, :], got1_ref[0:edge, :]))
+    to_blocks(src, 2, note_ref[edge:, :])
+    to_blocks(src, 4, note_ref[0:edge, :])
+    to_blocks(src, 6, pick(even, has_next, got1_ref[edge:, :], got2_ref[edge:, :]))
+    conv_blocks(src, 8, w_ref, xs, strip)
+    for n, a in enumerate((1, 2, 5, 6)):
+        m_ref[:, B * n : B * (n + 1), :] = strip[:, PITCH * a : PITCH * a + B, :]
     off_a, live_a = read_note(note_ref)
     off_b, live_b = note_before(got1_ref, got2_ref)
     for s, (side, first, last) in enumerate(((edge_a, off_a, off_a + rows), (edge_b, off_b - rows, off_b))):
@@ -324,11 +309,12 @@
         out_ref[share : share + B, :] = note.astype(BF16)
 
 
-def tile_kernel(sci_ref, note_ref, got1_ref, got2_ref, m1_ref, edge_ref, w_ref, out_ref, src, xs, big):
+def tile_kernel(sci_ref, note_ref, next_ref, m1_ref, edge_ref, w_ref, out_ref, src, xs, res, big):
     rows, cols = sci_ref.shape
-    even, _, has_next = place()
-    to_chunks(src, 0, pick(even, has_next, got1_ref[2 * B :, :], got2_ref[2 * B :, :]))
-    conv_blocks(src, rows // B, w_ref, xs, big, rows)
+    to_blocks(src, 0, next_ref[...])
+    conv_blocks(src, rows // B, w_ref, xs, res)
+    for a in range(1, rows // B):
+        big[:, rows + B * a : rows + B * (a + 1), :] = res[:, PITCH * a : PITCH * a + B, :]
     big[:, 0:B, :] = edge_ref[:, B : 2 * B, :]
     big[:, B : rows - B, :] = m1_ref[:, B : rows - B, :]
     big[:, rows - B : rows + B, :] = edge_ref[:, 2 * B : 4 * B, :]
@@ -385,35 +371,33 @@
     sci = science[:, 0, :]
     taps = psf_profile.shape[0]
     held = in_hbm(template, sci)
-    msg1, msg2, note = call(
-        pack_kernel,
-        (sds((edge + rows, cols), BF16), sds((edge + rows, cols), BF16), sds((edge, cols), BF16)),
-        [HBM] * 4,
-        [
-            pltpu.SMEM((1, 1), jnp.int32), pltpu.SMEM((1, 1), jnp.int32), pltpu.VMEM((edge, cols), BF16),
-            pltpu.SemaphoreType.DMA((5,)),
-        ],
+    index = jnp.swapaxes(basis_index, 1, 2)
+    before = shifted(science, "patch", 1)[:, 0, :]
+    following = shifted(template, "patch", -1)
+    note = call(
+        pack_kernel, sds((2 * edge, cols), BF16), [HBM] * 3,
+        [pltpu.SMEM((1, 1), jnp.int32), pltpu.SMEM((1, 1), jnp.int32), pltpu.SemaphoreType.DMA((4,))],
         1 << 20, "pack",
-    )(offsets, live_flags, *held)
+    )(offsets, live_flags, held[0])
     panels = lax.axis_size("patch")
     got1, got2 = (
-        lax.ppermute(msg, "patch", [(p, swap_partner(p, parity, panels)) for p in range(panels)])
-        for parity, msg in enumerate((msg1, msg2))
+        lax.ppermute(note, "patch", [(p, swap_partner(p, parity, panels)) for p in range(panels)])
+        for parity in range(2)
     )
-    index = jnp.swapaxes(basis_index, 1, 2)
     count = rows // B
     conv_scratch = [
-        pltpu.VMEM((chunks, rows, LANES), F32),
+        pltpu.VMEM((chunks, count * PITCH, LANES), F32),
         pltpu.VMEM((3, blocks + 2, count, CH), BF16),
+        pltpu.VMEM((chunks, count * PITCH, LANES), F32),
     ]
     conv_flops = 2 * rows * cols * deep
     sky_scratch = [pltpu.VMEM((chunks, 2 * rows + B, LANES), F32), pltpu.VMEM((inner, cols), BF16)]
     sides = (sds((chunks, 2 * edge, LANES), F32), sds((inner, cols), BF16))
-    w, pcol, prow, ends, tile, m1, edge_a, filt_a = call(
+    w, pcol, prow, tile, m1, edge_a, filt_a = call(
         first_kernel,
         (
-            sds((deep, CH), BF16), sds((cols, cols), BF16), sds((share, depth), BF16), sds((2 * edge, cols), BF16),
-             sds((rows, cols), BF16), sds((chunks, rows, LANES), F32),
+            sds((deep, CH), BF16), sds((cols, cols), BF16), sds((share, depth), BF16),
+            sds((rows, cols), BF16), sds((chunks, rows, LANES), F32),
         ) + sides,
         [VM] + [HBM] * 6,
         [
@@ -422,27 +406,27 @@
         ] + conv_scratch + sky_scratch,
         conv_flops, "first",
     )(note, *held, *in_hbm(bank, index, coeff, psf_profile[None]))
-    edge_b, filt_b = call(before_kernel, sides, [VM] * 4, sky_scratch, 1 << 28, "before")(got1, got2, m1, pcol)
+    edge_b, filt_b = call(before_kernel, sides, [VM] * 5, sky_scratch, 1 << 28, "before")(got1, got2, before, m1, pcol)
     *parts, m_edge = call(
         join_kernel,
         (sds((share + B, cols), BF16),) * sharers + (sds((chunks, 2 * edge, LANES), F32),),
-        [VM] * 11,
+        [VM] * 10,
         [
-            pltpu.VMEM((chunks, 8 * B, LANES), F32),
+            pltpu.VMEM((chunks, 8 * PITCH, LANES), F32),
             pltpu.VMEM((3, blocks + 2, 8, CH), F32),
-            pltpu.VMEM((chunks, 8 * B, LANES), F32),
+            pltpu.VMEM((chunks, 8 * PITCH, LANES), F32),
             pltpu.VMEM((4 * edge, cols), BF16),
             pltpu.VMEM((2, rows - share + depth, cols), BF16),
         ],
         1 << 29, "join",
-    )(note, ends, got1, got2, w, pcol, prow, edge_a, edge_b, filt_a, filt_b)
+    )(note, got1, got2, w, pcol, prow, edge_a, edge_b, filt_a, filt_b)
     for k in reversed(range(1, sharers)):
         pairs = [(i, partner(i, k, sharers)) for i in range(sharers)]
         parts[k] = lax.ppermute(parts[k], ("visit", "band"), pairs)
     difference = call(
-        tile_kernel, sds((rows, cols), BF16), [VM] * 7,
+        tile_kernel, sds((rows, cols), BF16), [VM] * 6,
         conv_scratch + [pltpu.VMEM((chunks, 2 * rows, LANES), F32)], conv_flops, "tile",
-    )(tile, note, got1, got2, m1, m_edge, w)
+    )(tile, note, following, m1, m_edge, w)
     detection = call(coadd_kernel, sds((share, cols), F32), [VM] * sharers, [], 1 << 20, "coadd")(parts[0], *parts[:0:-1])
     return (difference[:, None, :], detection)
 

time: 34.3 us -> 35.6 us (1.038)
  the two profiles are of different devices: /device:TPU:17 before, /device:TPU:0 now
where the time goes in v8:
time: 35.6 us; the launch traced here: 35.4 us
  Pallas kernels  12.5 us (35%)
  starting transfers between devices  11.5 us (32%)
  waiting for transfers between devices  9.38 us (26%)
  between operations  1.99 us (6%)
    ppermute x2, starting transfers between devices, shifted(): return lax.ppermute(shard, axis, pairs)  6.25 us
    ppermute x2, waiting for transfers between devices, on_device(): lax.ppermute(note, 'patch', [(p, swap_partner(p, parity, panels)) for p i...  5.19 us
    pallas_call x1, Pallas kernels, on_device(): call(first_kernel, (sds((deep, CH), BF16), sds((cols, cols), BF16), sds((...  4.89 us
    ppermute x3, waiting for transfers between devices, on_device(): parts[k] = lax.ppermute(parts[k], ('visit', 'band'), pairs)  4.18 us
    ppermute x2, starting transfers between devices, on_device(): lax.ppermute(note, 'patch', [(p, swap_partner(p, parity, panels)) for p i...  3.36 us
    pallas_call x1, Pallas kernels, on_device(): call(tile_kernel, sds((rows, cols), BF16), [VM] * 6, conv_scratch + [pltp...  3.26 us
    pallas_call x1, Pallas kernels, on_device(): call(join_kernel, (sds((share + B, cols), BF16),) * sharers + (sds((chunk...  1.96 us
    ppermute x3, starting transfers between devices, on_device(): parts[k] = lax.ppermute(parts[k], ('visit', 'band'), pairs)  1.92 us
  transfers between devices with their start and end apart: 7, of which 3 were waited for; matrix products, arithmetic and copies ran while one was open for 0% of the time, Pallas kernels for 33%

profile of v8, /device:TPU:0, one launch (start us, length us, event | category | flops | bytes accessed | tf_op | source)
XLA Modules:
  0.0 35.4 jit_solution(7008442137102552269)
XLA Ops:
  0.6 5.0 %collective-permute-start.3 = (bf16[512,1,512]{2,0,1:T(8,128)(2,1)}, bf16[512,1,512]{2,0,1:T(8,128)(2,1)S(1)}, u32[]{:S(2)}, u32[]{:S(2)}) collective-permute-start(bf16[512,1,512]{2,0,1:T(8,128)(2,1)} %param.9), channel_id=1, source_target_pairs={{0,4},{4,8},{8,12},{1,5},{5,9},{9,13},{2,6},{6,10},{10,14},{3,7},{... | collective-permute-start | bytes 1572872 | tf_op jit(solution)/shard_map/ppermute | solution.py:22
  5.6 1.3 %collective-permute-start = (bf16[512,512]{1,0:T(8,128)(2,1)}, bf16[512,512]{1,0:T(8,128)(2,1)S(1)}, u32[]{:S(2)}, u32[]{:S(2)}) collective-permute-start(bf16[512,512]{1,0:T(8,128)(2,1)} %t_hbm.3), channel_id=1, source_target_pairs={{4,0},{8,4},{12,8},{5,1},{9,5},{13,9},{6,2},{10,6},{14,10},{7,3},{... | collective-permute-start | bytes 1572872 | tf_op jit(solution)/shard_map/ppermute | solution.py:22
  8.2 0.8 %pack.1.note_ref = bf16[64,512]{1,0:T(8,128)(2,1)S(1)} custom-call(s32[1,1]{1,0:T(1,128)S(6)} %copy.10.off_hbm, s32[1,1]{1,0:T(1,128)S(6)} %copy.11.live_hbm, bf16[512,512]{1,0:T(8,128)(2,1)} %t_hbm.3), custom_call_target="tpu_custom_call" | custom-call | flops 1048576 | bytes 2097152 | tf_op jit(solution)/shard_map/pack/pallas_call | solution.py:377
  9.0 2.7 %collective-permute-start.1 = (bf16[64,512]{1,0:T(8,128)(2,1)S(1)}, bf16[64,512]{1,0:T(8,128)(2,1)S(1)}, u32[]{:S(2)}, u32[]{:S(2)}) collective-permute-start(bf16[64,512]{1,0:T(8,128)(2,1)S(1)} %pack.1.note_ref), channel_id=1, source_target_pairs={{0,4},{4,0},{8,12},{12,8},{1,5},{5,1},{9,13},{13,9},{2,6},{6,2},{1... | collective-permute-start | bytes 196616 | tf_op jit(solution)/shard_map/ppermute | solution.py:384
  11.8 0.7 %collective-permute-start.2 = (bf16[64,512]{1,0:T(8,128)(2,1)S(1)}, bf16[64,512]{1,0:T(8,128)(2,1)S(1)}, u32[]{:S(2)}, u32[]{:S(2)}) collective-permute-start(bf16[64,512]{1,0:T(8,128)(2,1)S(1)} %pack.1.note_ref), channel_id=1, source_target_pairs={{0,0},{4,8},{8,4},{12,12},{1,1},{5,9},{9,5},{13,13},{2,2},{6,10},{... | collective-permute-start | bytes 196616 | tf_op jit(solution)/shard_map/ppermute | solution.py:384
  12.4 4.9 %first.1 = (bf16[2304,256]{1,0:T(8,128)(2,1)S(1)}, bf16[512,512]{1,0:T(8,128)(2,1)S(1)}, bf16[128,256]{1,0:T(8,128)(2,1)S(1)}, bf16[512,512]{1,0:T(8,128)(2,1)S(...) custom-call(bf16[64,512]{1,0:T(8,128)(2,1)S(1)} %pack.1.note_ref, ...), custom_call_target="tpu_custom_call" | custom-call | flops 1207959552 | bytes 2097152 | tf_op jit(solution)/shard_map/first/pallas_call | solution.py:396
  17.3 5.2 %collective-permute-done.1.got1_ref = bf16[64,512]{1,0:T(8,128)(2,1)S(1)} collective-permute-done((bf16[64,512]{1,0:T(8,128)(2,1)S(1)}, bf16[64,512]{1,0:T(8,128)(2,1)S(1)}, u32[]{:S(2)}, u32[]{:S(2)}) %collective-permute-start.1) | collective-permute-done | bytes 65568 | tf_op jit(solution)/shard_map/ppermute | solution.py:384
  22.5 0.0 collective-permute-done.2.got2_ref
  22.5 0.0 collective-permute-done.3
  22.5 0.6 %before.1 = (f32[4,64,128]{2,1,0:T(8,128)S(1)}, bf16[480,512]{1,0:T(8,128)(2,1)S(1)}) custom-call(bf16[64,512]{1,0:T(8,128)(2,1)S(1)} %collective-permute-done.1.got1_ref, bf16[64,512]{1,0:T(8,128)(2,1)S(1)} %collective-permute-done.2.got2_ref, bf16[512,512]{1,0:T(8,128)(2,1)S(1)} %bitcast.5, f32[4,512,128]{2,1,0:T(8,128)S(1)} %get-tuple-element.17.m_ref.m1_ref, ...), custom_call_target="tpu_custom_call" | custom-call | flops 268435456 | bytes 2097152 | tf_op jit(solution)/shard_map/before/pallas_call | solution.py:409
  23.1 2.0 %join.1 = (bf16[144,512]{1,0:T(8,128)(2,1)S(1)}, bf16[144,512]{1,0:T(8,128)(2,1)S(1)}, bf16[144,512]{1,0:T(8,128)(2,1)S(1)}, bf16[144,512]{1,0:T(8,128)(2,1)S(1)}, f32[4,64,128]{2,1,0:T(8,128)S(1)}) custom-call(bf16[64,512]{1,0:T(8,128)(2,1)S(1)} %pack.1.note_ref, bf16[64,512]{1,0:T(8,128)(2,1)S(1)} %collective-permute-done.1.got1_ref, ...), custom_call_target="tpu_custom_call" | custom-call | flops 536870912 | bytes 2097152 | tf_op jit(solution)/shard_map/join/pallas_call | solution.py:410
  25.1 0.1 collective-permute-start.4
  25.1 1.6 %collective-permute-start.5 = (bf16[144,512]{1,0:T(8,128)(2,1)S(1)}, bf16[144,512]{1,0:T(8,128)(2,1)S(1)}, u32[]{:S(2)}, u32[]{:S(2)}) collective-permute-start(bf16[144,512]{1,0:T(8,128)(2,1)S(1)} %get-tuple-element.28), channel_id=1, source_target_pairs={{0,2},{1,3},{2,0},{3,1},{4,6},{5,7},{6,4},{7,5},{8,10},{9,11},{10,... | collective-permute-start | bytes 442376 | tf_op jit(solution)/shard_map/ppermute | solution.py:425
  26.7 0.3 collective-permute-start.6
  27.0 0.0 collective-permute-done.next_ref
  27.0 3.3 %tile.1 = bf16[512,512]{1,0:T(8,128)(2,1)} custom-call(bf16[512,512]{1,0:T(8,128)(2,1)S(1)} %get-tuple-element.16.sci_ref, bf16[64,512]{1,0:T(8,128)(2,1)S(1)} %pack.1.note_ref, bf16[512,512]{1,0:T(8,128)(2,1)S(1)} %collective-permute-done.next_ref, f32[4,512,128]{2,1,0:T(8,128)S(1)} %get-tuple-element.17.m_ref.m1_ref, ...), custom_call_target="tpu_custom_call" | custom-call | flops 1207959552 | bytes 2097152 | tf_op jit(solution)/shard_map/tile/pallas_call | solution.py:426
  30.3 1.0 %collective-permute-done.4.refs_1_ = bf16[144,512]{1,0:T(8,128)(2,1)S(1)} collective-permute-done((bf16[144,512]{1,0:T(8,128)(2,1)S(1)}, bf16[144,512]{1,0:T(8,128)(2,1)S(1)}, u32[]{:S(2)}, u32[]{:S(2)}) %collective-permute-start.4) | collective-permute-done | bytes 147488 | tf_op jit(solution)/shard_map/ppermute | solution.py:425
  31.2 3.2 %collective-permute-done.5.refs_2_ = bf16[144,512]{1,0:T(8,128)(2,1)S(1)} collective-permute-done((bf16[144,512]{1,0:T(8,128)(2,1)S(1)}, bf16[144,512]{1,0:T(8,128)(2,1)S(1)}, u32[]{:S(2)}, u32[]{:S(2)}) %collective-permute-start.5) | collective-permute-done | bytes 147488 | tf_op jit(solution)/shard_map/ppermute | solution.py:425
  34.4 0.0 collective-permute-done.6.refs_3_
  34.4 0.9 %coadd.1 = f32[128,512]{1,0:T(8,128)} custom-call(bf16[144,512]{1,0:T(8,128)(2,1)S(1)} %get-tuple-element.26.refs_0_, bf16[144,512]{1,0:T(8,128)(2,1)S(1)} %collective-permute-done.4.refs_1_, bf16[144,512]{1,0:T(8,128)(2,1)S(1)} %collective-permute-done.5.refs_2_, bf16[144,512]{1,0:T(8,128)(2,1)S(1)} %collective-permute-done.6.refs_3_), custom_call_target="tpu_custom_call" | custom-call | flops 1048576 | bytes 2097152 | tf_op jit(solution)/shard_map/coadd/pallas_call | solution.py:430
Async XLA Ops:
  0.6 21.9 %collective-permute-start.3 = (bf16[512,1,512]{2,0,1:T(8,128)(2,1)}, bf16[512,1,512]{2,0,1:T(8,128)(2,1)S(1)}, u32[]{:S(2)}, u32[]{:S(2)}) collective-permute-start(bf16[512,1,512]{2,0,1:T(8,128)(2,1)} %param.9), channel_id=1, source_target_pairs={{0,4},{4,8},{8,12},{1,5},{5,9},{9,13},{2,6},{6,10},{10,14},{3,7},{... | collective-permute-start | bytes 1572872 | tf_op jit(solution)/shard_map/ppermute | solution.py:22
  5.6 21.4 %collective-permute-start = (bf16[512,512]{1,0:T(8,128)(2,1)}, bf16[512,512]{1,0:T(8,128)(2,1)S(1)}, u32[]{:S(2)}, u32[]{:S(2)}) collective-permute-start(bf16[512,512]{1,0:T(8,128)(2,1)} %t_hbm.3), channel_id=1, source_target_pairs={{4,0},{8,4},{12,8},{5,1},{9,5},{13,9},{6,2},{10,6},{14,10},{7,3},{... | collective-permute-start | bytes 1572872 | tf_op jit(solution)/shard_map/ppermute | solution.py:22
  9.0 13.5 %collective-permute-start.1 = (bf16[64,512]{1,0:T(8,128)(2,1)S(1)}, bf16[64,512]{1,0:T(8,128)(2,1)S(1)}, u32[]{:S(2)}, u32[]{:S(2)}) collective-permute-start(bf16[64,512]{1,0:T(8,128)(2,1)S(1)} %pack.1.note_ref), channel_id=1, source_target_pairs={{0,4},{4,0},{8,12},{12,8},{1,5},{5,1},{9,13},{13,9},{2,6},{6,2},{1... | collective-permute-start | bytes 196616 | tf_op jit(solution)/shard_map/ppermute | solution.py:384
  11.8 10.7 %collective-permute-start.2 = (bf16[64,512]{1,0:T(8,128)(2,1)S(1)}, bf16[64,512]{1,0:T(8,128)(2,1)S(1)}, u32[]{:S(2)}, u32[]{:S(2)}) collective-permute-start(bf16[64,512]{1,0:T(8,128)(2,1)S(1)} %pack.1.note_ref), channel_id=1, source_target_pairs={{0,0},{4,8},{8,4},{12,12},{1,1},{5,9},{9,5},{13,13},{2,2},{6,10},{... | collective-permute-start | bytes 196616 | tf_op jit(solution)/shard_map/ppermute | solution.py:384
  25.1 6.2 %collective-permute-start.4 = (bf16[144,512]{1,0:T(8,128)(2,1)S(1)}, bf16[144,512]{1,0:T(8,128)(2,1)S(1)}, u32[]{:S(2)}, u32[]{:S(2)}) collective-permute-start(bf16[144,512]{1,0:T(8,128)(2,1)S(1)} %get-tuple-element.27), channel_id=1, source_target_pairs={{0,3},{1,2},{2,1},{3,0},{4,7},{5,6},{6,5},{7,4},{8,11},{9,10},{10,... | collective-permute-start | bytes 442376 | tf_op jit(solution)/shard_map/ppermute | solution.py:425
  25.1 9.3 %collective-permute-start.5 = (bf16[144,512]{1,0:T(8,128)(2,1)S(1)}, bf16[144,512]{1,0:T(8,128)(2,1)S(1)}, u32[]{:S(2)}, u32[]{:S(2)}) collective-permute-start(bf16[144,512]{1,0:T(8,128)(2,1)S(1)} %get-tuple-element.28), channel_id=1, source_target_pairs={{0,2},{1,3},{2,0},{3,1},{4,6},{5,7},{6,4},{7,5},{8,10},{9,11},{10,... | collective-permute-start | bytes 442376 | tf_op jit(solution)/shard_map/ppermute | solution.py:425
  26.7 7.7 %collective-permute-start.6 = (bf16[144,512]{1,0:T(8,128)(2,1)S(1)}, bf16[144,512]{1,0:T(8,128)(2,1)S(1)}, u32[]{:S(2)}, u32[]{:S(2)}) collective-permute-start(bf16[144,512]{1,0:T(8,128)(2,1)S(1)} %get-tuple-element.29), channel_id=1, source_target_pairs={{0,1},{1,0},{2,3},{3,2},{4,5},{5,4},{6,7},{7,6},{8,9},{9,8},{10,11... | collective-permute-start | bytes 442376 | tf_op jit(solution)/shard_map/ppermute | solution.py:425

commit v9 on v8

--- a/solution.py
+++ b/solution.py
@@ -22,23 +22,13 @@
     return lax.ppermute(shard, axis, pairs)
 
 
-def swap_partner(p, parity, count):
-    other = p + 1 if p % 2 == parity else p - 1
-    return other if 0 <= other < count else p
-
-
-def place():
-    p = lax.axis_index("patch")
-    return p % 2 == 0, p > 0, p < lax.axis_size("patch") - 1
-
-
-def pick(flag, valid, yes, no):
-    value = jnp.where(flag, yes.astype(F32), no.astype(F32))
-    return jnp.where(valid, value, 0.0)
-
-
 def partner(me, k, count):
     return me ^ k if count & (count - 1) == 0 else (me + k) % count
+
+
+def swapped(shard, axis, k):
+    devices = lax.axis_size(axis)
+    return lax.ppermute(shard, axis, [(i, partner(i, k, devices)) for i in range(devices)])
 
 
 def iota(shape, dim):
@@ -116,7 +106,7 @@
     return jnp.sum(jnp.where(diag, row, jnp.zeros_like(row)), axis=1, keepdims=True)
 
 
-def pack_kernel(off_hbm, live_hbm, t_hbm, msg_ref, off_ref, live_ref, sems):
+def pack_kernel(off_hbm, live_hbm, t_hbm, msg_ref, out_ref, off_ref, live_ref, sems):
     rows, cols = t_hbm.shape
     edge = 2 * B
     copies = [
@@ -134,6 +124,7 @@
     note = jnp.where(lane == 0, off // B, jnp.where(lane == 1, off % B, live_ref[0, 0])).astype(F32)
     block = msg_ref[0:B, :].astype(F32)
     msg_ref[0:B, :] = jnp.where(iota((B, cols), 0) == 0, note, block).astype(BF16)
+    out_ref[...] = msg_ref[0:edge, :]
 
 
 def first_kernel(
@@ -240,42 +231,33 @@
 
 
 def read_note(msg_ref):
-    return decode(msg_ref[0:B, 0:LANES].astype(F32))
-
-
-def decode(note):
+    note = msg_ref[0:B, 0:LANES].astype(F32)
     return (note[0, 0] * B + note[0, 1]).astype(jnp.int32), note[0, 2]
 
 
-def note_before(got1_ref, got2_ref):
-    even, has_before, _ = place()
-    return decode(pick(even, has_before, got2_ref[0:B, 0:LANES], got1_ref[0:B, 0:LANES]))
-
-
-def before_kernel(got1_ref, got2_ref, sci_ref, m_ref, pcol_ref, edge_ref, filt_ref, sci, diff):
+def before_kernel(msg_ref, sci_ref, m_ref, pcol_ref, edge_ref, filt_ref, sci, diff):
     rows = sci_ref.shape[0]
-    off, _ = note_before(got1_ref, got2_ref)
+    off, _ = read_note(msg_ref)
     to_chunks(sci, 0, sci_ref[...])
     filter_inner(sci, rows - B - off, off - rows, off, m_ref, pcol_ref, edge_ref, filt_ref, diff)
 
 
 def join_kernel(
-    note_ref, got1_ref, got2_ref, w_ref, pcol_ref, prow_ref, edge_a, edge_b, filt_a, filt_b,
+    note_ref, msg_ref, next_ref, w_ref, pcol_ref, prow_ref, edge_a, edge_b, filt_a, filt_b,
     *rest,
 ):
-    *outs, m_ref, src, xs, strip, diff, filt = rest
+    *outs, mark_ref, m_ref, src, xs, strip, diff, filt = rest
     edge = 2 * B
     rows, cols = filt_a.shape[0] + edge, filt_a.shape[1]
-    even, has_before, has_next = place()
-    to_blocks(src, 0, pick(even, has_before, got2_ref[0:edge, :], got1_ref[0:edge, :]))
+    to_blocks(src, 0, msg_ref[...])
     to_blocks(src, 2, note_ref[edge:, :])
     to_blocks(src, 4, note_ref[0:edge, :])
-    to_blocks(src, 6, pick(even, has_next, got1_ref[edge:, :], got2_ref[edge:, :]))
+    to_blocks(src, 6, next_ref[0:edge, :])
     conv_blocks(src, 8, w_ref, xs, strip)
     for n, a in enumerate((1, 2, 5, 6)):
         m_ref[:, B * n : B * (n + 1), :] = strip[:, PITCH * a : PITCH * a + B, :]
     off_a, live_a = read_note(note_ref)
-    off_b, live_b = note_before(got1_ref, got2_ref)
+    off_b, live_b = read_note(msg_ref)
     for s, (side, first, last) in enumerate(((edge_a, off_a, off_a + rows), (edge_b, off_b - rows, off_b))):
         for c in range(cols // LANES):
             part = slice(c * LANES, (c + 1) * LANES)
@@ -293,23 +275,53 @@
     prow = prow_ref[...].astype(F32)
     out_row = iota((share, depth), 0)
     lane = iota((B, cols), 1)
-    me = lax.axis_index("visit") * lax.axis_size("band") + lax.axis_index("band")
+    visits, bands = lax.axis_size("visit"), lax.axis_size("band")
+    hi, lo = off_b // B, off_b % B
+    marks = note_ref[0:B, 0:LANES].astype(F32)
+    marks = jnp.where(iota(marks.shape, 1) == 3, hi.astype(F32), marks)
+    marks = jnp.where(iota(marks.shape, 1) == 4, lo.astype(F32), marks)
+    marks = jnp.where(iota(marks.shape, 1) == 5, live_b, marks)
+    mark_ref[...] = marks.astype(BF16)
+    for j, out_ref in enumerate(outs):
+        for k in range(visits):
+            to_visit = partner(lax.axis_index("visit"), k, visits)
+            base = (to_visit * bands + partner(lax.axis_index("band"), j, bands)) * share
+            row = out_row + base
+            left = jnp.where(row >= off_a, prow * live_a, 0.0).astype(BF16)
+            right = jnp.where(row < off_b, prow * live_b, 0.0).astype(BF16)
+            span = pl.ds(pl.multiple_of(base, B), depth)
+            total = jnp.dot(left, filt[0, span, :], preferred_element_type=F32)
+            total += jnp.dot(right, filt[1, span, :], preferred_element_type=F32)
+            out_ref[k * share : (k + 1) * share, :] = total.astype(out_ref.dtype)
+        if j:
+            out_ref[visits * share :, 0:LANES] = marks.astype(BF16)
+            out_ref[visits * share :, LANES:] = jnp.zeros((B, cols - LANES), BF16)
+
+
+def pair_kernel(*refs):
+    bands = lax.axis_size("band")
+    visits = lax.axis_size("visit")
+    mark_ref, keep_ref, *got = refs[: bands + 1]
+    *outs, own_mark_ref = refs[bands + 1 :]
+    share, cols = outs[0].shape
+    rowid = iota((B, LANES), 0)
+    marks = jnp.where(rowid == 0, mark_ref[...].astype(F32), 0.0)
+    for n, ref in enumerate(got):
+        other = ref[visits * share :, 0:LANES].astype(F32)
+        marks = jnp.where(rowid == n + 1, other[0:1, :], marks)
+    own_mark_ref[...] = marks.astype(BF16)
     for k, out_ref in enumerate(outs):
-        base = partner(me, k, len(outs)) * share
-        row = out_row + base
-        left = jnp.where(row >= off_a, prow * live_a, 0.0).astype(BF16)
-        right = jnp.where(row < off_b, prow * live_b, 0.0).astype(BF16)
-        span = pl.ds(pl.multiple_of(base, B), depth)
-        total = jnp.dot(left, filt[0, span, :], preferred_element_type=F32)
-        total += jnp.dot(right, filt[1, span, :], preferred_element_type=F32)
-        out_ref[0:share, :] = total.astype(BF16)
-        start = jnp.clip(off_a - base, 0, share).astype(F32)
-        stop = jnp.clip(off_b - base, 0, share).astype(F32)
-        note = jnp.where(lane == 0, start, jnp.where(lane == 1, live_a, jnp.where(lane == 2, stop, live_b)))
-        out_ref[share : share + B, :] = note.astype(BF16)
-
-
-def tile_kernel(sci_ref, note_ref, next_ref, m1_ref, edge_ref, w_ref, out_ref, src, xs, res, big):
+        span = slice(k * share, (k + 1) * share)
+        total = keep_ref[span, :]
+        for ref in got:
+            total += ref[span, :].astype(F32)
+        out_ref[0:share, :] = total.astype(out_ref.dtype)
+        if k:
+            out_ref[share:, 0:LANES] = marks.astype(BF16)
+            out_ref[share:, LANES:] = jnp.zeros((B, cols - LANES), BF16)
+
+
+def tile_kernel(mark_ref, sci_ref, note_ref, next_ref, m1_ref, edge_ref, w_ref, out_ref, src, xs, res, big):
     rows, cols = sci_ref.shape
     to_blocks(src, 0, next_ref[...])
     conv_blocks(src, rows // B, w_ref, xs, res)
@@ -324,17 +336,22 @@
         out_ref[:, part] = (sci_ref[:, part].astype(F32) - big[c, pl.ds(off, rows), :]).astype(BF16)
 
 
-def coadd_kernel(*refs):
+def coadd_kernel(mark_ref, *refs):
     *parts, out_ref = refs
     share, cols = out_ref.shape
-    row = iota((share, LANES), 0).astype(F32)
-    accum = jnp.zeros((share, cols), F32)
+    bands = lax.axis_size("band")
+    base = (lax.axis_index("visit") * bands + lax.axis_index("band")) * share
+    row = (iota((share, LANES), 0) + base).astype(F32)
+    accum = parts[0][...]
     cover = jnp.zeros((share, LANES), F32)
-    for part in parts:
-        accum += part[0:share, :].astype(F32)
-        note = part[share : share + B, 0:LANES].astype(F32)[0:1, :]
-        cover += jnp.where(row >= note[:, 0:1], note[:, 1:2], 0.0)
-        cover += jnp.where(row < note[:, 2:3], note[:, 3:4], 0.0)
+    for n, part in enumerate(parts):
+        if n:
+            accum += part[0:share, :].astype(F32)
+        marks = (part[share : share + B, 0:LANES] if n else mark_ref[...]).astype(F32)
+        for m in range(bands):
+            mark = marks[m : m + 1, :]
+            cover += jnp.where(row >= mark[:, 0:1] * B + mark[:, 1:2], mark[:, 2:3], 0.0)
+            cover += jnp.where(row < mark[:, 3:4] * B + mark[:, 4:5], mark[:, 5:6], 0.0)
     scale = lax.rsqrt(jnp.maximum(cover, 1.0))
     for c in range(cols // LANES):
         part = slice(c * LANES, (c + 1) * LANES)
@@ -374,16 +391,12 @@
     index = jnp.swapaxes(basis_index, 1, 2)
     before = shifted(science, "patch", 1)[:, 0, :]
     following = shifted(template, "patch", -1)
-    note = call(
-        pack_kernel, sds((2 * edge, cols), BF16), [HBM] * 3,
+    note, msg = call(
+        pack_kernel, (sds((2 * edge, cols), BF16), sds((edge, cols), BF16)), [HBM] * 3,
         [pltpu.SMEM((1, 1), jnp.int32), pltpu.SMEM((1, 1), jnp.int32), pltpu.SemaphoreType.DMA((4,))],
         1 << 20, "pack",
     )(offsets, live_flags, held[0])
-    panels = lax.axis_size("patch")
-    got1, got2 = (
-        lax.ppermute(note, "patch", [(p, swap_partner(p, parity, panels)) for p in range(panels)])
-        for parity in range(2)
-    )
+    msg = shifted(msg, "patch", 1)
     count = rows // B
     conv_scratch = [
         pltpu.VMEM((chunks, count * PITCH, LANES), F32),
@@ -406,10 +419,13 @@
         ] + conv_scratch + sky_scratch,
         conv_flops, "first",
     )(note, *held, *in_hbm(bank, index, coeff, psf_profile[None]))
-    edge_b, filt_b = call(before_kernel, sides, [VM] * 5, sky_scratch, 1 << 28, "before")(got1, got2, before, m1, pcol)
-    *parts, m_edge = call(
+    edge_b, filt_b = call(before_kernel, sides, [VM] * 4, sky_scratch, 1 << 28, "before")(msg, before, m1, pcol)
+    bands, visits = lax.axis_size("band"), lax.axis_size("visit")
+    whole = visits * share
+    keep, *sent, mark, m_edge = call(
         join_kernel,
-        (sds((share + B, cols), BF16),) * sharers + (sds((chunks, 2 * edge, LANES), F32),),
+        (sds((whole, cols), F32),) + (sds((whole + B, cols), BF16),) * (bands - 1)
+        + (sds((B, LANES), BF16), sds((chunks, 2 * edge, LANES), F32)),
         [VM] * 10,
         [
             pltpu.VMEM((chunks, 8 * PITCH, LANES), F32),
@@ -419,15 +435,21 @@
             pltpu.VMEM((2, rows - share + depth, cols), BF16),
         ],
         1 << 29, "join",
-    )(note, got1, got2, w, pcol, prow, edge_a, edge_b, filt_a, filt_b)
-    for k in reversed(range(1, sharers)):
-        pairs = [(i, partner(i, k, sharers)) for i in range(sharers)]
-        parts[k] = lax.ppermute(parts[k], ("visit", "band"), pairs)
+    )(note, msg, following, w, pcol, prow, edge_a, edge_b, filt_a, filt_b)
+    got = [swapped(part, "band", k + 1) for k, part in enumerate(sent)]
+    own, *sent, mark = call(
+        pair_kernel,
+        (sds((share, cols), F32),) + (sds((share + B, cols), BF16),) * (visits - 1) + (sds((B, LANES), BF16),),
+        [VM] * (1 + bands), [], 1 << 20, "pair",
+    )(mark, keep, *got)
+    got = [swapped(part, "visit", k + 1) for k, part in enumerate(sent)]
     difference = call(
-        tile_kernel, sds((rows, cols), BF16), [VM] * 6,
+        tile_kernel, sds((rows, cols), BF16), [VM] * 7,
         conv_scratch + [pltpu.VMEM((chunks, 2 * rows, LANES), F32)], conv_flops, "tile",
-    )(tile, note, following, m1, m_edge, w)
-    detection = call(coadd_kernel, sds((share, cols), F32), [VM] * sharers, [], 1 << 20, "coadd")(parts[0], *parts[:0:-1])
+    )(mark, tile, note, following, m1, m_edge, w)
+    detection = call(
+        coadd_kernel, sds((share, cols), F32), [VM] * (1 + visits), [], 1 << 20, "coadd"
+    )(mark, own, *got)
     return (difference[:, None, :], detection)
 
 

time: 35.6 us -> 31.9 us (0.90)
  waiting for transfers between devices: 9.38 us -> 4.55 us
  starting transfers between devices: 11.5 us -> 12.4 us
    ppermute x5 -> x2, waiting for transfers between devices: 9.37 us -> 2.62 us  [swapped(): lax.ppermute(shard, axis, [(i, partner(i, k, devices)) for i in range(dev...]
    ppermute x2 -> x3, starting transfers between devices: 6.25 us -> 10.8 us  [shifted(): return lax.ppermute(shard, axis, pairs)]
    ppermute x5 -> x2, starting transfers between devices: 5.28 us -> 1.63 us  [swapped(): lax.ppermute(shard, axis, [(i, partner(i, k, devices)) for i in range(dev...]
    ppermute x2 -> x3, waiting for transfers between devices: 0.01 us -> 1.93 us  [shifted(): return lax.ppermute(shard, axis, pairs)]
    pallas_call x5 -> x6, Pallas kernels: 7.59 us -> 7.73 us  [the longest x1 3.32 us: on_device(): call(tile_kernel, sds((rows, cols), BF16), [VM] * 7, conv_scratch + [pltp...]
  transfers between devices with their start and end apart: 7 -> 5, of which waited for: 3 -> 3; matrix products, arithmetic and copies ran while one was open for 0% -> 0% of each run, Pallas kernels for 33% -> 31%
where the time goes in v9:
time: 31.9 us; the launch traced here: 31.7 us
  Pallas kernels  12.7 us (40%)
  starting transfers between devices  12.4 us (39%)
  waiting for transfers between devices  4.55 us (14%)
  between operations  2 us (6%)
    ppermute x3, starting transfers between devices, shifted(): return lax.ppermute(shard, axis, pairs)  10.8 us
    pallas_call x1, Pallas kernels, on_device(): call(first_kernel, (sds((deep, CH), BF16), sds((cols, cols), BF16), sds((...  4.94 us
    pallas_call x1, Pallas kernels, on_device(): call(tile_kernel, sds((rows, cols), BF16), [VM] * 7, conv_scratch + [pltp...  3.32 us
    ppermute x2, waiting for transfers between devices, swapped(): lax.ppermute(shard, axis, [(i, partner(i, k, devices)) for i in range(dev...  2.62 us
    pallas_call x1, Pallas kernels, on_device(): call(join_kernel, (sds((whole, cols), F32),) + (sds((whole + B, cols), BF...  1.96 us
    ppermute x3, waiting for transfers between devices, shifted(): return lax.ppermute(shard, axis, pairs)  1.93 us
    ppermute x2, starting transfers between devices, swapped(): lax.ppermute(shard, axis, [(i, partner(i, k, devices)) for i in range(dev...  1.63 us
    pallas_call x1, Pallas kernels, on_device(): call(coadd_kernel, sds((share, cols), F32), [VM] * (1 + visits), [], 1 <<...  0.95 us
  transfers between devices with their start and end apart: 5, of which 3 were waited for; matrix products, arithmetic and copies ran while one was open for 0% of the time, Pallas kernels for 31%

profile of v9, /device:TPU:0, one launch (start us, length us, event | category | flops | bytes accessed | tf_op | source)
XLA Modules:
  0.0 31.7 jit_solution(1214930313013550216)
XLA Ops:
  0.6 5.0 %collective-permute-start.2 = (bf16[512,1,512]{2,0,1:T(8,128)(2,1)}, bf16[512,1,512]{2,0,1:T(8,128)(2,1)S(1)}, u32[]{:S(2)}, u32[]{:S(2)}) collective-permute-start(bf16[512,1,512]{2,0,1:T(8,128)(2,1)} %param.9), channel_id=1, source_target_pairs={{0,4},{4,8},{8,12},{1,5},{5,9},{9,13},{2,6},{6,10},{10,14},{3,7},{... | collective-permute-start | bytes 1572872 | tf_op jit(solution)/shard_map/ppermute | solution.py:22
  5.6 1.3 %collective-permute-start.1 = (bf16[512,512]{1,0:T(8,128)(2,1)}, bf16[512,512]{1,0:T(8,128)(2,1)S(1)}, u32[]{:S(2)}, u32[]{:S(2)}) collective-permute-start(bf16[512,512]{1,0:T(8,128)(2,1)} %t_hbm.3), channel_id=1, source_target_pairs={{4,0},{8,4},{12,8},{5,1},{9,5},{13,9},{6,2},{10,6},{14,10},{7,3},{... | collective-permute-start | bytes 1572872 | tf_op jit(solution)/shard_map/ppermute | solution.py:22
  8.2 0.8 %pack.1 = (bf16[64,512]{1,0:T(8,128)(2,1)S(1)}, bf16[32,512]{1,0:T(8,128)(2,1)S(1)}) custom-call(s32[1,1]{1,0:T(1,128)S(6)} %copy.10.off_hbm, s32[1,1]{1,0:T(1,128)S(6)} %copy.11.live_hbm, bf16[512,512]{1,0:T(8,128)(2,1)} %t_hbm.3), custom_call_target="tpu_custom_call" | custom-call | flops 1048576 | bytes 2097152 | tf_op jit(solution)/shard_map/pack/pallas_call | solution.py:394
  9.0 4.5 %collective-permute-start = (bf16[32,512]{1,0:T(8,128)(2,1)S(1)}, bf16[32,512]{1,0:T(8,128)(2,1)S(1)}, u32[]{:S(2)}, u32[]{:S(2)}) collective-permute-start(bf16[32,512]{1,0:T(8,128)(2,1)S(1)} %get-tuple-element.21), channel_id=1, source_target_pairs={{0,4},{4,8},{8,12},{1,5},{5,9},{9,13},{2,6},{6,10},{10,14},{3,7},{... | collective-permute-start | bytes 98312 | tf_op jit(solution)/shard_map/ppermute | solution.py:22
  13.6 4.9 %first.1 = (bf16[2304,256]{1,0:T(8,128)(2,1)S(1)}, bf16[512,512]{1,0:T(8,128)(2,1)S(1)}, bf16[128,256]{1,0:T(8,128)(2,1)S(1)}, bf16[512,512]{1,0:T(8,128)(2,1)S(...) custom-call(bf16[64,512]{1,0:T(8,128)(2,1)S(1)} %get-tuple-element.20.note_ref, ...), custom_call_target="tpu_custom_call" | custom-call | flops 1207959552 | bytes 2097152 | tf_op jit(solution)/shard_map/first/pallas_call | solution.py:409
  18.5 0.0 collective-permute-done.msg_ref
  18.6 0.0 collective-permute-done.2
  18.6 0.6 %before.1 = (f32[4,64,128]{2,1,0:T(8,128)S(1)}, bf16[480,512]{1,0:T(8,128)(2,1)S(1)}) custom-call(bf16[32,512]{1,0:T(8,128)(2,1)S(1)} %collective-permute-done.msg_ref, bf16[512,512]{1,0:T(8,128)(2,1)S(1)} %bitcast.5, f32[4,512,128]{2,1,0:T(8,128)S(1)} %get-tuple-element.26.m_ref.m1_ref, bf16[512,512]{1,0:T(8,128)(2,1)S(1)} %get-tuple-element.23.pcol_ref), custom_call_target="tpu_custom_call" | custom-call | flops 268435456 | bytes 2097152 | tf_op jit(solution)/shard_map/before/pallas_call | solution.py:422
  19.2 1.9 %collective-permute-done.1.next_ref = bf16[512,512]{1,0:T(8,128)(2,1)S(1)} collective-permute-done((bf16[512,512]{1,0:T(8,128)(2,1)}, bf16[512,512]{1,0:T(8,128)(2,1)S(1)}, u32[]{:S(2)}, u32[]{:S(2)}) %collective-permute-start.1) | collective-permute-done | bytes 524320 | tf_op jit(solution)/shard_map/ppermute | solution.py:22
  21.1 2.0 %join.1 = (f32[256,512]{1,0:T(8,128)S(1)}, bf16[272,512]{1,0:T(8,128)(2,1)S(1)}, bf16[16,128]{1,0:T(8,128)(2,1)S(1)}, f32[4,64,128]{2,1,0:T(8,128)S(1)}) custom-call(bf16[64,512]{1,0:T(8,128)(2,1)S(1)} %get-tuple-element.20.note_ref, bf16[32,512]{1,0:T(8,128)(2,1)S(1)} %collective-permute-done.msg_ref, bf16[512,512]{1,0:T(8,128)(2,1)S(1)} %collective-permute-done.1.next_ref, ...), custom_call_target="tpu_custom_call" | custom-call | flops 536870912 | bytes 2097152 | tf_op jit(solution)/shard_map/join/pallas_call | solution.py:425
  23.1 0.1 collective-permute-start.3
  23.1 1.5 %collective-permute-done.3.refs_2_ = bf16[272,512]{1,0:T(8,128)(2,1)S(1)} collective-permute-done((bf16[272,512]{1,0:T(8,128)(2,1)S(1)}, bf16[272,512]{1,0:T(8,128)(2,1)S(1)}, u32[]{:S(2)}, u32[]{:S(2)}) %collective-permute-start.3) | collective-permute-done | bytes 278560 | tf_op jit(solution)/shard_map/ppermute | solution.py:31
  24.7 0.1 pair.1
  24.7 1.6 %collective-permute-start.4 = (bf16[144,512]{1,0:T(8,128)(2,1)S(1)}, bf16[144,512]{1,0:T(8,128)(2,1)S(1)}, u32[]{:S(2)}, u32[]{:S(2)}) collective-permute-start(bf16[144,512]{1,0:T(8,128)(2,1)S(1)} %get-tuple-element.37), channel_id=1, source_target_pairs={{0,2},{2,0},{1,3},{3,1},{4,6},{6,4},{5,7},{7,5},{8,10},{10,8},{9,1... | collective-permute-start | bytes 442376 | tf_op jit(solution)/shard_map/ppermute | solution.py:31
  26.3 3.3 %tile.1 = bf16[512,512]{1,0:T(8,128)(2,1)} custom-call(bf16[16,128]{1,0:T(8,128)(2,1)S(1)} %get-tuple-element.33.mark_ref, bf16[512,512]{1,0:T(8,128)(2,1)S(1)} %get-tuple-element.34.sci_ref, bf16[64,512]{1,0:T(8,128)(2,1)S(1)} %get-tuple-element.20.note_ref, bf16[512,512]{1,0:T(8,128)(2,1)S(1)} %collective-permute-done.1.next_ref, ...), custom_call_target="tpu_custom_call" | custom-call | flops 1207959552 | bytes 2097152 | tf_op jit(solution)/shard_map/tile/pallas_call | solution.py:446
  29.6 1.1 %collective-permute-done.4.refs_1_ = bf16[144,512]{1,0:T(8,128)(2,1)S(1)} collective-permute-done((bf16[144,512]{1,0:T(8,128)(2,1)S(1)}, bf16[144,512]{1,0:T(8,128)(2,1)S(1)}, u32[]{:S(2)}, u32[]{:S(2)}) %collective-permute-start.4) | collective-permute-done | bytes 147488 | tf_op jit(solution)/shard_map/ppermute | solution.py:31
  30.7 0.9 %coadd.1 = f32[128,512]{1,0:T(8,128)} custom-call(bf16[16,128]{1,0:T(8,128)(2,1)S(1)} %get-tuple-element.33.mark_ref, f32[128,512]{1,0:T(8,128)S(1)} %get-tuple-element.36.refs_0_, bf16[144,512]{1,0:T(8,128)(2,1)S(1)} %collective-permute-done.4.refs_1_), custom_call_target="tpu_custom_call" | custom-call | flops 1048576 | bytes 2097152 | tf_op jit(solution)/shard_map/coadd/pallas_call | solution.py:450
Async XLA Ops:
  0.6 17.9 %collective-permute-start.2 = (bf16[512,1,512]{2,0,1:T(8,128)(2,1)}, bf16[512,1,512]{2,0,1:T(8,128)(2,1)S(1)}, u32[]{:S(2)}, u32[]{:S(2)}) collective-permute-start(bf16[512,1,512]{2,0,1:T(8,128)(2,1)} %param.9), channel_id=1, source_target_pairs={{0,4},{4,8},{8,12},{1,5},{5,9},{9,13},{2,6},{6,10},{10,14},{3,7},{... | collective-permute-start | bytes 1572872 | tf_op jit(solution)/shard_map/ppermute | solution.py:22
  5.6 15.5 %collective-permute-start.1 = (bf16[512,512]{1,0:T(8,128)(2,1)}, bf16[512,512]{1,0:T(8,128)(2,1)S(1)}, u32[]{:S(2)}, u32[]{:S(2)}) collective-permute-start(bf16[512,512]{1,0:T(8,128)(2,1)} %t_hbm.3), channel_id=1, source_target_pairs={{4,0},{8,4},{12,8},{5,1},{9,5},{13,9},{6,2},{10,6},{14,10},{7,3},{... | collective-permute-start | bytes 1572872 | tf_op jit(solution)/shard_map/ppermute | solution.py:22
  9.0 9.5 %collective-permute-start = (bf16[32,512]{1,0:T(8,128)(2,1)S(1)}, bf16[32,512]{1,0:T(8,128)(2,1)S(1)}, u32[]{:S(2)}, u32[]{:S(2)}) collective-permute-start(bf16[32,512]{1,0:T(8,128)(2,1)S(1)} %get-tuple-element.21), channel_id=1, source_target_pairs={{0,4},{4,8},{8,12},{1,5},{5,9},{9,13},{2,6},{6,10},{10,14},{3,7},{... | collective-permute-start | bytes 98312 | tf_op jit(solution)/shard_map/ppermute | solution.py:22
  23.1 1.6 %collective-permute-start.3 = (bf16[272,512]{1,0:T(8,128)(2,1)S(1)}, bf16[272,512]{1,0:T(8,128)(2,1)S(1)}, u32[]{:S(2)}, u32[]{:S(2)}) collective-permute-start(bf16[272,512]{1,0:T(8,128)(2,1)S(1)} %get-tuple-element.32), channel_id=1, source_target_pairs={{0,1},{1,0},{2,3},{3,2},{4,5},{5,4},{6,7},{7,6},{8,9},{9,8},{10,11... | collective-permute-start | bytes 835592 | tf_op jit(solution)/shard_map/ppermute | solution.py:31
  24.7 6.0 %collective-permute-start.4 = (bf16[144,512]{1,0:T(8,128)(2,1)S(1)}, bf16[144,512]{1,0:T(8,128)(2,1)S(1)}, u32[]{:S(2)}, u32[]{:S(2)}) collective-permute-start(bf16[144,512]{1,0:T(8,128)(2,1)S(1)} %get-tuple-element.37), channel_id=1, source_target_pairs={{0,2},{2,0},{1,3},{3,1},{4,6},{6,4},{5,7},{7,5},{8,10},{10,8},{9,1... | collective-permute-start | bytes 442376 | tf_op jit(solution)/shard_map/ppermute | solution.py:31

commit v10 on v9

--- a/solution.py
+++ b/solution.py
@@ -106,14 +106,24 @@
     return jnp.sum(jnp.where(diag, row, jnp.zeros_like(row)), axis=1, keepdims=True)
 
 
-def pack_kernel(off_hbm, live_hbm, t_hbm, msg_ref, out_ref, off_ref, live_ref, sems):
+def pack_kernel(
+    off_hbm, live_hbm, t_hbm, bank_hbm, index_hbm, coeff_hbm, psf_hbm,
+    note_ref, msg_ref, half_ref, bank_ref, index_ref, coeff_ref, psf_ref, off_ref, live_ref, sems,
+):
     rows, cols = t_hbm.shape
     edge = 2 * B
+    piece = half_ref.shape[0] - edge
+    begin = pl.multiple_of(lax.axis_index("band") * piece, B)
     copies = [
-        pltpu.make_async_copy(t_hbm.at[pl.ds(rows - edge, edge)], msg_ref.at[pl.ds(0, edge)], sems.at[0]),
-        pltpu.make_async_copy(t_hbm.at[pl.ds(0, edge)], msg_ref.at[pl.ds(edge, edge)], sems.at[1]),
-        pltpu.make_async_copy(off_hbm, off_ref, sems.at[2]),
-        pltpu.make_async_copy(live_hbm, live_ref, sems.at[3]),
+        pltpu.make_async_copy(a, b, sems.at[n])
+        for n, (a, b) in enumerate((
+            (off_hbm, off_ref), (live_hbm, live_ref),
+            (t_hbm.at[pl.ds(rows - edge, edge)], note_ref.at[pl.ds(0, edge)]),
+            (t_hbm.at[pl.ds(0, edge)], note_ref.at[pl.ds(edge, edge)]),
+            (t_hbm.at[pl.ds(0, edge)], half_ref.at[pl.ds(0, edge)]),
+            (t_hbm.at[pl.ds(begin, piece)], half_ref.at[pl.ds(edge, piece)]),
+            (bank_hbm, bank_ref), (index_hbm, index_ref), (coeff_hbm, coeff_ref), (psf_hbm, psf_ref),
+        ))
     ]
     for copy in copies:
         copy.start()
@@ -122,26 +132,21 @@
     lane = iota((1, cols), 1)
     off = off_ref[0, 0]
     note = jnp.where(lane == 0, off // B, jnp.where(lane == 1, off % B, live_ref[0, 0])).astype(F32)
-    block = msg_ref[0:B, :].astype(F32)
-    msg_ref[0:B, :] = jnp.where(iota((B, cols), 0) == 0, note, block).astype(BF16)
-    out_ref[...] = msg_ref[0:edge, :]
+    block = note_ref[0:B, :].astype(F32)
+    note_ref[0:B, :] = jnp.where(iota((B, cols), 0) == 0, note, block).astype(BF16)
+    msg_ref[...] = note_ref[0:edge, :]
 
 
 def first_kernel(
-    note_ref, t_hbm, sci_hbm, bank_hbm, index_hbm, coeff_hbm, psf_hbm,
+    note_ref, t_hbm, sci_hbm, bank_ref, index_ref, coeff_ref, psf_ref,
     w_ref, pcol_ref, prow_ref, sci_ref, m_ref, edge_ref, filt_ref,
-    t_ref, bank_ref, index_ref, coeff_ref, psf_ref, sems,
-    src, xs, res, sci, diff,
+    t_ref, sems, src, xs, res, sci, diff,
 ):
-    pairs = (
-        (bank_hbm, bank_ref), (index_hbm, index_ref), (coeff_hbm, coeff_ref), (psf_hbm, psf_ref),
-        (t_hbm, t_ref), (sci_hbm, sci_ref),
-    )
-    copies = [pltpu.make_async_copy(a, b, sems.at[n]) for n, (a, b) in enumerate(pairs)]
+    copies = [
+        pltpu.make_async_copy(t_hbm, t_ref, sems.at[0]), pltpu.make_async_copy(sci_hbm, sci_ref, sems.at[1])
+    ]
     for copy in copies:
         copy.start()
-    for copy in copies[:4]:
-        copy.wait()
     profs, taps = bank_ref.shape
     half = taps // 2
     delta = B - half
@@ -193,7 +198,7 @@
     for t in range(taps):
         block = jnp.where(tap == t, psf[:, t : t + 1], block)
     prow_ref[...] = block.astype(BF16)
-    for copy in copies[4:]:
+    for copy in copies:
         copy.wait()
     edge = 2 * B
     rows, cols = t_ref.shape
@@ -321,9 +326,17 @@
             out_ref[share:, LANES:] = jnp.zeros((B, cols - LANES), BF16)
 
 
-def tile_kernel(mark_ref, sci_ref, note_ref, next_ref, m1_ref, edge_ref, w_ref, out_ref, src, xs, res, big):
+def tile_kernel(mark_ref, sci_ref, note_ref, m1_ref, edge_ref, w_ref, *rest):
     rows, cols = sci_ref.shape
-    to_blocks(src, 0, next_ref[...])
+    *halves, out_ref, src, xs, res, big = rest
+    bands = len(halves)
+    blocks = rows // B // bands
+    band = lax.axis_index("band")
+    for j in range(bands):
+        piece = halves[0][2 * B :, :].astype(F32)
+        for k in range(1, bands):
+            piece = jnp.where(partner(band, k, bands) == j, halves[k][2 * B :, :].astype(F32), piece)
+        to_blocks(src, j * blocks, piece)
     conv_blocks(src, rows // B, w_ref, xs, res)
     for a in range(1, rows // B):
         big[:, rows + B * a : rows + B * (a + 1), :] = res[:, PITCH * a : PITCH * a + B, :]
@@ -386,16 +399,22 @@
     deep = 9 * CH
     depth = -(-(share + edge) // LANES) * LANES
     sci = science[:, 0, :]
-    taps = psf_profile.shape[0]
     held = in_hbm(template, sci)
     index = jnp.swapaxes(basis_index, 1, 2)
     before = shifted(science, "patch", 1)[:, 0, :]
-    following = shifted(template, "patch", -1)
-    note, msg = call(
-        pack_kernel, (sds((2 * edge, cols), BF16), sds((edge, cols), BF16)), [HBM] * 3,
-        [pltpu.SMEM((1, 1), jnp.int32), pltpu.SMEM((1, 1), jnp.int32), pltpu.SemaphoreType.DMA((4,))],
+    bands, visits = lax.axis_size("band"), lax.axis_size("visit")
+    psf = psf_profile[None]
+    note, msg, half, *small = call(
+        pack_kernel,
+        (
+            sds((2 * edge, cols), BF16), sds((edge, cols), BF16), sds((edge + rows // bands, cols), BF16),
+            *(sds(x.shape, x.dtype) for x in (bank, index, coeff, psf)),
+        ),
+        [HBM] * 7,
+        [pltpu.SMEM((1, 1), jnp.int32), pltpu.SMEM((1, 1), jnp.int32), pltpu.SemaphoreType.DMA((10,))],
         1 << 20, "pack",
-    )(offsets, live_flags, held[0])
+    )(offsets, live_flags, held[0], *in_hbm(bank, index, coeff, psf))
+    half = shifted(half, "patch", -1)
     msg = shifted(msg, "patch", 1)
     count = rows // B
     conv_scratch = [
@@ -412,15 +431,11 @@
             sds((deep, CH), BF16), sds((cols, cols), BF16), sds((share, depth), BF16),
             sds((rows, cols), BF16), sds((chunks, rows, LANES), F32),
         ) + sides,
-        [VM] + [HBM] * 6,
-        [
-            pltpu.VMEM((rows, cols), BF16), pltpu.VMEM(bank.shape, BF16), pltpu.VMEM(index.shape, jnp.int32),
-            pltpu.VMEM(coeff.shape, F32), pltpu.VMEM((1, taps), BF16), pltpu.SemaphoreType.DMA((6,)),
-        ] + conv_scratch + sky_scratch,
+        [VM, HBM, HBM] + [VM] * 4,
+        [pltpu.VMEM((rows, cols), BF16), pltpu.SemaphoreType.DMA((2,))] + conv_scratch + sky_scratch,
         conv_flops, "first",
-    )(note, *held, *in_hbm(bank, index, coeff, psf_profile[None]))
+    )(note, *held, *small)
     edge_b, filt_b = call(before_kernel, sides, [VM] * 4, sky_scratch, 1 << 28, "before")(msg, before, m1, pcol)
-    bands, visits = lax.axis_size("band"), lax.axis_size("visit")
     whole = visits * share
     keep, *sent, mark, m_edge = call(
         join_kernel,
@@ -435,8 +450,9 @@
             pltpu.VMEM((2, rows - share + depth, cols), BF16),
         ],
         1 << 29, "join",
-    )(note, msg, following, w, pcol, prow, edge_a, edge_b, filt_a, filt_b)
+    )(note, msg, half, w, pcol, prow, edge_a, edge_b, filt_a, filt_b)
     got = [swapped(part, "band", k + 1) for k, part in enumerate(sent)]
+    halves = [half] + [swapped(half, "band", k) for k in range(1, bands)]
     own, *sent, mark = call(
         pair_kernel,
         (sds((share, cols), F32),) + (sds((share + B, cols), BF16),) * (visits - 1) + (sds((B, LANES), BF16),),
@@ -444,9 +460,9 @@
     )(mark, keep, *got)
     got = [swapped(part, "visit", k + 1) for k, part in enumerate(sent)]
     difference = call(
-        tile_kernel, sds((rows, cols), BF16), [VM] * 7,
+        tile_kernel, sds((rows, cols), BF16), [VM] * (6 + bands),
         conv_scratch + [pltpu.VMEM((chunks, 2 * rows, LANES), F32)], conv_flops, "tile",
-    )(mark, tile, note, following, m1, m_edge, w)
+    )(mark, tile, note, m1, m_edge, w, *halves)
     detection = call(
         coadd_kernel, sds((share, cols), F32), [VM] * (1 + visits), [], 1 << 20, "coadd"
     )(mark, own, *got)

time: 31.9 us -> 30.7 us (0.962)
  waiting for transfers between devices: 4.55 us -> 2.09 us
  Pallas kernels: 12.7 us -> 13.4 us
  starting transfers between devices: 12.4 us -> 12.9 us
    ppermute x3, waiting for transfers between devices: 1.93 us -> 0.01 us  [shifted(): return lax.ppermute(shard, axis, pairs)]
    ppermute x2 -> x3, waiting for transfers between devices: 2.62 us -> 2.08 us  [swapped(): lax.ppermute(shard, axis, [(i, partner(i, k, devices)) for i in range(dev...]
    ppermute x2 -> x3, starting transfers between devices: 1.63 us -> 2.1 us  [swapped(): lax.ppermute(shard, axis, [(i, partner(i, k, devices)) for i in range(dev...]
    pallas_call x2, Pallas kernels: 4.17 us -> 4.57 us  [the longest x1 3.39 us: on_device(): call(tile_kernel, sds((rows, cols), BF16), [VM] * (6 + bands), conv_scrat...]
    pallas_call x1, Pallas kernels: 4.94 us -> 5.31 us  [on_device(): call(first_kernel, (sds((deep, CH), BF16), sds((cols, cols), BF16), sds((...]
  transfers between devices with their start and end apart: 5 -> 6, of which waited for: 3 -> 2; matrix products, arithmetic and copies ran while one was open for 0% -> 0% of each run, Pallas kernels for 31% -> 35%
where the time goes in v10:
time: 30.7 us; the launch traced here: 30.4 us
  Pallas kernels  13.4 us (44%)
  starting transfers between devices  12.9 us (42%)
  waiting for transfers between devices  2.09 us (7%)
  between operations  2.01 us (7%)
    ppermute x3, starting transfers between devices, shifted(): return lax.ppermute(shard, axis, pairs)  10.8 us
    pallas_call x1, Pallas kernels, on_device(): call(first_kernel, (sds((deep, CH), BF16), sds((cols, cols), BF16), sds((...  5.31 us
    pallas_call x1, Pallas kernels, on_device(): call(tile_kernel, sds((rows, cols), BF16), [VM] * (6 + bands), conv_scrat...  3.39 us
    ppermute x3, starting transfers between devices, swapped(): lax.ppermute(shard, axis, [(i, partner(i, k, devices)) for i in range(dev...  2.1 us
    ppermute x3, waiting for transfers between devices, swapped(): lax.ppermute(shard, axis, [(i, partner(i, k, devices)) for i in range(dev...  2.08 us
    pallas_call x1, Pallas kernels, on_device(): call(join_kernel, (sds((whole, cols), F32),) + (sds((whole + B, cols), BF...  1.96 us
    pallas_call x1, Pallas kernels, on_device(): call(pack_kernel, (sds((2 * edge, cols), BF16), sds((edge, cols), BF16),...  1.18 us
    pallas_call x1, Pallas kernels, on_device(): call(coadd_kernel, sds((share, cols), F32), [VM] * (1 + visits), [], 1 <<...  0.95 us
  transfers between devices with their start and end apart: 6, of which 2 were waited for; matrix products, arithmetic and copies ran while one was open for 0% of the time, Pallas kernels for 35%

profile of v10, /device:TPU:0, one launch (start us, length us, event | category | flops | bytes accessed | tf_op | source)
XLA Modules:
  0.0 30.4 jit_solution(3926595793696434260)
XLA Ops:
  0.6 5.0 %collective-permute-start.2 = (bf16[512,1,512]{2,0,1:T(8,128)(2,1)}, bf16[512,1,512]{2,0,1:T(8,128)(2,1)S(1)}, u32[]{:S(2)}, u32[]{:S(2)}) collective-permute-start(bf16[512,1,512]{2,0,1:T(8,128)(2,1)} %param.9), channel_id=1, source_target_pairs={{0,4},{4,8},{8,12},{1,5},{5,9},{9,13},{2,6},{6,10},{10,14},{3,7},{... | collective-permute-start | bytes 1572872 | tf_op jit(solution)/shard_map/ppermute | solution.py:22
  6.9 1.2 %pack.1 = (bf16[64,512]{1,0:T(8,128)(2,1)S(1)}, bf16[32,512]{1,0:T(8,128)(2,1)S(1)}, bf16[288,512]{1,0:T(8,128)(2,1)S(1)}, bf16[16,31]{1,0:T(8,128)(2,1)S(1)}, s...) custom-call(s32[1,1]{1,0:T(1,128)S(6)} %copy.10.off_hbm, s32[1,1]{1,0:T(1,128)S(6)} %copy.11.live_hbm, ...), custom_call_target="tpu_custom_call" | custom-call | flops 1048576 | bytes 2097152 | tf_op jit(solution)/shard_map/pack/pallas_call | solution.py:407
  8.1 1.3 %collective-permute-start.1 = (bf16[288,512]{1,0:T(8,128)(2,1)S(1)}, bf16[288,512]{1,0:T(8,128)(2,1)S(1)}, u32[]{:S(2)}, u32[]{:S(2)}) collective-permute-start(bf16[288,512]{1,0:T(8,128)(2,1)S(1)} %get-tuple-element.27), channel_id=1, source_target_pairs={{4,0},{8,4},{12,8},{5,1},{9,5},{13,9},{6,2},{10,6},{14,10},{7,3},{... | collective-permute-start | bytes 884744 | tf_op jit(solution)/shard_map/ppermute | solution.py:22
  9.4 4.5 %collective-permute-start = (bf16[32,512]{1,0:T(8,128)(2,1)S(1)}, bf16[32,512]{1,0:T(8,128)(2,1)S(1)}, u32[]{:S(2)}, u32[]{:S(2)}) collective-permute-start(bf16[32,512]{1,0:T(8,128)(2,1)S(1)} %get-tuple-element.26), channel_id=1, source_target_pairs={{0,4},{4,8},{8,12},{1,5},{5,9},{9,13},{2,6},{6,10},{10,14},{3,7},{... | collective-permute-start | bytes 98312 | tf_op jit(solution)/shard_map/ppermute | solution.py:22
  13.9 5.3 %first.1 = (bf16[2304,256]{1,0:T(8,128)(2,1)S(1)}, bf16[512,512]{1,0:T(8,128)(2,1)S(1)}, bf16[128,256]{1,0:T(8,128)(2,1)S(1)}, bf16[512,512]{1,0:T(8,128)(2,1)S(...) custom-call(bf16[64,512]{1,0:T(8,128)(2,1)S(1)} %get-tuple-element.25.note_ref, ...), custom_call_target="tpu_custom_call" | custom-call | flops 1207959552 | bytes 2097152 | tf_op jit(solution)/shard_map/first/pallas_call | solution.py:428
  19.3 0.0 collective-permute-done.msg_ref
  19.3 0.0 collective-permute-done.2
  19.3 0.6 %before.1 = (f32[4,64,128]{2,1,0:T(8,128)S(1)}, bf16[480,512]{1,0:T(8,128)(2,1)S(1)}) custom-call(bf16[32,512]{1,0:T(8,128)(2,1)S(1)} %collective-permute-done.msg_ref, bf16[512,512]{1,0:T(8,128)(2,1)S(1)} %bitcast.5, f32[4,512,128]{2,1,0:T(8,128)S(1)} %get-tuple-element.36.m_ref.m1_ref, bf16[512,512]{1,0:T(8,128)(2,1)S(1)} %get-tuple-element.33.pcol_ref), custom_call_target="tpu_custom_call" | custom-call | flops 268435456 | bytes 2097152 | tf_op jit(solution)/shard_map/before/pallas_call | solution.py:438
  19.9 0.0 collective-permute-done.1.next_ref.rest_0_
  19.9 2.0 %join.1 = (f32[256,512]{1,0:T(8,128)S(1)}, bf16[272,512]{1,0:T(8,128)(2,1)S(1)}, bf16[16,128]{1,0:T(8,128)(2,1)S(1)}, f32[4,64,128]{2,1,0:T(8,128)S(1)}) custom-call(bf16[64,512]{1,0:T(8,128)(2,1)S(1)} %get-tuple-element.25.note_ref, bf16[32,512]{1,0:T(8,128)(2,1)S(1)} %collective-permute-done.msg_ref, ...), custom_call_target="tpu_custom_call" | custom-call | flops 536870912 | bytes 2097152 | tf_op jit(solution)/shard_map/join/pallas_call | solution.py:440
  21.9 0.1 collective-permute-start.3
  21.9 0.5 %collective-permute-start.4 = (bf16[288,512]{1,0:T(8,128)(2,1)S(1)}, bf16[288,512]{1,0:T(8,128)(2,1)S(1)}, u32[]{:S(2)}, u32[]{:S(2)}) collective-permute-start(bf16[288,512]{1,0:T(8,128)(2,1)S(1)} %collective-permute-done.1.next_ref.rest_0_), channel_id=1, source_target_pairs={{0,1},{1,0},{2,3},{3,2},{4,5},{5,4},{6,7},{7,6},{8,9},{9,8},{10,11... | collective-permute-start | bytes 884744 | tf_op jit(solution)/shard_map/ppermute | solution.py:31
  22.4 1.0 %collective-permute-done.3.refs_2_ = bf16[272,512]{1,0:T(8,128)(2,1)S(1)} collective-permute-done((bf16[272,512]{1,0:T(8,128)(2,1)S(1)}, bf16[272,512]{1,0:T(8,128)(2,1)S(1)}, u32[]{:S(2)}, u32[]{:S(2)}) %collective-permute-start.3) | collective-permute-done | bytes 278560 | tf_op jit(solution)/shard_map/ppermute | solution.py:31
  23.5 1.5 %collective-permute-start.5 = (bf16[144,512]{1,0:T(8,128)(2,1)S(1)}, bf16[144,512]{1,0:T(8,128)(2,1)S(1)}, u32[]{:S(2)}, u32[]{:S(2)}) collective-permute-start(bf16[144,512]{1,0:T(8,128)(2,1)S(1)} %get-tuple-element.47), channel_id=1, source_target_pairs={{0,2},{2,0},{1,3},{3,1},{4,6},{6,4},{5,7},{7,5},{8,10},{10,8},{9,1... | collective-permute-start | bytes 442376 | tf_op jit(solution)/shard_map/ppermute | solution.py:31
  25.1 0.0 collective-permute-done.4.rest_1_
  25.1 3.4 %tile.1 = bf16[512,512]{1,0:T(8,128)(2,1)} custom-call(bf16[16,128]{1,0:T(8,128)(2,1)S(1)} %get-tuple-element.43.mark_ref, bf16[512,512]{1,0:T(8,128)(2,1)S(1)} %get-tuple-element.44.sci_ref, bf16[64,512]{1,0:T(8,128)(2,1)S(1)} %get-tuple-element.25.note_ref, f32[4,512,128]{2,1,0:T(8,128)S(1)} %get-tuple-element.36.m_ref.m1_ref, ...), custom_call_target="tpu_custom_call" | custom-call | flops 1207959552 | bytes 2097152 | tf_op jit(solution)/shard_map/tile/pallas_call | solution.py:462
  28.5 1.0 %collective-permute-done.5.refs_1_ = bf16[144,512]{1,0:T(8,128)(2,1)S(1)} collective-permute-done((bf16[144,512]{1,0:T(8,128)(2,1)S(1)}, bf16[144,512]{1,0:T(8,128)(2,1)S(1)}, u32[]{:S(2)}, u32[]{:S(2)}) %collective-permute-start.5) | collective-permute-done | bytes 147488 | tf_op jit(solution)/shard_map/ppermute | solution.py:31
  29.5 0.9 %coadd.1 = f32[128,512]{1,0:T(8,128)} custom-call(bf16[16,128]{1,0:T(8,128)(2,1)S(1)} %get-tuple-element.43.mark_ref, f32[128,512]{1,0:T(8,128)S(1)} %get-tuple-element.46.refs_0_, bf16[144,512]{1,0:T(8,128)(2,1)S(1)} %collective-permute-done.5.refs_1_), custom_call_target="tpu_custom_call" | custom-call | flops 1048576 | bytes 2097152 | tf_op jit(solution)/shard_map/coadd/pallas_call | solution.py:466
  (1 shorter events, 0.0 us)
Async XLA Ops:
  0.6 18.6 %collective-permute-start.2 = (bf16[512,1,512]{2,0,1:T(8,128)(2,1)}, bf16[512,1,512]{2,0,1:T(8,128)(2,1)S(1)}, u32[]{:S(2)}, u32[]{:S(2)}) collective-permute-start(bf16[512,1,512]{2,0,1:T(8,128)(2,1)} %param.9), channel_id=1, source_target_pairs={{0,4},{4,8},{8,12},{1,5},{5,9},{9,13},{2,6},{6,10},{10,14},{3,7},{... | collective-permute-start | bytes 1572872 | tf_op jit(solution)/shard_map/ppermute | solution.py:22
  8.1 11.8 %collective-permute-start.1 = (bf16[288,512]{1,0:T(8,128)(2,1)S(1)}, bf16[288,512]{1,0:T(8,128)(2,1)S(1)}, u32[]{:S(2)}, u32[]{:S(2)}) collective-permute-start(bf16[288,512]{1,0:T(8,128)(2,1)S(1)} %get-tuple-element.27), channel_id=1, source_target_pairs={{4,0},{8,4},{12,8},{5,1},{9,5},{13,9},{6,2},{10,6},{14,10},{7,3},{... | collective-permute-start | bytes 884744 | tf_op jit(solution)/shard_map/ppermute | solution.py:22
  9.4 9.9 %collective-permute-start = (bf16[32,512]{1,0:T(8,128)(2,1)S(1)}, bf16[32,512]{1,0:T(8,128)(2,1)S(1)}, u32[]{:S(2)}, u32[]{:S(2)}) collective-permute-start(bf16[32,512]{1,0:T(8,128)(2,1)S(1)} %get-tuple-element.26), channel_id=1, source_target_pairs={{0,4},{4,8},{8,12},{1,5},{5,9},{9,13},{2,6},{6,10},{10,14},{3,7},{... | collective-permute-start | bytes 98312 | tf_op jit(solution)/shard_map/ppermute | solution.py:22
  21.9 1.6 %collective-permute-start.3 = (bf16[272,512]{1,0:T(8,128)(2,1)S(1)}, bf16[272,512]{1,0:T(8,128)(2,1)S(1)}, u32[]{:S(2)}, u32[]{:S(2)}) collective-permute-start(bf16[272,512]{1,0:T(8,128)(2,1)S(1)} %get-tuple-element.42), channel_id=1, source_target_pairs={{0,1},{1,0},{2,3},{3,2},{4,5},{5,4},{6,7},{7,6},{8,9},{9,8},{10,11... | collective-permute-start | bytes 835592 | tf_op jit(solution)/shard_map/ppermute | solution.py:31
  21.9 3.1 %collective-permute-start.4 = (bf16[288,512]{1,0:T(8,128)(2,1)S(1)}, bf16[288,512]{1,0:T(8,128)(2,1)S(1)}, u32[]{:S(2)}, u32[]{:S(2)}) collective-permute-start(bf16[288,512]{1,0:T(8,128)(2,1)S(1)} %collective-permute-done.1.next_ref.rest_0_), channel_id=1, source_target_pairs={{0,1},{1,0},{2,3},{3,2},{4,5},{5,4},{6,7},{7,6},{8,9},{9,8},{10,11... | collective-permute-start | bytes 884744 | tf_op jit(solution)/shard_map/ppermute | solution.py:31
  23.5 6.0 %collective-permute-start.5 = (bf16[144,512]{1,0:T(8,128)(2,1)S(1)}, bf16[144,512]{1,0:T(8,128)(2,1)S(1)}, u32[]{:S(2)}, u32[]{:S(2)}) collective-permute-start(bf16[144,512]{1,0:T(8,128)(2,1)S(1)} %get-tuple-element.47), channel_id=1, source_target_pairs={{0,2},{2,0},{1,3},{3,1},{4,6},{6,4},{5,7},{7,5},{8,10},{10,8},{9,1... | collective-permute-start | bytes 442376 | tf_op jit(solution)/shard_map/ppermute | solution.py:31

commit v11 on v10

--- a/solution.py
+++ b/solution.py
@@ -76,28 +76,35 @@
                 xs[1, at, :, part] = here.astype(xs.dtype)
                 xs[2, at, :, part] = pltpu.roll(here, count - 1, 0).astype(xs.dtype)
 
-    def solve(c):
-        b = c * GROUPS
+    def solve(first, last):
+        b, many = first * GROUPS, (last - first) * GROUPS
         pieces = [
-            xs[qr, b + qc : b + qc + GROUPS].reshape(GROUPS * count, CH).astype(BF16)
+            xs[qr, b + qc : b + qc + many].reshape(many * count, CH).astype(BF16)
             for qr in range(3)
             for qc in range(3)
         ]
         out = jnp.dot(jnp.concatenate(pieces, axis=1), w_ref[...], preferred_element_type=F32)
-        for h in range(2):
-            part = slice(h * LANES, (h + 1) * LANES)
-            rows = group_transpose([out[g * count : (g + 1) * count, part] for g in range(GROUPS)])
-            for i in range(GROUPS):
-                dst[c, pl.ds(GROUPS * h + i, count, stride=PITCH), :] = rows[i]
+        for c in range(first, last):
+            at = (c - first) * GROUPS
+            for h in range(2):
+                part = slice(h * LANES, (h + 1) * LANES)
+                rows = group_transpose([out[(at + g) * count : (at + g + 1) * count, part] for g in range(GROUPS)])
+                for i in range(GROUPS):
+                    dst[c, pl.ds(GROUPS * h + i, count, stride=PITCH), :] = rows[i]
 
     for q in range(3):
         xs[q, 0] = jnp.zeros((count, CH), xs.dtype)
         xs[q, blocks + 1] = jnp.zeros((count, CH), xs.dtype)
-    load(0)
+    group = max(1, 32 // count)
+    done = 0
     for c in range(chunks):
-        if c + 1 < chunks:
-            load(c + 1)
-        solve(c)
+        load(c)
+        while done + group < c + 1:
+            solve(done, done + group)
+            done += group
+    while done < chunks:
+        solve(done, min(done + group, chunks))
+        done += group
 
 
 def column(row):
@@ -240,9 +247,15 @@
     return (note[0, 0] * B + note[0, 1]).astype(jnp.int32), note[0, 2]
 
 
+def read_before(msg_ref):
+    valid = lax.axis_index("patch") > 0
+    off, live = read_note(msg_ref)
+    return jnp.where(valid, off, 0), jnp.where(valid, live, 0.0), valid
+
+
 def before_kernel(msg_ref, sci_ref, m_ref, pcol_ref, edge_ref, filt_ref, sci, diff):
     rows = sci_ref.shape[0]
-    off, _ = read_note(msg_ref)
+    off, _, _ = read_before(msg_ref)
     to_chunks(sci, 0, sci_ref[...])
     filter_inner(sci, rows - B - off, off - rows, off, m_ref, pcol_ref, edge_ref, filt_ref, diff)
 
@@ -254,7 +267,8 @@
     *outs, mark_ref, m_ref, src, xs, strip, diff, filt = rest
     edge = 2 * B
     rows, cols = filt_a.shape[0] + edge, filt_a.shape[1]
-    to_blocks(src, 0, msg_ref[...])
+    off_b, live_b, valid = read_before(msg_ref)
+    to_blocks(src, 0, jnp.where(valid, msg_ref[...].astype(F32), 0.0))
     to_blocks(src, 2, note_ref[edge:, :])
     to_blocks(src, 4, note_ref[0:edge, :])
     to_blocks(src, 6, next_ref[0:edge, :])
@@ -262,7 +276,6 @@
     for n, a in enumerate((1, 2, 5, 6)):
         m_ref[:, B * n : B * (n + 1), :] = strip[:, PITCH * a : PITCH * a + B, :]
     off_a, live_a = read_note(note_ref)
-    off_b, live_b = read_note(msg_ref)
     for s, (side, first, last) in enumerate(((edge_a, off_a, off_a + rows), (edge_b, off_b - rows, off_b))):
         for c in range(cols // LANES):
             part = slice(c * LANES, (c + 1) * LANES)
@@ -350,39 +363,45 @@
 
 
 def coadd_kernel(mark_ref, *refs):
-    *parts, out_ref = refs
+    *parts, out_ref, result, sems = refs
     share, cols = out_ref.shape
     bands = lax.axis_size("band")
     base = (lax.axis_index("visit") * bands + lax.axis_index("band")) * share
     row = (iota((share, LANES), 0) + base).astype(F32)
-    accum = parts[0][...]
     cover = jnp.zeros((share, LANES), F32)
     for n, part in enumerate(parts):
-        if n:
-            accum += part[0:share, :].astype(F32)
         marks = (part[share : share + B, 0:LANES] if n else mark_ref[...]).astype(F32)
         for m in range(bands):
             mark = marks[m : m + 1, :]
             cover += jnp.where(row >= mark[:, 0:1] * B + mark[:, 1:2], mark[:, 2:3], 0.0)
             cover += jnp.where(row < mark[:, 3:4] * B + mark[:, 4:5], mark[:, 5:6], 0.0)
     scale = lax.rsqrt(jnp.maximum(cover, 1.0))
+    copies = []
     for c in range(cols // LANES):
-        part = slice(c * LANES, (c + 1) * LANES)
-        out_ref[:, part] = accum[:, part] * scale
+        span = slice(c * LANES, (c + 1) * LANES)
+        value = parts[0][:, span]
+        for part in parts[1:]:
+            value += part[0:share, span].astype(F32)
+        result[:, span] = value * scale
+        there = pl.ds(c * LANES, LANES)
+        copies.append(pltpu.make_async_copy(result.at[:, there], out_ref.at[:, there], sems.at[c]))
+        copies[-1].start()
+    for copy in copies:
+        copy.wait()
 
 
 def in_hbm(*arrays):
     return [pltpu.with_memory_space_constraint(x, pltpu.HBM) for x in arrays]
 
 
-def call(body, shapes, specs, scratch, flops, name, limit=LIMIT):
+def call(body, shapes, specs, scratch, flops, name, out=VM):
     return pl.pallas_call(
         body,
         out_shape=shapes,
         in_specs=specs,
-        out_specs=jax.tree.map(lambda _: VM, shapes),
+        out_specs=jax.tree.map(lambda _: out, shapes),
         scratch_shapes=scratch,
-        compiler_params=pltpu.CompilerParams(vmem_limit_bytes=limit * 1024 * 1024),
+        compiler_params=pltpu.CompilerParams(vmem_limit_bytes=LIMIT * 1024 * 1024),
         cost_estimate=pl.CostEstimate(flops=flops, bytes_accessed=1 << 21, transcendentals=0),
         name=name,
     )
@@ -415,7 +434,8 @@
         1 << 20, "pack",
     )(offsets, live_flags, held[0], *in_hbm(bank, index, coeff, psf))
     half = shifted(half, "patch", -1)
-    msg = shifted(msg, "patch", 1)
+    panels = lax.axis_size("patch")
+    msg = lax.ppermute(msg, "patch", [(i, (i + 1) % panels) for i in range(panels)])
     count = rows // B
     conv_scratch = [
         pltpu.VMEM((chunks, count * PITCH, LANES), F32),
@@ -464,7 +484,8 @@
         conv_scratch + [pltpu.VMEM((chunks, 2 * rows, LANES), F32)], conv_flops, "tile",
     )(mark, tile, note, m1, m_edge, w, *halves)
     detection = call(
-        coadd_kernel, sds((share, cols), F32), [VM] * (1 + visits), [], 1 << 20, "coadd"
+        coadd_kernel, sds((share, cols), F32), [VM] * (1 + visits),
+        [pltpu.VMEM((share, cols), F32), pltpu.SemaphoreType.DMA((chunks,))], 1 << 20, "coadd", HBM,
     )(mark, own, *got)
     return (difference[:, None, :], detection)
 

time: 30.7 us -> 32.7 us (1.065)
  waiting for transfers between devices: 2.09 us -> 5.79 us
  starting transfers between devices: 12.9 us -> 11.1 us
    ppermute x3 -> x2, starting transfers between devices: 10.8 us -> 6.25 us  [shifted(): return lax.ppermute(shard, axis, pairs)]
    ppermute x0 -> x1, waiting for transfers between devices: none -> 3.72 us  [on_device(): lax.ppermute(msg, 'patch', [(i, (i + 1) % panels) for i in range(panels)])]
    ppermute x0 -> x1, starting transfers between devices: none -> 2.69 us  [on_device(): lax.ppermute(msg, 'patch', [(i, (i + 1) % panels) for i in range(panels)])]
  transfers between devices with their start and end apart: 6 -> 6, of which waited for: 2 -> 3; matrix products, arithmetic and copies ran while one was open for 0% -> 0% of each run, Pallas kernels for 35% -> 32%
where the time goes in v11:
time: 32.7 us; the launch traced here: 32.5 us
  Pallas kernels  13.7 us (42%)
  starting transfers between devices  11.1 us (34%)
  waiting for transfers between devices  5.79 us (18%)
  between operations  1.99 us (6%)
    ppermute x2, starting transfers between devices, shifted(): return lax.ppermute(shard, axis, pairs)  6.25 us
    pallas_call x1, Pallas kernels, on_device(): call(first_kernel, (sds((deep, CH), BF16), sds((cols, cols), BF16), sds((...  5.3 us
    ppermute x1, waiting for transfers between devices, on_device(): lax.ppermute(msg, 'patch', [(i, (i + 1) % panels) for i in range(panels)])  3.72 us
    pallas_call x1, Pallas kernels, on_device(): call(tile_kernel, sds((rows, cols), BF16), [VM] * (6 + bands), conv_scrat...  3.38 us
    ppermute x1, starting transfers between devices, on_device(): lax.ppermute(msg, 'patch', [(i, (i + 1) % panels) for i in range(panels)])  2.69 us
    pallas_call x1, Pallas kernels, on_device(): call(join_kernel, (sds((whole, cols), F32),) + (sds((whole + B, cols), BF...  2.17 us
    ppermute x3, starting transfers between devices, swapped(): lax.ppermute(shard, axis, [(i, partner(i, k, devices)) for i in range(dev...  2.12 us
    ppermute x3, waiting for transfers between devices, swapped(): lax.ppermute(shard, axis, [(i, partner(i, k, devices)) for i in range(dev...  2.07 us
  transfers between devices with their start and end apart: 6, of which 3 were waited for; matrix products, arithmetic and copies ran while one was open for 0% of the time, Pallas kernels for 32%

profile of v11, /device:TPU:0, one launch (start us, length us, event | category | flops | bytes accessed | tf_op | source)
XLA Modules:
  0.0 32.5 jit_solution(5672945271616658276)
XLA Ops:
  0.6 5.0 %collective-permute-start.2 = (bf16[512,1,512]{2,0,1:T(8,128)(2,1)}, bf16[512,1,512]{2,0,1:T(8,128)(2,1)S(1)}, u32[]{:S(2)}, u32[]{:S(2)}) collective-permute-start(bf16[512,1,512]{2,0,1:T(8,128)(2,1)} %param.9), channel_id=1, source_target_pairs={{0,4},{4,8},{8,12},{1,5},{5,9},{9,13},{2,6},{6,10},{10,14},{3,7},{... | collective-permute-start | bytes 1572872 | tf_op jit(solution)/shard_map/ppermute | solution.py:22
  6.9 1.2 %pack.1 = (bf16[64,512]{1,0:T(8,128)(2,1)S(1)}, bf16[32,512]{1,0:T(8,128)(2,1)S(1)}, bf16[288,512]{1,0:T(8,128)(2,1)S(1)}, bf16[16,31]{1,0:T(8,128)(2,1)S(1)}, s...) custom-call(s32[1,1]{1,0:T(1,128)S(6)} %copy.10.off_hbm, s32[1,1]{1,0:T(1,128)S(6)} %copy.11.live_hbm, ...), custom_call_target="tpu_custom_call" | custom-call | flops 1048576 | bytes 2097152 | tf_op jit(solution)/shard_map/pack/pallas_call | solution.py:426
  8.1 1.3 %collective-permute-start.1 = (bf16[288,512]{1,0:T(8,128)(2,1)S(1)}, bf16[288,512]{1,0:T(8,128)(2,1)S(1)}, u32[]{:S(2)}, u32[]{:S(2)}) collective-permute-start(bf16[288,512]{1,0:T(8,128)(2,1)S(1)} %get-tuple-element.27), channel_id=1, source_target_pairs={{4,0},{8,4},{12,8},{5,1},{9,5},{13,9},{6,2},{10,6},{14,10},{7,3},{... | collective-permute-start | bytes 884744 | tf_op jit(solution)/shard_map/ppermute | solution.py:22
  9.4 2.7 %collective-permute-start = (bf16[32,512]{1,0:T(8,128)(2,1)S(1)}, bf16[32,512]{1,0:T(8,128)(2,1)S(1)}, u32[]{:S(2)}, u32[]{:S(2)}) collective-permute-start(bf16[32,512]{1,0:T(8,128)(2,1)S(1)} %get-tuple-element.26), channel_id=1, source_target_pairs={{0,4},{4,8},{8,12},{12,0},{1,5},{5,9},{9,13},{13,1},{2,6},{6,10},{... | collective-permute-start | bytes 98312 | tf_op jit(solution)/shard_map/ppermute | solution.py:438
  12.1 5.3 %first.1 = (bf16[2304,256]{1,0:T(8,128)(2,1)S(1)}, bf16[512,512]{1,0:T(8,128)(2,1)S(1)}, bf16[128,256]{1,0:T(8,128)(2,1)S(1)}, bf16[512,512]{1,0:T(8,128)(2,1)S(...) custom-call(bf16[64,512]{1,0:T(8,128)(2,1)S(1)} %get-tuple-element.25.note_ref, ...), custom_call_target="tpu_custom_call" | custom-call | flops 1207959552 | bytes 2097152 | tf_op jit(solution)/shard_map/first/pallas_call | solution.py:448
  17.4 3.7 %collective-permute-done.msg_ref = bf16[32,512]{1,0:T(8,128)(2,1)S(1)} collective-permute-done((bf16[32,512]{1,0:T(8,128)(2,1)S(1)}, bf16[32,512]{1,0:T(8,128)(2,1)S(1)}, u32[]{:S(2)}, u32[]{:S(2)}) %collective-permute-start) | collective-permute-done | bytes 32800 | tf_op jit(solution)/shard_map/ppermute | solution.py:438
  21.1 0.0 collective-permute-done.2
  21.1 0.6 %before.1 = (f32[4,64,128]{2,1,0:T(8,128)S(1)}, bf16[480,512]{1,0:T(8,128)(2,1)S(1)}) custom-call(bf16[32,512]{1,0:T(8,128)(2,1)S(1)} %collective-permute-done.msg_ref, bf16[512,512]{1,0:T(8,128)(2,1)S(1)} %bitcast.5, f32[4,512,128]{2,1,0:T(8,128)S(1)} %get-tuple-element.36.m_ref.m1_ref, bf16[512,512]{1,0:T(8,128)(2,1)S(1)} %get-tuple-element.33.pcol_ref), custom_call_target="tpu_custom_call" | custom-call | flops 268435456 | bytes 2097152 | tf_op jit(solution)/shard_map/before/pallas_call | solution.py:458
  21.7 0.0 collective-permute-done.1.next_ref.rest_0_
  21.7 2.2 %join.1 = (f32[256,512]{1,0:T(8,128)S(1)}, bf16[272,512]{1,0:T(8,128)(2,1)S(1)}, bf16[16,128]{1,0:T(8,128)(2,1)S(1)}, f32[4,64,128]{2,1,0:T(8,128)S(1)}) custom-call(bf16[64,512]{1,0:T(8,128)(2,1)S(1)} %get-tuple-element.25.note_ref, bf16[32,512]{1,0:T(8,128)(2,1)S(1)} %collective-permute-done.msg_ref, ...), custom_call_target="tpu_custom_call" | custom-call | flops 536870912 | bytes 2097152 | tf_op jit(solution)/shard_map/join/pallas_call | solution.py:460
  23.9 0.1 collective-permute-start.3
  24.0 0.5 %collective-permute-start.4 = (bf16[288,512]{1,0:T(8,128)(2,1)S(1)}, bf16[288,512]{1,0:T(8,128)(2,1)S(1)}, u32[]{:S(2)}, u32[]{:S(2)}) collective-permute-start(bf16[288,512]{1,0:T(8,128)(2,1)S(1)} %collective-permute-done.1.next_ref.rest_0_), channel_id=1, source_target_pairs={{0,1},{1,0},{2,3},{3,2},{4,5},{5,4},{6,7},{7,6},{8,9},{9,8},{10,11... | collective-permute-start | bytes 884744 | tf_op jit(solution)/shard_map/ppermute | solution.py:31
  24.5 1.0 %collective-permute-done.3.refs_2_ = bf16[272,512]{1,0:T(8,128)(2,1)S(1)} collective-permute-done((bf16[272,512]{1,0:T(8,128)(2,1)S(1)}, bf16[272,512]{1,0:T(8,128)(2,1)S(1)}, u32[]{:S(2)}, u32[]{:S(2)}) %collective-permute-start.3) | collective-permute-done | bytes 278560 | tf_op jit(solution)/shard_map/ppermute | solution.py:31
  25.6 1.6 %collective-permute-start.5 = (bf16[144,512]{1,0:T(8,128)(2,1)S(1)}, bf16[144,512]{1,0:T(8,128)(2,1)S(1)}, u32[]{:S(2)}, u32[]{:S(2)}) collective-permute-start(bf16[144,512]{1,0:T(8,128)(2,1)S(1)} %get-tuple-element.47), channel_id=1, source_target_pairs={{0,2},{2,0},{1,3},{3,1},{4,6},{6,4},{5,7},{7,5},{8,10},{10,8},{9,1... | collective-permute-start | bytes 442376 | tf_op jit(solution)/shard_map/ppermute | solution.py:31
  27.1 0.0 collective-permute-done.4.rest_1_
  27.1 3.4 %tile.1 = bf16[512,512]{1,0:T(8,128)(2,1)} custom-call(bf16[16,128]{1,0:T(8,128)(2,1)S(1)} %get-tuple-element.43.mark_ref, bf16[512,512]{1,0:T(8,128)(2,1)S(1)} %get-tuple-element.44.sci_ref, bf16[64,512]{1,0:T(8,128)(2,1)S(1)} %get-tuple-element.25.note_ref, f32[4,512,128]{2,1,0:T(8,128)S(1)} %get-tuple-element.36.m_ref.m1_ref, ...), custom_call_target="tpu_custom_call" | custom-call | flops 1207959552 | bytes 2097152 | tf_op jit(solution)/shard_map/tile/pallas_call | solution.py:482
  30.5 1.0 %collective-permute-done.5.refs_1_ = bf16[144,512]{1,0:T(8,128)(2,1)S(1)} collective-permute-done((bf16[144,512]{1,0:T(8,128)(2,1)S(1)}, bf16[144,512]{1,0:T(8,128)(2,1)S(1)}, u32[]{:S(2)}, u32[]{:S(2)}) %collective-permute-start.5) | collective-permute-done | bytes 147488 | tf_op jit(solution)/shard_map/ppermute | solution.py:31
  31.5 1.0 %coadd.1 = f32[128,512]{1,0:T(8,128)} custom-call(bf16[16,128]{1,0:T(8,128)(2,1)S(1)} %get-tuple-element.43.mark_ref, f32[128,512]{1,0:T(8,128)S(1)} %get-tuple-element.46.refs_0_, bf16[144,512]{1,0:T(8,128)(2,1)S(1)} %collective-permute-done.5.refs_1_), custom_call_target="tpu_custom_call" | custom-call | flops 1048576 | bytes 2097152 | tf_op jit(solution)/shard_map/coadd/pallas_call | solution.py:486
  (1 shorter events, 0.0 us)
Async XLA Ops:
  0.6 20.5 %collective-permute-start.2 = (bf16[512,1,512]{2,0,1:T(8,128)(2,1)}, bf16[512,1,512]{2,0,1:T(8,128)(2,1)S(1)}, u32[]{:S(2)}, u32[]{:S(2)}) collective-permute-start(bf16[512,1,512]{2,0,1:T(8,128)(2,1)} %param.9), channel_id=1, source_target_pairs={{0,4},{4,8},{8,12},{1,5},{5,9},{9,13},{2,6},{6,10},{10,14},{3,7},{... | collective-permute-start | bytes 1572872 | tf_op jit(solution)/shard_map/ppermute | solution.py:22
  8.1 13.6 %collective-permute-start.1 = (bf16[288,512]{1,0:T(8,128)(2,1)S(1)}, bf16[288,512]{1,0:T(8,128)(2,1)S(1)}, u32[]{:S(2)}, u32[]{:S(2)}) collective-permute-start(bf16[288,512]{1,0:T(8,128)(2,1)S(1)} %get-tuple-element.27), channel_id=1, source_target_pairs={{4,0},{8,4},{12,8},{5,1},{9,5},{13,9},{6,2},{10,6},{14,10},{7,3},{... | collective-permute-start | bytes 884744 | tf_op jit(solution)/shard_map/ppermute | solution.py:22
  9.4 11.7 %collective-permute-start = (bf16[32,512]{1,0:T(8,128)(2,1)S(1)}, bf16[32,512]{1,0:T(8,128)(2,1)S(1)}, u32[]{:S(2)}, u32[]{:S(2)}) collective-permute-start(bf16[32,512]{1,0:T(8,128)(2,1)S(1)} %get-tuple-element.26), channel_id=1, source_target_pairs={{0,4},{4,8},{8,12},{12,0},{1,5},{5,9},{9,13},{13,1},{2,6},{6,10},{... | collective-permute-start | bytes 98312 | tf_op jit(solution)/shard_map/ppermute | solution.py:438
  23.9 1.6 %collective-permute-start.3 = (bf16[272,512]{1,0:T(8,128)(2,1)S(1)}, bf16[272,512]{1,0:T(8,128)(2,1)S(1)}, u32[]{:S(2)}, u32[]{:S(2)}) collective-permute-start(bf16[272,512]{1,0:T(8,128)(2,1)S(1)} %get-tuple-element.42), channel_id=1, source_target_pairs={{0,1},{1,0},{2,3},{3,2},{4,5},{5,4},{6,7},{7,6},{8,9},{9,8},{10,11... | collective-permute-start | bytes 835592 | tf_op jit(solution)/shard_map/ppermute | solution.py:31
  24.0 3.2 %collective-permute-start.4 = (bf16[288,512]{1,0:T(8,128)(2,1)S(1)}, bf16[288,512]{1,0:T(8,128)(2,1)S(1)}, u32[]{:S(2)}, u32[]{:S(2)}) collective-permute-start(bf16[288,512]{1,0:T(8,128)(2,1)S(1)} %collective-permute-done.1.next_ref.rest_0_), channel_id=1, source_target_pairs={{0,1},{1,0},{2,3},{3,2},{4,5},{5,4},{6,7},{7,6},{8,9},{9,8},{10,11... | collective-permute-start | bytes 884744 | tf_op jit(solution)/shard_map/ppermute | solution.py:31
  25.6 6.0 %collective-permute-start.5 = (bf16[144,512]{1,0:T(8,128)(2,1)S(1)}, bf16[144,512]{1,0:T(8,128)(2,1)S(1)}, u32[]{:S(2)}, u32[]{:S(2)}) collective-permute-start(bf16[144,512]{1,0:T(8,128)(2,1)S(1)} %get-tuple-element.47), channel_id=1, source_target_pairs={{0,2},{2,0},{1,3},{3,1},{4,6},{6,4},{5,7},{7,5},{8,10},{10,8},{9,1... | collective-permute-start | bytes 442376 | tf_op jit(solution)/shard_map/ppermute | solution.py:31

commit v12 on v10

--- a/solution.py
+++ b/solution.py
@@ -98,6 +98,16 @@
         if c + 1 < chunks:
             load(c + 1)
         solve(c)
+
+
+def slanted(row, count):
+    value = jnp.broadcast_to(row, (count, row.shape[1]))
+    index = iota(value.shape, 0)
+    bit = 1
+    while bit < count:
+        value = jnp.where((index & bit) != 0, pltpu.roll(value, bit, 1), value)
+        bit *= 2
+    return value
 
 
 def column(row):
@@ -179,25 +189,19 @@
             for qc in range(3):
                 row = (g // B) * 3 * CH + qc * CH + (g % B) * B
                 w_ref[row : row + B, :] = zp[qc * B : (qc + 1) * B, at : at + CH]
-    psf = psf_ref[...].astype(F32)
     size = pcol_ref.shape[0]
-    blank = jnp.zeros((LANES, LANES), F32)
-    bands = {}
-    for off in (-1, 0, 1):
-        tap = iota((LANES, LANES), 0) + off * LANES - iota((LANES, LANES), 1) + half
-        block = blank
-        for t in range(taps):
-            block = jnp.where(tap == t, psf[:, t : t + 1], block)
-        bands[off] = block.astype(BF16)
+    lanes = iota((taps, 3 * LANES), 1)
+    mirror = (lanes - LANES + iota(lanes.shape, 0) == half).astype(F32).astype(BF16)
+    bands = slanted(jnp.dot(psf_ref[...], mirror, preferred_element_type=F32), LANES)
+    bands = {1 - n: bands[:, n * LANES : (n + 1) * LANES].astype(BF16) for n in range(3)}
     for i in range(size // LANES):
         for j in range(size // LANES):
-            pcol_ref[i * LANES : (i + 1) * LANES, j * LANES : (j + 1) * LANES] = bands.get(i - j, blank.astype(BF16))
-    shape = prow_ref.shape
-    tap = iota(shape, 1) - iota(shape, 0) - delta
-    block = jnp.zeros(shape, F32)
-    for t in range(taps):
-        block = jnp.where(tap == t, psf[:, t : t + 1], block)
-    prow_ref[...] = block.astype(BF16)
+            block = bands.get(i - j, jnp.zeros((LANES, LANES), BF16))
+            pcol_ref[i * LANES : (i + 1) * LANES, j * LANES : (j + 1) * LANES] = block
+    share, depth = prow_ref.shape
+    lanes = iota((taps, depth), 1)
+    ahead = (lanes - iota(lanes.shape, 0) == delta).astype(F32).astype(BF16)
+    prow_ref[...] = slanted(jnp.dot(psf_ref[...], ahead, preferred_element_type=F32), share).astype(BF16)
     for copy in copies:
         copy.wait()
     edge = 2 * B
@@ -240,9 +244,15 @@
     return (note[0, 0] * B + note[0, 1]).astype(jnp.int32), note[0, 2]
 
 
+def read_before(msg_ref):
+    valid = lax.axis_index("patch") > 0
+    off, live = read_note(msg_ref)
+    return jnp.where(valid, off, 0), jnp.where(valid, live, 0.0), valid
+
+
 def before_kernel(msg_ref, sci_ref, m_ref, pcol_ref, edge_ref, filt_ref, sci, diff):
     rows = sci_ref.shape[0]
-    off, _ = read_note(msg_ref)
+    off, _, _ = read_before(msg_ref)
     to_chunks(sci, 0, sci_ref[...])
     filter_inner(sci, rows - B - off, off - rows, off, m_ref, pcol_ref, edge_ref, filt_ref, diff)
 
@@ -254,7 +264,8 @@
     *outs, mark_ref, m_ref, src, xs, strip, diff, filt = rest
     edge = 2 * B
     rows, cols = filt_a.shape[0] + edge, filt_a.shape[1]
-    to_blocks(src, 0, msg_ref[...])
+    off_b, live_b, valid = read_before(msg_ref)
+    to_blocks(src, 0, jnp.where(valid, msg_ref[...].astype(F32), 0.0))
     to_blocks(src, 2, note_ref[edge:, :])
     to_blocks(src, 4, note_ref[0:edge, :])
     to_blocks(src, 6, next_ref[0:edge, :])
@@ -262,7 +273,6 @@
     for n, a in enumerate((1, 2, 5, 6)):
         m_ref[:, B * n : B * (n + 1), :] = strip[:, PITCH * a : PITCH * a + B, :]
     off_a, live_a = read_note(note_ref)
-    off_b, live_b = read_note(msg_ref)
     for s, (side, first, last) in enumerate(((edge_a, off_a, off_a + rows), (edge_b, off_b - rows, off_b))):
         for c in range(cols // LANES):
             part = slice(c * LANES, (c + 1) * LANES)
@@ -355,11 +365,8 @@
     bands = lax.axis_size("band")
     base = (lax.axis_index("visit") * bands + lax.axis_index("band")) * share
     row = (iota((share, LANES), 0) + base).astype(F32)
-    accum = parts[0][...]
     cover = jnp.zeros((share, LANES), F32)
     for n, part in enumerate(parts):
-        if n:
-            accum += part[0:share, :].astype(F32)
         marks = (part[share : share + B, 0:LANES] if n else mark_ref[...]).astype(F32)
         for m in range(bands):
             mark = marks[m : m + 1, :]
@@ -367,22 +374,25 @@
             cover += jnp.where(row < mark[:, 3:4] * B + mark[:, 4:5], mark[:, 5:6], 0.0)
     scale = lax.rsqrt(jnp.maximum(cover, 1.0))
     for c in range(cols // LANES):
-        part = slice(c * LANES, (c + 1) * LANES)
-        out_ref[:, part] = accum[:, part] * scale
+        span = slice(c * LANES, (c + 1) * LANES)
+        value = parts[0][:, span]
+        for part in parts[1:]:
+            value += part[0:share, span].astype(F32)
+        out_ref[:, span] = value * scale
 
 
 def in_hbm(*arrays):
     return [pltpu.with_memory_space_constraint(x, pltpu.HBM) for x in arrays]
 
 
-def call(body, shapes, specs, scratch, flops, name, limit=LIMIT):
+def call(body, shapes, specs, scratch, flops, name):
     return pl.pallas_call(
         body,
         out_shape=shapes,
         in_specs=specs,
         out_specs=jax.tree.map(lambda _: VM, shapes),
         scratch_shapes=scratch,
-        compiler_params=pltpu.CompilerParams(vmem_limit_bytes=limit * 1024 * 1024),
+        compiler_params=pltpu.CompilerParams(vmem_limit_bytes=LIMIT * 1024 * 1024),
         cost_estimate=pl.CostEstimate(flops=flops, bytes_accessed=1 << 21, transcendentals=0),
         name=name,
     )
@@ -415,7 +425,8 @@
         1 << 20, "pack",
     )(offsets, live_flags, held[0], *in_hbm(bank, index, coeff, psf))
     half = shifted(half, "patch", -1)
-    msg = shifted(msg, "patch", 1)
+    panels = lax.axis_size("patch")
+    msg = lax.ppermute(msg, "patch", [(i, (i + 1) % panels) for i in range(panels)])
     count = rows // B
     conv_scratch = [
         pltpu.VMEM((chunks, count * PITCH, LANES), F32),
@@ -435,7 +446,7 @@
         [pltpu.VMEM((rows, cols), BF16), pltpu.SemaphoreType.DMA((2,))] + conv_scratch + sky_scratch,
         conv_flops, "first",
     )(note, *held, *small)
-    edge_b, filt_b = call(before_kernel, sides, [VM] * 4, sky_scratch, 1 << 28, "before")(msg, before, m1, pcol)
+    edge_b, filt_b = call(before_kernel, sides, [VM] * 4, sky_scratch, 1 << 34, "before")(msg, before, m1, pcol)
     whole = visits * share
     keep, *sent, mark, m_edge = call(
         join_kernel,

time: 30.7 us -> 30.8 us (level)
  waiting for transfers between devices: 2.09 us -> 5.82 us
  starting transfers between devices: 12.9 us -> 9.97 us
  Pallas kernels: 13.4 us -> 12.9 us
    ppermute x3 -> x2, starting transfers between devices: 10.8 us -> 6.24 us  [shifted(): return lax.ppermute(shard, axis, pairs)]
    ppermute x0 -> x1, waiting for transfers between devices: none -> 1.92 us  [on_device(): lax.ppermute(msg, 'patch', [(i, (i + 1) % panels) for i in range(panels)])]
    ppermute x3 -> x2, waiting for transfers between devices: 0.01 us -> 1.82 us  [shifted(): return lax.ppermute(shard, axis, pairs)]
    ppermute x0 -> x1, starting transfers between devices: none -> 1.6 us  [on_device(): lax.ppermute(msg, 'patch', [(i, (i + 1) % panels) for i in range(panels)])]
    pallas_call x1, Pallas kernels: 5.31 us -> 4.75 us  [on_device(): call(first_kernel, (sds((deep, CH), BF16), sds((cols, cols), BF16), sds((...]
  transfers between devices with their start and end apart: 6 -> 6, of which waited for: 2 -> 4; matrix products, arithmetic and copies ran while one was open for 0% -> 0% of each run, Pallas kernels for 35% -> 32%
where the time goes in v12:
time: 30.8 us; the launch traced here: 30.6 us
  Pallas kernels  12.9 us (42%)
  starting transfers between devices  9.97 us (32%)
  waiting for transfers between devices  5.82 us (19%)
  between operations  1.98 us (6%)
    ppermute x2, starting transfers between devices, shifted(): return lax.ppermute(shard, axis, pairs)  6.24 us
    pallas_call x1, Pallas kernels, on_device(): call(first_kernel, (sds((deep, CH), BF16), sds((cols, cols), BF16), sds((...  4.75 us
    pallas_call x1, Pallas kernels, on_device(): call(tile_kernel, sds((rows, cols), BF16), [VM] * (6 + bands), conv_scrat...  3.36 us
    ppermute x3, starting transfers between devices, swapped(): lax.ppermute(shard, axis, [(i, partner(i, k, devices)) for i in range(dev...  2.13 us
    ppermute x3, waiting for transfers between devices, swapped(): lax.ppermute(shard, axis, [(i, partner(i, k, devices)) for i in range(dev...  2.08 us
    pallas_call x1, Pallas kernels, on_device(): call(join_kernel, (sds((whole, cols), F32),) + (sds((whole + B, cols), BF...  1.96 us
    ppermute x1, waiting for transfers between devices, on_device(): lax.ppermute(msg, 'patch', [(i, (i + 1) % panels) for i in range(panels)])  1.92 us
    ppermute x2, waiting for transfers between devices, shifted(): return lax.ppermute(shard, axis, pairs)  1.82 us
  transfers between devices with their start and end apart: 6, of which 4 were waited for; matrix products, arithmetic and copies ran while one was open for 0% of the time, Pallas kernels for 32%

profile of v12, /device:TPU:0, one launch (start us, length us, event | category | flops | bytes accessed | tf_op | source)
XLA Modules:
  0.0 30.6 jit_solution(16486289218209641193)
XLA Ops:
  0.6 5.0 %collective-permute-start.2 = (bf16[512,1,512]{2,0,1:T(8,128)(2,1)}, bf16[512,1,512]{2,0,1:T(8,128)(2,1)S(1)}, u32[]{:S(2)}, u32[]{:S(2)}) collective-permute-start(bf16[512,1,512]{2,0,1:T(8,128)(2,1)} %param.9), channel_id=1, source_target_pairs={{0,4},{4,8},{8,12},{1,5},{5,9},{9,13},{2,6},{6,10},{10,14},{3,7},{... | collective-permute-start | bytes 1572872 | tf_op jit(solution)/shard_map/ppermute | solution.py:22
  6.9 1.2 %pack.1 = (bf16[64,512]{1,0:T(8,128)(2,1)S(1)}, bf16[32,512]{1,0:T(8,128)(2,1)S(1)}, bf16[288,512]{1,0:T(8,128)(2,1)S(1)}, bf16[16,31]{1,0:T(8,128)(2,1)S(1)}, s...) custom-call(s32[1,1]{1,0:T(1,128)S(6)} %copy.10.off_hbm, s32[1,1]{1,0:T(1,128)S(6)} %copy.11.live_hbm, ...), custom_call_target="tpu_custom_call" | custom-call | flops 1048576 | bytes 2097152 | tf_op jit(solution)/shard_map/pack/pallas_call | solution.py:417
  8.1 1.6 %collective-permute-start = (bf16[32,512]{1,0:T(8,128)(2,1)S(1)}, bf16[32,512]{1,0:T(8,128)(2,1)S(1)}, u32[]{:S(2)}, u32[]{:S(2)}) collective-permute-start(bf16[32,512]{1,0:T(8,128)(2,1)S(1)} %get-tuple-element.26), channel_id=1, source_target_pairs={{0,4},{4,8},{8,12},{12,0},{1,5},{5,9},{9,13},{13,1},{2,6},{6,10},{... | collective-permute-start | bytes 98312 | tf_op jit(solution)/shard_map/ppermute | solution.py:429
  9.7 1.3 %collective-permute-start.1 = (bf16[288,512]{1,0:T(8,128)(2,1)S(1)}, bf16[288,512]{1,0:T(8,128)(2,1)S(1)}, u32[]{:S(2)}, u32[]{:S(2)}) collective-permute-start(bf16[288,512]{1,0:T(8,128)(2,1)S(1)} %get-tuple-element.27), channel_id=1, source_target_pairs={{4,0},{8,4},{12,8},{5,1},{9,5},{13,9},{6,2},{10,6},{14,10},{7,3},{... | collective-permute-start | bytes 884744 | tf_op jit(solution)/shard_map/ppermute | solution.py:22
  11.0 4.7 %first.1 = (bf16[2304,256]{1,0:T(8,128)(2,1)S(1)}, bf16[512,512]{1,0:T(8,128)(2,1)S(1)}, bf16[128,256]{1,0:T(8,128)(2,1)S(1)}, bf16[512,512]{1,0:T(8,128)(2,1)S(...) custom-call(bf16[64,512]{1,0:T(8,128)(2,1)S(1)} %get-tuple-element.25.note_ref, ...), custom_call_target="tpu_custom_call" | custom-call | flops 1207959552 | bytes 2097152 | tf_op jit(solution)/shard_map/first/pallas_call | solution.py:439
  15.7 1.9 %collective-permute-done.msg_ref = bf16[32,512]{1,0:T(8,128)(2,1)S(1)} collective-permute-done((bf16[32,512]{1,0:T(8,128)(2,1)S(1)}, bf16[32,512]{1,0:T(8,128)(2,1)S(1)}, u32[]{:S(2)}, u32[]{:S(2)}) %collective-permute-start) | collective-permute-done | bytes 32800 | tf_op jit(solution)/shard_map/ppermute | solution.py:429
  17.6 0.0 collective-permute-done.2
  17.6 0.6 %before.1 = (f32[4,64,128]{2,1,0:T(8,128)S(1)}, bf16[480,512]{1,0:T(8,128)(2,1)S(1)}) custom-call(bf16[32,512]{1,0:T(8,128)(2,1)S(1)} %collective-permute-done.msg_ref, bf16[512,512]{1,0:T(8,128)(2,1)S(1)} %bitcast.5, f32[4,512,128]{2,1,0:T(8,128)S(1)} %get-tuple-element.36.m_ref.m1_ref, bf16[512,512]{1,0:T(8,128)(2,1)S(1)} %get-tuple-element.33.pcol_ref), custom_call_target="tpu_custom_call" | custom-call | flops 17179869184 | bytes 2097152 | tf_op jit(solution)/shard_map/before/pallas_call | solution.py:449
  18.3 1.8 %collective-permute-done.1.next_ref.rest_0_ = bf16[288,512]{1,0:T(8,128)(2,1)S(1)} collective-permute-done((bf16[288,512]{1,0:T(8,128)(2,1)S(1)}, bf16[288,512]{1,0:T(8,128)(2,1)S(1)}, u32[]{:S(2)}, u32[]{:S(2)}) %collective-permute-start.1) | collective-permute-done | bytes 294944 | tf_op jit(solution)/shard_map/ppermute | solution.py:22
  20.1 2.0 %join.1 = (f32[256,512]{1,0:T(8,128)S(1)}, bf16[272,512]{1,0:T(8,128)(2,1)S(1)}, bf16[16,128]{1,0:T(8,128)(2,1)S(1)}, f32[4,64,128]{2,1,0:T(8,128)S(1)}) custom-call(bf16[64,512]{1,0:T(8,128)(2,1)S(1)} %get-tuple-element.25.note_ref, bf16[32,512]{1,0:T(8,128)(2,1)S(1)} %collective-permute-done.msg_ref, ...), custom_call_target="tpu_custom_call" | custom-call | flops 536870912 | bytes 2097152 | tf_op jit(solution)/shard_map/join/pallas_call | solution.py:451
  22.0 0.1 collective-permute-start.3
  22.1 0.5 %collective-permute-start.4 = (bf16[288,512]{1,0:T(8,128)(2,1)S(1)}, bf16[288,512]{1,0:T(8,128)(2,1)S(1)}, u32[]{:S(2)}, u32[]{:S(2)}) collective-permute-start(bf16[288,512]{1,0:T(8,128)(2,1)S(1)} %collective-permute-done.1.next_ref.rest_0_), channel_id=1, source_target_pairs={{0,1},{1,0},{2,3},{3,2},{4,5},{5,4},{6,7},{7,6},{8,9},{9,8},{10,11... | collective-permute-start | bytes 884744 | tf_op jit(solution)/shard_map/ppermute | solution.py:31
  22.6 1.0 %collective-permute-done.3.refs_2_ = bf16[272,512]{1,0:T(8,128)(2,1)S(1)} collective-permute-done((bf16[272,512]{1,0:T(8,128)(2,1)S(1)}, bf16[272,512]{1,0:T(8,128)(2,1)S(1)}, u32[]{:S(2)}, u32[]{:S(2)}) %collective-permute-start.3) | collective-permute-done | bytes 278560 | tf_op jit(solution)/shard_map/ppermute | solution.py:31
  23.7 1.6 %collective-permute-start.5 = (bf16[144,512]{1,0:T(8,128)(2,1)S(1)}, bf16[144,512]{1,0:T(8,128)(2,1)S(1)}, u32[]{:S(2)}, u32[]{:S(2)}) collective-permute-start(bf16[144,512]{1,0:T(8,128)(2,1)S(1)} %get-tuple-element.47), channel_id=1, source_target_pairs={{0,2},{2,0},{1,3},{3,1},{4,6},{6,4},{5,7},{7,5},{8,10},{10,8},{9,1... | collective-permute-start | bytes 442376 | tf_op jit(solution)/shard_map/ppermute | solution.py:31
  25.3 0.0 collective-permute-done.4.rest_1_
  25.3 3.4 %tile.1 = bf16[512,512]{1,0:T(8,128)(2,1)} custom-call(bf16[16,128]{1,0:T(8,128)(2,1)S(1)} %get-tuple-element.43.mark_ref, bf16[512,512]{1,0:T(8,128)(2,1)S(1)} %get-tuple-element.44.sci_ref, bf16[64,512]{1,0:T(8,128)(2,1)S(1)} %get-tuple-element.25.note_ref, f32[4,512,128]{2,1,0:T(8,128)S(1)} %get-tuple-element.36.m_ref.m1_ref, ...), custom_call_target="tpu_custom_call" | custom-call | flops 1207959552 | bytes 2097152 | tf_op jit(solution)/shard_map/tile/pallas_call | solution.py:473
  28.6 1.0 %collective-permute-done.5.refs_1_ = bf16[144,512]{1,0:T(8,128)(2,1)S(1)} collective-permute-done((bf16[144,512]{1,0:T(8,128)(2,1)S(1)}, bf16[144,512]{1,0:T(8,128)(2,1)S(1)}, u32[]{:S(2)}, u32[]{:S(2)}) %collective-permute-start.5) | collective-permute-done | bytes 147488 | tf_op jit(solution)/shard_map/ppermute | solution.py:31
  29.7 1.0 %coadd.1 = f32[128,512]{1,0:T(8,128)} custom-call(bf16[16,128]{1,0:T(8,128)(2,1)S(1)} %get-tuple-element.43.mark_ref, f32[128,512]{1,0:T(8,128)S(1)} %get-tuple-element.46.refs_0_, bf16[144,512]{1,0:T(8,128)(2,1)S(1)} %collective-permute-done.5.refs_1_), custom_call_target="tpu_custom_call" | custom-call | flops 1048576 | bytes 2097152 | tf_op jit(solution)/shard_map/coadd/pallas_call | solution.py:477
  (1 shorter events, 0.0 us)
Async XLA Ops:
  0.6 17.0 %collective-permute-start.2 = (bf16[512,1,512]{2,0,1:T(8,128)(2,1)}, bf16[512,1,512]{2,0,1:T(8,128)(2,1)S(1)}, u32[]{:S(2)}, u32[]{:S(2)}) collective-permute-start(bf16[512,1,512]{2,0,1:T(8,128)(2,1)} %param.9), channel_id=1, source_target_pairs={{0,4},{4,8},{8,12},{1,5},{5,9},{9,13},{2,6},{6,10},{10,14},{3,7},{... | collective-permute-start | bytes 1572872 | tf_op jit(solution)/shard_map/ppermute | solution.py:22
  8.1 9.6 %collective-permute-start = (bf16[32,512]{1,0:T(8,128)(2,1)S(1)}, bf16[32,512]{1,0:T(8,128)(2,1)S(1)}, u32[]{:S(2)}, u32[]{:S(2)}) collective-permute-start(bf16[32,512]{1,0:T(8,128)(2,1)S(1)} %get-tuple-element.26), channel_id=1, source_target_pairs={{0,4},{4,8},{8,12},{12,0},{1,5},{5,9},{9,13},{13,1},{2,6},{6,10},{... | collective-permute-start | bytes 98312 | tf_op jit(solution)/shard_map/ppermute | solution.py:429
  9.7 10.4 %collective-permute-start.1 = (bf16[288,512]{1,0:T(8,128)(2,1)S(1)}, bf16[288,512]{1,0:T(8,128)(2,1)S(1)}, u32[]{:S(2)}, u32[]{:S(2)}) collective-permute-start(bf16[288,512]{1,0:T(8,128)(2,1)S(1)} %get-tuple-element.27), channel_id=1, source_target_pairs={{4,0},{8,4},{12,8},{5,1},{9,5},{13,9},{6,2},{10,6},{14,10},{7,3},{... | collective-permute-start | bytes 884744 | tf_op jit(solution)/shard_map/ppermute | solution.py:22
  22.0 1.6 %collective-permute-start.3 = (bf16[272,512]{1,0:T(8,128)(2,1)S(1)}, bf16[272,512]{1,0:T(8,128)(2,1)S(1)}, u32[]{:S(2)}, u32[]{:S(2)}) collective-permute-start(bf16[272,512]{1,0:T(8,128)(2,1)S(1)} %get-tuple-element.42), channel_id=1, source_target_pairs={{0,1},{1,0},{2,3},{3,2},{4,5},{5,4},{6,7},{7,6},{8,9},{9,8},{10,11... | collective-permute-start | bytes 835592 | tf_op jit(solution)/shard_map/ppermute | solution.py:31
  22.1 3.2 %collective-permute-start.4 = (bf16[288,512]{1,0:T(8,128)(2,1)S(1)}, bf16[288,512]{1,0:T(8,128)(2,1)S(1)}, u32[]{:S(2)}, u32[]{:S(2)}) collective-permute-start(bf16[288,512]{1,0:T(8,128)(2,1)S(1)} %collective-permute-done.1.next_ref.rest_0_), channel_id=1, source_target_pairs={{0,1},{1,0},{2,3},{3,2},{4,5},{5,4},{6,7},{7,6},{8,9},{9,8},{10,11... | collective-permute-start | bytes 884744 | tf_op jit(solution)/shard_map/ppermute | solution.py:31
  23.7 6.0 %collective-permute-start.5 = (bf16[144,512]{1,0:T(8,128)(2,1)S(1)}, bf16[144,512]{1,0:T(8,128)(2,1)S(1)}, u32[]{:S(2)}, u32[]{:S(2)}) collective-permute-start(bf16[144,512]{1,0:T(8,128)(2,1)S(1)} %get-tuple-element.47), channel_id=1, source_target_pairs={{0,2},{2,0},{1,3},{3,1},{4,6},{6,4},{5,7},{7,5},{8,10},{10,8},{9,1... | collective-permute-start | bytes 442376 | tf_op jit(solution)/shard_map/ppermute | solution.py:31

commit v13 on v12

--- a/solution.py
+++ b/solution.py
@@ -118,11 +118,11 @@
 
 def pack_kernel(
     off_hbm, live_hbm, t_hbm, bank_hbm, index_hbm, coeff_hbm, psf_hbm,
-    note_ref, msg_ref, half_ref, bank_ref, index_ref, coeff_ref, psf_ref, off_ref, live_ref, sems,
+    note_ref, msg_ref, head_ref, half_ref, bank_ref, index_ref, coeff_ref, psf_ref, off_ref, live_ref, sems,
 ):
     rows, cols = t_hbm.shape
     edge = 2 * B
-    piece = half_ref.shape[0] - edge
+    piece = half_ref.shape[0]
     begin = pl.multiple_of(lax.axis_index("band") * piece, B)
     copies = [
         pltpu.make_async_copy(a, b, sems.at[n])
@@ -130,8 +130,8 @@
             (off_hbm, off_ref), (live_hbm, live_ref),
             (t_hbm.at[pl.ds(rows - edge, edge)], note_ref.at[pl.ds(0, edge)]),
             (t_hbm.at[pl.ds(0, edge)], note_ref.at[pl.ds(edge, edge)]),
-            (t_hbm.at[pl.ds(0, edge)], half_ref.at[pl.ds(0, edge)]),
-            (t_hbm.at[pl.ds(begin, piece)], half_ref.at[pl.ds(edge, piece)]),
+            (t_hbm.at[pl.ds(0, edge)], head_ref),
+            (t_hbm.at[pl.ds(begin, piece)], half_ref),
             (bank_hbm, bank_ref), (index_hbm, index_ref), (coeff_hbm, coeff_ref), (psf_hbm, psf_ref),
         ))
     ]
@@ -258,7 +258,7 @@
 
 
 def join_kernel(
-    note_ref, msg_ref, next_ref, w_ref, pcol_ref, prow_ref, edge_a, edge_b, filt_a, filt_b,
+    note_ref, msg_ref, head_ref, w_ref, pcol_ref, prow_ref, edge_a, edge_b, filt_a, filt_b,
     *rest,
 ):
     *outs, mark_ref, m_ref, src, xs, strip, diff, filt = rest
@@ -268,7 +268,8 @@
     to_blocks(src, 0, jnp.where(valid, msg_ref[...].astype(F32), 0.0))
     to_blocks(src, 2, note_ref[edge:, :])
     to_blocks(src, 4, note_ref[0:edge, :])
-    to_blocks(src, 6, next_ref[0:edge, :])
+    last = lax.axis_index("patch") == lax.axis_size("patch") - 1
+    to_blocks(src, 6, jnp.where(last, 0.0, head_ref[...].astype(F32)))
     conv_blocks(src, 8, w_ref, xs, strip)
     for n, a in enumerate((1, 2, 5, 6)):
         m_ref[:, B * n : B * (n + 1), :] = strip[:, PITCH * a : PITCH * a + B, :]
@@ -343,9 +344,9 @@
     blocks = rows // B // bands
     band = lax.axis_index("band")
     for j in range(bands):
-        piece = halves[0][2 * B :, :].astype(F32)
+        piece = halves[0][...].astype(F32)
         for k in range(1, bands):
-            piece = jnp.where(partner(band, k, bands) == j, halves[k][2 * B :, :].astype(F32), piece)
+            piece = jnp.where(partner(band, k, bands) == j, halves[k][...].astype(F32), piece)
         to_blocks(src, j * blocks, piece)
     conv_blocks(src, rows // B, w_ref, xs, res)
     for a in range(1, rows // B):
@@ -414,10 +415,11 @@
     before = shifted(science, "patch", 1)[:, 0, :]
     bands, visits = lax.axis_size("band"), lax.axis_size("visit")
     psf = psf_profile[None]
-    note, msg, half, *small = call(
+    note, msg, head, half, *small = call(
         pack_kernel,
         (
-            sds((2 * edge, cols), BF16), sds((edge, cols), BF16), sds((edge + rows // bands, cols), BF16),
+            sds((2 * edge, cols), BF16), sds((edge, cols), BF16), sds((edge, cols), BF16),
+            sds((rows // bands, cols), BF16),
             *(sds(x.shape, x.dtype) for x in (bank, index, coeff, psf)),
         ),
         [HBM] * 7,
@@ -427,6 +429,7 @@
     half = shifted(half, "patch", -1)
     panels = lax.axis_size("patch")
     msg = lax.ppermute(msg, "patch", [(i, (i + 1) % panels) for i in range(panels)])
+    head = lax.ppermute(head, "patch", [((i + 1) % panels, i) for i in range(panels)])
     count = rows // B
     conv_scratch = [
         pltpu.VMEM((chunks, count * PITCH, LANES), F32),
@@ -461,7 +464,7 @@
             pltpu.VMEM((2, rows - share + depth, cols), BF16),
         ],
         1 << 29, "join",
-    )(note, msg, half, w, pcol, prow, edge_a, edge_b, filt_a, filt_b)
+    )(note, msg, head, w, pcol, prow, edge_a, edge_b, filt_a, filt_b)
     got = [swapped(part, "band", k + 1) for k, part in enumerate(sent)]
     halves = [half] + [swapped(half, "band", k) for k in range(1, bands)]
     own, *sent, mark = call(

time: 30.8 us -> 29.4 us (0.955)
  waiting for transfers between devices: 5.82 us -> 2.38 us
  starting transfers between devices: 9.97 us -> 11.9 us
    ppermute x0 -> x1, starting transfers between devices: none -> 2.28 us  [on_device(): lax.ppermute(head, 'patch', [((i + 1) % panels, i) for i in range(panels)])]
    ppermute x1, waiting for transfers between devices: 1.92 us -> 0.01 us  [on_device(): lax.ppermute(msg, 'patch', [(i, (i + 1) % panels) for i in range(panels)])]
    ppermute x2, waiting for transfers between devices: 1.82 us -> 0.31 us  [shifted(): return lax.ppermute(shard, axis, pairs)]
  transfers between devices with their start and end apart: 6 -> 7, of which waited for: 4 -> 3; matrix products, arithmetic and copies ran while one was open for 0% -> 0% of each run, Pallas kernels for 32% -> 41%
where the time goes in v13:
time: 29.4 us; the launch traced here: 29.2 us
  Pallas kernels  12.9 us (44%)
  starting transfers between devices  11.9 us (40%)
  waiting for transfers between devices  2.38 us (8%)
  between operations  2.01 us (7%)
    ppermute x2, starting transfers between devices, shifted(): return lax.ppermute(shard, axis, pairs)  6.24 us
    pallas_call x1, Pallas kernels, on_device(): call(first_kernel, (sds((deep, CH), BF16), sds((cols, cols), BF16), sds((...  4.75 us
    pallas_call x1, Pallas kernels, on_device(): call(tile_kernel, sds((rows, cols), BF16), [VM] * (6 + bands), conv_scrat...  3.37 us
    ppermute x1, starting transfers between devices, on_device(): lax.ppermute(head, 'patch', [((i + 1) % panels, i) for i in range(panels)])  2.28 us
    ppermute x3, waiting for transfers between devices, swapped(): lax.ppermute(shard, axis, [(i, partner(i, k, devices)) for i in range(dev...  2.06 us
    pallas_call x1, Pallas kernels, on_device(): call(join_kernel, (sds((whole, cols), F32),) + (sds((whole + B, cols), BF...  1.97 us
    ppermute x3, starting transfers between devices, swapped(): lax.ppermute(shard, axis, [(i, partner(i, k, devices)) for i in range(dev...  1.83 us
    ppermute x1, starting transfers between devices, on_device(): lax.ppermute(msg, 'patch', [(i, (i + 1) % panels) for i in range(panels)])  1.6 us
  transfers between devices with their start and end apart: 7, of which 3 were waited for; matrix products, arithmetic and copies ran while one was open for 0% of the time, Pallas kernels for 41%

profile of v13, /device:TPU:0, one launch (start us, length us, event | category | flops | bytes accessed | tf_op | source)
XLA Modules:
  0.0 29.2 jit_solution(4567946014455521885)
XLA Ops:
  0.6 5.0 %collective-permute-start.2 = (bf16[512,1,512]{2,0,1:T(8,128)(2,1)}, bf16[512,1,512]{2,0,1:T(8,128)(2,1)S(1)}, u32[]{:S(2)}, u32[]{:S(2)}) collective-permute-start(bf16[512,1,512]{2,0,1:T(8,128)(2,1)} %param.9), channel_id=1, source_target_pairs={{0,4},{4,8},{8,12},{1,5},{5,9},{9,13},{2,6},{6,10},{10,14},{3,7},{... | collective-permute-start | bytes 1572872 | tf_op jit(solution)/shard_map/ppermute | solution.py:22
  6.9 1.2 %pack.1 = (bf16[64,512]{1,0:T(8,128)(2,1)S(1)}, bf16[32,512]{1,0:T(8,128)(2,1)S(1)}, bf16[32,512]{1,0:T(8,128)(2,1)S(1)}, bf16[256,512]{1,0:T(8,128)(2,1)S(1)}, ...) custom-call(s32[1,1]{1,0:T(1,128)S(6)} %copy.10.off_hbm, ...), custom_call_target="tpu_custom_call" | custom-call | flops 1048576 | bytes 2097152 | tf_op jit(solution)/shard_map/pack/pallas_call | solution.py:418
  8.1 1.6 %collective-permute-start = (bf16[32,512]{1,0:T(8,128)(2,1)S(1)}, bf16[32,512]{1,0:T(8,128)(2,1)S(1)}, u32[]{:S(2)}, u32[]{:S(2)}) collective-permute-start(bf16[32,512]{1,0:T(8,128)(2,1)S(1)} %get-tuple-element.27), channel_id=1, source_target_pairs={{0,4},{4,8},{8,12},{12,0},{1,5},{5,9},{9,13},{13,1},{2,6},{6,10},{... | collective-permute-start | bytes 98312 | tf_op jit(solution)/shard_map/ppermute | solution.py:431
  9.7 2.3 %collective-permute-start.1 = (bf16[32,512]{1,0:T(8,128)(2,1)S(1)}, bf16[32,512]{1,0:T(8,128)(2,1)S(1)}, u32[]{:S(2)}, u32[]{:S(2)}) collective-permute-start(bf16[32,512]{1,0:T(8,128)(2,1)S(1)} %get-tuple-element.28), channel_id=1, source_target_pairs={{4,0},{8,4},{12,8},{0,12},{5,1},{9,5},{13,9},{1,13},{6,2},{10,6},{... | collective-permute-start | bytes 98312 | tf_op jit(solution)/shard_map/ppermute | solution.py:432
  12.0 1.3 %collective-permute-start.4 = (bf16[256,512]{1,0:T(8,128)(2,1)S(1)}, bf16[256,512]{1,0:T(8,128)(2,1)S(1)}, u32[]{:S(2)}, u32[]{:S(2)}) collective-permute-start(bf16[256,512]{1,0:T(8,128)(2,1)S(1)} %get-tuple-element.47), channel_id=1, source_target_pairs={{4,0},{8,4},{12,8},{5,1},{9,5},{13,9},{6,2},{10,6},{14,10},{7,3},{... | collective-permute-start | bytes 786440 | tf_op jit(solution)/shard_map/ppermute | solution.py:22
  13.2 4.8 %first.1 = (bf16[2304,256]{1,0:T(8,128)(2,1)S(1)}, bf16[512,512]{1,0:T(8,128)(2,1)S(1)}, bf16[128,256]{1,0:T(8,128)(2,1)S(1)}, bf16[512,512]{1,0:T(8,128)(2,1)S(...) custom-call(bf16[64,512]{1,0:T(8,128)(2,1)S(1)} %get-tuple-element.26.note_ref, ...), custom_call_target="tpu_custom_call" | custom-call | flops 1207959552 | bytes 2097152 | tf_op jit(solution)/shard_map/first/pallas_call | solution.py:442
  18.0 0.0 collective-permute-done.msg_ref
  18.0 0.0 collective-permute-done.2
  18.0 0.6 %before.1 = (f32[4,64,128]{2,1,0:T(8,128)S(1)}, bf16[480,512]{1,0:T(8,128)(2,1)S(1)}) custom-call(bf16[32,512]{1,0:T(8,128)(2,1)S(1)} %collective-permute-done.msg_ref, bf16[512,512]{1,0:T(8,128)(2,1)S(1)} %bitcast.5, f32[4,512,128]{2,1,0:T(8,128)S(1)} %get-tuple-element.37.m_ref.m1_ref, bf16[512,512]{1,0:T(8,128)(2,1)S(1)} %get-tuple-element.34.pcol_ref), custom_call_target="tpu_custom_call" | custom-call | flops 17179869184 | bytes 2097152 | tf_op jit(solution)/shard_map/before/pallas_call | solution.py:452
  18.6 0.0 collective-permute-done.1.head_ref
  18.6 2.0 %join.1 = (f32[256,512]{1,0:T(8,128)S(1)}, bf16[272,512]{1,0:T(8,128)(2,1)S(1)}, bf16[16,128]{1,0:T(8,128)(2,1)S(1)}, f32[4,64,128]{2,1,0:T(8,128)S(1)}) custom-call(bf16[64,512]{1,0:T(8,128)(2,1)S(1)} %get-tuple-element.26.note_ref, bf16[32,512]{1,0:T(8,128)(2,1)S(1)} %collective-permute-done.msg_ref, bf16[32,512]{1,0:T(8,128)(2,1)S(1)} %collective-permute-done.1.head_ref, ...), custom_call_target="tpu_custom_call" | custom-call | flops 536870912 | bytes 2097152 | tf_op jit(solution)/shard_map/join/pallas_call | solution.py:454
  20.6 0.1 collective-permute-start.3
  20.7 0.3 %collective-permute-done.4.rest_0_ = bf16[256,512]{1,0:T(8,128)(2,1)S(1)} collective-permute-done((bf16[256,512]{1,0:T(8,128)(2,1)S(1)}, bf16[256,512]{1,0:T(8,128)(2,1)S(1)}, u32[]{:S(2)}, u32[]{:S(2)}) %collective-permute-start.4) | collective-permute-done | bytes 262176 | tf_op jit(solution)/shard_map/ppermute | solution.py:22
  21.0 0.2 collective-permute-start.5
  21.2 1.0 %collective-permute-done.3.refs_2_ = bf16[272,512]{1,0:T(8,128)(2,1)S(1)} collective-permute-done((bf16[272,512]{1,0:T(8,128)(2,1)S(1)}, bf16[272,512]{1,0:T(8,128)(2,1)S(1)}, u32[]{:S(2)}, u32[]{:S(2)}) %collective-permute-start.3) | collective-permute-done | bytes 278560 | tf_op jit(solution)/shard_map/ppermute | solution.py:31
  22.3 1.6 %collective-permute-start.6 = (bf16[144,512]{1,0:T(8,128)(2,1)S(1)}, bf16[144,512]{1,0:T(8,128)(2,1)S(1)}, u32[]{:S(2)}, u32[]{:S(2)}) collective-permute-start(bf16[144,512]{1,0:T(8,128)(2,1)S(1)} %get-tuple-element.49), channel_id=1, source_target_pairs={{0,2},{2,0},{1,3},{3,1},{4,6},{6,4},{5,7},{7,5},{8,10},{10,8},{9,1... | collective-permute-start | bytes 442376 | tf_op jit(solution)/shard_map/ppermute | solution.py:31
  23.9 0.0 collective-permute-done.5.rest_1_
  23.9 3.4 %tile.1 = bf16[512,512]{1,0:T(8,128)(2,1)} custom-call(bf16[16,128]{1,0:T(8,128)(2,1)S(1)} %get-tuple-element.44.mark_ref, bf16[512,512]{1,0:T(8,128)(2,1)S(1)} %get-tuple-element.45.sci_ref, bf16[64,512]{1,0:T(8,128)(2,1)S(1)} %get-tuple-element.26.note_ref, f32[4,512,128]{2,1,0:T(8,128)S(1)} %get-tuple-element.37.m_ref.m1_ref, ...), custom_call_target="tpu_custom_call" | custom-call | flops 1207959552 | bytes 2097152 | tf_op jit(solution)/shard_map/tile/pallas_call | solution.py:476
  27.2 1.0 %collective-permute-done.6.refs_1_ = bf16[144,512]{1,0:T(8,128)(2,1)S(1)} collective-permute-done((bf16[144,512]{1,0:T(8,128)(2,1)S(1)}, bf16[144,512]{1,0:T(8,128)(2,1)S(1)}, u32[]{:S(2)}, u32[]{:S(2)}) %collective-permute-start.6) | collective-permute-done | bytes 147488 | tf_op jit(solution)/shard_map/ppermute | solution.py:31
  28.3 1.0 %coadd.1 = f32[128,512]{1,0:T(8,128)} custom-call(bf16[16,128]{1,0:T(8,128)(2,1)S(1)} %get-tuple-element.44.mark_ref, f32[128,512]{1,0:T(8,128)S(1)} %get-tuple-element.48.refs_0_, bf16[144,512]{1,0:T(8,128)(2,1)S(1)} %collective-permute-done.6.refs_1_), custom_call_target="tpu_custom_call" | custom-call | flops 1048576 | bytes 2097152 | tf_op jit(solution)/shard_map/coadd/pallas_call | solution.py:480
  (1 shorter events, 0.0 us)
Async XLA Ops:
  0.6 17.4 %collective-permute-start.2 = (bf16[512,1,512]{2,0,1:T(8,128)(2,1)}, bf16[512,1,512]{2,0,1:T(8,128)(2,1)S(1)}, u32[]{:S(2)}, u32[]{:S(2)}) collective-permute-start(bf16[512,1,512]{2,0,1:T(8,128)(2,1)} %param.9), channel_id=1, source_target_pairs={{0,4},{4,8},{8,12},{1,5},{5,9},{9,13},{2,6},{6,10},{10,14},{3,7},{... | collective-permute-start | bytes 1572872 | tf_op jit(solution)/shard_map/ppermute | solution.py:22
  8.1 9.9 %collective-permute-start = (bf16[32,512]{1,0:T(8,128)(2,1)S(1)}, bf16[32,512]{1,0:T(8,128)(2,1)S(1)}, u32[]{:S(2)}, u32[]{:S(2)}) collective-permute-start(bf16[32,512]{1,0:T(8,128)(2,1)S(1)} %get-tuple-element.27), channel_id=1, source_target_pairs={{0,4},{4,8},{8,12},{12,0},{1,5},{5,9},{9,13},{13,1},{2,6},{6,10},{... | collective-permute-start | bytes 98312 | tf_op jit(solution)/shard_map/ppermute | solution.py:431
  9.7 9.0 %collective-permute-start.1 = (bf16[32,512]{1,0:T(8,128)(2,1)S(1)}, bf16[32,512]{1,0:T(8,128)(2,1)S(1)}, u32[]{:S(2)}, u32[]{:S(2)}) collective-permute-start(bf16[32,512]{1,0:T(8,128)(2,1)S(1)} %get-tuple-element.28), channel_id=1, source_target_pairs={{4,0},{8,4},{12,8},{0,12},{5,1},{9,5},{13,9},{1,13},{6,2},{10,6},{... | collective-permute-start | bytes 98312 | tf_op jit(solution)/shard_map/ppermute | solution.py:432
  12.0 9.1 %collective-permute-start.4 = (bf16[256,512]{1,0:T(8,128)(2,1)S(1)}, bf16[256,512]{1,0:T(8,128)(2,1)S(1)}, u32[]{:S(2)}, u32[]{:S(2)}) collective-permute-start(bf16[256,512]{1,0:T(8,128)(2,1)S(1)} %get-tuple-element.47), channel_id=1, source_target_pairs={{4,0},{8,4},{12,8},{5,1},{9,5},{13,9},{6,2},{10,6},{14,10},{7,3},{... | collective-permute-start | bytes 786440 | tf_op jit(solution)/shard_map/ppermute | solution.py:22
  20.6 1.6 %collective-permute-start.3 = (bf16[272,512]{1,0:T(8,128)(2,1)S(1)}, bf16[272,512]{1,0:T(8,128)(2,1)S(1)}, u32[]{:S(2)}, u32[]{:S(2)}) collective-permute-start(bf16[272,512]{1,0:T(8,128)(2,1)S(1)} %get-tuple-element.43), channel_id=1, source_target_pairs={{0,1},{1,0},{2,3},{3,2},{4,5},{5,4},{6,7},{7,6},{8,9},{9,8},{10,11... | collective-permute-start | bytes 835592 | tf_op jit(solution)/shard_map/ppermute | solution.py:31
  21.0 2.9 %collective-permute-start.5 = (bf16[256,512]{1,0:T(8,128)(2,1)S(1)}, bf16[256,512]{1,0:T(8,128)(2,1)S(1)}, u32[]{:S(2)}, u32[]{:S(2)}) collective-permute-start(bf16[256,512]{1,0:T(8,128)(2,1)S(1)} %collective-permute-done.4.rest_0_), channel_id=1, source_target_pairs={{0,1},{1,0},{2,3},{3,2},{4,5},{5,4},{6,7},{7,6},{8,9},{9,8},{10,11... | collective-permute-start | bytes 786440 | tf_op jit(solution)/shard_map/ppermute | solution.py:31
  22.3 6.0 %collective-permute-start.6 = (bf16[144,512]{1,0:T(8,128)(2,1)S(1)}, bf16[144,512]{1,0:T(8,128)(2,1)S(1)}, u32[]{:S(2)}, u32[]{:S(2)}) collective-permute-start(bf16[144,512]{1,0:T(8,128)(2,1)S(1)} %get-tuple-element.49), channel_id=1, source_target_pairs={{0,2},{2,0},{1,3},{3,1},{4,6},{6,4},{5,7},{7,5},{8,10},{10,8},{9,1... | collective-permute-start | bytes 442376 | tf_op jit(solution)/shard_map/ppermute | solution.py:31

commit v14 on v13

--- a/solution.py
+++ b/solution.py
@@ -250,26 +250,21 @@
     return jnp.where(valid, off, 0), jnp.where(valid, live, 0.0), valid
 
 
-def before_kernel(msg_ref, sci_ref, m_ref, pcol_ref, edge_ref, filt_ref, sci, diff):
-    rows = sci_ref.shape[0]
-    off, _, _ = read_before(msg_ref)
-    to_chunks(sci, 0, sci_ref[...])
-    filter_inner(sci, rows - B - off, off - rows, off, m_ref, pcol_ref, edge_ref, filt_ref, diff)
-
-
 def join_kernel(
-    note_ref, msg_ref, head_ref, w_ref, pcol_ref, prow_ref, edge_a, edge_b, filt_a, filt_b,
+    note_ref, msg_ref, head_ref, sci_ref, m1_ref, w_ref, pcol_ref, prow_ref, edge_a, filt_a,
     *rest,
 ):
-    *outs, mark_ref, m_ref, src, xs, strip, diff, filt = rest
+    *outs, mark_ref, m_ref, src, xs, strip, diff, filt, sci, inner, edge_b, filt_b = rest
     edge = 2 * B
     rows, cols = filt_a.shape[0] + edge, filt_a.shape[1]
     off_b, live_b, valid = read_before(msg_ref)
+    to_chunks(sci, 0, sci_ref[...])
     to_blocks(src, 0, jnp.where(valid, msg_ref[...].astype(F32), 0.0))
     to_blocks(src, 2, note_ref[edge:, :])
     to_blocks(src, 4, note_ref[0:edge, :])
     last = lax.axis_index("patch") == lax.axis_size("patch") - 1
     to_blocks(src, 6, jnp.where(last, 0.0, head_ref[...].astype(F32)))
+    filter_inner(sci, rows - B - off_b, off_b - rows, off_b, m1_ref, pcol_ref, edge_b, filt_b, inner)
     conv_blocks(src, 8, w_ref, xs, strip)
     for n, a in enumerate((1, 2, 5, 6)):
         m_ref[:, B * n : B * (n + 1), :] = strip[:, PITCH * a : PITCH * a + B, :]
@@ -331,10 +326,7 @@
         total = keep_ref[span, :]
         for ref in got:
             total += ref[span, :].astype(F32)
-        out_ref[0:share, :] = total.astype(out_ref.dtype)
-        if k:
-            out_ref[share:, 0:LANES] = marks.astype(BF16)
-            out_ref[share:, LANES:] = jnp.zeros((B, cols - LANES), BF16)
+        out_ref[...] = total.astype(out_ref.dtype)
 
 
 def tile_kernel(mark_ref, sci_ref, note_ref, m1_ref, edge_ref, w_ref, *rest):
@@ -360,17 +352,17 @@
         out_ref[:, part] = (sci_ref[:, part].astype(F32) - big[c, pl.ds(off, rows), :]).astype(BF16)
 
 
-def coadd_kernel(mark_ref, *refs):
+def coadd_kernel(*refs):
     *parts, out_ref = refs
+    marks, parts = parts[: len(parts) // 2], parts[len(parts) // 2 :]
     share, cols = out_ref.shape
     bands = lax.axis_size("band")
     base = (lax.axis_index("visit") * bands + lax.axis_index("band")) * share
     row = (iota((share, LANES), 0) + base).astype(F32)
     cover = jnp.zeros((share, LANES), F32)
-    for n, part in enumerate(parts):
-        marks = (part[share : share + B, 0:LANES] if n else mark_ref[...]).astype(F32)
+    for ref in marks:
         for m in range(bands):
-            mark = marks[m : m + 1, :]
+            mark = ref[...].astype(F32)[m : m + 1, :]
             cover += jnp.where(row >= mark[:, 0:1] * B + mark[:, 1:2], mark[:, 2:3], 0.0)
             cover += jnp.where(row < mark[:, 3:4] * B + mark[:, 4:5], mark[:, 5:6], 0.0)
     scale = lax.rsqrt(jnp.maximum(cover, 1.0))
@@ -378,7 +370,7 @@
         span = slice(c * LANES, (c + 1) * LANES)
         value = parts[0][:, span]
         for part in parts[1:]:
-            value += part[0:share, span].astype(F32)
+            value += part[:, span].astype(F32)
         out_ref[:, span] = value * scale
 
 
@@ -449,7 +441,6 @@
         [pltpu.VMEM((rows, cols), BF16), pltpu.SemaphoreType.DMA((2,))] + conv_scratch + sky_scratch,
         conv_flops, "first",
     )(note, *held, *small)
-    edge_b, filt_b = call(before_kernel, sides, [VM] * 4, sky_scratch, 1 << 34, "before")(msg, before, m1, pcol)
     whole = visits * share
     keep, *sent, mark, m_edge = call(
         join_kernel,
@@ -462,24 +453,25 @@
             pltpu.VMEM((chunks, 8 * PITCH, LANES), F32),
             pltpu.VMEM((4 * edge, cols), BF16),
             pltpu.VMEM((2, rows - share + depth, cols), BF16),
-        ],
-        1 << 29, "join",
-    )(note, msg, head, w, pcol, prow, edge_a, edge_b, filt_a, filt_b)
+        ] + sky_scratch + [pltpu.VMEM((chunks, 2 * edge, LANES), F32), pltpu.VMEM((inner, cols), BF16)],
+        1 << 34, "join",
+    )(note, msg, head, before, m1, w, pcol, prow, edge_a, filt_a)
     got = [swapped(part, "band", k + 1) for k, part in enumerate(sent)]
     halves = [half] + [swapped(half, "band", k) for k in range(1, bands)]
     own, *sent, mark = call(
         pair_kernel,
-        (sds((share, cols), F32),) + (sds((share + B, cols), BF16),) * (visits - 1) + (sds((B, LANES), BF16),),
+        (sds((share, cols), F32),) + (sds((share, cols), BF16),) * (visits - 1) + (sds((B, LANES), BF16),),
         [VM] * (1 + bands), [], 1 << 20, "pair",
     )(mark, keep, *got)
     got = [swapped(part, "visit", k + 1) for k, part in enumerate(sent)]
+    marks = [mark] + [swapped(mark, "visit", k) for k in range(1, visits)]
     difference = call(
         tile_kernel, sds((rows, cols), BF16), [VM] * (6 + bands),
         conv_scratch + [pltpu.VMEM((chunks, 2 * rows, LANES), F32)], conv_flops, "tile",
     )(mark, tile, note, m1, m_edge, w, *halves)
     detection = call(
-        coadd_kernel, sds((share, cols), F32), [VM] * (1 + visits), [], 1 << 20, "coadd"
-    )(mark, own, *got)
+        coadd_kernel, sds((share, cols), F32), [VM] * (2 * visits), [], 1 << 20, "coadd"
+    )(*marks, own, *got)
     return (difference[:, None, :], detection)
 
 

time: 29.4 us -> 29.2 us (level)
  starting transfers between devices: 11.9 us -> 12.5 us
  waiting for transfers between devices: 2.38 us -> 1.85 us
  Pallas kernels: 12.9 us -> 12.6 us
    ppermute x3 -> x4, waiting for transfers between devices: 2.06 us -> 1.26 us  [swapped(): lax.ppermute(shard, axis, [(i, partner(i, k, devices)) for i in range(dev...]
    pallas_call x3 -> x2, Pallas kernels: 1.6 us -> 1 us  [the longest x1 0.96 us: on_device(): call(coadd_kernel, sds((share, cols), F32), [VM] * (2 * visits), [], 1 <<...]
    ppermute x3 -> x4, starting transfers between devices: 1.83 us -> 2.4 us  [swapped(): lax.ppermute(shard, axis, [(i, partner(i, k, devices)) for i in range(dev...]
    pallas_call x1, Pallas kernels: 1.97 us -> 2.31 us  [on_device(): call(join_kernel, (sds((whole, cols), F32),) + (sds((whole + B, cols), BF...]
    ppermute x1, waiting for transfers between devices: 0.01 us -> 0.32 us  [on_device(): lax.ppermute(head, 'patch', [((i + 1) % panels, i) for i in range(panels)])]
  transfers between devices with their start and end apart: 7 -> 8, of which waited for: 3 -> 4; matrix products, arithmetic and copies ran while one was open for 0% -> 0% of each run, Pallas kernels for 41% -> 40%
where the time goes in v14:
time: 29.2 us; the launch traced here: 29 us
  Pallas kernels  12.6 us (43%)
  starting transfers between devices  12.5 us (43%)
  between operations  1.99 us (7%)
  waiting for transfers between devices  1.85 us (6%)
    ppermute x2, starting transfers between devices, shifted(): return lax.ppermute(shard, axis, pairs)  6.24 us
    pallas_call x1, Pallas kernels, on_device(): call(first_kernel, (sds((deep, CH), BF16), sds((cols, cols), BF16), sds((...  4.76 us
    pallas_call x1, Pallas kernels, on_device(): call(tile_kernel, sds((rows, cols), BF16), [VM] * (6 + bands), conv_scrat...  3.39 us
    ppermute x4, starting transfers between devices, swapped(): lax.ppermute(shard, axis, [(i, partner(i, k, devices)) for i in range(dev...  2.4 us
    pallas_call x1, Pallas kernels, on_device(): call(join_kernel, (sds((whole, cols), F32),) + (sds((whole + B, cols), BF...  2.31 us
    ppermute x1, starting transfers between devices, on_device(): lax.ppermute(head, 'patch', [((i + 1) % panels, i) for i in range(panels)])  2.28 us
    ppermute x1, starting transfers between devices, on_device(): lax.ppermute(msg, 'patch', [(i, (i + 1) % panels) for i in range(panels)])  1.6 us
    ppermute x4, waiting for transfers between devices, swapped(): lax.ppermute(shard, axis, [(i, partner(i, k, devices)) for i in range(dev...  1.26 us
  transfers between devices with their start and end apart: 8, of which 4 were waited for; matrix products, arithmetic and copies ran while one was open for 0% of the time, Pallas kernels for 40%

profile of v14, /device:TPU:0, one launch (start us, length us, event | category | flops | bytes accessed | tf_op | source)
XLA Modules:
  0.0 29.0 jit_solution(12690529840839135854)
XLA Ops:
  0.6 5.0 %collective-permute-start.2 = (bf16[512,1,512]{2,0,1:T(8,128)(2,1)}, bf16[512,1,512]{2,0,1:T(8,128)(2,1)S(1)}, u32[]{:S(2)}, u32[]{:S(2)}) collective-permute-start(bf16[512,1,512]{2,0,1:T(8,128)(2,1)} %param.9), channel_id=1, source_target_pairs={{0,4},{4,8},{8,12},{1,5},{5,9},{9,13},{2,6},{6,10},{10,14},{3,7},{... | collective-permute-start | bytes 1572872 | tf_op jit(solution)/shard_map/ppermute | solution.py:22
  6.9 1.2 %pack.1 = (bf16[64,512]{1,0:T(8,128)(2,1)S(1)}, bf16[32,512]{1,0:T(8,128)(2,1)S(1)}, bf16[32,512]{1,0:T(8,128)(2,1)S(1)}, bf16[256,512]{1,0:T(8,128)(2,1)S(1)}, ...) custom-call(s32[1,1]{1,0:T(1,128)S(6)} %copy.10.off_hbm, ...), custom_call_target="tpu_custom_call" | custom-call | flops 1048576 | bytes 2097152 | tf_op jit(solution)/shard_map/pack/pallas_call | solution.py:410
  8.1 1.6 %collective-permute-start = (bf16[32,512]{1,0:T(8,128)(2,1)S(1)}, bf16[32,512]{1,0:T(8,128)(2,1)S(1)}, u32[]{:S(2)}, u32[]{:S(2)}) collective-permute-start(bf16[32,512]{1,0:T(8,128)(2,1)S(1)} %get-tuple-element.25), channel_id=1, source_target_pairs={{0,4},{4,8},{8,12},{12,0},{1,5},{5,9},{9,13},{13,1},{2,6},{6,10},{... | collective-permute-start | bytes 98312 | tf_op jit(solution)/shard_map/ppermute | solution.py:423
  9.7 2.3 %collective-permute-start.1 = (bf16[32,512]{1,0:T(8,128)(2,1)S(1)}, bf16[32,512]{1,0:T(8,128)(2,1)S(1)}, u32[]{:S(2)}, u32[]{:S(2)}) collective-permute-start(bf16[32,512]{1,0:T(8,128)(2,1)S(1)} %get-tuple-element.26), channel_id=1, source_target_pairs={{4,0},{8,4},{12,8},{0,12},{5,1},{9,5},{13,9},{1,13},{6,2},{10,6},{... | collective-permute-start | bytes 98312 | tf_op jit(solution)/shard_map/ppermute | solution.py:424
  12.0 1.3 %collective-permute-start.4 = (bf16[256,512]{1,0:T(8,128)(2,1)S(1)}, bf16[256,512]{1,0:T(8,128)(2,1)S(1)}, u32[]{:S(2)}, u32[]{:S(2)}) collective-permute-start(bf16[256,512]{1,0:T(8,128)(2,1)S(1)} %get-tuple-element.43), channel_id=1, source_target_pairs={{4,0},{8,4},{12,8},{5,1},{9,5},{13,9},{6,2},{10,6},{14,10},{7,3},{... | collective-permute-start | bytes 786440 | tf_op jit(solution)/shard_map/ppermute | solution.py:22
  13.2 4.8 %first.1 = (bf16[2304,256]{1,0:T(8,128)(2,1)S(1)}, bf16[512,512]{1,0:T(8,128)(2,1)S(1)}, bf16[128,256]{1,0:T(8,128)(2,1)S(1)}, bf16[512,512]{1,0:T(8,128)(2,1)S(...) custom-call(bf16[64,512]{1,0:T(8,128)(2,1)S(1)} %get-tuple-element.24.note_ref, ...), custom_call_target="tpu_custom_call" | custom-call | flops 1207959552 | bytes 2097152 | tf_op jit(solution)/shard_map/first/pallas_call | solution.py:434
  18.0 0.0 collective-permute-done.msg_ref
  18.0 0.3 %collective-permute-done.1.head_ref = bf16[32,512]{1,0:T(8,128)(2,1)S(1)} collective-permute-done((bf16[32,512]{1,0:T(8,128)(2,1)S(1)}, bf16[32,512]{1,0:T(8,128)(2,1)S(1)}, u32[]{:S(2)}, u32[]{:S(2)}) %collective-permute-start.1) | collective-permute-done | bytes 32800 | tf_op jit(solution)/shard_map/ppermute | solution.py:424
  18.3 0.0 collective-permute-done.2
  18.4 2.3 %join.1 = (f32[256,512]{1,0:T(8,128)S(1)}, bf16[272,512]{1,0:T(8,128)(2,1)S(1)}, bf16[16,128]{1,0:T(8,128)(2,1)S(1)}, f32[4,64,128]{2,1,0:T(8,128)S(1)}) custom-call(bf16[64,512]{1,0:T(8,128)(2,1)S(1)} %get-tuple-element.24.note_ref, bf16[32,512]{1,0:T(8,128)(2,1)S(1)} %collective-permute-done.msg_ref, bf16[32,512]{1,0:T(8,128)(2,1)S(1)} %collective-permute-done.1.head_ref, ...), custom_call_target="tpu_custom_call" | custom-call | flops 17179869184 | bytes 2097152 | tf_op jit(solution)/shard_map/join/pallas_call | solution.py:445
  20.7 0.1 collective-permute-start.3
  20.7 0.3 collective-permute-done.4.rest_0_
  21.0 0.2 collective-permute-start.5
  21.2 1.0 %collective-permute-done.3.refs_2_ = bf16[272,512]{1,0:T(8,128)(2,1)S(1)} collective-permute-done((bf16[272,512]{1,0:T(8,128)(2,1)S(1)}, bf16[272,512]{1,0:T(8,128)(2,1)S(1)}, u32[]{:S(2)}, u32[]{:S(2)}) %collective-permute-start.3) | collective-permute-done | bytes 278560 | tf_op jit(solution)/shard_map/ppermute | solution.py:31
  22.3 1.6 %collective-permute-start.7 = (bf16[128,512]{1,0:T(8,128)(2,1)S(1)}, bf16[128,512]{1,0:T(8,128)(2,1)S(1)}, u32[]{:S(2)}, u32[]{:S(2)}) collective-permute-start(bf16[128,512]{1,0:T(8,128)(2,1)S(1)} %get-tuple-element.45), channel_id=1, source_target_pairs={{0,2},{2,0},{1,3},{3,1},{4,6},{6,4},{5,7},{7,5},{8,10},{10,8},{9,1... | collective-permute-start | bytes 393224 | tf_op jit(solution)/shard_map/ppermute | solution.py:31
  23.9 0.5 %collective-permute-start.6 = (bf16[16,128]{1,0:T(8,128)(2,1)S(1)}, bf16[16,128]{1,0:T(8,128)(2,1)S(1)}, u32[]{:S(2)}, u32[]{:S(2)}) collective-permute-start(bf16[16,128]{1,0:T(8,128)(2,1)S(1)} %get-tuple-element.40.mark_ref.refs_0_), channel_id=1, source_target_pairs={{0,2},{2,0},{1,3},{3,1},{4,6},{6,4},{5,7},{7,5},{8,10},{10,8},{9,1... | collective-permute-start | bytes 12296 | tf_op jit(solution)/shard_map/ppermute | solution.py:31
  24.4 0.0 collective-permute-done.5.rest_1_
  24.4 3.4 %tile.1 = bf16[512,512]{1,0:T(8,128)(2,1)} custom-call(bf16[16,128]{1,0:T(8,128)(2,1)S(1)} %get-tuple-element.40.mark_ref.refs_0_, bf16[512,512]{1,0:T(8,128)(2,1)S(1)} %get-tuple-element.41.sci_ref, bf16[64,512]{1,0:T(8,128)(2,1)S(1)} %get-tuple-element.24.note_ref, f32[4,512,128]{2,1,0:T(8,128)S(1)} %get-tuple-element.31.m1_ref, ...), custom_call_target="tpu_custom_call" | custom-call | flops 1207959552 | bytes 2097152 | tf_op jit(solution)/shard_map/tile/pallas_call | solution.py:468
  27.8 0.2 collective-permute-done.6.refs_1_
  28.0 0.0 collective-permute-done.7.refs_3_
  28.0 1.0 %coadd.1 = f32[128,512]{1,0:T(8,128)} custom-call(bf16[16,128]{1,0:T(8,128)(2,1)S(1)} %get-tuple-element.40.mark_ref.refs_0_, bf16[16,128]{1,0:T(8,128)(2,1)S(1)} %collective-permute-done.6.refs_1_, f32[128,512]{1,0:T(8,128)S(1)} %get-tuple-element.44.refs_2_, bf16[128,512]{1,0:T(8,128)(2,1)S(1)} %collective-permute-done.7.refs_3_), custom_call_target="tpu_custom_call" | custom-call | flops 1048576 | bytes 2097152 | tf_op jit(solution)/shard_map/coadd/pallas_call | solution.py:472
  (1 shorter events, 0.0 us)
Async XLA Ops:
  0.6 17.7 %collective-permute-start.2 = (bf16[512,1,512]{2,0,1:T(8,128)(2,1)}, bf16[512,1,512]{2,0,1:T(8,128)(2,1)S(1)}, u32[]{:S(2)}, u32[]{:S(2)}) collective-permute-start(bf16[512,1,512]{2,0,1:T(8,128)(2,1)} %param.9), channel_id=1, source_target_pairs={{0,4},{4,8},{8,12},{1,5},{5,9},{9,13},{2,6},{6,10},{10,14},{3,7},{... | collective-permute-start | bytes 1572872 | tf_op jit(solution)/shard_map/ppermute | solution.py:22
  8.1 9.9 %collective-permute-start = (bf16[32,512]{1,0:T(8,128)(2,1)S(1)}, bf16[32,512]{1,0:T(8,128)(2,1)S(1)}, u32[]{:S(2)}, u32[]{:S(2)}) collective-permute-start(bf16[32,512]{1,0:T(8,128)(2,1)S(1)} %get-tuple-element.25), channel_id=1, source_target_pairs={{0,4},{4,8},{8,12},{12,0},{1,5},{5,9},{9,13},{13,1},{2,6},{6,10},{... | collective-permute-start | bytes 98312 | tf_op jit(solution)/shard_map/ppermute | solution.py:423
  9.7 8.7 %collective-permute-start.1 = (bf16[32,512]{1,0:T(8,128)(2,1)S(1)}, bf16[32,512]{1,0:T(8,128)(2,1)S(1)}, u32[]{:S(2)}, u32[]{:S(2)}) collective-permute-start(bf16[32,512]{1,0:T(8,128)(2,1)S(1)} %get-tuple-element.26), channel_id=1, source_target_pairs={{4,0},{8,4},{12,8},{0,12},{5,1},{9,5},{13,9},{1,13},{6,2},{10,6},{... | collective-permute-start | bytes 98312 | tf_op jit(solution)/shard_map/ppermute | solution.py:424
  12.0 9.1 %collective-permute-start.4 = (bf16[256,512]{1,0:T(8,128)(2,1)S(1)}, bf16[256,512]{1,0:T(8,128)(2,1)S(1)}, u32[]{:S(2)}, u32[]{:S(2)}) collective-permute-start(bf16[256,512]{1,0:T(8,128)(2,1)S(1)} %get-tuple-element.43), channel_id=1, source_target_pairs={{4,0},{8,4},{12,8},{5,1},{9,5},{13,9},{6,2},{10,6},{14,10},{7,3},{... | collective-permute-start | bytes 786440 | tf_op jit(solution)/shard_map/ppermute | solution.py:22
  20.7 1.6 %collective-permute-start.3 = (bf16[272,512]{1,0:T(8,128)(2,1)S(1)}, bf16[272,512]{1,0:T(8,128)(2,1)S(1)}, u32[]{:S(2)}, u32[]{:S(2)}) collective-permute-start(bf16[272,512]{1,0:T(8,128)(2,1)S(1)} %get-tuple-element.39), channel_id=1, source_target_pairs={{0,1},{1,0},{2,3},{3,2},{4,5},{5,4},{6,7},{7,6},{8,9},{9,8},{10,11... | collective-permute-start | bytes 835592 | tf_op jit(solution)/shard_map/ppermute | solution.py:31
  21.0 3.4 %collective-permute-start.5 = (bf16[256,512]{1,0:T(8,128)(2,1)S(1)}, bf16[256,512]{1,0:T(8,128)(2,1)S(1)}, u32[]{:S(2)}, u32[]{:S(2)}) collective-permute-start(bf16[256,512]{1,0:T(8,128)(2,1)S(1)} %collective-permute-done.4.rest_0_), channel_id=1, source_target_pairs={{0,1},{1,0},{2,3},{3,2},{4,5},{5,4},{6,7},{7,6},{8,9},{9,8},{10,11... | collective-permute-start | bytes 786440 | tf_op jit(solution)/shard_map/ppermute | solution.py:31
  22.3 5.7 %collective-permute-start.7 = (bf16[128,512]{1,0:T(8,128)(2,1)S(1)}, bf16[128,512]{1,0:T(8,128)(2,1)S(1)}, u32[]{:S(2)}, u32[]{:S(2)}) collective-permute-start(bf16[128,512]{1,0:T(8,128)(2,1)S(1)} %get-tuple-element.45), channel_id=1, source_target_pairs={{0,2},{2,0},{1,3},{3,1},{4,6},{6,4},{5,7},{7,5},{8,10},{10,8},{9,1... | collective-permute-start | bytes 393224 | tf_op jit(solution)/shard_map/ppermute | solution.py:31
  23.9 4.1 %collective-permute-start.6 = (bf16[16,128]{1,0:T(8,128)(2,1)S(1)}, bf16[16,128]{1,0:T(8,128)(2,1)S(1)}, u32[]{:S(2)}, u32[]{:S(2)}) collective-permute-start(bf16[16,128]{1,0:T(8,128)(2,1)S(1)} %get-tuple-element.40.mark_ref.refs_0_), channel_id=1, source_target_pairs={{0,2},{2,0},{1,3},{3,1},{4,6},{6,4},{5,7},{7,5},{8,10},{10,8},{9,1... | collective-permute-start | bytes 12296 | tf_op jit(solution)/shard_map/ppermute | solution.py:31

commit v15 on v14

--- a/solution.py
+++ b/solution.py
@@ -62,7 +62,7 @@
             dst[c, at : at + B, :] = value[a * B : (a + 1) * B, c * LANES : (c + 1) * LANES]
 
 
-def conv_blocks(src, count, w_ref, xs, dst):
+def conv_blocks(src, count, w_ref, xs, dst, after=None):
     chunks = src.shape[0]
     blocks = chunks * GROUPS
 
@@ -98,6 +98,8 @@
         if c + 1 < chunks:
             load(c + 1)
         solve(c)
+        if after is not None:
+            after(c)
 
 
 def slanted(row, count):
@@ -331,7 +333,7 @@
 
 def tile_kernel(mark_ref, sci_ref, note_ref, m1_ref, edge_ref, w_ref, *rest):
     rows, cols = sci_ref.shape
-    *halves, out_ref, src, xs, res, big = rest
+    *halves, out_hbm, src, xs, res, big, out, sems = rest
     bands = len(halves)
     blocks = rows // B // bands
     band = lax.axis_index("band")
@@ -340,16 +342,24 @@
         for k in range(1, bands):
             piece = jnp.where(partner(band, k, bands) == j, halves[k][...].astype(F32), piece)
         to_blocks(src, j * blocks, piece)
-    conv_blocks(src, rows // B, w_ref, xs, res)
-    for a in range(1, rows // B):
-        big[:, rows + B * a : rows + B * (a + 1), :] = res[:, PITCH * a : PITCH * a + B, :]
-    big[:, 0:B, :] = edge_ref[:, B : 2 * B, :]
-    big[:, B : rows - B, :] = m1_ref[:, B : rows - B, :]
-    big[:, rows - B : rows + B, :] = edge_ref[:, 2 * B : 4 * B, :]
     off, _ = read_note(note_ref)
-    for c in range(cols // LANES):
+    copies = []
+
+    def after(c):
+        big[c, 0:B, :] = edge_ref[c, B : 2 * B, :]
+        big[c, B : rows - B, :] = m1_ref[c, B : rows - B, :]
+        big[c, rows - B : rows + B, :] = edge_ref[c, 2 * B : 4 * B, :]
+        for a in range(1, rows // B):
+            big[c, rows + B * a : rows + B * (a + 1), :] = res[c, PITCH * a : PITCH * a + B, :]
         part = slice(c * LANES, (c + 1) * LANES)
-        out_ref[:, part] = (sci_ref[:, part].astype(F32) - big[c, pl.ds(off, rows), :]).astype(BF16)
+        out[:, part] = (sci_ref[:, part].astype(F32) - big[c, pl.ds(off, rows), :]).astype(BF16)
+        there = pl.ds(c * LANES, LANES)
+        copies.append(pltpu.make_async_copy(out.at[:, there], out_hbm.at[:, there], sems.at[c]))
+        copies[-1].start()
+
+    conv_blocks(src, rows // B, w_ref, xs, res, after)
+    for copy in copies:
+        copy.wait()
 
 
 def coadd_kernel(*refs):
@@ -378,12 +388,12 @@
     return [pltpu.with_memory_space_constraint(x, pltpu.HBM) for x in arrays]
 
 
-def call(body, shapes, specs, scratch, flops, name):
+def call(body, shapes, specs, scratch, flops, name, out=VM):
     return pl.pallas_call(
         body,
         out_shape=shapes,
         in_specs=specs,
-        out_specs=jax.tree.map(lambda _: VM, shapes),
+        out_specs=jax.tree.map(lambda _: out, shapes),
         scratch_shapes=scratch,
         compiler_params=pltpu.CompilerParams(vmem_limit_bytes=LIMIT * 1024 * 1024),
         cost_estimate=pl.CostEstimate(flops=flops, bytes_accessed=1 << 21, transcendentals=0),
@@ -467,7 +477,11 @@
     marks = [mark] + [swapped(mark, "visit", k) for k in range(1, visits)]
     difference = call(
         tile_kernel, sds((rows, cols), BF16), [VM] * (6 + bands),
-        conv_scratch + [pltpu.VMEM((chunks, 2 * rows, LANES), F32)], conv_flops, "tile",
+        conv_scratch + [
+            pltpu.VMEM((chunks, 2 * rows, LANES), F32), pltpu.VMEM((rows, cols), BF16),
+            pltpu.SemaphoreType.DMA((chunks,)),
+        ],
+        conv_flops, "tile", HBM,
     )(mark, tile, note, m1, m_edge, w, *halves)
     detection = call(
         coadd_kernel, sds((share, cols), F32), [VM] * (2 * visits), [], 1 << 20, "coadd"

time: 29.2 us -> 29.2 us (level)
  no operation moved by 1% of the time
where the time goes in v15:
time: 29.2 us; the launch traced here: 29 us
  starting transfers between devices  12.5 us (43%)
  Pallas kernels  12.5 us (43%)
  waiting for transfers between devices  2.03 us (7%)
  between operations  1.99 us (7%)
    ppermute x2, starting transfers between devices, shifted(): return lax.ppermute(shard, axis, pairs)  6.24 us
    pallas_call x1, Pallas kernels, on_device(): call(first_kernel, (sds((deep, CH), BF16), sds((cols, cols), BF16), sds((...  4.72 us
    pallas_call x1, Pallas kernels, on_device(): call(tile_kernel, sds((rows, cols), BF16), [VM] * (6 + bands), conv_scrat...  3.24 us
    ppermute x4, starting transfers between devices, swapped(): lax.ppermute(shard, axis, [(i, partner(i, k, devices)) for i in range(dev...  2.4 us
    pallas_call x1, Pallas kernels, on_device(): call(join_kernel, (sds((whole, cols), F32),) + (sds((whole + B, cols), BF...  2.31 us
    ppermute x1, starting transfers between devices, on_device(): lax.ppermute(head, 'patch', [((i + 1) % panels, i) for i in range(panels)])  2.28 us
    ppermute x1, starting transfers between devices, on_device(): lax.ppermute(msg, 'patch', [(i, (i + 1) % panels) for i in range(panels)])  1.6 us
    ppermute x4, waiting for transfers between devices, swapped(): lax.ppermute(shard, axis, [(i, partner(i, k, devices)) for i in range(dev...  1.4 us
  transfers between devices with their start and end apart: 8, of which 4 were waited for; matrix products, arithmetic and copies ran while one was open for 0% of the time, Pallas kernels for 40%

profile of v15, /device:TPU:0, one launch (start us, length us, event | category | flops | bytes accessed | tf_op | source)
XLA Modules:
  0.0 29.0 jit_solution(14390050714018224670)
XLA Ops:
  0.6 5.0 %collective-permute-start.2 = (bf16[512,1,512]{2,0,1:T(8,128)(2,1)}, bf16[512,1,512]{2,0,1:T(8,128)(2,1)S(1)}, u32[]{:S(2)}, u32[]{:S(2)}) collective-permute-start(bf16[512,1,512]{2,0,1:T(8,128)(2,1)} %param.9), channel_id=1, source_target_pairs={{0,4},{4,8},{8,12},{1,5},{5,9},{9,13},{2,6},{6,10},{10,14},{3,7},{... | collective-permute-start | bytes 1572872 | tf_op jit(solution)/shard_map/ppermute | solution.py:22
  6.9 1.2 %pack.1 = (bf16[64,512]{1,0:T(8,128)(2,1)S(1)}, bf16[32,512]{1,0:T(8,128)(2,1)S(1)}, bf16[32,512]{1,0:T(8,128)(2,1)S(1)}, bf16[256,512]{1,0:T(8,128)(2,1)S(1)}, ...) custom-call(s32[1,1]{1,0:T(1,128)S(6)} %copy.10.off_hbm, ...), custom_call_target="tpu_custom_call" | custom-call | flops 1048576 | bytes 2097152 | tf_op jit(solution)/shard_map/pack/pallas_call | solution.py:420
  8.1 1.6 %collective-permute-start = (bf16[32,512]{1,0:T(8,128)(2,1)S(1)}, bf16[32,512]{1,0:T(8,128)(2,1)S(1)}, u32[]{:S(2)}, u32[]{:S(2)}) collective-permute-start(bf16[32,512]{1,0:T(8,128)(2,1)S(1)} %get-tuple-element.25), channel_id=1, source_target_pairs={{0,4},{4,8},{8,12},{12,0},{1,5},{5,9},{9,13},{13,1},{2,6},{6,10},{... | collective-permute-start | bytes 98312 | tf_op jit(solution)/shard_map/ppermute | solution.py:433
  9.7 2.3 %collective-permute-start.1 = (bf16[32,512]{1,0:T(8,128)(2,1)S(1)}, bf16[32,512]{1,0:T(8,128)(2,1)S(1)}, u32[]{:S(2)}, u32[]{:S(2)}) collective-permute-start(bf16[32,512]{1,0:T(8,128)(2,1)S(1)} %get-tuple-element.26), channel_id=1, source_target_pairs={{4,0},{8,4},{12,8},{0,12},{5,1},{9,5},{13,9},{1,13},{6,2},{10,6},{... | collective-permute-start | bytes 98312 | tf_op jit(solution)/shard_map/ppermute | solution.py:434
  12.0 1.3 %collective-permute-start.4 = (bf16[256,512]{1,0:T(8,128)(2,1)S(1)}, bf16[256,512]{1,0:T(8,128)(2,1)S(1)}, u32[]{:S(2)}, u32[]{:S(2)}) collective-permute-start(bf16[256,512]{1,0:T(8,128)(2,1)S(1)} %get-tuple-element.43), channel_id=1, source_target_pairs={{4,0},{8,4},{12,8},{5,1},{9,5},{13,9},{6,2},{10,6},{14,10},{7,3},{... | collective-permute-start | bytes 786440 | tf_op jit(solution)/shard_map/ppermute | solution.py:22
  13.2 4.7 %first.1 = (bf16[2304,256]{1,0:T(8,128)(2,1)S(1)}, bf16[512,512]{1,0:T(8,128)(2,1)S(1)}, bf16[128,256]{1,0:T(8,128)(2,1)S(1)}, bf16[512,512]{1,0:T(8,128)(2,1)S(...) custom-call(bf16[64,512]{1,0:T(8,128)(2,1)S(1)} %get-tuple-element.24.note_ref, ...), custom_call_target="tpu_custom_call" | custom-call | flops 1207959552 | bytes 2097152 | tf_op jit(solution)/shard_map/first/pallas_call | solution.py:444
  18.0 0.0 collective-permute-done.msg_ref
  18.0 0.4 %collective-permute-done.1.head_ref = bf16[32,512]{1,0:T(8,128)(2,1)S(1)} collective-permute-done((bf16[32,512]{1,0:T(8,128)(2,1)S(1)}, bf16[32,512]{1,0:T(8,128)(2,1)S(1)}, u32[]{:S(2)}, u32[]{:S(2)}) %collective-permute-start.1) | collective-permute-done | bytes 32800 | tf_op jit(solution)/shard_map/ppermute | solution.py:434
  18.3 0.0 collective-permute-done.2
  18.4 2.3 %join.1 = (f32[256,512]{1,0:T(8,128)S(1)}, bf16[272,512]{1,0:T(8,128)(2,1)S(1)}, bf16[16,128]{1,0:T(8,128)(2,1)S(1)}, f32[4,64,128]{2,1,0:T(8,128)S(1)}) custom-call(bf16[64,512]{1,0:T(8,128)(2,1)S(1)} %get-tuple-element.24.note_ref, bf16[32,512]{1,0:T(8,128)(2,1)S(1)} %collective-permute-done.msg_ref, bf16[32,512]{1,0:T(8,128)(2,1)S(1)} %collective-permute-done.1.head_ref, ...), custom_call_target="tpu_custom_call" | custom-call | flops 17179869184 | bytes 2097152 | tf_op jit(solution)/shard_map/join/pallas_call | solution.py:455
  20.7 0.1 collective-permute-start.3
  20.7 0.3 collective-permute-done.4.rest_0_
  21.0 0.2 collective-permute-start.5
  21.2 1.0 %collective-permute-done.3.refs_2_ = bf16[272,512]{1,0:T(8,128)(2,1)S(1)} collective-permute-done((bf16[272,512]{1,0:T(8,128)(2,1)S(1)}, bf16[272,512]{1,0:T(8,128)(2,1)S(1)}, u32[]{:S(2)}, u32[]{:S(2)}) %collective-permute-start.3) | collective-permute-done | bytes 278560 | tf_op jit(solution)/shard_map/ppermute | solution.py:31
  22.3 1.6 %collective-permute-start.7 = (bf16[128,512]{1,0:T(8,128)(2,1)S(1)}, bf16[128,512]{1,0:T(8,128)(2,1)S(1)}, u32[]{:S(2)}, u32[]{:S(2)}) collective-permute-start(bf16[128,512]{1,0:T(8,128)(2,1)S(1)} %get-tuple-element.45), channel_id=1, source_target_pairs={{0,2},{2,0},{1,3},{3,1},{4,6},{6,4},{5,7},{7,5},{8,10},{10,8},{9,1... | collective-permute-start | bytes 393224 | tf_op jit(solution)/shard_map/ppermute | solution.py:31
  23.9 0.5 %collective-permute-start.6 = (bf16[16,128]{1,0:T(8,128)(2,1)S(1)}, bf16[16,128]{1,0:T(8,128)(2,1)S(1)}, u32[]{:S(2)}, u32[]{:S(2)}) collective-permute-start(bf16[16,128]{1,0:T(8,128)(2,1)S(1)} %get-tuple-element.40.mark_ref.refs_0_), channel_id=1, source_target_pairs={{0,2},{2,0},{1,3},{3,1},{4,6},{6,4},{5,7},{7,5},{8,10},{10,8},{9,1... | collective-permute-start | bytes 12296 | tf_op jit(solution)/shard_map/ppermute | solution.py:31
  24.4 0.0 collective-permute-done.5.rest_1_
  24.4 3.2 %tile.1 = bf16[512,512]{1,0:T(8,128)(2,1)} custom-call(bf16[16,128]{1,0:T(8,128)(2,1)S(1)} %get-tuple-element.40.mark_ref.refs_0_, bf16[512,512]{1,0:T(8,128)(2,1)S(1)} %get-tuple-element.41.sci_ref, bf16[64,512]{1,0:T(8,128)(2,1)S(1)} %get-tuple-element.24.note_ref, f32[4,512,128]{2,1,0:T(8,128)S(1)} %get-tuple-element.31.m1_ref, ...), custom_call_target="tpu_custom_call" | custom-call | flops 1207959552 | bytes 2097152 | tf_op jit(solution)/shard_map/tile/pallas_call | solution.py:478
  27.7 0.3 %collective-permute-done.6.refs_1_ = bf16[16,128]{1,0:T(8,128)(2,1)S(1)} collective-permute-done((bf16[16,128]{1,0:T(8,128)(2,1)S(1)}, bf16[16,128]{1,0:T(8,128)(2,1)S(1)}, u32[]{:S(2)}, u32[]{:S(2)}) %collective-permute-start.6) | collective-permute-done | bytes 4128 | tf_op jit(solution)/shard_map/ppermute | solution.py:31
  28.0 0.0 collective-permute-done.7.refs_3_
  28.0 1.0 %coadd.1 = f32[128,512]{1,0:T(8,128)} custom-call(bf16[16,128]{1,0:T(8,128)(2,1)S(1)} %get-tuple-element.40.mark_ref.refs_0_, bf16[16,128]{1,0:T(8,128)(2,1)S(1)} %collective-permute-done.6.refs_1_, f32[128,512]{1,0:T(8,128)S(1)} %get-tuple-element.44.refs_2_, bf16[128,512]{1,0:T(8,128)(2,1)S(1)} %collective-permute-done.7.refs_3_), custom_call_target="tpu_custom_call" | custom-call | flops 1048576 | bytes 2097152 | tf_op jit(solution)/shard_map/coadd/pallas_call | solution.py:486
  (1 shorter events, 0.0 us)
Async XLA Ops:
  0.6 17.7 %collective-permute-start.2 = (bf16[512,1,512]{2,0,1:T(8,128)(2,1)}, bf16[512,1,512]{2,0,1:T(8,128)(2,1)S(1)}, u32[]{:S(2)}, u32[]{:S(2)}) collective-permute-start(bf16[512,1,512]{2,0,1:T(8,128)(2,1)} %param.9), channel_id=1, source_target_pairs={{0,4},{4,8},{8,12},{1,5},{5,9},{9,13},{2,6},{6,10},{10,14},{3,7},{... | collective-permute-start | bytes 1572872 | tf_op jit(solution)/shard_map/ppermute | solution.py:22
  8.1 9.9 %collective-permute-start = (bf16[32,512]{1,0:T(8,128)(2,1)S(1)}, bf16[32,512]{1,0:T(8,128)(2,1)S(1)}, u32[]{:S(2)}, u32[]{:S(2)}) collective-permute-start(bf16[32,512]{1,0:T(8,128)(2,1)S(1)} %get-tuple-element.25), channel_id=1, source_target_pairs={{0,4},{4,8},{8,12},{12,0},{1,5},{5,9},{9,13},{13,1},{2,6},{6,10},{... | collective-permute-start | bytes 98312 | tf_op jit(solution)/shard_map/ppermute | solution.py:433
  9.7 8.7 %collective-permute-start.1 = (bf16[32,512]{1,0:T(8,128)(2,1)S(1)}, bf16[32,512]{1,0:T(8,128)(2,1)S(1)}, u32[]{:S(2)}, u32[]{:S(2)}) collective-permute-start(bf16[32,512]{1,0:T(8,128)(2,1)S(1)} %get-tuple-element.26), channel_id=1, source_target_pairs={{4,0},{8,4},{12,8},{0,12},{5,1},{9,5},{13,9},{1,13},{6,2},{10,6},{... | collective-permute-start | bytes 98312 | tf_op jit(solution)/shard_map/ppermute | solution.py:434
  12.0 9.1 %collective-permute-start.4 = (bf16[256,512]{1,0:T(8,128)(2,1)S(1)}, bf16[256,512]{1,0:T(8,128)(2,1)S(1)}, u32[]{:S(2)}, u32[]{:S(2)}) collective-permute-start(bf16[256,512]{1,0:T(8,128)(2,1)S(1)} %get-tuple-element.43), channel_id=1, source_target_pairs={{4,0},{8,4},{12,8},{5,1},{9,5},{13,9},{6,2},{10,6},{14,10},{7,3},{... | collective-permute-start | bytes 786440 | tf_op jit(solution)/shard_map/ppermute | solution.py:22
  20.7 1.6 %collective-permute-start.3 = (bf16[272,512]{1,0:T(8,128)(2,1)S(1)}, bf16[272,512]{1,0:T(8,128)(2,1)S(1)}, u32[]{:S(2)}, u32[]{:S(2)}) collective-permute-start(bf16[272,512]{1,0:T(8,128)(2,1)S(1)} %get-tuple-element.39), channel_id=1, source_target_pairs={{0,1},{1,0},{2,3},{3,2},{4,5},{5,4},{6,7},{7,6},{8,9},{9,8},{10,11... | collective-permute-start | bytes 835592 | tf_op jit(solution)/shard_map/ppermute | solution.py:31
  21.0 3.4 %collective-permute-start.5 = (bf16[256,512]{1,0:T(8,128)(2,1)S(1)}, bf16[256,512]{1,0:T(8,128)(2,1)S(1)}, u32[]{:S(2)}, u32[]{:S(2)}) collective-permute-start(bf16[256,512]{1,0:T(8,128)(2,1)S(1)} %collective-permute-done.4.rest_0_), channel_id=1, source_target_pairs={{0,1},{1,0},{2,3},{3,2},{4,5},{5,4},{6,7},{7,6},{8,9},{9,8},{10,11... | collective-permute-start | bytes 786440 | tf_op jit(solution)/shard_map/ppermute | solution.py:31
  22.3 5.7 %collective-permute-start.7 = (bf16[128,512]{1,0:T(8,128)(2,1)S(1)}, bf16[128,512]{1,0:T(8,128)(2,1)S(1)}, u32[]{:S(2)}, u32[]{:S(2)}) collective-permute-start(bf16[128,512]{1,0:T(8,128)(2,1)S(1)} %get-tuple-element.45), channel_id=1, source_target_pairs={{0,2},{2,0},{1,3},{3,1},{4,6},{6,4},{5,7},{7,5},{8,10},{10,8},{9,1... | collective-permute-start | bytes 393224 | tf_op jit(solution)/shard_map/ppermute | solution.py:31
  23.9 4.1 %collective-permute-start.6 = (bf16[16,128]{1,0:T(8,128)(2,1)S(1)}, bf16[16,128]{1,0:T(8,128)(2,1)S(1)}, u32[]{:S(2)}, u32[]{:S(2)}) collective-permute-start(bf16[16,128]{1,0:T(8,128)(2,1)S(1)} %get-tuple-element.40.mark_ref.refs_0_), channel_id=1, source_target_pairs={{0,2},{2,0},{1,3},{3,1},{4,6},{6,4},{5,7},{7,5},{8,10},{10,8},{9,1... | collective-permute-start | bytes 12296 | tf_op jit(solution)/shard_map/ppermute | solution.py:31

commit v16 on v15

--- a/solution.py
+++ b/solution.py
@@ -120,20 +120,16 @@
 
 def pack_kernel(
     off_hbm, live_hbm, t_hbm, bank_hbm, index_hbm, coeff_hbm, psf_hbm,
-    note_ref, msg_ref, head_ref, half_ref, bank_ref, index_ref, coeff_ref, psf_ref, off_ref, live_ref, sems,
+    note_ref, msg_ref, bank_ref, index_ref, coeff_ref, psf_ref, off_ref, live_ref, sems,
 ):
     rows, cols = t_hbm.shape
     edge = 2 * B
-    piece = half_ref.shape[0]
-    begin = pl.multiple_of(lax.axis_index("band") * piece, B)
     copies = [
         pltpu.make_async_copy(a, b, sems.at[n])
         for n, (a, b) in enumerate((
             (off_hbm, off_ref), (live_hbm, live_ref),
             (t_hbm.at[pl.ds(rows - edge, edge)], note_ref.at[pl.ds(0, edge)]),
             (t_hbm.at[pl.ds(0, edge)], note_ref.at[pl.ds(edge, edge)]),
-            (t_hbm.at[pl.ds(0, edge)], head_ref),
-            (t_hbm.at[pl.ds(begin, piece)], half_ref),
             (bank_hbm, bank_ref), (index_hbm, index_ref), (coeff_hbm, coeff_ref), (psf_hbm, psf_ref),
         ))
     ]
@@ -149,16 +145,20 @@
     msg_ref[...] = note_ref[0:edge, :]
 
 
-def first_kernel(
+def weights_kernel(
     note_ref, t_hbm, sci_hbm, bank_ref, index_ref, coeff_ref, psf_ref,
-    w_ref, pcol_ref, prow_ref, sci_ref, m_ref, edge_ref, filt_ref,
-    t_ref, sems, src, xs, res, sci, diff,
+    w_ref, pcol_ref, prow_ref, head_ref, half_ref, t_ref, sci_ref, sems,
 ):
+    piece = half_ref.shape[0]
+    begin = pl.multiple_of(lax.axis_index("band") * piece, B)
     copies = [
-        pltpu.make_async_copy(t_hbm, t_ref, sems.at[0]), pltpu.make_async_copy(sci_hbm, sci_ref, sems.at[1])
+        pltpu.make_async_copy(t_hbm.at[pl.ds(begin, piece)], half_ref, sems.at[0]),
+        pltpu.make_async_copy(t_hbm, t_ref, sems.at[1]),
+        pltpu.make_async_copy(sci_hbm, sci_ref, sems.at[2]),
     ]
     for copy in copies:
         copy.start()
+    head_ref[...] = note_ref[2 * B :, :]
     profs, taps = bank_ref.shape
     half = taps // 2
     delta = B - half
@@ -206,8 +206,10 @@
     prow_ref[...] = slanted(jnp.dot(psf_ref[...], ahead, preferred_element_type=F32), share).astype(BF16)
     for copy in copies:
         copy.wait()
-    edge = 2 * B
-    rows, cols = t_ref.shape
+
+
+def own_kernel(note_ref, t_ref, sci_ref, w_ref, pcol_ref, m_ref, edge_ref, filt_ref, src, xs, res, sci, diff):
+    rows = t_ref.shape[0]
     off, _ = read_note(note_ref)
     to_blocks(src, 0, t_ref[...])
     conv_blocks(src, rows // B, w_ref, xs, res)
@@ -246,10 +248,9 @@
     return (note[0, 0] * B + note[0, 1]).astype(jnp.int32), note[0, 2]
 
 
-def read_before(msg_ref):
+def halo_kernel(msg_ref, out_ref):
     valid = lax.axis_index("patch") > 0
-    off, live = read_note(msg_ref)
-    return jnp.where(valid, off, 0), jnp.where(valid, live, 0.0), valid
+    out_ref[...] = jnp.where(valid, msg_ref[...].astype(F32), 0.0).astype(BF16)
 
 
 def join_kernel(
@@ -259,9 +260,9 @@
     *outs, mark_ref, m_ref, src, xs, strip, diff, filt, sci, inner, edge_b, filt_b = rest
     edge = 2 * B
     rows, cols = filt_a.shape[0] + edge, filt_a.shape[1]
-    off_b, live_b, valid = read_before(msg_ref)
+    off_b, live_b = read_note(msg_ref)
     to_chunks(sci, 0, sci_ref[...])
-    to_blocks(src, 0, jnp.where(valid, msg_ref[...].astype(F32), 0.0))
+    to_blocks(src, 0, msg_ref[...])
     to_blocks(src, 2, note_ref[edge:, :])
     to_blocks(src, 4, note_ref[0:edge, :])
     last = lax.axis_index("patch") == lax.axis_size("patch") - 1
@@ -417,21 +418,28 @@
     before = shifted(science, "patch", 1)[:, 0, :]
     bands, visits = lax.axis_size("band"), lax.axis_size("visit")
     psf = psf_profile[None]
-    note, msg, head, half, *small = call(
+    note, msg, *small = call(
         pack_kernel,
         (
-            sds((2 * edge, cols), BF16), sds((edge, cols), BF16), sds((edge, cols), BF16),
-            sds((rows // bands, cols), BF16),
+            sds((2 * edge, cols), BF16), sds((edge, cols), BF16),
             *(sds(x.shape, x.dtype) for x in (bank, index, coeff, psf)),
         ),
         [HBM] * 7,
-        [pltpu.SMEM((1, 1), jnp.int32), pltpu.SMEM((1, 1), jnp.int32), pltpu.SemaphoreType.DMA((10,))],
+        [pltpu.SMEM((1, 1), jnp.int32), pltpu.SMEM((1, 1), jnp.int32), pltpu.SemaphoreType.DMA((8,))],
         1 << 20, "pack",
     )(offsets, live_flags, held[0], *in_hbm(bank, index, coeff, psf))
-    half = shifted(half, "patch", -1)
     panels = lax.axis_size("patch")
     msg = lax.ppermute(msg, "patch", [(i, (i + 1) % panels) for i in range(panels)])
+    w, pcol, prow, head, half, panel, tile = call(
+        weights_kernel,
+        (
+            sds((deep, CH), BF16), sds((cols, cols), BF16), sds((share, depth), BF16), sds((edge, cols), BF16),
+            sds((rows // bands, cols), BF16), sds((rows, cols), BF16), sds((rows, cols), BF16),
+        ),
+        [VM, HBM, HBM] + [VM] * 4, [pltpu.SemaphoreType.DMA((3,))], 1 << 28, "weights",
+    )(note, *held, *small)
     head = lax.ppermute(head, "patch", [((i + 1) % panels, i) for i in range(panels)])
+    half = shifted(half, "patch", -1)
     count = rows // B
     conv_scratch = [
         pltpu.VMEM((chunks, count * PITCH, LANES), F32),
@@ -441,16 +449,11 @@
     conv_flops = 2 * rows * cols * deep
     sky_scratch = [pltpu.VMEM((chunks, 2 * rows + B, LANES), F32), pltpu.VMEM((inner, cols), BF16)]
     sides = (sds((chunks, 2 * edge, LANES), F32), sds((inner, cols), BF16))
-    w, pcol, prow, tile, m1, edge_a, filt_a = call(
-        first_kernel,
-        (
-            sds((deep, CH), BF16), sds((cols, cols), BF16), sds((share, depth), BF16),
-            sds((rows, cols), BF16), sds((chunks, rows, LANES), F32),
-        ) + sides,
-        [VM, HBM, HBM] + [VM] * 4,
-        [pltpu.VMEM((rows, cols), BF16), pltpu.SemaphoreType.DMA((2,))] + conv_scratch + sky_scratch,
-        conv_flops, "first",
-    )(note, *held, *small)
+    m1, edge_a, filt_a = call(
+        own_kernel, (sds((chunks, rows, LANES), F32),) + sides, [VM] * 5,
+        conv_scratch + sky_scratch, 1 << 20, "own",
+    )(note, panel, tile, w, pcol)
+    msg = call(halo_kernel, sds((edge, cols), BF16), [VM], [], 1 << 32, "halo")(msg)
     whole = visits * share
     keep, *sent, mark, m_edge = call(
         join_kernel,

time: 29.2 us -> 30.6 us (1.048)
  waiting for transfers between devices: 2.03 us -> 3.44 us
    ppermute x2, waiting for transfers between devices: 0.27 us -> 2.53 us  [shifted(): return lax.ppermute(shard, axis, pairs)]
    ppermute x4, waiting for transfers between devices: 1.4 us -> 0.72 us  [swapped(): lax.ppermute(shard, axis, [(i, partner(i, k, devices)) for i in range(dev...]
    pallas_call x1 -> x3, Pallas kernels: 4.72 us -> 5.15 us  [the longest x1 2.67 us: on_device(): call(own_kernel, (sds((chunks, rows, LANES), F32),) + sides, [VM] * 5, co...]
    pallas_call x1, Pallas kernels: 1.18 us -> 0.87 us  [on_device(): call(pack_kernel, (sds((2 * edge, cols), BF16), sds((edge, cols), BF16),...]
  transfers between devices with their start and end apart: 8 -> 8, of which waited for: 4 -> 3; matrix products, arithmetic and copies ran while one was open for 0% -> 0% of each run, Pallas kernels for 40% -> 38%
where the time goes in v16:
time: 30.6 us; the launch traced here: 30.3 us
  Pallas kernels  12.6 us (41%)
  starting transfers between devices  12.3 us (40%)
  waiting for transfers between devices  3.44 us (11%)
  between operations  2.01 us (7%)
    ppermute x2, starting transfers between devices, shifted(): return lax.ppermute(shard, axis, pairs)  6.24 us
    pallas_call x1, Pallas kernels, on_device(): call(tile_kernel, sds((rows, cols), BF16), [VM] * (6 + bands), conv_scrat...  3.24 us
    pallas_call x1, Pallas kernels, on_device(): call(own_kernel, (sds((chunks, rows, LANES), F32),) + sides, [VM] * 5, co...  2.67 us
    ppermute x2, waiting for transfers between devices, shifted(): return lax.ppermute(shard, axis, pairs)  2.53 us
    pallas_call x1, Pallas kernels, on_device(): call(weights_kernel, (sds((deep, CH), BF16), sds((cols, cols), BF16), sds...  2.47 us
    ppermute x1, starting transfers between devices, on_device(): lax.ppermute(head, 'patch', [((i + 1) % panels, i) for i in range(panels)])  2.33 us
    pallas_call x1, Pallas kernels, on_device(): call(join_kernel, (sds((whole, cols), F32),) + (sds((whole + B, cols), BF...  2.29 us
    ppermute x4, starting transfers between devices, swapped(): lax.ppermute(shard, axis, [(i, partner(i, k, devices)) for i in range(dev...  2.16 us
  transfers between devices with their start and end apart: 8, of which 3 were waited for; matrix products, arithmetic and copies ran while one was open for 0% of the time, Pallas kernels for 38%

profile of v16, /device:TPU:0, one launch (start us, length us, event | category | flops | bytes accessed | tf_op | source)
XLA Modules:
  0.0 30.3 jit_solution(13628052409712953416)
XLA Ops:
  0.6 5.0 %collective-permute-start.2 = (bf16[512,1,512]{2,0,1:T(8,128)(2,1)}, bf16[512,1,512]{2,0,1:T(8,128)(2,1)S(1)}, u32[]{:S(2)}, u32[]{:S(2)}) collective-permute-start(bf16[512,1,512]{2,0,1:T(8,128)(2,1)} %param.9), channel_id=1, source_target_pairs={{0,4},{4,8},{8,12},{1,5},{5,9},{9,13},{2,6},{6,10},{10,14},{3,7},{... | collective-permute-start | bytes 1572872 | tf_op jit(solution)/shard_map/ppermute | solution.py:22
  6.9 0.9 %pack.1 = (bf16[64,512]{1,0:T(8,128)(2,1)S(1)}, bf16[32,512]{1,0:T(8,128)(2,1)S(1)}, bf16[16,31]{1,0:T(8,128)(2,1)S(1)}, s32[1,2,15]{2,1,0:T(2,128)S(1)}, f32[1,...) custom-call(s32[1,1]{1,0:T(1,128)S(6)} %copy.10.off_hbm, s32[1,1]{1,0:T(1,128)S(6)} %copy.11.live_hbm, bf16[512,512]{1,0:T(8,128)(2,1)} %t_hbm.3, ...), custom_call_target="tpu_custom_call" | custom-call | flops 1048576 | bytes 2097152 | tf_op jit(solution)/shard_map/pack/pallas_call | solution.py:421
  7.8 1.6 %collective-permute-start = (bf16[32,512]{1,0:T(8,128)(2,1)S(1)}, bf16[32,512]{1,0:T(8,128)(2,1)S(1)}, u32[]{:S(2)}, u32[]{:S(2)}) collective-permute-start(bf16[32,512]{1,0:T(8,128)(2,1)S(1)} %get-tuple-element.26), channel_id=1, source_target_pairs={{0,4},{4,8},{8,12},{12,0},{1,5},{5,9},{9,13},{13,1},{2,6},{6,10},{... | collective-permute-start | bytes 98312 | tf_op jit(solution)/shard_map/ppermute | solution.py:432
  9.4 2.5 %weights.1 = (bf16[2304,256]{1,0:T(8,128)(2,1)S(1)}, bf16[512,512]{1,0:T(8,128)(2,1)S(1)}, bf16[128,256]{1,0:T(8,128)(2,1)S(1)}, bf16[32,512]{1,0:T(8,128)(2,1)S...) custom-call(bf16[64,512]{1,0:T(8,128)(2,1)S(1)} %get-tuple-element.25.note_ref, ...), custom_call_target="tpu_custom_call" | custom-call | flops 268435456 | bytes 2097152 | tf_op jit(solution)/shard_map/weights/pallas_call | solution.py:433
  11.8 2.3 %collective-permute-start.1 = (bf16[32,512]{1,0:T(8,128)(2,1)S(1)}, bf16[32,512]{1,0:T(8,128)(2,1)S(1)}, u32[]{:S(2)}, u32[]{:S(2)}) collective-permute-start(bf16[32,512]{1,0:T(8,128)(2,1)S(1)} %get-tuple-element.31), channel_id=1, source_target_pairs={{4,0},{8,4},{12,8},{0,12},{5,1},{9,5},{13,9},{1,13},{6,2},{10,6},{... | collective-permute-start | bytes 98312 | tf_op jit(solution)/shard_map/ppermute | solution.py:441
  14.2 1.3 %collective-permute-start.4 = (bf16[256,512]{1,0:T(8,128)(2,1)S(1)}, bf16[256,512]{1,0:T(8,128)(2,1)S(1)}, u32[]{:S(2)}, u32[]{:S(2)}) collective-permute-start(bf16[256,512]{1,0:T(8,128)(2,1)S(1)} %get-tuple-element.45), channel_id=1, source_target_pairs={{4,0},{8,4},{12,8},{5,1},{9,5},{13,9},{6,2},{10,6},{14,10},{7,3},{... | collective-permute-start | bytes 786440 | tf_op jit(solution)/shard_map/ppermute | solution.py:22
  15.5 2.7 %own.1 = (f32[4,512,128]{2,1,0:T(8,128)S(1)}, f32[4,64,128]{2,1,0:T(8,128)S(1)}, bf16[480,512]{1,0:T(8,128)(2,1)S(1)}) custom-call(bf16[64,512]{1,0:T(8,128)(2,1)S(1)} %get-tuple-element.25.note_ref, bf16[512,512]{1,0:T(8,128)(2,1)S(1)} %get-tuple-element.32.t_ref, bf16[512,512]{1,0:T(8,128)(2,1)S(1)} %get-tuple-element.33.sci_ref, ...), custom_call_target="tpu_custom_call" | custom-call | flops 1048576 | bytes 2097152 | tf_op jit(solution)/shard_map/own/pallas_call | solution.py:452
  18.1 0.0 collective-permute-done.msg_ref
  18.2 0.2 collective-permute-done.1.head_ref
  18.3 0.0 collective-permute-done.2
  18.4 2.3 %join.1 = (f32[256,512]{1,0:T(8,128)S(1)}, bf16[272,512]{1,0:T(8,128)(2,1)S(1)}, bf16[16,128]{1,0:T(8,128)(2,1)S(1)}, f32[4,64,128]{2,1,0:T(8,128)S(1)}) custom-call(bf16[64,512]{1,0:T(8,128)(2,1)S(1)} %get-tuple-element.25.note_ref, bf16[32,512]{1,0:T(8,128)(2,1)S(1)} %halo.1.msg_ref, bf16[32,512]{1,0:T(8,128)(2,1)S(1)} %collective-permute-done.1.head_ref, ...), custom_call_target="tpu_custom_call" | custom-call | flops 17179869184 | bytes 2097152 | tf_op jit(solution)/shard_map/join/pallas_call | solution.py:458
  20.7 0.1 collective-permute-start.3
  20.7 2.5 %collective-permute-done.4.rest_0_ = bf16[256,512]{1,0:T(8,128)(2,1)S(1)} collective-permute-done((bf16[256,512]{1,0:T(8,128)(2,1)S(1)}, bf16[256,512]{1,0:T(8,128)(2,1)S(1)}, u32[]{:S(2)}, u32[]{:S(2)}) %collective-permute-start.4) | collective-permute-done | bytes 262176 | tf_op jit(solution)/shard_map/ppermute | solution.py:22
  23.3 0.0 collective-permute-start.5
  23.3 0.0 collective-permute-done.3.refs_2_
  23.3 1.6 %collective-permute-start.7 = (bf16[128,512]{1,0:T(8,128)(2,1)S(1)}, bf16[128,512]{1,0:T(8,128)(2,1)S(1)}, u32[]{:S(2)}, u32[]{:S(2)}) collective-permute-start(bf16[128,512]{1,0:T(8,128)(2,1)S(1)} %get-tuple-element.47), channel_id=1, source_target_pairs={{0,2},{2,0},{1,3},{3,1},{4,6},{6,4},{5,7},{7,5},{8,10},{10,8},{9,1... | collective-permute-start | bytes 393224 | tf_op jit(solution)/shard_map/ppermute | solution.py:31
  24.9 0.5 %collective-permute-start.6 = (bf16[16,128]{1,0:T(8,128)(2,1)S(1)}, bf16[16,128]{1,0:T(8,128)(2,1)S(1)}, u32[]{:S(2)}, u32[]{:S(2)}) collective-permute-start(bf16[16,128]{1,0:T(8,128)(2,1)S(1)} %get-tuple-element.43.mark_ref.refs_0_), channel_id=1, source_target_pairs={{0,2},{2,0},{1,3},{3,1},{4,6},{6,4},{5,7},{7,5},{8,10},{10,8},{9,1... | collective-permute-start | bytes 12296 | tf_op jit(solution)/shard_map/ppermute | solution.py:31
  25.4 0.0 collective-permute-done.5.rest_1_
  25.4 3.2 %tile.1 = bf16[512,512]{1,0:T(8,128)(2,1)} custom-call(bf16[16,128]{1,0:T(8,128)(2,1)S(1)} %get-tuple-element.43.mark_ref.refs_0_, bf16[512,512]{1,0:T(8,128)(2,1)S(1)} %get-tuple-element.33.sci_ref, bf16[64,512]{1,0:T(8,128)(2,1)S(1)} %get-tuple-element.25.note_ref, f32[4,512,128]{2,1,0:T(8,128)S(1)} %get-tuple-element.36.m1_ref, ...), custom_call_target="tpu_custom_call" | custom-call | flops 1207959552 | bytes 2097152 | tf_op jit(solution)/shard_map/tile/pallas_call | solution.py:481
  28.7 0.7 %collective-permute-done.6.refs_1_ = bf16[16,128]{1,0:T(8,128)(2,1)S(1)} collective-permute-done((bf16[16,128]{1,0:T(8,128)(2,1)S(1)}, bf16[16,128]{1,0:T(8,128)(2,1)S(1)}, u32[]{:S(2)}, u32[]{:S(2)}) %collective-permute-start.6) | collective-permute-done | bytes 4128 | tf_op jit(solution)/shard_map/ppermute | solution.py:31
  29.4 0.0 collective-permute-done.7.refs_3_
  29.4 1.0 %coadd.1 = f32[128,512]{1,0:T(8,128)} custom-call(bf16[16,128]{1,0:T(8,128)(2,1)S(1)} %get-tuple-element.43.mark_ref.refs_0_, bf16[16,128]{1,0:T(8,128)(2,1)S(1)} %collective-permute-done.6.refs_1_, f32[128,512]{1,0:T(8,128)S(1)} %get-tuple-element.46.refs_2_, bf16[128,512]{1,0:T(8,128)(2,1)S(1)} %collective-permute-done.7.refs_3_), custom_call_target="tpu_custom_call" | custom-call | flops 1048576 | bytes 2097152 | tf_op jit(solution)/shard_map/coadd/pallas_call | solution.py:489
  (2 shorter events, 0.1 us)
Async XLA Ops:
  0.6 17.7 %collective-permute-start.2 = (bf16[512,1,512]{2,0,1:T(8,128)(2,1)}, bf16[512,1,512]{2,0,1:T(8,128)(2,1)S(1)}, u32[]{:S(2)}, u32[]{:S(2)}) collective-permute-start(bf16[512,1,512]{2,0,1:T(8,128)(2,1)} %param.9), channel_id=1, source_target_pairs={{0,4},{4,8},{8,12},{1,5},{5,9},{9,13},{2,6},{6,10},{10,14},{3,7},{... | collective-permute-start | bytes 1572872 | tf_op jit(solution)/shard_map/ppermute | solution.py:22
  7.8 10.4 %collective-permute-start = (bf16[32,512]{1,0:T(8,128)(2,1)S(1)}, bf16[32,512]{1,0:T(8,128)(2,1)S(1)}, u32[]{:S(2)}, u32[]{:S(2)}) collective-permute-start(bf16[32,512]{1,0:T(8,128)(2,1)S(1)} %get-tuple-element.26), channel_id=1, source_target_pairs={{0,4},{4,8},{8,12},{12,0},{1,5},{5,9},{9,13},{13,1},{2,6},{6,10},{... | collective-permute-start | bytes 98312 | tf_op jit(solution)/shard_map/ppermute | solution.py:432
  11.8 6.5 %collective-permute-start.1 = (bf16[32,512]{1,0:T(8,128)(2,1)S(1)}, bf16[32,512]{1,0:T(8,128)(2,1)S(1)}, u32[]{:S(2)}, u32[]{:S(2)}) collective-permute-start(bf16[32,512]{1,0:T(8,128)(2,1)S(1)} %get-tuple-element.31), channel_id=1, source_target_pairs={{4,0},{8,4},{12,8},{0,12},{5,1},{9,5},{13,9},{1,13},{6,2},{10,6},{... | collective-permute-start | bytes 98312 | tf_op jit(solution)/shard_map/ppermute | solution.py:441
  14.2 9.1 %collective-permute-start.4 = (bf16[256,512]{1,0:T(8,128)(2,1)S(1)}, bf16[256,512]{1,0:T(8,128)(2,1)S(1)}, u32[]{:S(2)}, u32[]{:S(2)}) collective-permute-start(bf16[256,512]{1,0:T(8,128)(2,1)S(1)} %get-tuple-element.45), channel_id=1, source_target_pairs={{4,0},{8,4},{12,8},{5,1},{9,5},{13,9},{6,2},{10,6},{14,10},{7,3},{... | collective-permute-start | bytes 786440 | tf_op jit(solution)/shard_map/ppermute | solution.py:22
  20.7 2.6 %collective-permute-start.3 = (bf16[272,512]{1,0:T(8,128)(2,1)S(1)}, bf16[272,512]{1,0:T(8,128)(2,1)S(1)}, u32[]{:S(2)}, u32[]{:S(2)}) collective-permute-start(bf16[272,512]{1,0:T(8,128)(2,1)S(1)} %get-tuple-element.42), channel_id=1, source_target_pairs={{0,1},{1,0},{2,3},{3,2},{4,5},{5,4},{6,7},{7,6},{8,9},{9,8},{10,11... | collective-permute-start | bytes 835592 | tf_op jit(solution)/shard_map/ppermute | solution.py:31
  23.3 2.2 %collective-permute-start.5 = (bf16[256,512]{1,0:T(8,128)(2,1)S(1)}, bf16[256,512]{1,0:T(8,128)(2,1)S(1)}, u32[]{:S(2)}, u32[]{:S(2)}) collective-permute-start(bf16[256,512]{1,0:T(8,128)(2,1)S(1)} %collective-permute-done.4.rest_0_), channel_id=1, source_target_pairs={{0,1},{1,0},{2,3},{3,2},{4,5},{5,4},{6,7},{7,6},{8,9},{9,8},{10,11... | collective-permute-start | bytes 786440 | tf_op jit(solution)/shard_map/ppermute | solution.py:31
  23.3 6.1 %collective-permute-start.7 = (bf16[128,512]{1,0:T(8,128)(2,1)S(1)}, bf16[128,512]{1,0:T(8,128)(2,1)S(1)}, u32[]{:S(2)}, u32[]{:S(2)}) collective-permute-start(bf16[128,512]{1,0:T(8,128)(2,1)S(1)} %get-tuple-element.47), channel_id=1, source_target_pairs={{0,2},{2,0},{1,3},{3,1},{4,6},{6,4},{5,7},{7,5},{8,10},{10,8},{9,1... | collective-permute-start | bytes 393224 | tf_op jit(solution)/shard_map/ppermute | solution.py:31
  24.9 4.5 %collective-permute-start.6 = (bf16[16,128]{1,0:T(8,128)(2,1)S(1)}, bf16[16,128]{1,0:T(8,128)(2,1)S(1)}, u32[]{:S(2)}, u32[]{:S(2)}) collective-permute-start(bf16[16,128]{1,0:T(8,128)(2,1)S(1)} %get-tuple-element.43.mark_ref.refs_0_), channel_id=1, source_target_pairs={{0,2},{2,0},{1,3},{3,1},{4,6},{6,4},{5,7},{7,5},{8,10},{10,8},{9,1... | collective-permute-start | bytes 12296 | tf_op jit(solution)/shard_map/ppermute | solution.py:31

commit v17 on v15

--- a/solution.py
+++ b/solution.py
@@ -35,7 +35,7 @@
     return lax.broadcasted_iota(jnp.int32, shape, dim)
 
 
-LIMIT = 10
+LIMIT = 14
 VM = pl.BlockSpec(memory_space=pltpu.VMEM)
 HBM = pl.BlockSpec(memory_space=pltpu.HBM)
 
@@ -62,7 +62,7 @@
             dst[c, at : at + B, :] = value[a * B : (a + 1) * B, c * LANES : (c + 1) * LANES]
 
 
-def conv_blocks(src, count, w_ref, xs, dst, after=None):
+def conv_blocks(src, count, w_ref, xs, stage, dst, after=None):
     chunks = src.shape[0]
     blocks = chunks * GROUPS
 
@@ -72,9 +72,10 @@
             part = slice(h * LANES, (h + 1) * LANES)
             for g, here in enumerate(group_transpose(rows)):
                 at = 1 + c * GROUPS + g
-                xs[0, at, :, part] = pltpu.roll(here, 1, 0).astype(xs.dtype)
-                xs[1, at, :, part] = here.astype(xs.dtype)
-                xs[2, at, :, part] = pltpu.roll(here, count - 1, 0).astype(xs.dtype)
+                slot = (c * 2 + h) * GROUPS + g
+                stage[slot, 8 : 8 + count, :] = here
+                for q in range(3):
+                    xs[q, at, :, part] = stage[slot, 7 + q : 7 + q + count, :].astype(xs.dtype)
 
     def solve(c):
         b = c * GROUPS
@@ -152,7 +153,7 @@
 def first_kernel(
     note_ref, t_hbm, sci_hbm, bank_ref, index_ref, coeff_ref, psf_ref,
     w_ref, pcol_ref, prow_ref, sci_ref, m_ref, edge_ref, filt_ref,
-    t_ref, sems, src, xs, res, sci, diff,
+    t_ref, sems, src, xs, stage, res, sci, diff,
 ):
     copies = [
         pltpu.make_async_copy(t_hbm, t_ref, sems.at[0]), pltpu.make_async_copy(sci_hbm, sci_ref, sems.at[1])
@@ -210,7 +211,7 @@
     rows, cols = t_ref.shape
     off, _ = read_note(note_ref)
     to_blocks(src, 0, t_ref[...])
-    conv_blocks(src, rows // B, w_ref, xs, res)
+    conv_blocks(src, rows // B, w_ref, xs, stage, res)
     for a in range(1, rows // B - 1):
         m_ref[:, B * a : B * (a + 1), :] = res[:, PITCH * a : PITCH * a + B, :]
     to_chunks(sci, rows, sci_ref[...])
@@ -256,7 +257,7 @@
     note_ref, msg_ref, head_ref, sci_ref, m1_ref, w_ref, pcol_ref, prow_ref, edge_a, filt_a,
     *rest,
 ):
-    *outs, mark_ref, m_ref, src, xs, strip, diff, filt, sci, inner, edge_b, filt_b = rest
+    *outs, mark_ref, m_ref, src, xs, stage, strip, diff, filt, sci, inner, edge_b, filt_b = rest
     edge = 2 * B
     rows, cols = filt_a.shape[0] + edge, filt_a.shape[1]
     off_b, live_b, valid = read_before(msg_ref)
@@ -264,10 +265,9 @@
     to_blocks(src, 0, jnp.where(valid, msg_ref[...].astype(F32), 0.0))
     to_blocks(src, 2, note_ref[edge:, :])
     to_blocks(src, 4, note_ref[0:edge, :])
-    last = lax.axis_index("patch") == lax.axis_size("patch") - 1
-    to_blocks(src, 6, jnp.where(last, 0.0, head_ref[...].astype(F32)))
+    to_blocks(src, 6, head_ref[...])
     filter_inner(sci, rows - B - off_b, off_b - rows, off_b, m1_ref, pcol_ref, edge_b, filt_b, inner)
-    conv_blocks(src, 8, w_ref, xs, strip)
+    conv_blocks(src, 8, w_ref, xs, stage, strip)
     for n, a in enumerate((1, 2, 5, 6)):
         m_ref[:, B * n : B * (n + 1), :] = strip[:, PITCH * a : PITCH * a + B, :]
     off_a, live_a = read_note(note_ref)
@@ -333,7 +333,7 @@
 
 def tile_kernel(mark_ref, sci_ref, note_ref, m1_ref, edge_ref, w_ref, *rest):
     rows, cols = sci_ref.shape
-    *halves, out_hbm, src, xs, res, big, out, sems = rest
+    *halves, out_hbm, src, xs, stage, res, big, out, sems = rest
     bands = len(halves)
     blocks = rows // B // bands
     band = lax.axis_index("band")
@@ -357,7 +357,7 @@
         copies.append(pltpu.make_async_copy(out.at[:, there], out_hbm.at[:, there], sems.at[c]))
         copies[-1].start()
 
-    conv_blocks(src, rows // B, w_ref, xs, res, after)
+    conv_blocks(src, rows // B, w_ref, xs, stage, res, after)
     for copy in copies:
         copy.wait()
 
@@ -431,11 +431,12 @@
     half = shifted(half, "patch", -1)
     panels = lax.axis_size("patch")
     msg = lax.ppermute(msg, "patch", [(i, (i + 1) % panels) for i in range(panels)])
-    head = lax.ppermute(head, "patch", [((i + 1) % panels, i) for i in range(panels)])
+    head = shifted(head, "patch", -1)
     count = rows // B
     conv_scratch = [
         pltpu.VMEM((chunks, count * PITCH, LANES), F32),
         pltpu.VMEM((3, blocks + 2, count, CH), BF16),
+        pltpu.VMEM((2 * blocks, count + 16, LANES), F32),
         pltpu.VMEM((chunks, count * PITCH, LANES), F32),
     ]
     conv_flops = 2 * rows * cols * deep
@@ -460,6 +461,7 @@
         [
             pltpu.VMEM((chunks, 8 * PITCH, LANES), F32),
             pltpu.VMEM((3, blocks + 2, 8, CH), F32),
+            pltpu.VMEM((2 * blocks, 24, LANES), F32),
             pltpu.VMEM((chunks, 8 * PITCH, LANES), F32),
             pltpu.VMEM((4 * edge, cols), BF16),
             pltpu.VMEM((2, rows - share + depth, cols), BF16),

time: 29.2 us -> 28.9 us (0.990); the launches traced: 29 us -> 28.3 us
  starting transfers between devices: 12.5 us -> 11.3 us
    ppermute x1 -> x0, starting transfers between devices: 2.28 us -> none  [on_device(): lax.ppermute(head, 'patch', [((i + 1) % panels, i) for i in range(panels)])]
    ppermute x2 -> x3, starting transfers between devices: 6.24 us -> 7.53 us  [shifted(): return lax.ppermute(shard, axis, pairs)]
    ppermute x2 -> x3, waiting for transfers between devices: 0.27 us -> 1.03 us  [shifted(): return lax.ppermute(shard, axis, pairs)]
    ppermute x4, waiting for transfers between devices: 1.4 us -> 0.84 us  [swapped(): lax.ppermute(shard, axis, [(i, partner(i, k, devices)) for i in range(dev...]
    ppermute x1, waiting for transfers between devices: 0.02 us -> 0.43 us  [on_device(): lax.ppermute(msg, 'patch', [(i, (i + 1) % panels) for i in range(panels)])]
    ppermute x1 -> x0, waiting for transfers between devices: 0.35 us -> none  [on_device(): lax.ppermute(head, 'patch', [((i + 1) % panels, i) for i in range(panels)])]
  transfers between devices with their start and end apart: 8 -> 8, of which waited for: 4 -> 4; matrix products, arithmetic and copies ran while one was open for 0% -> 0% of each run, Pallas kernels for 40% -> 42%
where the time goes in v17:
time: 28.9 us; the launch traced here: 28.3 us
  Pallas kernels  12.7 us (44%)
  starting transfers between devices  11.3 us (39%)
  waiting for transfers between devices  2.31 us (8%)
  between operations  1.99 us (7%)
    ppermute x3, starting transfers between devices, shifted(): return lax.ppermute(shard, axis, pairs)  7.53 us
    pallas_call x1, Pallas kernels, on_device(): call(first_kernel, (sds((deep, CH), BF16), sds((cols, cols), BF16), sds((...  4.93 us
    pallas_call x1, Pallas kernels, on_device(): call(tile_kernel, sds((rows, cols), BF16), [VM] * (6 + bands), conv_scrat...  3.27 us
    pallas_call x1, Pallas kernels, on_device(): call(join_kernel, (sds((whole, cols), F32),) + (sds((whole + B, cols), BF...  2.33 us
    ppermute x4, starting transfers between devices, swapped(): lax.ppermute(shard, axis, [(i, partner(i, k, devices)) for i in range(dev...  2.16 us
    ppermute x1, starting transfers between devices, on_device(): lax.ppermute(msg, 'patch', [(i, (i + 1) % panels) for i in range(panels)])  1.6 us
    pallas_call x1, Pallas kernels, on_device(): call(pack_kernel, (sds((2 * edge, cols), BF16), sds((edge, cols), BF16),...  1.18 us
    ppermute x3, waiting for transfers between devices, shifted(): return lax.ppermute(shard, axis, pairs)  1.03 us
  transfers between devices with their start and end apart: 8, of which 4 were waited for; matrix products, arithmetic and copies ran while one was open for 0% of the time, Pallas kernels for 42%

profile of v17, /device:TPU:0, one launch (start us, length us, event | category | flops | bytes accessed | tf_op | source)
XLA Modules:
  0.0 28.3 jit_solution(15499489600542889970)
XLA Ops:
  0.6 5.0 %collective-permute-start.2 = (bf16[512,1,512]{2,0,1:T(8,128)(2,1)}, bf16[512,1,512]{2,0,1:T(8,128)(2,1)S(1)}, u32[]{:S(2)}, u32[]{:S(2)}) collective-permute-start(bf16[512,1,512]{2,0,1:T(8,128)(2,1)} %param.9), channel_id=1, source_target_pairs={{0,4},{4,8},{8,12},{1,5},{5,9},{9,13},{2,6},{6,10},{10,14},{3,7},{... | collective-permute-start | bytes 1572872 | tf_op jit(solution)/shard_map/ppermute | solution.py:22
  6.9 1.2 %pack.1 = (bf16[64,512]{1,0:T(8,128)(2,1)S(1)}, bf16[32,512]{1,0:T(8,128)(2,1)S(1)}, bf16[32,512]{1,0:T(8,128)(2,1)S(1)}, bf16[256,512]{1,0:T(8,128)(2,1)S(1)}, ...) custom-call(s32[1,1]{1,0:T(1,128)S(6)} %copy.10.off_hbm, ...), custom_call_target="tpu_custom_call" | custom-call | flops 1048576 | bytes 2097152 | tf_op jit(solution)/shard_map/pack/pallas_call | solution.py:420
  8.1 1.6 %collective-permute-start = (bf16[32,512]{1,0:T(8,128)(2,1)S(1)}, bf16[32,512]{1,0:T(8,128)(2,1)S(1)}, u32[]{:S(2)}, u32[]{:S(2)}) collective-permute-start(bf16[32,512]{1,0:T(8,128)(2,1)S(1)} %get-tuple-element.25), channel_id=1, source_target_pairs={{0,4},{4,8},{8,12},{12,0},{1,5},{5,9},{9,13},{13,1},{2,6},{6,10},{... | collective-permute-start | bytes 98312 | tf_op jit(solution)/shard_map/ppermute | solution.py:433
  9.7 1.3 %collective-permute-start.1 = (bf16[32,512]{1,0:T(8,128)(2,1)S(1)}, bf16[32,512]{1,0:T(8,128)(2,1)S(1)}, u32[]{:S(2)}, u32[]{:S(2)}) collective-permute-start(bf16[32,512]{1,0:T(8,128)(2,1)S(1)} %get-tuple-element.26), channel_id=1, source_target_pairs={{4,0},{8,4},{12,8},{5,1},{9,5},{13,9},{6,2},{10,6},{14,10},{7,3},{... | collective-permute-start | bytes 98312 | tf_op jit(solution)/shard_map/ppermute | solution.py:22
  11.0 1.3 %collective-permute-start.4 = (bf16[256,512]{1,0:T(8,128)(2,1)S(1)}, bf16[256,512]{1,0:T(8,128)(2,1)S(1)}, u32[]{:S(2)}, u32[]{:S(2)}) collective-permute-start(bf16[256,512]{1,0:T(8,128)(2,1)S(1)} %get-tuple-element.43), channel_id=1, source_target_pairs={{4,0},{8,4},{12,8},{5,1},{9,5},{13,9},{6,2},{10,6},{14,10},{7,3},{... | collective-permute-start | bytes 786440 | tf_op jit(solution)/shard_map/ppermute | solution.py:22
  12.3 4.9 %first.1 = (bf16[2304,256]{1,0:T(8,128)(2,1)S(1)}, bf16[512,512]{1,0:T(8,128)(2,1)S(1)}, bf16[128,256]{1,0:T(8,128)(2,1)S(1)}, bf16[512,512]{1,0:T(8,128)(2,1)S(...) custom-call(bf16[64,512]{1,0:T(8,128)(2,1)S(1)} %get-tuple-element.24.note_ref, ...), custom_call_target="tpu_custom_call" | custom-call | flops 1207959552 | bytes 2097152 | tf_op jit(solution)/shard_map/first/pallas_call | solution.py:445
  17.2 0.4 %collective-permute-done.msg_ref = bf16[32,512]{1,0:T(8,128)(2,1)S(1)} collective-permute-done((bf16[32,512]{1,0:T(8,128)(2,1)S(1)}, bf16[32,512]{1,0:T(8,128)(2,1)S(1)}, u32[]{:S(2)}, u32[]{:S(2)}) %collective-permute-start) | collective-permute-done | bytes 32800 | tf_op jit(solution)/shard_map/ppermute | solution.py:433
  17.6 0.0 collective-permute-done.1.head_ref
  17.6 0.0 collective-permute-done.2
  17.7 2.3 %join.1 = (f32[256,512]{1,0:T(8,128)S(1)}, bf16[272,512]{1,0:T(8,128)(2,1)S(1)}, bf16[16,128]{1,0:T(8,128)(2,1)S(1)}, f32[4,64,128]{2,1,0:T(8,128)S(1)}) custom-call(bf16[64,512]{1,0:T(8,128)(2,1)S(1)} %get-tuple-element.24.note_ref, bf16[32,512]{1,0:T(8,128)(2,1)S(1)} %collective-permute-done.msg_ref, bf16[32,512]{1,0:T(8,128)(2,1)S(1)} %collective-permute-done.1.head_ref, ...), custom_call_target="tpu_custom_call" | custom-call | flops 17179869184 | bytes 2097152 | tf_op jit(solution)/shard_map/join/pallas_call | solution.py:456
  20.0 0.1 collective-permute-start.3
  20.1 1.0 %collective-permute-done.4.rest_0_ = bf16[256,512]{1,0:T(8,128)(2,1)S(1)} collective-permute-done((bf16[256,512]{1,0:T(8,128)(2,1)S(1)}, bf16[256,512]{1,0:T(8,128)(2,1)S(1)}, u32[]{:S(2)}, u32[]{:S(2)}) %collective-permute-start.4) | collective-permute-done | bytes 262176 | tf_op jit(solution)/shard_map/ppermute | solution.py:22
  21.1 0.0 collective-permute-start.5
  21.1 0.5 %collective-permute-done.3.refs_2_ = bf16[272,512]{1,0:T(8,128)(2,1)S(1)} collective-permute-done((bf16[272,512]{1,0:T(8,128)(2,1)S(1)}, bf16[272,512]{1,0:T(8,128)(2,1)S(1)}, u32[]{:S(2)}, u32[]{:S(2)}) %collective-permute-start.3) | collective-permute-done | bytes 278560 | tf_op jit(solution)/shard_map/ppermute | solution.py:31
  21.7 1.6 %collective-permute-start.7 = (bf16[128,512]{1,0:T(8,128)(2,1)S(1)}, bf16[128,512]{1,0:T(8,128)(2,1)S(1)}, u32[]{:S(2)}, u32[]{:S(2)}) collective-permute-start(bf16[128,512]{1,0:T(8,128)(2,1)S(1)} %get-tuple-element.45), channel_id=1, source_target_pairs={{0,2},{2,0},{1,3},{3,1},{4,6},{6,4},{5,7},{7,5},{8,10},{10,8},{9,1... | collective-permute-start | bytes 393224 | tf_op jit(solution)/shard_map/ppermute | solution.py:31
  23.3 0.5 %collective-permute-start.6 = (bf16[16,128]{1,0:T(8,128)(2,1)S(1)}, bf16[16,128]{1,0:T(8,128)(2,1)S(1)}, u32[]{:S(2)}, u32[]{:S(2)}) collective-permute-start(bf16[16,128]{1,0:T(8,128)(2,1)S(1)} %get-tuple-element.40.mark_ref.refs_0_), channel_id=1, source_target_pairs={{0,2},{2,0},{1,3},{3,1},{4,6},{6,4},{5,7},{7,5},{8,10},{10,8},{9,1... | collective-permute-start | bytes 12296 | tf_op jit(solution)/shard_map/ppermute | solution.py:31
  23.8 0.0 collective-permute-done.5.rest_1_
  23.8 3.3 %tile.1 = bf16[512,512]{1,0:T(8,128)(2,1)} custom-call(bf16[16,128]{1,0:T(8,128)(2,1)S(1)} %get-tuple-element.40.mark_ref.refs_0_, bf16[512,512]{1,0:T(8,128)(2,1)S(1)} %get-tuple-element.41.sci_ref, bf16[64,512]{1,0:T(8,128)(2,1)S(1)} %get-tuple-element.24.note_ref, f32[4,512,128]{2,1,0:T(8,128)S(1)} %get-tuple-element.31.m1_ref, ...), custom_call_target="tpu_custom_call" | custom-call | flops 1207959552 | bytes 2097152 | tf_op jit(solution)/shard_map/tile/pallas_call | solution.py:480
  27.0 0.3 %collective-permute-done.6.refs_1_ = bf16[16,128]{1,0:T(8,128)(2,1)S(1)} collective-permute-done((bf16[16,128]{1,0:T(8,128)(2,1)S(1)}, bf16[16,128]{1,0:T(8,128)(2,1)S(1)}, u32[]{:S(2)}, u32[]{:S(2)}) %collective-permute-start.6) | collective-permute-done | bytes 4128 | tf_op jit(solution)/shard_map/ppermute | solution.py:31
  27.4 0.0 collective-permute-done.7.refs_3_
  27.4 1.0 %coadd.1 = f32[128,512]{1,0:T(8,128)} custom-call(bf16[16,128]{1,0:T(8,128)(2,1)S(1)} %get-tuple-element.40.mark_ref.refs_0_, bf16[16,128]{1,0:T(8,128)(2,1)S(1)} %collective-permute-done.6.refs_1_, f32[128,512]{1,0:T(8,128)S(1)} %get-tuple-element.44.refs_2_, bf16[128,512]{1,0:T(8,128)(2,1)S(1)} %collective-permute-done.7.refs_3_), custom_call_target="tpu_custom_call" | custom-call | flops 1048576 | bytes 2097152 | tf_op jit(solution)/shard_map/coadd/pallas_call | solution.py:488
  (1 shorter events, 0.0 us)
Async XLA Ops:
  0.6 17.0 %collective-permute-start.2 = (bf16[512,1,512]{2,0,1:T(8,128)(2,1)}, bf16[512,1,512]{2,0,1:T(8,128)(2,1)S(1)}, u32[]{:S(2)}, u32[]{:S(2)}) collective-permute-start(bf16[512,1,512]{2,0,1:T(8,128)(2,1)} %param.9), channel_id=1, source_target_pairs={{0,4},{4,8},{8,12},{1,5},{5,9},{9,13},{2,6},{6,10},{10,14},{3,7},{... | collective-permute-start | bytes 1572872 | tf_op jit(solution)/shard_map/ppermute | solution.py:22
  8.1 9.6 %collective-permute-start = (bf16[32,512]{1,0:T(8,128)(2,1)S(1)}, bf16[32,512]{1,0:T(8,128)(2,1)S(1)}, u32[]{:S(2)}, u32[]{:S(2)}) collective-permute-start(bf16[32,512]{1,0:T(8,128)(2,1)S(1)} %get-tuple-element.25), channel_id=1, source_target_pairs={{0,4},{4,8},{8,12},{12,0},{1,5},{5,9},{9,13},{13,1},{2,6},{6,10},{... | collective-permute-start | bytes 98312 | tf_op jit(solution)/shard_map/ppermute | solution.py:433
  9.7 8.0 %collective-permute-start.1 = (bf16[32,512]{1,0:T(8,128)(2,1)S(1)}, bf16[32,512]{1,0:T(8,128)(2,1)S(1)}, u32[]{:S(2)}, u32[]{:S(2)}) collective-permute-start(bf16[32,512]{1,0:T(8,128)(2,1)S(1)} %get-tuple-element.26), channel_id=1, source_target_pairs={{4,0},{8,4},{12,8},{5,1},{9,5},{13,9},{6,2},{10,6},{14,10},{7,3},{... | collective-permute-start | bytes 98312 | tf_op jit(solution)/shard_map/ppermute | solution.py:22
  11.0 10.1 %collective-permute-start.4 = (bf16[256,512]{1,0:T(8,128)(2,1)S(1)}, bf16[256,512]{1,0:T(8,128)(2,1)S(1)}, u32[]{:S(2)}, u32[]{:S(2)}) collective-permute-start(bf16[256,512]{1,0:T(8,128)(2,1)S(1)} %get-tuple-element.43), channel_id=1, source_target_pairs={{4,0},{8,4},{12,8},{5,1},{9,5},{13,9},{6,2},{10,6},{14,10},{7,3},{... | collective-permute-start | bytes 786440 | tf_op jit(solution)/shard_map/ppermute | solution.py:22
  20.0 1.6 %collective-permute-start.3 = (bf16[272,512]{1,0:T(8,128)(2,1)S(1)}, bf16[272,512]{1,0:T(8,128)(2,1)S(1)}, u32[]{:S(2)}, u32[]{:S(2)}) collective-permute-start(bf16[272,512]{1,0:T(8,128)(2,1)S(1)} %get-tuple-element.39), channel_id=1, source_target_pairs={{0,1},{1,0},{2,3},{3,2},{4,5},{5,4},{6,7},{7,6},{8,9},{9,8},{10,11... | collective-permute-start | bytes 835592 | tf_op jit(solution)/shard_map/ppermute | solution.py:31
  21.1 2.7 %collective-permute-start.5 = (bf16[256,512]{1,0:T(8,128)(2,1)S(1)}, bf16[256,512]{1,0:T(8,128)(2,1)S(1)}, u32[]{:S(2)}, u32[]{:S(2)}) collective-permute-start(bf16[256,512]{1,0:T(8,128)(2,1)S(1)} %collective-permute-done.4.rest_0_), channel_id=1, source_target_pairs={{0,1},{1,0},{2,3},{3,2},{4,5},{5,4},{6,7},{7,6},{8,9},{9,8},{10,11... | collective-permute-start | bytes 786440 | tf_op jit(solution)/shard_map/ppermute | solution.py:31
  21.7 5.7 %collective-permute-start.7 = (bf16[128,512]{1,0:T(8,128)(2,1)S(1)}, bf16[128,512]{1,0:T(8,128)(2,1)S(1)}, u32[]{:S(2)}, u32[]{:S(2)}) collective-permute-start(bf16[128,512]{1,0:T(8,128)(2,1)S(1)} %get-tuple-element.45), channel_id=1, source_target_pairs={{0,2},{2,0},{1,3},{3,1},{4,6},{6,4},{5,7},{7,5},{8,10},{10,8},{9,1... | collective-permute-start | bytes 393224 | tf_op jit(solution)/shard_map/ppermute | solution.py:31
  23.3 4.1 %collective-permute-start.6 = (bf16[16,128]{1,0:T(8,128)(2,1)S(1)}, bf16[16,128]{1,0:T(8,128)(2,1)S(1)}, u32[]{:S(2)}, u32[]{:S(2)}) collective-permute-start(bf16[16,128]{1,0:T(8,128)(2,1)S(1)} %get-tuple-element.40.mark_ref.refs_0_), channel_id=1, source_target_pairs={{0,2},{2,0},{1,3},{3,1},{4,6},{6,4},{5,7},{7,5},{8,10},{10,8},{9,1... | collective-permute-start | bytes 12296 | tf_op jit(solution)/shard_map/ppermute | solution.py:31

commit v18 on v15

--- a/solution.py
+++ b/solution.py
@@ -35,7 +35,7 @@
     return lax.broadcasted_iota(jnp.int32, shape, dim)
 
 
-LIMIT = 10
+LIMIT = 14
 VM = pl.BlockSpec(memory_space=pltpu.VMEM)
 HBM = pl.BlockSpec(memory_space=pltpu.HBM)
 
@@ -152,7 +152,7 @@
 def first_kernel(
     note_ref, t_hbm, sci_hbm, bank_ref, index_ref, coeff_ref, psf_ref,
     w_ref, pcol_ref, prow_ref, sci_ref, m_ref, edge_ref, filt_ref,
-    t_ref, sems, src, xs, res, sci, diff,
+    t_ref, sems, src, xs, sci, diff,
 ):
     copies = [
         pltpu.make_async_copy(t_hbm, t_ref, sems.at[0]), pltpu.make_async_copy(sci_hbm, sci_ref, sems.at[1])
@@ -210,9 +210,7 @@
     rows, cols = t_ref.shape
     off, _ = read_note(note_ref)
     to_blocks(src, 0, t_ref[...])
-    conv_blocks(src, rows // B, w_ref, xs, res)
-    for a in range(1, rows // B - 1):
-        m_ref[:, B * a : B * (a + 1), :] = res[:, PITCH * a : PITCH * a + B, :]
+    conv_blocks(src, rows // B, w_ref, xs, m_ref)
     to_chunks(sci, rows, sci_ref[...])
     filter_inner(sci, rows - B - off, off, off + rows, m_ref, pcol_ref, edge_ref, filt_ref, diff)
 
@@ -230,14 +228,15 @@
 
 
 def filter_inner(sci, start, first, last, m_ref, pcol_ref, edge_ref, filt_ref, diff):
-    chunks, rows, _ = m_ref.shape
-    edge = 2 * B
+    chunks, blocks = m_ref.shape[0], m_ref.shape[1] // PITCH
+    rows, edge = blocks * B, 2 * B
     for c in range(chunks):
         part = slice(c * LANES, (c + 1) * LANES)
         sky = sci[c, pl.ds(start, rows + edge), :]
+        inner = jnp.concatenate([m_ref[c, PITCH * a : PITCH * a + B, :] for a in range(1, blocks - 1)], axis=0)
         edge_ref[c, 0:edge, :] = sky[0:edge]
         edge_ref[c, edge:, :] = sky[rows:]
-        diff[:, part] = tile_diff(sky[edge:rows], m_ref[c, B : rows - B, :], edge, first, last)
+        diff[:, part] = tile_diff(sky[edge:rows], inner, edge, first, last)
     filt_ref[...] = jnp.dot(diff[...], pcol_ref[...], preferred_element_type=F32).astype(BF16)
 
 
@@ -264,8 +263,7 @@
     to_blocks(src, 0, jnp.where(valid, msg_ref[...].astype(F32), 0.0))
     to_blocks(src, 2, note_ref[edge:, :])
     to_blocks(src, 4, note_ref[0:edge, :])
-    last = lax.axis_index("patch") == lax.axis_size("patch") - 1
-    to_blocks(src, 6, jnp.where(last, 0.0, head_ref[...].astype(F32)))
+    to_blocks(src, 6, head_ref[...])
     filter_inner(sci, rows - B - off_b, off_b - rows, off_b, m1_ref, pcol_ref, edge_b, filt_b, inner)
     conv_blocks(src, 8, w_ref, xs, strip)
     for n, a in enumerate((1, 2, 5, 6)):
@@ -347,7 +345,8 @@
 
     def after(c):
         big[c, 0:B, :] = edge_ref[c, B : 2 * B, :]
-        big[c, B : rows - B, :] = m1_ref[c, B : rows - B, :]
+        for a in range(1, rows // B - 1):
+            big[c, B * a : B * (a + 1), :] = m1_ref[c, PITCH * a : PITCH * a + B, :]
         big[c, rows - B : rows + B, :] = edge_ref[c, 2 * B : 4 * B, :]
         for a in range(1, rows // B):
             big[c, rows + B * a : rows + B * (a + 1), :] = res[c, PITCH * a : PITCH * a + B, :]
@@ -431,7 +430,7 @@
     half = shifted(half, "patch", -1)
     panels = lax.axis_size("patch")
     msg = lax.ppermute(msg, "patch", [(i, (i + 1) % panels) for i in range(panels)])
-    head = lax.ppermute(head, "patch", [((i + 1) % panels, i) for i in range(panels)])
+    head = shifted(head, "patch", -1)
     count = rows // B
     conv_scratch = [
         pltpu.VMEM((chunks, count * PITCH, LANES), F32),
@@ -445,10 +444,10 @@
         first_kernel,
         (
             sds((deep, CH), BF16), sds((cols, cols), BF16), sds((share, depth), BF16),
-            sds((rows, cols), BF16), sds((chunks, rows, LANES), F32),
+            sds((rows, cols), BF16), sds((chunks, count * PITCH, LANES), F32),
         ) + sides,
         [VM, HBM, HBM] + [VM] * 4,
-        [pltpu.VMEM((rows, cols), BF16), pltpu.SemaphoreType.DMA((2,))] + conv_scratch + sky_scratch,
+        [pltpu.VMEM((rows, cols), BF16), pltpu.SemaphoreType.DMA((2,))] + conv_scratch[:2] + sky_scratch,
         conv_flops, "first",
     )(note, *held, *small)
     whole = visits * share

time: 29.2 us -> 28.6 us (0.979)
  starting transfers between devices: 12.5 us -> 11.3 us
  waiting for transfers between devices: 2.03 us -> 2.52 us
    ppermute x1 -> x0, starting transfers between devices: 2.28 us -> none  [on_device(): lax.ppermute(head, 'patch', [((i + 1) % panels, i) for i in range(panels)])]
    ppermute x2 -> x3, starting transfers between devices: 6.24 us -> 7.53 us  [shifted(): return lax.ppermute(shard, axis, pairs)]
    ppermute x2 -> x3, waiting for transfers between devices: 0.27 us -> 1.07 us  [shifted(): return lax.ppermute(shard, axis, pairs)]
    ppermute x1, waiting for transfers between devices: 0.02 us -> 0.62 us  [on_device(): lax.ppermute(msg, 'patch', [(i, (i + 1) % panels) for i in range(panels)])]
    ppermute x4, waiting for transfers between devices: 1.4 us -> 0.83 us  [swapped(): lax.ppermute(shard, axis, [(i, partner(i, k, devices)) for i in range(dev...]
    ppermute x1 -> x0, waiting for transfers between devices: 0.35 us -> none  [on_device(): lax.ppermute(head, 'patch', [((i + 1) % panels, i) for i in range(panels)])]
  transfers between devices with their start and end apart: 8 -> 8, of which waited for: 4 -> 4; matrix products, arithmetic and copies ran while one was open for 0% -> 0% of each run, Pallas kernels for 40% -> 41%
where the time goes in v18:
time: 28.6 us; the launch traced here: 28.3 us
  Pallas kernels  12.5 us (44%)
  starting transfers between devices  11.3 us (40%)
  waiting for transfers between devices  2.52 us (9%)
  between operations  1.99 us (7%)
    ppermute x3, starting transfers between devices, shifted(): return lax.ppermute(shard, axis, pairs)  7.53 us
    pallas_call x1, Pallas kernels, on_device(): call(first_kernel, (sds((deep, CH), BF16), sds((cols, cols), BF16), sds((...  4.75 us
    pallas_call x1, Pallas kernels, on_device(): call(tile_kernel, sds((rows, cols), BF16), [VM] * (6 + bands), conv_scrat...  3.24 us
    pallas_call x1, Pallas kernels, on_device(): call(join_kernel, (sds((whole, cols), F32),) + (sds((whole + B, cols), BF...  2.29 us
    ppermute x4, starting transfers between devices, swapped(): lax.ppermute(shard, axis, [(i, partner(i, k, devices)) for i in range(dev...  2.16 us
    ppermute x1, starting transfers between devices, on_device(): lax.ppermute(msg, 'patch', [(i, (i + 1) % panels) for i in range(panels)])  1.6 us
    pallas_call x1, Pallas kernels, on_device(): call(pack_kernel, (sds((2 * edge, cols), BF16), sds((edge, cols), BF16),...  1.18 us
    ppermute x3, waiting for transfers between devices, shifted(): return lax.ppermute(shard, axis, pairs)  1.07 us
  transfers between devices with their start and end apart: 8, of which 4 were waited for; matrix products, arithmetic and copies ran while one was open for 0% of the time, Pallas kernels for 41%

profile of v18, /device:TPU:0, one launch (start us, length us, event | category | flops | bytes accessed | tf_op | source)
XLA Modules:
  0.0 28.3 jit_solution(17427185426985500638)
XLA Ops:
  0.6 5.0 %collective-permute-start.2 = (bf16[512,1,512]{2,0,1:T(8,128)(2,1)}, bf16[512,1,512]{2,0,1:T(8,128)(2,1)S(1)}, u32[]{:S(2)}, u32[]{:S(2)}) collective-permute-start(bf16[512,1,512]{2,0,1:T(8,128)(2,1)} %param.9), channel_id=1, source_target_pairs={{0,4},{4,8},{8,12},{1,5},{5,9},{9,13},{2,6},{6,10},{10,14},{3,7},{... | collective-permute-start | bytes 1572872 | tf_op jit(solution)/shard_map/ppermute | solution.py:22
  6.9 1.2 %pack.1 = (bf16[64,512]{1,0:T(8,128)(2,1)S(1)}, bf16[32,512]{1,0:T(8,128)(2,1)S(1)}, bf16[32,512]{1,0:T(8,128)(2,1)S(1)}, bf16[256,512]{1,0:T(8,128)(2,1)S(1)}, ...) custom-call(s32[1,1]{1,0:T(1,128)S(6)} %copy.10.off_hbm, ...), custom_call_target="tpu_custom_call" | custom-call | flops 1048576 | bytes 2097152 | tf_op jit(solution)/shard_map/pack/pallas_call | solution.py:419
  8.1 1.6 %collective-permute-start = (bf16[32,512]{1,0:T(8,128)(2,1)S(1)}, bf16[32,512]{1,0:T(8,128)(2,1)S(1)}, u32[]{:S(2)}, u32[]{:S(2)}) collective-permute-start(bf16[32,512]{1,0:T(8,128)(2,1)S(1)} %get-tuple-element.25), channel_id=1, source_target_pairs={{0,4},{4,8},{8,12},{12,0},{1,5},{5,9},{9,13},{13,1},{2,6},{6,10},{... | collective-permute-start | bytes 98312 | tf_op jit(solution)/shard_map/ppermute | solution.py:432
  9.7 1.3 %collective-permute-start.1 = (bf16[32,512]{1,0:T(8,128)(2,1)S(1)}, bf16[32,512]{1,0:T(8,128)(2,1)S(1)}, u32[]{:S(2)}, u32[]{:S(2)}) collective-permute-start(bf16[32,512]{1,0:T(8,128)(2,1)S(1)} %get-tuple-element.26), channel_id=1, source_target_pairs={{4,0},{8,4},{12,8},{5,1},{9,5},{13,9},{6,2},{10,6},{14,10},{7,3},{... | collective-permute-start | bytes 98312 | tf_op jit(solution)/shard_map/ppermute | solution.py:22
  11.0 1.3 %collective-permute-start.4 = (bf16[256,512]{1,0:T(8,128)(2,1)S(1)}, bf16[256,512]{1,0:T(8,128)(2,1)S(1)}, u32[]{:S(2)}, u32[]{:S(2)}) collective-permute-start(bf16[256,512]{1,0:T(8,128)(2,1)S(1)} %get-tuple-element.43), channel_id=1, source_target_pairs={{4,0},{8,4},{12,8},{5,1},{9,5},{13,9},{6,2},{10,6},{14,10},{7,3},{... | collective-permute-start | bytes 786440 | tf_op jit(solution)/shard_map/ppermute | solution.py:22
  12.3 4.7 %first.1 = (bf16[2304,256]{1,0:T(8,128)(2,1)S(1)}, bf16[512,512]{1,0:T(8,128)(2,1)S(1)}, bf16[128,256]{1,0:T(8,128)(2,1)S(1)}, bf16[512,512]{1,0:T(8,128)(2,1)S(...) custom-call(bf16[64,512]{1,0:T(8,128)(2,1)S(1)} %get-tuple-element.24.note_ref, ...), custom_call_target="tpu_custom_call" | custom-call | flops 1207959552 | bytes 2097152 | tf_op jit(solution)/shard_map/first/pallas_call | solution.py:443
  17.0 0.6 %collective-permute-done.msg_ref = bf16[32,512]{1,0:T(8,128)(2,1)S(1)} collective-permute-done((bf16[32,512]{1,0:T(8,128)(2,1)S(1)}, bf16[32,512]{1,0:T(8,128)(2,1)S(1)}, u32[]{:S(2)}, u32[]{:S(2)}) %collective-permute-start) | collective-permute-done | bytes 32800 | tf_op jit(solution)/shard_map/ppermute | solution.py:432
  17.6 0.0 collective-permute-done.1.head_ref
  17.6 0.0 collective-permute-done.2
  17.7 2.3 %join.1 = (f32[256,512]{1,0:T(8,128)S(1)}, bf16[272,512]{1,0:T(8,128)(2,1)S(1)}, bf16[16,128]{1,0:T(8,128)(2,1)S(1)}, f32[4,64,128]{2,1,0:T(8,128)S(1)}) custom-call(bf16[64,512]{1,0:T(8,128)(2,1)S(1)} %get-tuple-element.24.note_ref, bf16[32,512]{1,0:T(8,128)(2,1)S(1)} %collective-permute-done.msg_ref, bf16[32,512]{1,0:T(8,128)(2,1)S(1)} %collective-permute-done.1.head_ref, ...), custom_call_target="tpu_custom_call" | custom-call | flops 17179869184 | bytes 2097152 | tf_op jit(solution)/shard_map/join/pallas_call | solution.py:454
  20.0 0.1 collective-permute-start.3
  20.0 1.1 %collective-permute-done.4.rest_0_ = bf16[256,512]{1,0:T(8,128)(2,1)S(1)} collective-permute-done((bf16[256,512]{1,0:T(8,128)(2,1)S(1)}, bf16[256,512]{1,0:T(8,128)(2,1)S(1)}, u32[]{:S(2)}, u32[]{:S(2)}) %collective-permute-start.4) | collective-permute-done | bytes 262176 | tf_op jit(solution)/shard_map/ppermute | solution.py:22
  21.1 0.0 collective-permute-start.5
  21.1 0.5 %collective-permute-done.3.refs_2_ = bf16[272,512]{1,0:T(8,128)(2,1)S(1)} collective-permute-done((bf16[272,512]{1,0:T(8,128)(2,1)S(1)}, bf16[272,512]{1,0:T(8,128)(2,1)S(1)}, u32[]{:S(2)}, u32[]{:S(2)}) %collective-permute-start.3) | collective-permute-done | bytes 278560 | tf_op jit(solution)/shard_map/ppermute | solution.py:31
  21.6 1.6 %collective-permute-start.7 = (bf16[128,512]{1,0:T(8,128)(2,1)S(1)}, bf16[128,512]{1,0:T(8,128)(2,1)S(1)}, u32[]{:S(2)}, u32[]{:S(2)}) collective-permute-start(bf16[128,512]{1,0:T(8,128)(2,1)S(1)} %get-tuple-element.45), channel_id=1, source_target_pairs={{0,2},{2,0},{1,3},{3,1},{4,6},{6,4},{5,7},{7,5},{8,10},{10,8},{9,1... | collective-permute-start | bytes 393224 | tf_op jit(solution)/shard_map/ppermute | solution.py:31
  23.2 0.5 %collective-permute-start.6 = (bf16[16,128]{1,0:T(8,128)(2,1)S(1)}, bf16[16,128]{1,0:T(8,128)(2,1)S(1)}, u32[]{:S(2)}, u32[]{:S(2)}) collective-permute-start(bf16[16,128]{1,0:T(8,128)(2,1)S(1)} %get-tuple-element.40.mark_ref.refs_0_), channel_id=1, source_target_pairs={{0,2},{2,0},{1,3},{3,1},{4,6},{6,4},{5,7},{7,5},{8,10},{10,8},{9,1... | collective-permute-start | bytes 12296 | tf_op jit(solution)/shard_map/ppermute | solution.py:31
  23.7 0.0 collective-permute-done.5.rest_1_
  23.7 3.2 %tile.1 = bf16[512,512]{1,0:T(8,128)(2,1)} custom-call(bf16[16,128]{1,0:T(8,128)(2,1)S(1)} %get-tuple-element.40.mark_ref.refs_0_, bf16[512,512]{1,0:T(8,128)(2,1)S(1)} %get-tuple-element.41.sci_ref, bf16[64,512]{1,0:T(8,128)(2,1)S(1)} %get-tuple-element.24.note_ref, f32[4,544,128]{2,1,0:T(8,128)S(1)} %get-tuple-element.31.m1_ref, ...), custom_call_target="tpu_custom_call" | custom-call | flops 1207959552 | bytes 2097152 | tf_op jit(solution)/shard_map/tile/pallas_call | solution.py:477
  27.0 0.3 %collective-permute-done.6.refs_1_ = bf16[16,128]{1,0:T(8,128)(2,1)S(1)} collective-permute-done((bf16[16,128]{1,0:T(8,128)(2,1)S(1)}, bf16[16,128]{1,0:T(8,128)(2,1)S(1)}, u32[]{:S(2)}, u32[]{:S(2)}) %collective-permute-start.6) | collective-permute-done | bytes 4128 | tf_op jit(solution)/shard_map/ppermute | solution.py:31
  27.3 0.0 collective-permute-done.7.refs_3_
  27.3 1.0 %coadd.1 = f32[128,512]{1,0:T(8,128)} custom-call(bf16[16,128]{1,0:T(8,128)(2,1)S(1)} %get-tuple-element.40.mark_ref.refs_0_, bf16[16,128]{1,0:T(8,128)(2,1)S(1)} %collective-permute-done.6.refs_1_, f32[128,512]{1,0:T(8,128)S(1)} %get-tuple-element.44.refs_2_, bf16[128,512]{1,0:T(8,128)(2,1)S(1)} %collective-permute-done.7.refs_3_), custom_call_target="tpu_custom_call" | custom-call | flops 1048576 | bytes 2097152 | tf_op jit(solution)/shard_map/coadd/pallas_call | solution.py:485
  (1 shorter events, 0.0 us)
Async XLA Ops:
  0.6 17.0 %collective-permute-start.2 = (bf16[512,1,512]{2,0,1:T(8,128)(2,1)}, bf16[512,1,512]{2,0,1:T(8,128)(2,1)S(1)}, u32[]{:S(2)}, u32[]{:S(2)}) collective-permute-start(bf16[512,1,512]{2,0,1:T(8,128)(2,1)} %param.9), channel_id=1, source_target_pairs={{0,4},{4,8},{8,12},{1,5},{5,9},{9,13},{2,6},{6,10},{10,14},{3,7},{... | collective-permute-start | bytes 1572872 | tf_op jit(solution)/shard_map/ppermute | solution.py:22
  8.1 9.6 %collective-permute-start = (bf16[32,512]{1,0:T(8,128)(2,1)S(1)}, bf16[32,512]{1,0:T(8,128)(2,1)S(1)}, u32[]{:S(2)}, u32[]{:S(2)}) collective-permute-start(bf16[32,512]{1,0:T(8,128)(2,1)S(1)} %get-tuple-element.25), channel_id=1, source_target_pairs={{0,4},{4,8},{8,12},{12,0},{1,5},{5,9},{9,13},{13,1},{2,6},{6,10},{... | collective-permute-start | bytes 98312 | tf_op jit(solution)/shard_map/ppermute | solution.py:432
  9.7 8.0 %collective-permute-start.1 = (bf16[32,512]{1,0:T(8,128)(2,1)S(1)}, bf16[32,512]{1,0:T(8,128)(2,1)S(1)}, u32[]{:S(2)}, u32[]{:S(2)}) collective-permute-start(bf16[32,512]{1,0:T(8,128)(2,1)S(1)} %get-tuple-element.26), channel_id=1, source_target_pairs={{4,0},{8,4},{12,8},{5,1},{9,5},{13,9},{6,2},{10,6},{14,10},{7,3},{... | collective-permute-start | bytes 98312 | tf_op jit(solution)/shard_map/ppermute | solution.py:22
  11.0 10.1 %collective-permute-start.4 = (bf16[256,512]{1,0:T(8,128)(2,1)S(1)}, bf16[256,512]{1,0:T(8,128)(2,1)S(1)}, u32[]{:S(2)}, u32[]{:S(2)}) collective-permute-start(bf16[256,512]{1,0:T(8,128)(2,1)S(1)} %get-tuple-element.43), channel_id=1, source_target_pairs={{4,0},{8,4},{12,8},{5,1},{9,5},{13,9},{6,2},{10,6},{14,10},{7,3},{... | collective-permute-start | bytes 786440 | tf_op jit(solution)/shard_map/ppermute | solution.py:22
  20.0 1.6 %collective-permute-start.3 = (bf16[272,512]{1,0:T(8,128)(2,1)S(1)}, bf16[272,512]{1,0:T(8,128)(2,1)S(1)}, u32[]{:S(2)}, u32[]{:S(2)}) collective-permute-start(bf16[272,512]{1,0:T(8,128)(2,1)S(1)} %get-tuple-element.39), channel_id=1, source_target_pairs={{0,1},{1,0},{2,3},{3,2},{4,5},{5,4},{6,7},{7,6},{8,9},{9,8},{10,11... | collective-permute-start | bytes 835592 | tf_op jit(solution)/shard_map/ppermute | solution.py:31
  21.1 2.6 %collective-permute-start.5 = (bf16[256,512]{1,0:T(8,128)(2,1)S(1)}, bf16[256,512]{1,0:T(8,128)(2,1)S(1)}, u32[]{:S(2)}, u32[]{:S(2)}) collective-permute-start(bf16[256,512]{1,0:T(8,128)(2,1)S(1)} %collective-permute-done.4.rest_0_), channel_id=1, source_target_pairs={{0,1},{1,0},{2,3},{3,2},{4,5},{5,4},{6,7},{7,6},{8,9},{9,8},{10,11... | collective-permute-start | bytes 786440 | tf_op jit(solution)/shard_map/ppermute | solution.py:31
  21.6 5.7 %collective-permute-start.7 = (bf16[128,512]{1,0:T(8,128)(2,1)S(1)}, bf16[128,512]{1,0:T(8,128)(2,1)S(1)}, u32[]{:S(2)}, u32[]{:S(2)}) collective-permute-start(bf16[128,512]{1,0:T(8,128)(2,1)S(1)} %get-tuple-element.45), channel_id=1, source_target_pairs={{0,2},{2,0},{1,3},{3,1},{4,6},{6,4},{5,7},{7,5},{8,10},{10,8},{9,1... | collective-permute-start | bytes 393224 | tf_op jit(solution)/shard_map/ppermute | solution.py:31
  23.2 4.1 %collective-permute-start.6 = (bf16[16,128]{1,0:T(8,128)(2,1)S(1)}, bf16[16,128]{1,0:T(8,128)(2,1)S(1)}, u32[]{:S(2)}, u32[]{:S(2)}) collective-permute-start(bf16[16,128]{1,0:T(8,128)(2,1)S(1)} %get-tuple-element.40.mark_ref.refs_0_), channel_id=1, source_target_pairs={{0,2},{2,0},{1,3},{3,1},{4,6},{6,4},{5,7},{7,5},{8,10},{10,8},{9,1... | collective-permute-start | bytes 12296 | tf_op jit(solution)/shard_map/ppermute | solution.py:31

commit v19 on v18

--- a/solution.py
+++ b/solution.py
@@ -204,13 +204,13 @@
     lanes = iota((taps, depth), 1)
     ahead = (lanes - iota(lanes.shape, 0) == delta).astype(F32).astype(BF16)
     prow_ref[...] = slanted(jnp.dot(psf_ref[...], ahead, preferred_element_type=F32), share).astype(BF16)
-    for copy in copies:
-        copy.wait()
+    copies[0].wait()
     edge = 2 * B
     rows, cols = t_ref.shape
     off, _ = read_note(note_ref)
     to_blocks(src, 0, t_ref[...])
     conv_blocks(src, rows // B, w_ref, xs, m_ref)
+    copies[1].wait()
     to_chunks(sci, rows, sci_ref[...])
     filter_inner(sci, rows - B - off, off, off + rows, m_ref, pcol_ref, edge_ref, filt_ref, diff)
 
@@ -326,7 +326,10 @@
         total = keep_ref[span, :]
         for ref in got:
             total += ref[span, :].astype(F32)
-        out_ref[...] = total.astype(out_ref.dtype)
+        out_ref[0:share, :] = total.astype(out_ref.dtype)
+        if k:
+            out_ref[share:, 0:LANES] = marks.astype(BF16)
+            out_ref[share:, LANES:] = jnp.zeros((B, cols - LANES), BF16)
 
 
 def tile_kernel(mark_ref, sci_ref, note_ref, m1_ref, edge_ref, w_ref, *rest):
@@ -361,17 +364,17 @@
         copy.wait()
 
 
-def coadd_kernel(*refs):
+def coadd_kernel(mark_ref, *refs):
     *parts, out_ref = refs
-    marks, parts = parts[: len(parts) // 2], parts[len(parts) // 2 :]
     share, cols = out_ref.shape
     bands = lax.axis_size("band")
     base = (lax.axis_index("visit") * bands + lax.axis_index("band")) * share
     row = (iota((share, LANES), 0) + base).astype(F32)
     cover = jnp.zeros((share, LANES), F32)
-    for ref in marks:
+    for n, part in enumerate(parts):
+        marks = (part[share : share + B, 0:LANES] if n else mark_ref[...]).astype(F32)
         for m in range(bands):
-            mark = ref[...].astype(F32)[m : m + 1, :]
+            mark = marks[m : m + 1, :]
             cover += jnp.where(row >= mark[:, 0:1] * B + mark[:, 1:2], mark[:, 2:3], 0.0)
             cover += jnp.where(row < mark[:, 3:4] * B + mark[:, 4:5], mark[:, 5:6], 0.0)
     scale = lax.rsqrt(jnp.maximum(cover, 1.0))
@@ -379,7 +382,7 @@
         span = slice(c * LANES, (c + 1) * LANES)
         value = parts[0][:, span]
         for part in parts[1:]:
-            value += part[:, span].astype(F32)
+            value += part[0:share, span].astype(F32)
         out_ref[:, span] = value * scale
 
 
@@ -469,11 +472,10 @@
     halves = [half] + [swapped(half, "band", k) for k in range(1, bands)]
     own, *sent, mark = call(
         pair_kernel,
-        (sds((share, cols), F32),) + (sds((share, cols), BF16),) * (visits - 1) + (sds((B, LANES), BF16),),
+        (sds((share, cols), F32),) + (sds((share + B, cols), BF16),) * (visits - 1) + (sds((B, LANES), BF16),),
         [VM] * (1 + bands), [], 1 << 20, "pair",
     )(mark, keep, *got)
     got = [swapped(part, "visit", k + 1) for k, part in enumerate(sent)]
-    marks = [mark] + [swapped(mark, "visit", k) for k in range(1, visits)]
     difference = call(
         tile_kernel, sds((rows, cols), BF16), [VM] * (6 + bands),
         conv_scratch + [
@@ -483,8 +485,8 @@
         conv_flops, "tile", HBM,
     )(mark, tile, note, m1, m_edge, w, *halves)
     detection = call(
-        coadd_kernel, sds((share, cols), F32), [VM] * (2 * visits), [], 1 << 20, "coadd"
-    )(*marks, own, *got)
+        coadd_kernel, sds((share, cols), F32), [VM] * (1 + visits), [], 1 << 20, "coadd"
+    )(mark, own, *got)
     return (difference[:, None, :], detection)
 
 

time: 28.6 us -> 28.8 us (level)
  waiting for transfers between devices: 2.52 us -> 4.02 us
  Pallas kernels: 12.5 us -> 11.8 us
  starting transfers between devices: 11.3 us -> 10.8 us
    ppermute x4 -> x3, waiting for transfers between devices: 0.83 us -> 1.62 us  [swapped(): lax.ppermute(shard, axis, [(i, partner(i, k, devices)) for i in range(dev...]
    ppermute x1, waiting for transfers between devices: 0.62 us -> 1.32 us  [on_device(): lax.ppermute(msg, 'patch', [(i, (i + 1) % panels) for i in range(panels)])]
    pallas_call x1, Pallas kernels: 4.75 us -> 4.04 us  [on_device(): call(first_kernel, (sds((deep, CH), BF16), sds((cols, cols), BF16), sds((...]
    ppermute x4 -> x3, starting transfers between devices: 2.16 us -> 1.64 us  [swapped(): lax.ppermute(shard, axis, [(i, partner(i, k, devices)) for i in range(dev...]
  transfers between devices with their start and end apart: 8 -> 7, of which waited for: 4 -> 4; matrix products, arithmetic and copies ran while one was open for 0% -> 0% of each run, Pallas kernels for 41% -> 38%
where the time goes in v19:
time: 28.8 us; the launch traced here: 28.5 us
  Pallas kernels  11.8 us (41%)
  starting transfers between devices  10.8 us (38%)
  waiting for transfers between devices  4.02 us (14%)
  between operations  1.99 us (7%)
    ppermute x3, starting transfers between devices, shifted(): return lax.ppermute(shard, axis, pairs)  7.53 us
    pallas_call x1, Pallas kernels, on_device(): call(first_kernel, (sds((deep, CH), BF16), sds((cols, cols), BF16), sds((...  4.04 us
    pallas_call x1, Pallas kernels, on_device(): call(tile_kernel, sds((rows, cols), BF16), [VM] * (6 + bands), conv_scrat...  3.24 us
    pallas_call x1, Pallas kernels, on_device(): call(join_kernel, (sds((whole, cols), F32),) + (sds((whole + B, cols), BF...  2.29 us
    ppermute x3, starting transfers between devices, swapped(): lax.ppermute(shard, axis, [(i, partner(i, k, devices)) for i in range(dev...  1.64 us
    ppermute x3, waiting for transfers between devices, swapped(): lax.ppermute(shard, axis, [(i, partner(i, k, devices)) for i in range(dev...  1.62 us
    ppermute x1, starting transfers between devices, on_device(): lax.ppermute(msg, 'patch', [(i, (i + 1) % panels) for i in range(panels)])  1.6 us
    ppermute x1, waiting for transfers between devices, on_device(): lax.ppermute(msg, 'patch', [(i, (i + 1) % panels) for i in range(panels)])  1.32 us
  transfers between devices with their start and end apart: 7, of which 4 were waited for; matrix products, arithmetic and copies ran while one was open for 0% of the time, Pallas kernels for 38%

profile of v19, /device:TPU:0, one launch (start us, length us, event | category | flops | bytes accessed | tf_op | source)
XLA Modules:
  0.0 28.5 jit_solution(2206594669433108936)
XLA Ops:
  0.6 5.0 %collective-permute-start.2 = (bf16[512,1,512]{2,0,1:T(8,128)(2,1)}, bf16[512,1,512]{2,0,1:T(8,128)(2,1)S(1)}, u32[]{:S(2)}, u32[]{:S(2)}) collective-permute-start(bf16[512,1,512]{2,0,1:T(8,128)(2,1)} %param.9), channel_id=1, source_target_pairs={{0,4},{4,8},{8,12},{1,5},{5,9},{9,13},{2,6},{6,10},{10,14},{3,7},{... | collective-permute-start | bytes 1572872 | tf_op jit(solution)/shard_map/ppermute | solution.py:22
  6.9 1.2 %pack.1 = (bf16[64,512]{1,0:T(8,128)(2,1)S(1)}, bf16[32,512]{1,0:T(8,128)(2,1)S(1)}, bf16[32,512]{1,0:T(8,128)(2,1)S(1)}, bf16[256,512]{1,0:T(8,128)(2,1)S(1)}, ...) custom-call(s32[1,1]{1,0:T(1,128)S(6)} %copy.10.off_hbm, ...), custom_call_target="tpu_custom_call" | custom-call | flops 1048576 | bytes 2097152 | tf_op jit(solution)/shard_map/pack/pallas_call | solution.py:422
  8.1 1.6 %collective-permute-start = (bf16[32,512]{1,0:T(8,128)(2,1)S(1)}, bf16[32,512]{1,0:T(8,128)(2,1)S(1)}, u32[]{:S(2)}, u32[]{:S(2)}) collective-permute-start(bf16[32,512]{1,0:T(8,128)(2,1)S(1)} %get-tuple-element.25), channel_id=1, source_target_pairs={{0,4},{4,8},{8,12},{12,0},{1,5},{5,9},{9,13},{13,1},{2,6},{6,10},{... | collective-permute-start | bytes 98312 | tf_op jit(solution)/shard_map/ppermute | solution.py:435
  9.7 1.3 %collective-permute-start.1 = (bf16[32,512]{1,0:T(8,128)(2,1)S(1)}, bf16[32,512]{1,0:T(8,128)(2,1)S(1)}, u32[]{:S(2)}, u32[]{:S(2)}) collective-permute-start(bf16[32,512]{1,0:T(8,128)(2,1)S(1)} %get-tuple-element.26), channel_id=1, source_target_pairs={{4,0},{8,4},{12,8},{5,1},{9,5},{13,9},{6,2},{10,6},{14,10},{7,3},{... | collective-permute-start | bytes 98312 | tf_op jit(solution)/shard_map/ppermute | solution.py:22
  11.0 1.3 %collective-permute-start.4 = (bf16[256,512]{1,0:T(8,128)(2,1)S(1)}, bf16[256,512]{1,0:T(8,128)(2,1)S(1)}, u32[]{:S(2)}, u32[]{:S(2)}) collective-permute-start(bf16[256,512]{1,0:T(8,128)(2,1)S(1)} %get-tuple-element.43), channel_id=1, source_target_pairs={{4,0},{8,4},{12,8},{5,1},{9,5},{13,9},{6,2},{10,6},{14,10},{7,3},{... | collective-permute-start | bytes 786440 | tf_op jit(solution)/shard_map/ppermute | solution.py:22
  12.3 4.0 %first.1 = (bf16[2304,256]{1,0:T(8,128)(2,1)S(1)}, bf16[512,512]{1,0:T(8,128)(2,1)S(1)}, bf16[128,256]{1,0:T(8,128)(2,1)S(1)}, bf16[512,512]{1,0:T(8,128)(2,1)S(...) custom-call(bf16[64,512]{1,0:T(8,128)(2,1)S(1)} %get-tuple-element.24.note_ref, ...), custom_call_target="tpu_custom_call" | custom-call | flops 1207959552 | bytes 2097152 | tf_op jit(solution)/shard_map/first/pallas_call | solution.py:446
  16.3 1.3 %collective-permute-done.msg_ref = bf16[32,512]{1,0:T(8,128)(2,1)S(1)} collective-permute-done((bf16[32,512]{1,0:T(8,128)(2,1)S(1)}, bf16[32,512]{1,0:T(8,128)(2,1)S(1)}, u32[]{:S(2)}, u32[]{:S(2)}) %collective-permute-start) | collective-permute-done | bytes 32800 | tf_op jit(solution)/shard_map/ppermute | solution.py:435
  17.6 0.0 collective-permute-done.1.head_ref
  17.6 0.0 collective-permute-done.2
  17.7 2.3 %join.1 = (f32[256,512]{1,0:T(8,128)S(1)}, bf16[272,512]{1,0:T(8,128)(2,1)S(1)}, bf16[16,128]{1,0:T(8,128)(2,1)S(1)}, f32[4,64,128]{2,1,0:T(8,128)S(1)}) custom-call(bf16[64,512]{1,0:T(8,128)(2,1)S(1)} %get-tuple-element.24.note_ref, bf16[32,512]{1,0:T(8,128)(2,1)S(1)} %collective-permute-done.msg_ref, bf16[32,512]{1,0:T(8,128)(2,1)S(1)} %collective-permute-done.1.head_ref, ...), custom_call_target="tpu_custom_call" | custom-call | flops 17179869184 | bytes 2097152 | tf_op jit(solution)/shard_map/join/pallas_call | solution.py:457
  20.0 0.1 collective-permute-start.3
  20.0 1.1 %collective-permute-done.4.rest_0_ = bf16[256,512]{1,0:T(8,128)(2,1)S(1)} collective-permute-done((bf16[256,512]{1,0:T(8,128)(2,1)S(1)}, bf16[256,512]{1,0:T(8,128)(2,1)S(1)}, u32[]{:S(2)}, u32[]{:S(2)}) %collective-permute-start.4) | collective-permute-done | bytes 262176 | tf_op jit(solution)/shard_map/ppermute | solution.py:22
  21.1 0.0 collective-permute-start.5
  21.1 0.5 %collective-permute-done.3.refs_2_ = bf16[272,512]{1,0:T(8,128)(2,1)S(1)} collective-permute-done((bf16[272,512]{1,0:T(8,128)(2,1)S(1)}, bf16[272,512]{1,0:T(8,128)(2,1)S(1)}, u32[]{:S(2)}, u32[]{:S(2)}) %collective-permute-start.3) | collective-permute-done | bytes 278560 | tf_op jit(solution)/shard_map/ppermute | solution.py:31
  21.6 1.6 %collective-permute-start.6 = (bf16[144,512]{1,0:T(8,128)(2,1)S(1)}, bf16[144,512]{1,0:T(8,128)(2,1)S(1)}, u32[]{:S(2)}, u32[]{:S(2)}) collective-permute-start(bf16[144,512]{1,0:T(8,128)(2,1)S(1)} %get-tuple-element.45), channel_id=1, source_target_pairs={{0,2},{2,0},{1,3},{3,1},{4,6},{6,4},{5,7},{7,5},{8,10},{10,8},{9,1... | collective-permute-start | bytes 442376 | tf_op jit(solution)/shard_map/ppermute | solution.py:31
  23.2 0.0 collective-permute-done.5.rest_1_
  23.2 3.2 %tile.1 = bf16[512,512]{1,0:T(8,128)(2,1)} custom-call(bf16[16,128]{1,0:T(8,128)(2,1)S(1)} %get-tuple-element.40.mark_ref, bf16[512,512]{1,0:T(8,128)(2,1)S(1)} %get-tuple-element.41.sci_ref, bf16[64,512]{1,0:T(8,128)(2,1)S(1)} %get-tuple-element.24.note_ref, f32[4,544,128]{2,1,0:T(8,128)S(1)} %get-tuple-element.31.m1_ref, ...), custom_call_target="tpu_custom_call" | custom-call | flops 1207959552 | bytes 2097152 | tf_op jit(solution)/shard_map/tile/pallas_call | solution.py:479
  26.4 1.1 %collective-permute-done.6.refs_1_ = bf16[144,512]{1,0:T(8,128)(2,1)S(1)} collective-permute-done((bf16[144,512]{1,0:T(8,128)(2,1)S(1)}, bf16[144,512]{1,0:T(8,128)(2,1)S(1)}, u32[]{:S(2)}, u32[]{:S(2)}) %collective-permute-start.6) | collective-permute-done | bytes 147488 | tf_op jit(solution)/shard_map/ppermute | solution.py:31
  27.6 1.0 %coadd.1 = f32[128,512]{1,0:T(8,128)} custom-call(bf16[16,128]{1,0:T(8,128)(2,1)S(1)} %get-tuple-element.40.mark_ref, f32[128,512]{1,0:T(8,128)S(1)} %get-tuple-element.44.refs_0_, bf16[144,512]{1,0:T(8,128)(2,1)S(1)} %collective-permute-done.6.refs_1_), custom_call_target="tpu_custom_call" | custom-call | flops 1048576 | bytes 2097152 | tf_op jit(solution)/shard_map/coadd/pallas_call | solution.py:487
  (1 shorter events, 0.0 us)
Async XLA Ops:
  0.6 17.0 %collective-permute-start.2 = (bf16[512,1,512]{2,0,1:T(8,128)(2,1)}, bf16[512,1,512]{2,0,1:T(8,128)(2,1)S(1)}, u32[]{:S(2)}, u32[]{:S(2)}) collective-permute-start(bf16[512,1,512]{2,0,1:T(8,128)(2,1)} %param.9), channel_id=1, source_target_pairs={{0,4},{4,8},{8,12},{1,5},{5,9},{9,13},{2,6},{6,10},{10,14},{3,7},{... | collective-permute-start | bytes 1572872 | tf_op jit(solution)/shard_map/ppermute | solution.py:22
  8.1 9.6 %collective-permute-start = (bf16[32,512]{1,0:T(8,128)(2,1)S(1)}, bf16[32,512]{1,0:T(8,128)(2,1)S(1)}, u32[]{:S(2)}, u32[]{:S(2)}) collective-permute-start(bf16[32,512]{1,0:T(8,128)(2,1)S(1)} %get-tuple-element.25), channel_id=1, source_target_pairs={{0,4},{4,8},{8,12},{12,0},{1,5},{5,9},{9,13},{13,1},{2,6},{6,10},{... | collective-permute-start | bytes 98312 | tf_op jit(solution)/shard_map/ppermute | solution.py:435
  9.7 8.0 %collective-permute-start.1 = (bf16[32,512]{1,0:T(8,128)(2,1)S(1)}, bf16[32,512]{1,0:T(8,128)(2,1)S(1)}, u32[]{:S(2)}, u32[]{:S(2)}) collective-permute-start(bf16[32,512]{1,0:T(8,128)(2,1)S(1)} %get-tuple-element.26), channel_id=1, source_target_pairs={{4,0},{8,4},{12,8},{5,1},{9,5},{13,9},{6,2},{10,6},{14,10},{7,3},{... | collective-permute-start | bytes 98312 | tf_op jit(solution)/shard_map/ppermute | solution.py:22
  11.0 10.1 %collective-permute-start.4 = (bf16[256,512]{1,0:T(8,128)(2,1)S(1)}, bf16[256,512]{1,0:T(8,128)(2,1)S(1)}, u32[]{:S(2)}, u32[]{:S(2)}) collective-permute-start(bf16[256,512]{1,0:T(8,128)(2,1)S(1)} %get-tuple-element.43), channel_id=1, source_target_pairs={{4,0},{8,4},{12,8},{5,1},{9,5},{13,9},{6,2},{10,6},{14,10},{7,3},{... | collective-permute-start | bytes 786440 | tf_op jit(solution)/shard_map/ppermute | solution.py:22
  20.0 1.6 %collective-permute-start.3 = (bf16[272,512]{1,0:T(8,128)(2,1)S(1)}, bf16[272,512]{1,0:T(8,128)(2,1)S(1)}, u32[]{:S(2)}, u32[]{:S(2)}) collective-permute-start(bf16[272,512]{1,0:T(8,128)(2,1)S(1)} %get-tuple-element.39), channel_id=1, source_target_pairs={{0,1},{1,0},{2,3},{3,2},{4,5},{5,4},{6,7},{7,6},{8,9},{9,8},{10,11... | collective-permute-start | bytes 835592 | tf_op jit(solution)/shard_map/ppermute | solution.py:31
  21.1 2.1 %collective-permute-start.5 = (bf16[256,512]{1,0:T(8,128)(2,1)S(1)}, bf16[256,512]{1,0:T(8,128)(2,1)S(1)}, u32[]{:S(2)}, u32[]{:S(2)}) collective-permute-start(bf16[256,512]{1,0:T(8,128)(2,1)S(1)} %collective-permute-done.4.rest_0_), channel_id=1, source_target_pairs={{0,1},{1,0},{2,3},{3,2},{4,5},{5,4},{6,7},{7,6},{8,9},{9,8},{10,11... | collective-permute-start | bytes 786440 | tf_op jit(solution)/shard_map/ppermute | solution.py:31
  21.6 6.0 %collective-permute-start.6 = (bf16[144,512]{1,0:T(8,128)(2,1)S(1)}, bf16[144,512]{1,0:T(8,128)(2,1)S(1)}, u32[]{:S(2)}, u32[]{:S(2)}) collective-permute-start(bf16[144,512]{1,0:T(8,128)(2,1)S(1)} %get-tuple-element.45), channel_id=1, source_target_pairs={{0,2},{2,0},{1,3},{3,1},{4,6},{6,4},{5,7},{7,5},{8,10},{10,8},{9,1... | collective-permute-start | bytes 442376 | tf_op jit(solution)/shard_map/ppermute | solution.py:31

commit v20 on v18

--- a/solution.py
+++ b/solution.py
@@ -204,13 +204,13 @@
     lanes = iota((taps, depth), 1)
     ahead = (lanes - iota(lanes.shape, 0) == delta).astype(F32).astype(BF16)
     prow_ref[...] = slanted(jnp.dot(psf_ref[...], ahead, preferred_element_type=F32), share).astype(BF16)
-    for copy in copies:
-        copy.wait()
+    copies[0].wait()
     edge = 2 * B
     rows, cols = t_ref.shape
     off, _ = read_note(note_ref)
     to_blocks(src, 0, t_ref[...])
     conv_blocks(src, rows // B, w_ref, xs, m_ref)
+    copies[1].wait()
     to_chunks(sci, rows, sci_ref[...])
     filter_inner(sci, rows - B - off, off, off + rows, m_ref, pcol_ref, edge_ref, filt_ref, diff)
 

time: 28.6 us -> 28.5 us (level)
  Pallas kernels: 12.5 us -> 11.8 us
  waiting for transfers between devices: 2.52 us -> 3.18 us
    pallas_call x1, Pallas kernels: 4.75 us -> 4.08 us  [on_device(): call(first_kernel, (sds((deep, CH), BF16), sds((cols, cols), BF16), sds((...]
    ppermute x1, waiting for transfers between devices: 0.62 us -> 1.28 us  [on_device(): lax.ppermute(msg, 'patch', [(i, (i + 1) % panels) for i in range(panels)])]
  transfers between devices with their start and end apart: 8 -> 8, of which waited for: 4 -> 4; matrix products, arithmetic and copies ran while one was open for 0% -> 0% of each run, Pallas kernels for 41% -> 38%
where the time goes in v20:
time: 28.5 us; the launch traced here: 28.3 us
  Pallas kernels  11.8 us (41%)
  starting transfers between devices  11.3 us (40%)
  waiting for transfers between devices  3.18 us (11%)
  between operations  1.99 us (7%)
    ppermute x3, starting transfers between devices, shifted(): return lax.ppermute(shard, axis, pairs)  7.53 us
    pallas_call x1, Pallas kernels, on_device(): call(first_kernel, (sds((deep, CH), BF16), sds((cols, cols), BF16), sds((...  4.08 us
    pallas_call x1, Pallas kernels, on_device(): call(tile_kernel, sds((rows, cols), BF16), [VM] * (6 + bands), conv_scrat...  3.24 us
    pallas_call x1, Pallas kernels, on_device(): call(join_kernel, (sds((whole, cols), F32),) + (sds((whole + B, cols), BF...  2.29 us
    ppermute x4, starting transfers between devices, swapped(): lax.ppermute(shard, axis, [(i, partner(i, k, devices)) for i in range(dev...  2.16 us
    ppermute x1, starting transfers between devices, on_device(): lax.ppermute(msg, 'patch', [(i, (i + 1) % panels) for i in range(panels)])  1.6 us
    ppermute x1, waiting for transfers between devices, on_device(): lax.ppermute(msg, 'patch', [(i, (i + 1) % panels) for i in range(panels)])  1.28 us
    pallas_call x1, Pallas kernels, on_device(): call(pack_kernel, (sds((2 * edge, cols), BF16), sds((edge, cols), BF16),...  1.18 us
  transfers between devices with their start and end apart: 8, of which 4 were waited for; matrix products, arithmetic and copies ran while one was open for 0% of the time, Pallas kernels for 38%

profile of v20, /device:TPU:0, one launch (start us, length us, event | category | flops | bytes accessed | tf_op | source)
XLA Modules:
  0.0 28.3 jit_solution(6490223303990494713)
XLA Ops:
  0.6 5.0 %collective-permute-start.2 = (bf16[512,1,512]{2,0,1:T(8,128)(2,1)}, bf16[512,1,512]{2,0,1:T(8,128)(2,1)S(1)}, u32[]{:S(2)}, u32[]{:S(2)}) collective-permute-start(bf16[512,1,512]{2,0,1:T(8,128)(2,1)} %param.9), channel_id=1, source_target_pairs={{0,4},{4,8},{8,12},{1,5},{5,9},{9,13},{2,6},{6,10},{10,14},{3,7},{... | collective-permute-start | bytes 1572872 | tf_op jit(solution)/shard_map/ppermute | solution.py:22
  6.9 1.2 %pack.1 = (bf16[64,512]{1,0:T(8,128)(2,1)S(1)}, bf16[32,512]{1,0:T(8,128)(2,1)S(1)}, bf16[32,512]{1,0:T(8,128)(2,1)S(1)}, bf16[256,512]{1,0:T(8,128)(2,1)S(1)}, ...) custom-call(s32[1,1]{1,0:T(1,128)S(6)} %copy.10.off_hbm, ...), custom_call_target="tpu_custom_call" | custom-call | flops 1048576 | bytes 2097152 | tf_op jit(solution)/shard_map/pack/pallas_call | solution.py:419
  8.1 1.6 %collective-permute-start = (bf16[32,512]{1,0:T(8,128)(2,1)S(1)}, bf16[32,512]{1,0:T(8,128)(2,1)S(1)}, u32[]{:S(2)}, u32[]{:S(2)}) collective-permute-start(bf16[32,512]{1,0:T(8,128)(2,1)S(1)} %get-tuple-element.25), channel_id=1, source_target_pairs={{0,4},{4,8},{8,12},{12,0},{1,5},{5,9},{9,13},{13,1},{2,6},{6,10},{... | collective-permute-start | bytes 98312 | tf_op jit(solution)/shard_map/ppermute | solution.py:432
  9.7 1.3 %collective-permute-start.1 = (bf16[32,512]{1,0:T(8,128)(2,1)S(1)}, bf16[32,512]{1,0:T(8,128)(2,1)S(1)}, u32[]{:S(2)}, u32[]{:S(2)}) collective-permute-start(bf16[32,512]{1,0:T(8,128)(2,1)S(1)} %get-tuple-element.26), channel_id=1, source_target_pairs={{4,0},{8,4},{12,8},{5,1},{9,5},{13,9},{6,2},{10,6},{14,10},{7,3},{... | collective-permute-start | bytes 98312 | tf_op jit(solution)/shard_map/ppermute | solution.py:22
  11.0 1.3 %collective-permute-start.4 = (bf16[256,512]{1,0:T(8,128)(2,1)S(1)}, bf16[256,512]{1,0:T(8,128)(2,1)S(1)}, u32[]{:S(2)}, u32[]{:S(2)}) collective-permute-start(bf16[256,512]{1,0:T(8,128)(2,1)S(1)} %get-tuple-element.43), channel_id=1, source_target_pairs={{4,0},{8,4},{12,8},{5,1},{9,5},{13,9},{6,2},{10,6},{14,10},{7,3},{... | collective-permute-start | bytes 786440 | tf_op jit(solution)/shard_map/ppermute | solution.py:22
  12.3 4.1 %first.1 = (bf16[2304,256]{1,0:T(8,128)(2,1)S(1)}, bf16[512,512]{1,0:T(8,128)(2,1)S(1)}, bf16[128,256]{1,0:T(8,128)(2,1)S(1)}, bf16[512,512]{1,0:T(8,128)(2,1)S(...) custom-call(bf16[64,512]{1,0:T(8,128)(2,1)S(1)} %get-tuple-element.24.note_ref, ...), custom_call_target="tpu_custom_call" | custom-call | flops 1207959552 | bytes 2097152 | tf_op jit(solution)/shard_map/first/pallas_call | solution.py:443
  16.4 1.3 %collective-permute-done.msg_ref = bf16[32,512]{1,0:T(8,128)(2,1)S(1)} collective-permute-done((bf16[32,512]{1,0:T(8,128)(2,1)S(1)}, bf16[32,512]{1,0:T(8,128)(2,1)S(1)}, u32[]{:S(2)}, u32[]{:S(2)}) %collective-permute-start) | collective-permute-done | bytes 32800 | tf_op jit(solution)/shard_map/ppermute | solution.py:432
  17.6 0.0 collective-permute-done.1.head_ref
  17.6 0.0 collective-permute-done.2
  17.7 2.3 %join.1 = (f32[256,512]{1,0:T(8,128)S(1)}, bf16[272,512]{1,0:T(8,128)(2,1)S(1)}, bf16[16,128]{1,0:T(8,128)(2,1)S(1)}, f32[4,64,128]{2,1,0:T(8,128)S(1)}) custom-call(bf16[64,512]{1,0:T(8,128)(2,1)S(1)} %get-tuple-element.24.note_ref, bf16[32,512]{1,0:T(8,128)(2,1)S(1)} %collective-permute-done.msg_ref, bf16[32,512]{1,0:T(8,128)(2,1)S(1)} %collective-permute-done.1.head_ref, ...), custom_call_target="tpu_custom_call" | custom-call | flops 17179869184 | bytes 2097152 | tf_op jit(solution)/shard_map/join/pallas_call | solution.py:454
  20.0 0.1 collective-permute-start.3
  20.0 1.1 %collective-permute-done.4.rest_0_ = bf16[256,512]{1,0:T(8,128)(2,1)S(1)} collective-permute-done((bf16[256,512]{1,0:T(8,128)(2,1)S(1)}, bf16[256,512]{1,0:T(8,128)(2,1)S(1)}, u32[]{:S(2)}, u32[]{:S(2)}) %collective-permute-start.4) | collective-permute-done | bytes 262176 | tf_op jit(solution)/shard_map/ppermute | solution.py:22
  21.1 0.0 collective-permute-start.5
  21.1 0.5 %collective-permute-done.3.refs_2_ = bf16[272,512]{1,0:T(8,128)(2,1)S(1)} collective-permute-done((bf16[272,512]{1,0:T(8,128)(2,1)S(1)}, bf16[272,512]{1,0:T(8,128)(2,1)S(1)}, u32[]{:S(2)}, u32[]{:S(2)}) %collective-permute-start.3) | collective-permute-done | bytes 278560 | tf_op jit(solution)/shard_map/ppermute | solution.py:31
  21.6 1.6 %collective-permute-start.7 = (bf16[128,512]{1,0:T(8,128)(2,1)S(1)}, bf16[128,512]{1,0:T(8,128)(2,1)S(1)}, u32[]{:S(2)}, u32[]{:S(2)}) collective-permute-start(bf16[128,512]{1,0:T(8,128)(2,1)S(1)} %get-tuple-element.45), channel_id=1, source_target_pairs={{0,2},{2,0},{1,3},{3,1},{4,6},{6,4},{5,7},{7,5},{8,10},{10,8},{9,1... | collective-permute-start | bytes 393224 | tf_op jit(solution)/shard_map/ppermute | solution.py:31
  23.2 0.5 %collective-permute-start.6 = (bf16[16,128]{1,0:T(8,128)(2,1)S(1)}, bf16[16,128]{1,0:T(8,128)(2,1)S(1)}, u32[]{:S(2)}, u32[]{:S(2)}) collective-permute-start(bf16[16,128]{1,0:T(8,128)(2,1)S(1)} %get-tuple-element.40.mark_ref.refs_0_), channel_id=1, source_target_pairs={{0,2},{2,0},{1,3},{3,1},{4,6},{6,4},{5,7},{7,5},{8,10},{10,8},{9,1... | collective-permute-start | bytes 12296 | tf_op jit(solution)/shard_map/ppermute | solution.py:31
  23.7 0.0 collective-permute-done.5.rest_1_
  23.7 3.2 %tile.1 = bf16[512,512]{1,0:T(8,128)(2,1)} custom-call(bf16[16,128]{1,0:T(8,128)(2,1)S(1)} %get-tuple-element.40.mark_ref.refs_0_, bf16[512,512]{1,0:T(8,128)(2,1)S(1)} %get-tuple-element.41.sci_ref, bf16[64,512]{1,0:T(8,128)(2,1)S(1)} %get-tuple-element.24.note_ref, f32[4,544,128]{2,1,0:T(8,128)S(1)} %get-tuple-element.31.m1_ref, ...), custom_call_target="tpu_custom_call" | custom-call | flops 1207959552 | bytes 2097152 | tf_op jit(solution)/shard_map/tile/pallas_call | solution.py:477
  27.0 0.3 %collective-permute-done.6.refs_1_ = bf16[16,128]{1,0:T(8,128)(2,1)S(1)} collective-permute-done((bf16[16,128]{1,0:T(8,128)(2,1)S(1)}, bf16[16,128]{1,0:T(8,128)(2,1)S(1)}, u32[]{:S(2)}, u32[]{:S(2)}) %collective-permute-start.6) | collective-permute-done | bytes 4128 | tf_op jit(solution)/shard_map/ppermute | solution.py:31
  27.3 0.0 collective-permute-done.7.refs_3_
  27.3 1.0 %coadd.1 = f32[128,512]{1,0:T(8,128)} custom-call(bf16[16,128]{1,0:T(8,128)(2,1)S(1)} %get-tuple-element.40.mark_ref.refs_0_, bf16[16,128]{1,0:T(8,128)(2,1)S(1)} %collective-permute-done.6.refs_1_, f32[128,512]{1,0:T(8,128)S(1)} %get-tuple-element.44.refs_2_, bf16[128,512]{1,0:T(8,128)(2,1)S(1)} %collective-permute-done.7.refs_3_), custom_call_target="tpu_custom_call" | custom-call | flops 1048576 | bytes 2097152 | tf_op jit(solution)/shard_map/coadd/pallas_call | solution.py:485
  (1 shorter events, 0.0 us)
Async XLA Ops:
  0.6 17.0 %collective-permute-start.2 = (bf16[512,1,512]{2,0,1:T(8,128)(2,1)}, bf16[512,1,512]{2,0,1:T(8,128)(2,1)S(1)}, u32[]{:S(2)}, u32[]{:S(2)}) collective-permute-start(bf16[512,1,512]{2,0,1:T(8,128)(2,1)} %param.9), channel_id=1, source_target_pairs={{0,4},{4,8},{8,12},{1,5},{5,9},{9,13},{2,6},{6,10},{10,14},{3,7},{... | collective-permute-start | bytes 1572872 | tf_op jit(solution)/shard_map/ppermute | solution.py:22
  8.1 9.6 %collective-permute-start = (bf16[32,512]{1,0:T(8,128)(2,1)S(1)}, bf16[32,512]{1,0:T(8,128)(2,1)S(1)}, u32[]{:S(2)}, u32[]{:S(2)}) collective-permute-start(bf16[32,512]{1,0:T(8,128)(2,1)S(1)} %get-tuple-element.25), channel_id=1, source_target_pairs={{0,4},{4,8},{8,12},{12,0},{1,5},{5,9},{9,13},{13,1},{2,6},{6,10},{... | collective-permute-start | bytes 98312 | tf_op jit(solution)/shard_map/ppermute | solution.py:432
  9.7 8.0 %collective-permute-start.1 = (bf16[32,512]{1,0:T(8,128)(2,1)S(1)}, bf16[32,512]{1,0:T(8,128)(2,1)S(1)}, u32[]{:S(2)}, u32[]{:S(2)}) collective-permute-start(bf16[32,512]{1,0:T(8,128)(2,1)S(1)} %get-tuple-element.26), channel_id=1, source_target_pairs={{4,0},{8,4},{12,8},{5,1},{9,5},{13,9},{6,2},{10,6},{14,10},{7,3},{... | collective-permute-start | bytes 98312 | tf_op jit(solution)/shard_map/ppermute | solution.py:22
  11.0 10.1 %collective-permute-start.4 = (bf16[256,512]{1,0:T(8,128)(2,1)S(1)}, bf16[256,512]{1,0:T(8,128)(2,1)S(1)}, u32[]{:S(2)}, u32[]{:S(2)}) collective-permute-start(bf16[256,512]{1,0:T(8,128)(2,1)S(1)} %get-tuple-element.43), channel_id=1, source_target_pairs={{4,0},{8,4},{12,8},{5,1},{9,5},{13,9},{6,2},{10,6},{14,10},{7,3},{... | collective-permute-start | bytes 786440 | tf_op jit(solution)/shard_map/ppermute | solution.py:22
  20.0 1.6 %collective-permute-start.3 = (bf16[272,512]{1,0:T(8,128)(2,1)S(1)}, bf16[272,512]{1,0:T(8,128)(2,1)S(1)}, u32[]{:S(2)}, u32[]{:S(2)}) collective-permute-start(bf16[272,512]{1,0:T(8,128)(2,1)S(1)} %get-tuple-element.39), channel_id=1, source_target_pairs={{0,1},{1,0},{2,3},{3,2},{4,5},{5,4},{6,7},{7,6},{8,9},{9,8},{10,11... | collective-permute-start | bytes 835592 | tf_op jit(solution)/shard_map/ppermute | solution.py:31
  21.1 2.6 %collective-permute-start.5 = (bf16[256,512]{1,0:T(8,128)(2,1)S(1)}, bf16[256,512]{1,0:T(8,128)(2,1)S(1)}, u32[]{:S(2)}, u32[]{:S(2)}) collective-permute-start(bf16[256,512]{1,0:T(8,128)(2,1)S(1)} %collective-permute-done.4.rest_0_), channel_id=1, source_target_pairs={{0,1},{1,0},{2,3},{3,2},{4,5},{5,4},{6,7},{7,6},{8,9},{9,8},{10,11... | collective-permute-start | bytes 786440 | tf_op jit(solution)/shard_map/ppermute | solution.py:31
  21.6 5.7 %collective-permute-start.7 = (bf16[128,512]{1,0:T(8,128)(2,1)S(1)}, bf16[128,512]{1,0:T(8,128)(2,1)S(1)}, u32[]{:S(2)}, u32[]{:S(2)}) collective-permute-start(bf16[128,512]{1,0:T(8,128)(2,1)S(1)} %get-tuple-element.45), channel_id=1, source_target_pairs={{0,2},{2,0},{1,3},{3,1},{4,6},{6,4},{5,7},{7,5},{8,10},{10,8},{9,1... | collective-permute-start | bytes 393224 | tf_op jit(solution)/shard_map/ppermute | solution.py:31
  23.2 4.1 %collective-permute-start.6 = (bf16[16,128]{1,0:T(8,128)(2,1)S(1)}, bf16[16,128]{1,0:T(8,128)(2,1)S(1)}, u32[]{:S(2)}, u32[]{:S(2)}) collective-permute-start(bf16[16,128]{1,0:T(8,128)(2,1)S(1)} %get-tuple-element.40.mark_ref.refs_0_), channel_id=1, source_target_pairs={{0,2},{2,0},{1,3},{3,1},{4,6},{6,4},{5,7},{7,5},{8,10},{10,8},{9,1... | collective-permute-start | bytes 12296 | tf_op jit(solution)/shard_map/ppermute | solution.py:31

commit v21 on v20

--- a/solution.py
+++ b/solution.py
@@ -335,11 +335,13 @@
     bands = len(halves)
     blocks = rows // B // bands
     band = lax.axis_index("band")
-    for j in range(bands):
-        piece = halves[0][...].astype(F32)
-        for k in range(1, bands):
-            piece = jnp.where(partner(band, k, bands) == j, halves[k][...].astype(F32), piece)
-        to_blocks(src, j * blocks, piece)
+
+    def place_halves(own):
+        for k in range(bands):
+            to_blocks(src, partner(own, k, bands) * blocks, halves[k][...])
+
+    for own in range(bands):
+        pl.when(band == own)(functools.partial(place_halves, own))
     off, _ = read_note(note_ref)
     copies = []
 

time: 28.5 us -> 28.5 us (level)
  no operation moved by 1% of the time
where the time goes in v21:
time: 28.5 us; the launch traced here: 28.3 us
  Pallas kernels  11.7 us (41%)
  starting transfers between devices  11.3 us (40%)
  waiting for transfers between devices  3.26 us (11%)
  between operations  1.99 us (7%)
    ppermute x3, starting transfers between devices, shifted(): return lax.ppermute(shard, axis, pairs)  7.53 us
    pallas_call x1, Pallas kernels, on_device(): call(first_kernel, (sds((deep, CH), BF16), sds((cols, cols), BF16), sds((...  4.05 us
    pallas_call x1, Pallas kernels, on_device(): call(tile_kernel, sds((rows, cols), BF16), [VM] * (6 + bands), conv_scrat...  3.19 us
    pallas_call x1, Pallas kernels, on_device(): call(join_kernel, (sds((whole, cols), F32),) + (sds((whole + B, cols), BF...  2.29 us
    ppermute x4, starting transfers between devices, swapped(): lax.ppermute(shard, axis, [(i, partner(i, k, devices)) for i in range(dev...  2.16 us
    ppermute x1, starting transfers between devices, on_device(): lax.ppermute(msg, 'patch', [(i, (i + 1) % panels) for i in range(panels)])  1.6 us
    ppermute x1, waiting for transfers between devices, on_device(): lax.ppermute(msg, 'patch', [(i, (i + 1) % panels) for i in range(panels)])  1.32 us
    pallas_call x1, Pallas kernels, on_device(): call(pack_kernel, (sds((2 * edge, cols), BF16), sds((edge, cols), BF16),...  1.18 us
  transfers between devices with their start and end apart: 8, of which 4 were waited for; matrix products, arithmetic and copies ran while one was open for 0% of the time, Pallas kernels for 38%

profile of v21, /device:TPU:0, one launch (start us, length us, event | category | flops | bytes accessed | tf_op | source)
XLA Modules:
  0.0 28.3 jit_solution(18369207130577923163)
XLA Ops:
  0.6 5.0 %collective-permute-start.2 = (bf16[512,1,512]{2,0,1:T(8,128)(2,1)}, bf16[512,1,512]{2,0,1:T(8,128)(2,1)S(1)}, u32[]{:S(2)}, u32[]{:S(2)}) collective-permute-start(bf16[512,1,512]{2,0,1:T(8,128)(2,1)} %param.9), channel_id=1, source_target_pairs={{0,4},{4,8},{8,12},{1,5},{5,9},{9,13},{2,6},{6,10},{10,14},{3,7},{... | collective-permute-start | bytes 1572872 | tf_op jit(solution)/shard_map/ppermute | solution.py:22
  6.9 1.2 %pack.1 = (bf16[64,512]{1,0:T(8,128)(2,1)S(1)}, bf16[32,512]{1,0:T(8,128)(2,1)S(1)}, bf16[32,512]{1,0:T(8,128)(2,1)S(1)}, bf16[256,512]{1,0:T(8,128)(2,1)S(1)}, ...) custom-call(s32[1,1]{1,0:T(1,128)S(6)} %copy.10.off_hbm, ...), custom_call_target="tpu_custom_call" | custom-call | flops 1048576 | bytes 2097152 | tf_op jit(solution)/shard_map/pack/pallas_call | solution.py:421
  8.1 1.6 %collective-permute-start = (bf16[32,512]{1,0:T(8,128)(2,1)S(1)}, bf16[32,512]{1,0:T(8,128)(2,1)S(1)}, u32[]{:S(2)}, u32[]{:S(2)}) collective-permute-start(bf16[32,512]{1,0:T(8,128)(2,1)S(1)} %get-tuple-element.25), channel_id=1, source_target_pairs={{0,4},{4,8},{8,12},{12,0},{1,5},{5,9},{9,13},{13,1},{2,6},{6,10},{... | collective-permute-start | bytes 98312 | tf_op jit(solution)/shard_map/ppermute | solution.py:434
  9.7 1.3 %collective-permute-start.1 = (bf16[32,512]{1,0:T(8,128)(2,1)S(1)}, bf16[32,512]{1,0:T(8,128)(2,1)S(1)}, u32[]{:S(2)}, u32[]{:S(2)}) collective-permute-start(bf16[32,512]{1,0:T(8,128)(2,1)S(1)} %get-tuple-element.26), channel_id=1, source_target_pairs={{4,0},{8,4},{12,8},{5,1},{9,5},{13,9},{6,2},{10,6},{14,10},{7,3},{... | collective-permute-start | bytes 98312 | tf_op jit(solution)/shard_map/ppermute | solution.py:22
  11.0 1.3 %collective-permute-start.4 = (bf16[256,512]{1,0:T(8,128)(2,1)S(1)}, bf16[256,512]{1,0:T(8,128)(2,1)S(1)}, u32[]{:S(2)}, u32[]{:S(2)}) collective-permute-start(bf16[256,512]{1,0:T(8,128)(2,1)S(1)} %get-tuple-element.43), channel_id=1, source_target_pairs={{4,0},{8,4},{12,8},{5,1},{9,5},{13,9},{6,2},{10,6},{14,10},{7,3},{... | collective-permute-start | bytes 786440 | tf_op jit(solution)/shard_map/ppermute | solution.py:22
  12.3 4.0 %first.1 = (bf16[2304,256]{1,0:T(8,128)(2,1)S(1)}, bf16[512,512]{1,0:T(8,128)(2,1)S(1)}, bf16[128,256]{1,0:T(8,128)(2,1)S(1)}, bf16[512,512]{1,0:T(8,128)(2,1)S(...) custom-call(bf16[64,512]{1,0:T(8,128)(2,1)S(1)} %get-tuple-element.24.note_ref, ...), custom_call_target="tpu_custom_call" | custom-call | flops 1207959552 | bytes 2097152 | tf_op jit(solution)/shard_map/first/pallas_call | solution.py:445
  16.3 1.3 %collective-permute-done.msg_ref = bf16[32,512]{1,0:T(8,128)(2,1)S(1)} collective-permute-done((bf16[32,512]{1,0:T(8,128)(2,1)S(1)}, bf16[32,512]{1,0:T(8,128)(2,1)S(1)}, u32[]{:S(2)}, u32[]{:S(2)}) %collective-permute-start) | collective-permute-done | bytes 32800 | tf_op jit(solution)/shard_map/ppermute | solution.py:434
  17.6 0.0 collective-permute-done.1.head_ref
  17.6 0.0 collective-permute-done.2
  17.7 2.3 %join.1 = (f32[256,512]{1,0:T(8,128)S(1)}, bf16[272,512]{1,0:T(8,128)(2,1)S(1)}, bf16[16,128]{1,0:T(8,128)(2,1)S(1)}, f32[4,64,128]{2,1,0:T(8,128)S(1)}) custom-call(bf16[64,512]{1,0:T(8,128)(2,1)S(1)} %get-tuple-element.24.note_ref, bf16[32,512]{1,0:T(8,128)(2,1)S(1)} %collective-permute-done.msg_ref, bf16[32,512]{1,0:T(8,128)(2,1)S(1)} %collective-permute-done.1.head_ref, ...), custom_call_target="tpu_custom_call" | custom-call | flops 17179869184 | bytes 2097152 | tf_op jit(solution)/shard_map/join/pallas_call | solution.py:456
  20.0 0.1 collective-permute-start.3
  20.0 1.1 %collective-permute-done.4.rest_0_ = bf16[256,512]{1,0:T(8,128)(2,1)S(1)} collective-permute-done((bf16[256,512]{1,0:T(8,128)(2,1)S(1)}, bf16[256,512]{1,0:T(8,128)(2,1)S(1)}, u32[]{:S(2)}, u32[]{:S(2)}) %collective-permute-start.4) | collective-permute-done | bytes 262176 | tf_op jit(solution)/shard_map/ppermute | solution.py:22
  21.1 0.0 collective-permute-start.5
  21.1 0.5 %collective-permute-done.3.refs_2_ = bf16[272,512]{1,0:T(8,128)(2,1)S(1)} collective-permute-done((bf16[272,512]{1,0:T(8,128)(2,1)S(1)}, bf16[272,512]{1,0:T(8,128)(2,1)S(1)}, u32[]{:S(2)}, u32[]{:S(2)}) %collective-permute-start.3) | collective-permute-done | bytes 278560 | tf_op jit(solution)/shard_map/ppermute | solution.py:31
  21.6 1.6 %collective-permute-start.7 = (bf16[128,512]{1,0:T(8,128)(2,1)S(1)}, bf16[128,512]{1,0:T(8,128)(2,1)S(1)}, u32[]{:S(2)}, u32[]{:S(2)}) collective-permute-start(bf16[128,512]{1,0:T(8,128)(2,1)S(1)} %get-tuple-element.45), channel_id=1, source_target_pairs={{0,2},{2,0},{1,3},{3,1},{4,6},{6,4},{5,7},{7,5},{8,10},{10,8},{9,1... | collective-permute-start | bytes 393224 | tf_op jit(solution)/shard_map/ppermute | solution.py:31
  23.2 0.5 %collective-permute-start.6 = (bf16[16,128]{1,0:T(8,128)(2,1)S(1)}, bf16[16,128]{1,0:T(8,128)(2,1)S(1)}, u32[]{:S(2)}, u32[]{:S(2)}) collective-permute-start(bf16[16,128]{1,0:T(8,128)(2,1)S(1)} %get-tuple-element.40.mark_ref.refs_0_), channel_id=1, source_target_pairs={{0,2},{2,0},{1,3},{3,1},{4,6},{6,4},{5,7},{7,5},{8,10},{10,8},{9,1... | collective-permute-start | bytes 12296 | tf_op jit(solution)/shard_map/ppermute | solution.py:31
  23.7 0.0 collective-permute-done.5.rest_1_
  23.7 3.2 %tile.1 = bf16[512,512]{1,0:T(8,128)(2,1)} custom-call(bf16[16,128]{1,0:T(8,128)(2,1)S(1)} %get-tuple-element.40.mark_ref.refs_0_, bf16[512,512]{1,0:T(8,128)(2,1)S(1)} %get-tuple-element.41.sci_ref, bf16[64,512]{1,0:T(8,128)(2,1)S(1)} %get-tuple-element.24.note_ref, f32[4,544,128]{2,1,0:T(8,128)S(1)} %get-tuple-element.31.m1_ref, ...), custom_call_target="tpu_custom_call" | custom-call | flops 1207959552 | bytes 2097152 | tf_op jit(solution)/shard_map/tile/pallas_call | solution.py:479
  26.9 0.4 %collective-permute-done.6.refs_1_ = bf16[16,128]{1,0:T(8,128)(2,1)S(1)} collective-permute-done((bf16[16,128]{1,0:T(8,128)(2,1)S(1)}, bf16[16,128]{1,0:T(8,128)(2,1)S(1)}, u32[]{:S(2)}, u32[]{:S(2)}) %collective-permute-start.6) | collective-permute-done | bytes 4128 | tf_op jit(solution)/shard_map/ppermute | solution.py:31
  27.3 0.0 collective-permute-done.7.refs_3_
  27.3 1.0 %coadd.1 = f32[128,512]{1,0:T(8,128)} custom-call(bf16[16,128]{1,0:T(8,128)(2,1)S(1)} %get-tuple-element.40.mark_ref.refs_0_, bf16[16,128]{1,0:T(8,128)(2,1)S(1)} %collective-permute-done.6.refs_1_, f32[128,512]{1,0:T(8,128)S(1)} %get-tuple-element.44.refs_2_, bf16[128,512]{1,0:T(8,128)(2,1)S(1)} %collective-permute-done.7.refs_3_), custom_call_target="tpu_custom_call" | custom-call | flops 1048576 | bytes 2097152 | tf_op jit(solution)/shard_map/coadd/pallas_call | solution.py:487
  (1 shorter events, 0.0 us)
Async XLA Ops:
  0.6 17.0 %collective-permute-start.2 = (bf16[512,1,512]{2,0,1:T(8,128)(2,1)}, bf16[512,1,512]{2,0,1:T(8,128)(2,1)S(1)}, u32[]{:S(2)}, u32[]{:S(2)}) collective-permute-start(bf16[512,1,512]{2,0,1:T(8,128)(2,1)} %param.9), channel_id=1, source_target_pairs={{0,4},{4,8},{8,12},{1,5},{5,9},{9,13},{2,6},{6,10},{10,14},{3,7},{... | collective-permute-start | bytes 1572872 | tf_op jit(solution)/shard_map/ppermute | solution.py:22
  8.1 9.6 %collective-permute-start = (bf16[32,512]{1,0:T(8,128)(2,1)S(1)}, bf16[32,512]{1,0:T(8,128)(2,1)S(1)}, u32[]{:S(2)}, u32[]{:S(2)}) collective-permute-start(bf16[32,512]{1,0:T(8,128)(2,1)S(1)} %get-tuple-element.25), channel_id=1, source_target_pairs={{0,4},{4,8},{8,12},{12,0},{1,5},{5,9},{9,13},{13,1},{2,6},{6,10},{... | collective-permute-start | bytes 98312 | tf_op jit(solution)/shard_map/ppermute | solution.py:434
  9.7 8.0 %collective-permute-start.1 = (bf16[32,512]{1,0:T(8,128)(2,1)S(1)}, bf16[32,512]{1,0:T(8,128)(2,1)S(1)}, u32[]{:S(2)}, u32[]{:S(2)}) collective-permute-start(bf16[32,512]{1,0:T(8,128)(2,1)S(1)} %get-tuple-element.26), channel_id=1, source_target_pairs={{4,0},{8,4},{12,8},{5,1},{9,5},{13,9},{6,2},{10,6},{14,10},{7,3},{... | collective-permute-start | bytes 98312 | tf_op jit(solution)/shard_map/ppermute | solution.py:22
  11.0 10.1 %collective-permute-start.4 = (bf16[256,512]{1,0:T(8,128)(2,1)S(1)}, bf16[256,512]{1,0:T(8,128)(2,1)S(1)}, u32[]{:S(2)}, u32[]{:S(2)}) collective-permute-start(bf16[256,512]{1,0:T(8,128)(2,1)S(1)} %get-tuple-element.43), channel_id=1, source_target_pairs={{4,0},{8,4},{12,8},{5,1},{9,5},{13,9},{6,2},{10,6},{14,10},{7,3},{... | collective-permute-start | bytes 786440 | tf_op jit(solution)/shard_map/ppermute | solution.py:22
  20.0 1.6 %collective-permute-start.3 = (bf16[272,512]{1,0:T(8,128)(2,1)S(1)}, bf16[272,512]{1,0:T(8,128)(2,1)S(1)}, u32[]{:S(2)}, u32[]{:S(2)}) collective-permute-start(bf16[272,512]{1,0:T(8,128)(2,1)S(1)} %get-tuple-element.39), channel_id=1, source_target_pairs={{0,1},{1,0},{2,3},{3,2},{4,5},{5,4},{6,7},{7,6},{8,9},{9,8},{10,11... | collective-permute-start | bytes 835592 | tf_op jit(solution)/shard_map/ppermute | solution.py:31
  21.1 2.6 %collective-permute-start.5 = (bf16[256,512]{1,0:T(8,128)(2,1)S(1)}, bf16[256,512]{1,0:T(8,128)(2,1)S(1)}, u32[]{:S(2)}, u32[]{:S(2)}) collective-permute-start(bf16[256,512]{1,0:T(8,128)(2,1)S(1)} %collective-permute-done.4.rest_0_), channel_id=1, source_target_pairs={{0,1},{1,0},{2,3},{3,2},{4,5},{5,4},{6,7},{7,6},{8,9},{9,8},{10,11... | collective-permute-start | bytes 786440 | tf_op jit(solution)/shard_map/ppermute | solution.py:31
  21.6 5.7 %collective-permute-start.7 = (bf16[128,512]{1,0:T(8,128)(2,1)S(1)}, bf16[128,512]{1,0:T(8,128)(2,1)S(1)}, u32[]{:S(2)}, u32[]{:S(2)}) collective-permute-start(bf16[128,512]{1,0:T(8,128)(2,1)S(1)} %get-tuple-element.45), channel_id=1, source_target_pairs={{0,2},{2,0},{1,3},{3,1},{4,6},{6,4},{5,7},{7,5},{8,10},{10,8},{9,1... | collective-permute-start | bytes 393224 | tf_op jit(solution)/shard_map/ppermute | solution.py:31
  23.2 4.1 %collective-permute-start.6 = (bf16[16,128]{1,0:T(8,128)(2,1)S(1)}, bf16[16,128]{1,0:T(8,128)(2,1)S(1)}, u32[]{:S(2)}, u32[]{:S(2)}) collective-permute-start(bf16[16,128]{1,0:T(8,128)(2,1)S(1)} %get-tuple-element.40.mark_ref.refs_0_), channel_id=1, source_target_pairs={{0,2},{2,0},{1,3},{3,1},{4,6},{6,4},{5,7},{7,5},{8,10},{10,8},{9,1... | collective-permute-start | bytes 12296 | tf_op jit(solution)/shard_map/ppermute | solution.py:31

commit v22 on v20

--- a/solution.py
+++ b/solution.py
@@ -120,12 +120,10 @@
 
 def pack_kernel(
     off_hbm, live_hbm, t_hbm, bank_hbm, index_hbm, coeff_hbm, psf_hbm,
-    note_ref, msg_ref, head_ref, half_ref, bank_ref, index_ref, coeff_ref, psf_ref, off_ref, live_ref, sems,
+    note_ref, msg_ref, head_ref, bank_ref, index_ref, coeff_ref, psf_ref, off_ref, live_ref, sems,
 ):
     rows, cols = t_hbm.shape
     edge = 2 * B
-    piece = half_ref.shape[0]
-    begin = pl.multiple_of(lax.axis_index("band") * piece, B)
     copies = [
         pltpu.make_async_copy(a, b, sems.at[n])
         for n, (a, b) in enumerate((
@@ -133,7 +131,6 @@
             (t_hbm.at[pl.ds(rows - edge, edge)], note_ref.at[pl.ds(0, edge)]),
             (t_hbm.at[pl.ds(0, edge)], note_ref.at[pl.ds(edge, edge)]),
             (t_hbm.at[pl.ds(0, edge)], head_ref),
-            (t_hbm.at[pl.ds(begin, piece)], half_ref),
             (bank_hbm, bank_ref), (index_hbm, index_ref), (coeff_hbm, coeff_ref), (psf_hbm, psf_ref),
         ))
     ]
@@ -147,6 +144,14 @@
     block = note_ref[0:B, :].astype(F32)
     note_ref[0:B, :] = jnp.where(iota((B, cols), 0) == 0, note, block).astype(BF16)
     msg_ref[...] = note_ref[0:edge, :]
+
+
+def cut_kernel(note_ref, t_hbm, half_ref, sem):
+    piece = half_ref.shape[0]
+    begin = pl.multiple_of(lax.axis_index("band") * piece, B)
+    copy = pltpu.make_async_copy(t_hbm.at[pl.ds(begin, piece)], half_ref, sem)
+    copy.start()
+    copy.wait()
 
 
 def first_kernel(
@@ -416,17 +421,19 @@
     before = shifted(science, "patch", 1)[:, 0, :]
     bands, visits = lax.axis_size("band"), lax.axis_size("visit")
     psf = psf_profile[None]
-    note, msg, head, half, *small = call(
+    note, msg, head, *small = call(
         pack_kernel,
         (
             sds((2 * edge, cols), BF16), sds((edge, cols), BF16), sds((edge, cols), BF16),
-            sds((rows // bands, cols), BF16),
             *(sds(x.shape, x.dtype) for x in (bank, index, coeff, psf)),
         ),
         [HBM] * 7,
         [pltpu.SMEM((1, 1), jnp.int32), pltpu.SMEM((1, 1), jnp.int32), pltpu.SemaphoreType.DMA((10,))],
         1 << 20, "pack",
     )(offsets, live_flags, held[0], *in_hbm(bank, index, coeff, psf))
+    half = call(
+        cut_kernel, sds((rows // bands, cols), BF16), [VM, HBM], [pltpu.SemaphoreType.DMA], 1, "cut"
+    )(note, held[0])
     half = shifted(half, "patch", -1)
     panels = lax.axis_size("patch")
     msg = lax.ppermute(msg, "patch", [(i, (i + 1) % panels) for i in range(panels)])

time: 28.5 us -> 29.1 us (1.021)
  Pallas kernels: 11.8 us -> 12.5 us
    pallas_call x0 -> x1, Pallas kernels: none -> 0.97 us  [on_device(): call(cut_kernel, sds((rows // bands, cols), BF16), [VM, HBM], [pltpu.Sema...]
    ppermute x1, waiting for transfers between devices: 1.28 us -> 0.56 us  [on_device(): lax.ppermute(msg, 'patch', [(i, (i + 1) % panels) for i in range(panels)])]
    ppermute x3, waiting for transfers between devices: 1.07 us -> 1.69 us  [shifted(): return lax.ppermute(shard, axis, pairs)]
  transfers between devices with their start and end apart: 8 -> 8, of which waited for: 4 -> 3; matrix products, arithmetic and copies ran while one was open for 0% -> 0% of each run, Pallas kernels for 38% -> 40%
where the time goes in v22:
time: 29.1 us; the launch traced here: 28.8 us
  Pallas kernels  12.5 us (43%)
  starting transfers between devices  11.3 us (39%)
  waiting for transfers between devices  2.97 us (10%)
  between operations  2 us (7%)
    ppermute x3, starting transfers between devices, shifted(): return lax.ppermute(shard, axis, pairs)  7.53 us
    pallas_call x1, Pallas kernels, on_device(): call(first_kernel, (sds((deep, CH), BF16), sds((cols, cols), BF16), sds((...  4.07 us
    pallas_call x1, Pallas kernels, on_device(): call(tile_kernel, sds((rows, cols), BF16), [VM] * (6 + bands), conv_scrat...  3.25 us
    pallas_call x1, Pallas kernels, on_device(): call(join_kernel, (sds((whole, cols), F32),) + (sds((whole + B, cols), BF...  2.29 us
    ppermute x4, starting transfers between devices, swapped(): lax.ppermute(shard, axis, [(i, partner(i, k, devices)) for i in range(dev...  2.16 us
    ppermute x3, waiting for transfers between devices, shifted(): return lax.ppermute(shard, axis, pairs)  1.69 us
    ppermute x1, starting transfers between devices, on_device(): lax.ppermute(msg, 'patch', [(i, (i + 1) % panels) for i in range(panels)])  1.6 us
    pallas_call x1, Pallas kernels, on_device(): call(cut_kernel, sds((rows // bands, cols), BF16), [VM, HBM], [pltpu.Sema...  0.97 us
  transfers between devices with their start and end apart: 8, of which 3 were waited for; matrix products, arithmetic and copies ran while one was open for 0% of the time, Pallas kernels for 40%

profile of v22, /device:TPU:0, one launch (start us, length us, event | category | flops | bytes accessed | tf_op | source)
XLA Modules:
  0.0 28.8 jit_solution(2300080841961703135)
XLA Ops:
  0.6 5.0 %collective-permute-start.2 = (bf16[512,1,512]{2,0,1:T(8,128)(2,1)}, bf16[512,1,512]{2,0,1:T(8,128)(2,1)S(1)}, u32[]{:S(2)}, u32[]{:S(2)}) collective-permute-start(bf16[512,1,512]{2,0,1:T(8,128)(2,1)} %param.9), channel_id=1, source_target_pairs={{0,4},{4,8},{8,12},{1,5},{5,9},{9,13},{2,6},{6,10},{10,14},{3,7},{... | collective-permute-start | bytes 1572872 | tf_op jit(solution)/shard_map/ppermute | solution.py:22
  6.9 0.9 %pack.1 = (bf16[64,512]{1,0:T(8,128)(2,1)S(1)}, bf16[32,512]{1,0:T(8,128)(2,1)S(1)}, bf16[32,512]{1,0:T(8,128)(2,1)S(1)}, bf16[16,31]{1,0:T(8,128)(2,1)S(1)}, s3...) custom-call(s32[1,1]{1,0:T(1,128)S(6)} %copy.10.off_hbm, s32[1,1]{1,0:T(1,128)S(6)} %copy.11.live_hbm, ...), custom_call_target="tpu_custom_call" | custom-call | flops 1048576 | bytes 2097152 | tf_op jit(solution)/shard_map/pack/pallas_call | solution.py:424
  7.8 1.6 %collective-permute-start = (bf16[32,512]{1,0:T(8,128)(2,1)S(1)}, bf16[32,512]{1,0:T(8,128)(2,1)S(1)}, u32[]{:S(2)}, u32[]{:S(2)}) collective-permute-start(bf16[32,512]{1,0:T(8,128)(2,1)S(1)} %get-tuple-element.24), channel_id=1, source_target_pairs={{0,4},{4,8},{8,12},{12,0},{1,5},{5,9},{9,13},{13,1},{2,6},{6,10},{... | collective-permute-start | bytes 98312 | tf_op jit(solution)/shard_map/ppermute | solution.py:439
  9.4 1.3 %collective-permute-start.1 = (bf16[32,512]{1,0:T(8,128)(2,1)S(1)}, bf16[32,512]{1,0:T(8,128)(2,1)S(1)}, u32[]{:S(2)}, u32[]{:S(2)}) collective-permute-start(bf16[32,512]{1,0:T(8,128)(2,1)S(1)} %get-tuple-element.25), channel_id=1, source_target_pairs={{4,0},{8,4},{12,8},{5,1},{9,5},{13,9},{6,2},{10,6},{14,10},{7,3},{... | collective-permute-start | bytes 98312 | tf_op jit(solution)/shard_map/ppermute | solution.py:22
  10.7 1.0 %cut.1 = bf16[256,512]{1,0:T(8,128)(2,1)S(1)} custom-call(bf16[64,512]{1,0:T(8,128)(2,1)S(1)} %get-tuple-element.23.note_ref, bf16[512,512]{1,0:T(8,128)(2,1)} %t_hbm.5), custom_call_target="tpu_custom_call" | custom-call | flops 1 | bytes 2097152 | tf_op jit(solution)/shard_map/cut/pallas_call | solution.py:434
  11.7 1.3 %collective-permute-start.4 = (bf16[256,512]{1,0:T(8,128)(2,1)S(1)}, bf16[256,512]{1,0:T(8,128)(2,1)S(1)}, u32[]{:S(2)}, u32[]{:S(2)}) collective-permute-start(bf16[256,512]{1,0:T(8,128)(2,1)S(1)} %cut.1), channel_id=1, source_target_pairs={{4,0},{8,4},{12,8},{5,1},{9,5},{13,9},{6,2},{10,6},{14,10},{7,3},{... | collective-permute-start | bytes 786440 | tf_op jit(solution)/shard_map/ppermute | solution.py:22
  13.0 4.1 %first.1 = (bf16[2304,256]{1,0:T(8,128)(2,1)S(1)}, bf16[512,512]{1,0:T(8,128)(2,1)S(1)}, bf16[128,256]{1,0:T(8,128)(2,1)S(1)}, bf16[512,512]{1,0:T(8,128)(2,1)S(...) custom-call(bf16[64,512]{1,0:T(8,128)(2,1)S(1)} %get-tuple-element.23.note_ref, ...), custom_call_target="tpu_custom_call" | custom-call | flops 1207959552 | bytes 2097152 | tf_op jit(solution)/shard_map/first/pallas_call | solution.py:450
  17.1 0.6 %collective-permute-done.msg_ref = bf16[32,512]{1,0:T(8,128)(2,1)S(1)} collective-permute-done((bf16[32,512]{1,0:T(8,128)(2,1)S(1)}, bf16[32,512]{1,0:T(8,128)(2,1)S(1)}, u32[]{:S(2)}, u32[]{:S(2)}) %collective-permute-start) | collective-permute-done | bytes 32800 | tf_op jit(solution)/shard_map/ppermute | solution.py:439
  17.6 0.0 collective-permute-done.1.head_ref
  17.6 0.0 collective-permute-done.2
  17.7 2.3 %join.1 = (f32[256,512]{1,0:T(8,128)S(1)}, bf16[272,512]{1,0:T(8,128)(2,1)S(1)}, bf16[16,128]{1,0:T(8,128)(2,1)S(1)}, f32[4,64,128]{2,1,0:T(8,128)S(1)}) custom-call(bf16[64,512]{1,0:T(8,128)(2,1)S(1)} %get-tuple-element.23.note_ref, bf16[32,512]{1,0:T(8,128)(2,1)S(1)} %collective-permute-done.msg_ref, bf16[32,512]{1,0:T(8,128)(2,1)S(1)} %collective-permute-done.1.head_ref, ...), custom_call_target="tpu_custom_call" | custom-call | flops 17179869184 | bytes 2097152 | tf_op jit(solution)/shard_map/join/pallas_call | solution.py:461
  20.0 0.1 collective-permute-start.3
  20.0 1.7 %collective-permute-done.4.rest_0_ = bf16[256,512]{1,0:T(8,128)(2,1)S(1)} collective-permute-done((bf16[256,512]{1,0:T(8,128)(2,1)S(1)}, bf16[256,512]{1,0:T(8,128)(2,1)S(1)}, u32[]{:S(2)}, u32[]{:S(2)}) %collective-permute-start.4) | collective-permute-done | bytes 262176 | tf_op jit(solution)/shard_map/ppermute | solution.py:22
  21.7 0.0 collective-permute-start.5
  21.7 0.0 collective-permute-done.3.refs_2_
  21.8 1.6 %collective-permute-start.7 = (bf16[128,512]{1,0:T(8,128)(2,1)S(1)}, bf16[128,512]{1,0:T(8,128)(2,1)S(1)}, u32[]{:S(2)}, u32[]{:S(2)}) collective-permute-start(bf16[128,512]{1,0:T(8,128)(2,1)S(1)} %get-tuple-element.43), channel_id=1, source_target_pairs={{0,2},{2,0},{1,3},{3,1},{4,6},{6,4},{5,7},{7,5},{8,10},{10,8},{9,1... | collective-permute-start | bytes 393224 | tf_op jit(solution)/shard_map/ppermute | solution.py:31
  23.3 0.5 %collective-permute-start.6 = (bf16[16,128]{1,0:T(8,128)(2,1)S(1)}, bf16[16,128]{1,0:T(8,128)(2,1)S(1)}, u32[]{:S(2)}, u32[]{:S(2)}) collective-permute-start(bf16[16,128]{1,0:T(8,128)(2,1)S(1)} %get-tuple-element.39.mark_ref.refs_0_), channel_id=1, source_target_pairs={{0,2},{2,0},{1,3},{3,1},{4,6},{6,4},{5,7},{7,5},{8,10},{10,8},{9,1... | collective-permute-start | bytes 12296 | tf_op jit(solution)/shard_map/ppermute | solution.py:31
  23.9 0.0 collective-permute-done.5.rest_1_
  23.9 3.2 %tile.1 = bf16[512,512]{1,0:T(8,128)(2,1)} custom-call(bf16[16,128]{1,0:T(8,128)(2,1)S(1)} %get-tuple-element.39.mark_ref.refs_0_, bf16[512,512]{1,0:T(8,128)(2,1)S(1)} %get-tuple-element.40.sci_ref, bf16[64,512]{1,0:T(8,128)(2,1)S(1)} %get-tuple-element.23.note_ref, f32[4,544,128]{2,1,0:T(8,128)S(1)} %get-tuple-element.30.m1_ref, ...), custom_call_target="tpu_custom_call" | custom-call | flops 1207959552 | bytes 2097152 | tf_op jit(solution)/shard_map/tile/pallas_call | solution.py:484
  27.1 0.7 %collective-permute-done.6.refs_1_ = bf16[16,128]{1,0:T(8,128)(2,1)S(1)} collective-permute-done((bf16[16,128]{1,0:T(8,128)(2,1)S(1)}, bf16[16,128]{1,0:T(8,128)(2,1)S(1)}, u32[]{:S(2)}, u32[]{:S(2)}) %collective-permute-start.6) | collective-permute-done | bytes 4128 | tf_op jit(solution)/shard_map/ppermute | solution.py:31
  27.8 0.0 collective-permute-done.7.refs_3_
  27.8 1.0 %coadd.1 = f32[128,512]{1,0:T(8,128)} custom-call(bf16[16,128]{1,0:T(8,128)(2,1)S(1)} %get-tuple-element.39.mark_ref.refs_0_, bf16[16,128]{1,0:T(8,128)(2,1)S(1)} %collective-permute-done.6.refs_1_, f32[128,512]{1,0:T(8,128)S(1)} %get-tuple-element.42.refs_2_, bf16[128,512]{1,0:T(8,128)(2,1)S(1)} %collective-permute-done.7.refs_3_), custom_call_target="tpu_custom_call" | custom-call | flops 1048576 | bytes 2097152 | tf_op jit(solution)/shard_map/coadd/pallas_call | solution.py:492
  (1 shorter events, 0.0 us)
Async XLA Ops:
  0.6 17.0 %collective-permute-start.2 = (bf16[512,1,512]{2,0,1:T(8,128)(2,1)}, bf16[512,1,512]{2,0,1:T(8,128)(2,1)S(1)}, u32[]{:S(2)}, u32[]{:S(2)}) collective-permute-start(bf16[512,1,512]{2,0,1:T(8,128)(2,1)} %param.9), channel_id=1, source_target_pairs={{0,4},{4,8},{8,12},{1,5},{5,9},{9,13},{2,6},{6,10},{10,14},{3,7},{... | collective-permute-start | bytes 1572872 | tf_op jit(solution)/shard_map/ppermute | solution.py:22
  7.8 9.8 %collective-permute-start = (bf16[32,512]{1,0:T(8,128)(2,1)S(1)}, bf16[32,512]{1,0:T(8,128)(2,1)S(1)}, u32[]{:S(2)}, u32[]{:S(2)}) collective-permute-start(bf16[32,512]{1,0:T(8,128)(2,1)S(1)} %get-tuple-element.24), channel_id=1, source_target_pairs={{0,4},{4,8},{8,12},{12,0},{1,5},{5,9},{9,13},{13,1},{2,6},{6,10},{... | collective-permute-start | bytes 98312 | tf_op jit(solution)/shard_map/ppermute | solution.py:439
  9.4 8.2 %collective-permute-start.1 = (bf16[32,512]{1,0:T(8,128)(2,1)S(1)}, bf16[32,512]{1,0:T(8,128)(2,1)S(1)}, u32[]{:S(2)}, u32[]{:S(2)}) collective-permute-start(bf16[32,512]{1,0:T(8,128)(2,1)S(1)} %get-tuple-element.25), channel_id=1, source_target_pairs={{4,0},{8,4},{12,8},{5,1},{9,5},{13,9},{6,2},{10,6},{14,10},{7,3},{... | collective-permute-start | bytes 98312 | tf_op jit(solution)/shard_map/ppermute | solution.py:22
  11.7 10.0 %collective-permute-start.4 = (bf16[256,512]{1,0:T(8,128)(2,1)S(1)}, bf16[256,512]{1,0:T(8,128)(2,1)S(1)}, u32[]{:S(2)}, u32[]{:S(2)}) collective-permute-start(bf16[256,512]{1,0:T(8,128)(2,1)S(1)} %cut.1), channel_id=1, source_target_pairs={{4,0},{8,4},{12,8},{5,1},{9,5},{13,9},{6,2},{10,6},{14,10},{7,3},{... | collective-permute-start | bytes 786440 | tf_op jit(solution)/shard_map/ppermute | solution.py:22
  20.0 1.8 %collective-permute-start.3 = (bf16[272,512]{1,0:T(8,128)(2,1)S(1)}, bf16[272,512]{1,0:T(8,128)(2,1)S(1)}, u32[]{:S(2)}, u32[]{:S(2)}) collective-permute-start(bf16[272,512]{1,0:T(8,128)(2,1)S(1)} %get-tuple-element.38), channel_id=1, source_target_pairs={{0,1},{1,0},{2,3},{3,2},{4,5},{5,4},{6,7},{7,6},{8,9},{9,8},{10,11... | collective-permute-start | bytes 835592 | tf_op jit(solution)/shard_map/ppermute | solution.py:31
  21.7 2.2 %collective-permute-start.5 = (bf16[256,512]{1,0:T(8,128)(2,1)S(1)}, bf16[256,512]{1,0:T(8,128)(2,1)S(1)}, u32[]{:S(2)}, u32[]{:S(2)}) collective-permute-start(bf16[256,512]{1,0:T(8,128)(2,1)S(1)} %collective-permute-done.4.rest_0_), channel_id=1, source_target_pairs={{0,1},{1,0},{2,3},{3,2},{4,5},{5,4},{6,7},{7,6},{8,9},{9,8},{10,11... | collective-permute-start | bytes 786440 | tf_op jit(solution)/shard_map/ppermute | solution.py:31
  21.8 6.1 %collective-permute-start.7 = (bf16[128,512]{1,0:T(8,128)(2,1)S(1)}, bf16[128,512]{1,0:T(8,128)(2,1)S(1)}, u32[]{:S(2)}, u32[]{:S(2)}) collective-permute-start(bf16[128,512]{1,0:T(8,128)(2,1)S(1)} %get-tuple-element.43), channel_id=1, source_target_pairs={{0,2},{2,0},{1,3},{3,1},{4,6},{6,4},{5,7},{7,5},{8,10},{10,8},{9,1... | collective-permute-start | bytes 393224 | tf_op jit(solution)/shard_map/ppermute | solution.py:31
  23.3 4.5 %collective-permute-start.6 = (bf16[16,128]{1,0:T(8,128)(2,1)S(1)}, bf16[16,128]{1,0:T(8,128)(2,1)S(1)}, u32[]{:S(2)}, u32[]{:S(2)}) collective-permute-start(bf16[16,128]{1,0:T(8,128)(2,1)S(1)} %get-tuple-element.39.mark_ref.refs_0_), channel_id=1, source_target_pairs={{0,2},{2,0},{1,3},{3,1},{4,6},{6,4},{5,7},{7,5},{8,10},{10,8},{9,1... | collective-permute-start | bytes 12296 | tf_op jit(solution)/shard_map/ppermute | solution.py:31

commit v23 on v21

--- a/solution.py
+++ b/solution.py
@@ -132,7 +132,6 @@
             (off_hbm, off_ref), (live_hbm, live_ref),
             (t_hbm.at[pl.ds(rows - edge, edge)], note_ref.at[pl.ds(0, edge)]),
             (t_hbm.at[pl.ds(0, edge)], note_ref.at[pl.ds(edge, edge)]),
-            (t_hbm.at[pl.ds(0, edge)], head_ref),
             (t_hbm.at[pl.ds(begin, piece)], half_ref),
             (bank_hbm, bank_ref), (index_hbm, index_ref), (coeff_hbm, coeff_ref), (psf_hbm, psf_ref),
         ))
@@ -147,6 +146,7 @@
     block = note_ref[0:B, :].astype(F32)
     note_ref[0:B, :] = jnp.where(iota((B, cols), 0) == 0, note, block).astype(BF16)
     msg_ref[...] = note_ref[0:edge, :]
+    head_ref[...] = note_ref[edge:, :]
 
 
 def first_kernel(
@@ -285,6 +285,8 @@
     share, depth = prow_ref.shape
     prow = prow_ref[...].astype(F32)
     out_row = iota((share, depth), 0)
+    from_a = jnp.where(live_a > 0.5, off_a, 2 * rows)
+    until_b = jnp.where(live_b > 0.5, off_b, 0)
     lane = iota((B, cols), 1)
     visits, bands = lax.axis_size("visit"), lax.axis_size("band")
     hi, lo = off_b // B, off_b % B
@@ -298,8 +300,8 @@
             to_visit = partner(lax.axis_index("visit"), k, visits)
             base = (to_visit * bands + partner(lax.axis_index("band"), j, bands)) * share
             row = out_row + base
-            left = jnp.where(row >= off_a, prow * live_a, 0.0).astype(BF16)
-            right = jnp.where(row < off_b, prow * live_b, 0.0).astype(BF16)
+            left = jnp.where(row >= from_a, prow, 0.0).astype(BF16)
+            right = jnp.where(row < until_b, prow, 0.0).astype(BF16)
             span = pl.ds(pl.multiple_of(base, B), depth)
             total = jnp.dot(left, filt[0, span, :], preferred_element_type=F32)
             total += jnp.dot(right, filt[1, span, :], preferred_element_type=F32)

time: 28.5 us -> 28.5 us (level)
  no operation moved by 1% of the time
where the time goes in v23:
time: 28.5 us; the launch traced here: 28.3 us
  Pallas kernels  11.7 us (41%)
  starting transfers between devices  11.3 us (40%)
  waiting for transfers between devices  3.27 us (11%)
  between operations  1.99 us (7%)
    ppermute x3, starting transfers between devices, shifted(): return lax.ppermute(shard, axis, pairs)  7.53 us
    pallas_call x1, Pallas kernels, on_device(): call(first_kernel, (sds((deep, CH), BF16), sds((cols, cols), BF16), sds((...  4.07 us
    pallas_call x1, Pallas kernels, on_device(): call(tile_kernel, sds((rows, cols), BF16), [VM] * (6 + bands), conv_scrat...  3.2 us
    pallas_call x1, Pallas kernels, on_device(): call(join_kernel, (sds((whole, cols), F32),) + (sds((whole + B, cols), BF...  2.29 us
    ppermute x4, starting transfers between devices, swapped(): lax.ppermute(shard, axis, [(i, partner(i, k, devices)) for i in range(dev...  2.16 us
    ppermute x1, starting transfers between devices, on_device(): lax.ppermute(msg, 'patch', [(i, (i + 1) % panels) for i in range(panels)])  1.6 us
    ppermute x1, waiting for transfers between devices, on_device(): lax.ppermute(msg, 'patch', [(i, (i + 1) % panels) for i in range(panels)])  1.33 us
    pallas_call x1, Pallas kernels, on_device(): call(pack_kernel, (sds((2 * edge, cols), BF16), sds((edge, cols), BF16),...  1.15 us
  transfers between devices with their start and end apart: 8, of which 4 were waited for; matrix products, arithmetic and copies ran while one was open for 0% of the time, Pallas kernels for 38%

profile of v23, /device:TPU:0, one launch (start us, length us, event | category | flops | bytes accessed | tf_op | source)
XLA Modules:
  0.0 28.3 jit_solution(6026197453432297432)
XLA Ops:
  0.6 5.0 %collective-permute-start.2 = (bf16[512,1,512]{2,0,1:T(8,128)(2,1)}, bf16[512,1,512]{2,0,1:T(8,128)(2,1)S(1)}, u32[]{:S(2)}, u32[]{:S(2)}) collective-permute-start(bf16[512,1,512]{2,0,1:T(8,128)(2,1)} %param.9), channel_id=1, source_target_pairs={{0,4},{4,8},{8,12},{1,5},{5,9},{9,13},{2,6},{6,10},{10,14},{3,7},{... | collective-permute-start | bytes 1572872 | tf_op jit(solution)/shard_map/ppermute | solution.py:22
  6.9 1.1 %pack.1 = (bf16[64,512]{1,0:T(8,128)(2,1)S(1)}, bf16[32,512]{1,0:T(8,128)(2,1)S(1)}, bf16[32,512]{1,0:T(8,128)(2,1)S(1)}, bf16[256,512]{1,0:T(8,128)(2,1)S(1)}, ...) custom-call(s32[1,1]{1,0:T(1,128)S(6)} %copy.10.off_hbm, ...), custom_call_target="tpu_custom_call" | custom-call | flops 1048576 | bytes 2097152 | tf_op jit(solution)/shard_map/pack/pallas_call | solution.py:423
  8.0 1.6 %collective-permute-start = (bf16[32,512]{1,0:T(8,128)(2,1)S(1)}, bf16[32,512]{1,0:T(8,128)(2,1)S(1)}, u32[]{:S(2)}, u32[]{:S(2)}) collective-permute-start(bf16[32,512]{1,0:T(8,128)(2,1)S(1)} %get-tuple-element.25), channel_id=1, source_target_pairs={{0,4},{4,8},{8,12},{12,0},{1,5},{5,9},{9,13},{13,1},{2,6},{6,10},{... | collective-permute-start | bytes 98312 | tf_op jit(solution)/shard_map/ppermute | solution.py:436
  9.6 1.3 %collective-permute-start.1 = (bf16[32,512]{1,0:T(8,128)(2,1)S(1)}, bf16[32,512]{1,0:T(8,128)(2,1)S(1)}, u32[]{:S(2)}, u32[]{:S(2)}) collective-permute-start(bf16[32,512]{1,0:T(8,128)(2,1)S(1)} %get-tuple-element.26), channel_id=1, source_target_pairs={{4,0},{8,4},{12,8},{5,1},{9,5},{13,9},{6,2},{10,6},{14,10},{7,3},{... | collective-permute-start | bytes 98312 | tf_op jit(solution)/shard_map/ppermute | solution.py:22
  10.9 1.3 %collective-permute-start.4 = (bf16[256,512]{1,0:T(8,128)(2,1)S(1)}, bf16[256,512]{1,0:T(8,128)(2,1)S(1)}, u32[]{:S(2)}, u32[]{:S(2)}) collective-permute-start(bf16[256,512]{1,0:T(8,128)(2,1)S(1)} %get-tuple-element.43), channel_id=1, source_target_pairs={{4,0},{8,4},{12,8},{5,1},{9,5},{13,9},{6,2},{10,6},{14,10},{7,3},{... | collective-permute-start | bytes 786440 | tf_op jit(solution)/shard_map/ppermute | solution.py:22
  12.2 4.1 %first.1 = (bf16[2304,256]{1,0:T(8,128)(2,1)S(1)}, bf16[512,512]{1,0:T(8,128)(2,1)S(1)}, bf16[128,256]{1,0:T(8,128)(2,1)S(1)}, bf16[512,512]{1,0:T(8,128)(2,1)S(...) custom-call(bf16[64,512]{1,0:T(8,128)(2,1)S(1)} %get-tuple-element.24.note_ref, ...), custom_call_target="tpu_custom_call" | custom-call | flops 1207959552 | bytes 2097152 | tf_op jit(solution)/shard_map/first/pallas_call | solution.py:447
  16.3 1.3 %collective-permute-done.msg_ref = bf16[32,512]{1,0:T(8,128)(2,1)S(1)} collective-permute-done((bf16[32,512]{1,0:T(8,128)(2,1)S(1)}, bf16[32,512]{1,0:T(8,128)(2,1)S(1)}, u32[]{:S(2)}, u32[]{:S(2)}) %collective-permute-start) | collective-permute-done | bytes 32800 | tf_op jit(solution)/shard_map/ppermute | solution.py:436
  17.6 0.0 collective-permute-done.1.head_ref
  17.6 0.0 collective-permute-done.2
  17.7 2.3 %join.1 = (f32[256,512]{1,0:T(8,128)S(1)}, bf16[272,512]{1,0:T(8,128)(2,1)S(1)}, bf16[16,128]{1,0:T(8,128)(2,1)S(1)}, f32[4,64,128]{2,1,0:T(8,128)S(1)}) custom-call(bf16[64,512]{1,0:T(8,128)(2,1)S(1)} %get-tuple-element.24.note_ref, bf16[32,512]{1,0:T(8,128)(2,1)S(1)} %collective-permute-done.msg_ref, bf16[32,512]{1,0:T(8,128)(2,1)S(1)} %collective-permute-done.1.head_ref, ...), custom_call_target="tpu_custom_call" | custom-call | flops 17179869184 | bytes 2097152 | tf_op jit(solution)/shard_map/join/pallas_call | solution.py:458
  20.0 0.1 collective-permute-start.3
  20.0 1.0 %collective-permute-done.4.rest_0_ = bf16[256,512]{1,0:T(8,128)(2,1)S(1)} collective-permute-done((bf16[256,512]{1,0:T(8,128)(2,1)S(1)}, bf16[256,512]{1,0:T(8,128)(2,1)S(1)}, u32[]{:S(2)}, u32[]{:S(2)}) %collective-permute-start.4) | collective-permute-done | bytes 262176 | tf_op jit(solution)/shard_map/ppermute | solution.py:22
  21.1 0.0 collective-permute-start.5
  21.1 0.5 %collective-permute-done.3.refs_2_ = bf16[272,512]{1,0:T(8,128)(2,1)S(1)} collective-permute-done((bf16[272,512]{1,0:T(8,128)(2,1)S(1)}, bf16[272,512]{1,0:T(8,128)(2,1)S(1)}, u32[]{:S(2)}, u32[]{:S(2)}) %collective-permute-start.3) | collective-permute-done | bytes 278560 | tf_op jit(solution)/shard_map/ppermute | solution.py:31
  21.6 1.6 %collective-permute-start.7 = (bf16[128,512]{1,0:T(8,128)(2,1)S(1)}, bf16[128,512]{1,0:T(8,128)(2,1)S(1)}, u32[]{:S(2)}, u32[]{:S(2)}) collective-permute-start(bf16[128,512]{1,0:T(8,128)(2,1)S(1)} %get-tuple-element.45), channel_id=1, source_target_pairs={{0,2},{2,0},{1,3},{3,1},{4,6},{6,4},{5,7},{7,5},{8,10},{10,8},{9,1... | collective-permute-start | bytes 393224 | tf_op jit(solution)/shard_map/ppermute | solution.py:31
  23.2 0.5 %collective-permute-start.6 = (bf16[16,128]{1,0:T(8,128)(2,1)S(1)}, bf16[16,128]{1,0:T(8,128)(2,1)S(1)}, u32[]{:S(2)}, u32[]{:S(2)}) collective-permute-start(bf16[16,128]{1,0:T(8,128)(2,1)S(1)} %get-tuple-element.40.mark_ref.refs_0_), channel_id=1, source_target_pairs={{0,2},{2,0},{1,3},{3,1},{4,6},{6,4},{5,7},{7,5},{8,10},{10,8},{9,1... | collective-permute-start | bytes 12296 | tf_op jit(solution)/shard_map/ppermute | solution.py:31
  23.7 0.0 collective-permute-done.5.rest_1_
  23.7 3.2 %tile.1 = bf16[512,512]{1,0:T(8,128)(2,1)} custom-call(bf16[16,128]{1,0:T(8,128)(2,1)S(1)} %get-tuple-element.40.mark_ref.refs_0_, bf16[512,512]{1,0:T(8,128)(2,1)S(1)} %get-tuple-element.41.sci_ref, bf16[64,512]{1,0:T(8,128)(2,1)S(1)} %get-tuple-element.24.note_ref, f32[4,544,128]{2,1,0:T(8,128)S(1)} %get-tuple-element.31.m1_ref, ...), custom_call_target="tpu_custom_call" | custom-call | flops 1207959552 | bytes 2097152 | tf_op jit(solution)/shard_map/tile/pallas_call | solution.py:481
  26.9 0.4 %collective-permute-done.6.refs_1_ = bf16[16,128]{1,0:T(8,128)(2,1)S(1)} collective-permute-done((bf16[16,128]{1,0:T(8,128)(2,1)S(1)}, bf16[16,128]{1,0:T(8,128)(2,1)S(1)}, u32[]{:S(2)}, u32[]{:S(2)}) %collective-permute-start.6) | collective-permute-done | bytes 4128 | tf_op jit(solution)/shard_map/ppermute | solution.py:31
  27.3 0.0 collective-permute-done.7.refs_3_
  27.3 1.0 %coadd.1 = f32[128,512]{1,0:T(8,128)} custom-call(bf16[16,128]{1,0:T(8,128)(2,1)S(1)} %get-tuple-element.40.mark_ref.refs_0_, bf16[16,128]{1,0:T(8,128)(2,1)S(1)} %collective-permute-done.6.refs_1_, f32[128,512]{1,0:T(8,128)S(1)} %get-tuple-element.44.refs_2_, bf16[128,512]{1,0:T(8,128)(2,1)S(1)} %collective-permute-done.7.refs_3_), custom_call_target="tpu_custom_call" | custom-call | flops 1048576 | bytes 2097152 | tf_op jit(solution)/shard_map/coadd/pallas_call | solution.py:489
  (1 shorter events, 0.0 us)
Async XLA Ops:
  0.6 17.0 %collective-permute-start.2 = (bf16[512,1,512]{2,0,1:T(8,128)(2,1)}, bf16[512,1,512]{2,0,1:T(8,128)(2,1)S(1)}, u32[]{:S(2)}, u32[]{:S(2)}) collective-permute-start(bf16[512,1,512]{2,0,1:T(8,128)(2,1)} %param.9), channel_id=1, source_target_pairs={{0,4},{4,8},{8,12},{1,5},{5,9},{9,13},{2,6},{6,10},{10,14},{3,7},{... | collective-permute-start | bytes 1572872 | tf_op jit(solution)/shard_map/ppermute | solution.py:22
  8.0 9.6 %collective-permute-start = (bf16[32,512]{1,0:T(8,128)(2,1)S(1)}, bf16[32,512]{1,0:T(8,128)(2,1)S(1)}, u32[]{:S(2)}, u32[]{:S(2)}) collective-permute-start(bf16[32,512]{1,0:T(8,128)(2,1)S(1)} %get-tuple-element.25), channel_id=1, source_target_pairs={{0,4},{4,8},{8,12},{12,0},{1,5},{5,9},{9,13},{13,1},{2,6},{6,10},{... | collective-permute-start | bytes 98312 | tf_op jit(solution)/shard_map/ppermute | solution.py:436
  9.6 8.0 %collective-permute-start.1 = (bf16[32,512]{1,0:T(8,128)(2,1)S(1)}, bf16[32,512]{1,0:T(8,128)(2,1)S(1)}, u32[]{:S(2)}, u32[]{:S(2)}) collective-permute-start(bf16[32,512]{1,0:T(8,128)(2,1)S(1)} %get-tuple-element.26), channel_id=1, source_target_pairs={{4,0},{8,4},{12,8},{5,1},{9,5},{13,9},{6,2},{10,6},{14,10},{7,3},{... | collective-permute-start | bytes 98312 | tf_op jit(solution)/shard_map/ppermute | solution.py:22
  10.9 10.1 %collective-permute-start.4 = (bf16[256,512]{1,0:T(8,128)(2,1)S(1)}, bf16[256,512]{1,0:T(8,128)(2,1)S(1)}, u32[]{:S(2)}, u32[]{:S(2)}) collective-permute-start(bf16[256,512]{1,0:T(8,128)(2,1)S(1)} %get-tuple-element.43), channel_id=1, source_target_pairs={{4,0},{8,4},{12,8},{5,1},{9,5},{13,9},{6,2},{10,6},{14,10},{7,3},{... | collective-permute-start | bytes 786440 | tf_op jit(solution)/shard_map/ppermute | solution.py:22
  20.0 1.6 %collective-permute-start.3 = (bf16[272,512]{1,0:T(8,128)(2,1)S(1)}, bf16[272,512]{1,0:T(8,128)(2,1)S(1)}, u32[]{:S(2)}, u32[]{:S(2)}) collective-permute-start(bf16[272,512]{1,0:T(8,128)(2,1)S(1)} %get-tuple-element.39), channel_id=1, source_target_pairs={{0,1},{1,0},{2,3},{3,2},{4,5},{5,4},{6,7},{7,6},{8,9},{9,8},{10,11... | collective-permute-start | bytes 835592 | tf_op jit(solution)/shard_map/ppermute | solution.py:31
  21.1 2.7 %collective-permute-start.5 = (bf16[256,512]{1,0:T(8,128)(2,1)S(1)}, bf16[256,512]{1,0:T(8,128)(2,1)S(1)}, u32[]{:S(2)}, u32[]{:S(2)}) collective-permute-start(bf16[256,512]{1,0:T(8,128)(2,1)S(1)} %collective-permute-done.4.rest_0_), channel_id=1, source_target_pairs={{0,1},{1,0},{2,3},{3,2},{4,5},{5,4},{6,7},{7,6},{8,9},{9,8},{10,11... | collective-permute-start | bytes 786440 | tf_op jit(solution)/shard_map/ppermute | solution.py:31
  21.6 5.7 %collective-permute-start.7 = (bf16[128,512]{1,0:T(8,128)(2,1)S(1)}, bf16[128,512]{1,0:T(8,128)(2,1)S(1)}, u32[]{:S(2)}, u32[]{:S(2)}) collective-permute-start(bf16[128,512]{1,0:T(8,128)(2,1)S(1)} %get-tuple-element.45), channel_id=1, source_target_pairs={{0,2},{2,0},{1,3},{3,1},{4,6},{6,4},{5,7},{7,5},{8,10},{10,8},{9,1... | collective-permute-start | bytes 393224 | tf_op jit(solution)/shard_map/ppermute | solution.py:31
  23.2 4.1 %collective-permute-start.6 = (bf16[16,128]{1,0:T(8,128)(2,1)S(1)}, bf16[16,128]{1,0:T(8,128)(2,1)S(1)}, u32[]{:S(2)}, u32[]{:S(2)}) collective-permute-start(bf16[16,128]{1,0:T(8,128)(2,1)S(1)} %get-tuple-element.40.mark_ref.refs_0_), channel_id=1, source_target_pairs={{0,2},{2,0},{1,3},{3,1},{4,6},{6,4},{5,7},{7,5},{8,10},{10,8},{9,1... | collective-permute-start | bytes 12296 | tf_op jit(solution)/shard_map/ppermute | solution.py:31

commit v24 on v23

--- a/solution.py
+++ b/solution.py
@@ -264,8 +264,8 @@
     to_blocks(src, 2, note_ref[edge:, :])
     to_blocks(src, 4, note_ref[0:edge, :])
     to_blocks(src, 6, head_ref[...])
+    conv_blocks(src, 8, w_ref, xs, strip)
     filter_inner(sci, rows - B - off_b, off_b - rows, off_b, m1_ref, pcol_ref, edge_b, filt_b, inner)
-    conv_blocks(src, 8, w_ref, xs, strip)
     for n, a in enumerate((1, 2, 5, 6)):
         m_ref[:, B * n : B * (n + 1), :] = strip[:, PITCH * a : PITCH * a + B, :]
     off_a, live_a = read_note(note_ref)

time: 28.5 us -> 28.4 us (level)
  transfers between devices with their start and end apart: 8 -> 8, of which waited for: 4 -> 4; matrix products, arithmetic and copies ran while one was open for 0% -> 0% of each run, Pallas kernels for 38% -> 37%
where the time goes in v24:
time: 28.4 us; the launch traced here: 28.1 us
  Pallas kernels  11.5 us (40%)
  starting transfers between devices  11.3 us (40%)
  waiting for transfers between devices  3.37 us (12%)
  between operations  1.99 us (7%)
    ppermute x3, starting transfers between devices, shifted(): return lax.ppermute(shard, axis, pairs)  7.53 us
    pallas_call x1, Pallas kernels, on_device(): call(first_kernel, (sds((deep, CH), BF16), sds((cols, cols), BF16), sds((...  4.04 us
    pallas_call x1, Pallas kernels, on_device(): call(tile_kernel, sds((rows, cols), BF16), [VM] * (6 + bands), conv_scrat...  3.19 us
    ppermute x4, starting transfers between devices, swapped(): lax.ppermute(shard, axis, [(i, partner(i, k, devices)) for i in range(dev...  2.16 us
    pallas_call x1, Pallas kernels, on_device(): call(join_kernel, (sds((whole, cols), F32),) + (sds((whole + B, cols), BF...  2.1 us
    ppermute x1, starting transfers between devices, on_device(): lax.ppermute(msg, 'patch', [(i, (i + 1) % panels) for i in range(panels)])  1.6 us
    ppermute x1, waiting for transfers between devices, on_device(): lax.ppermute(msg, 'patch', [(i, (i + 1) % panels) for i in range(panels)])  1.36 us
    ppermute x3, waiting for transfers between devices, shifted(): return lax.ppermute(shard, axis, pairs)  1.22 us
  transfers between devices with their start and end apart: 8, of which 4 were waited for; matrix products, arithmetic and copies ran while one was open for 0% of the time, Pallas kernels for 37%

profile of v24, /device:TPU:0, one launch (start us, length us, event | category | flops | bytes accessed | tf_op | source)
XLA Modules:
  0.0 28.1 jit_solution(17393343427631865202)
XLA Ops:
  0.6 5.0 %collective-permute-start.2 = (bf16[512,1,512]{2,0,1:T(8,128)(2,1)}, bf16[512,1,512]{2,0,1:T(8,128)(2,1)S(1)}, u32[]{:S(2)}, u32[]{:S(2)}) collective-permute-start(bf16[512,1,512]{2,0,1:T(8,128)(2,1)} %param.9), channel_id=1, source_target_pairs={{0,4},{4,8},{8,12},{1,5},{5,9},{9,13},{2,6},{6,10},{10,14},{3,7},{... | collective-permute-start | bytes 1572872 | tf_op jit(solution)/shard_map/ppermute | solution.py:22
  6.9 1.1 %pack.1 = (bf16[64,512]{1,0:T(8,128)(2,1)S(1)}, bf16[32,512]{1,0:T(8,128)(2,1)S(1)}, bf16[32,512]{1,0:T(8,128)(2,1)S(1)}, bf16[256,512]{1,0:T(8,128)(2,1)S(1)}, ...) custom-call(s32[1,1]{1,0:T(1,128)S(6)} %copy.10.off_hbm, ...), custom_call_target="tpu_custom_call" | custom-call | flops 1048576 | bytes 2097152 | tf_op jit(solution)/shard_map/pack/pallas_call | solution.py:423
  8.0 1.6 %collective-permute-start = (bf16[32,512]{1,0:T(8,128)(2,1)S(1)}, bf16[32,512]{1,0:T(8,128)(2,1)S(1)}, u32[]{:S(2)}, u32[]{:S(2)}) collective-permute-start(bf16[32,512]{1,0:T(8,128)(2,1)S(1)} %get-tuple-element.25), channel_id=1, source_target_pairs={{0,4},{4,8},{8,12},{12,0},{1,5},{5,9},{9,13},{13,1},{2,6},{6,10},{... | collective-permute-start | bytes 98312 | tf_op jit(solution)/shard_map/ppermute | solution.py:436
  9.6 1.3 %collective-permute-start.1 = (bf16[32,512]{1,0:T(8,128)(2,1)S(1)}, bf16[32,512]{1,0:T(8,128)(2,1)S(1)}, u32[]{:S(2)}, u32[]{:S(2)}) collective-permute-start(bf16[32,512]{1,0:T(8,128)(2,1)S(1)} %get-tuple-element.26), channel_id=1, source_target_pairs={{4,0},{8,4},{12,8},{5,1},{9,5},{13,9},{6,2},{10,6},{14,10},{7,3},{... | collective-permute-start | bytes 98312 | tf_op jit(solution)/shard_map/ppermute | solution.py:22
  10.9 1.3 %collective-permute-start.4 = (bf16[256,512]{1,0:T(8,128)(2,1)S(1)}, bf16[256,512]{1,0:T(8,128)(2,1)S(1)}, u32[]{:S(2)}, u32[]{:S(2)}) collective-permute-start(bf16[256,512]{1,0:T(8,128)(2,1)S(1)} %get-tuple-element.43), channel_id=1, source_target_pairs={{4,0},{8,4},{12,8},{5,1},{9,5},{13,9},{6,2},{10,6},{14,10},{7,3},{... | collective-permute-start | bytes 786440 | tf_op jit(solution)/shard_map/ppermute | solution.py:22
  12.2 4.0 %first.1 = (bf16[2304,256]{1,0:T(8,128)(2,1)S(1)}, bf16[512,512]{1,0:T(8,128)(2,1)S(1)}, bf16[128,256]{1,0:T(8,128)(2,1)S(1)}, bf16[512,512]{1,0:T(8,128)(2,1)S(...) custom-call(bf16[64,512]{1,0:T(8,128)(2,1)S(1)} %get-tuple-element.24.note_ref, ...), custom_call_target="tpu_custom_call" | custom-call | flops 1207959552 | bytes 2097152 | tf_op jit(solution)/shard_map/first/pallas_call | solution.py:447
  16.3 1.4 %collective-permute-done.msg_ref = bf16[32,512]{1,0:T(8,128)(2,1)S(1)} collective-permute-done((bf16[32,512]{1,0:T(8,128)(2,1)S(1)}, bf16[32,512]{1,0:T(8,128)(2,1)S(1)}, u32[]{:S(2)}, u32[]{:S(2)}) %collective-permute-start) | collective-permute-done | bytes 32800 | tf_op jit(solution)/shard_map/ppermute | solution.py:436
  17.6 0.0 collective-permute-done.1.head_ref
  17.6 0.0 collective-permute-done.2
  17.7 2.1 %join.1 = (f32[256,512]{1,0:T(8,128)S(1)}, bf16[272,512]{1,0:T(8,128)(2,1)S(1)}, bf16[16,128]{1,0:T(8,128)(2,1)S(1)}, f32[4,64,128]{2,1,0:T(8,128)S(1)}) custom-call(bf16[64,512]{1,0:T(8,128)(2,1)S(1)} %get-tuple-element.24.note_ref, bf16[32,512]{1,0:T(8,128)(2,1)S(1)} %collective-permute-done.msg_ref, bf16[32,512]{1,0:T(8,128)(2,1)S(1)} %collective-permute-done.1.head_ref, ...), custom_call_target="tpu_custom_call" | custom-call | flops 17179869184 | bytes 2097152 | tf_op jit(solution)/shard_map/join/pallas_call | solution.py:458
  19.8 0.1 collective-permute-start.3
  19.8 1.2 %collective-permute-done.4.rest_0_ = bf16[256,512]{1,0:T(8,128)(2,1)S(1)} collective-permute-done((bf16[256,512]{1,0:T(8,128)(2,1)S(1)}, bf16[256,512]{1,0:T(8,128)(2,1)S(1)}, u32[]{:S(2)}, u32[]{:S(2)}) %collective-permute-start.4) | collective-permute-done | bytes 262176 | tf_op jit(solution)/shard_map/ppermute | solution.py:22
  21.1 0.0 collective-permute-start.5
  21.1 0.3 %collective-permute-done.3.refs_2_ = bf16[272,512]{1,0:T(8,128)(2,1)S(1)} collective-permute-done((bf16[272,512]{1,0:T(8,128)(2,1)S(1)}, bf16[272,512]{1,0:T(8,128)(2,1)S(1)}, u32[]{:S(2)}, u32[]{:S(2)}) %collective-permute-start.3) | collective-permute-done | bytes 278560 | tf_op jit(solution)/shard_map/ppermute | solution.py:31
  21.4 1.6 %collective-permute-start.7 = (bf16[128,512]{1,0:T(8,128)(2,1)S(1)}, bf16[128,512]{1,0:T(8,128)(2,1)S(1)}, u32[]{:S(2)}, u32[]{:S(2)}) collective-permute-start(bf16[128,512]{1,0:T(8,128)(2,1)S(1)} %get-tuple-element.45), channel_id=1, source_target_pairs={{0,2},{2,0},{1,3},{3,1},{4,6},{6,4},{5,7},{7,5},{8,10},{10,8},{9,1... | collective-permute-start | bytes 393224 | tf_op jit(solution)/shard_map/ppermute | solution.py:31
  23.0 0.5 %collective-permute-start.6 = (bf16[16,128]{1,0:T(8,128)(2,1)S(1)}, bf16[16,128]{1,0:T(8,128)(2,1)S(1)}, u32[]{:S(2)}, u32[]{:S(2)}) collective-permute-start(bf16[16,128]{1,0:T(8,128)(2,1)S(1)} %get-tuple-element.40.mark_ref.refs_0_), channel_id=1, source_target_pairs={{0,2},{2,0},{1,3},{3,1},{4,6},{6,4},{5,7},{7,5},{8,10},{10,8},{9,1... | collective-permute-start | bytes 12296 | tf_op jit(solution)/shard_map/ppermute | solution.py:31
  23.5 0.0 collective-permute-done.5.rest_1_
  23.5 3.2 %tile.1 = bf16[512,512]{1,0:T(8,128)(2,1)} custom-call(bf16[16,128]{1,0:T(8,128)(2,1)S(1)} %get-tuple-element.40.mark_ref.refs_0_, bf16[512,512]{1,0:T(8,128)(2,1)S(1)} %get-tuple-element.41.sci_ref, bf16[64,512]{1,0:T(8,128)(2,1)S(1)} %get-tuple-element.24.note_ref, f32[4,544,128]{2,1,0:T(8,128)S(1)} %get-tuple-element.31.m1_ref, ...), custom_call_target="tpu_custom_call" | custom-call | flops 1207959552 | bytes 2097152 | tf_op jit(solution)/shard_map/tile/pallas_call | solution.py:481
  26.7 0.5 %collective-permute-done.6.refs_1_ = bf16[16,128]{1,0:T(8,128)(2,1)S(1)} collective-permute-done((bf16[16,128]{1,0:T(8,128)(2,1)S(1)}, bf16[16,128]{1,0:T(8,128)(2,1)S(1)}, u32[]{:S(2)}, u32[]{:S(2)}) %collective-permute-start.6) | collective-permute-done | bytes 4128 | tf_op jit(solution)/shard_map/ppermute | solution.py:31
  27.2 0.0 collective-permute-done.7.refs_3_
  27.2 1.0 %coadd.1 = f32[128,512]{1,0:T(8,128)} custom-call(bf16[16,128]{1,0:T(8,128)(2,1)S(1)} %get-tuple-element.40.mark_ref.refs_0_, bf16[16,128]{1,0:T(8,128)(2,1)S(1)} %collective-permute-done.6.refs_1_, f32[128,512]{1,0:T(8,128)S(1)} %get-tuple-element.44.refs_2_, bf16[128,512]{1,0:T(8,128)(2,1)S(1)} %collective-permute-done.7.refs_3_), custom_call_target="tpu_custom_call" | custom-call | flops 1048576 | bytes 2097152 | tf_op jit(solution)/shard_map/coadd/pallas_call | solution.py:489
  (1 shorter events, 0.0 us)
Async XLA Ops:
  0.6 17.0 %collective-permute-start.2 = (bf16[512,1,512]{2,0,1:T(8,128)(2,1)}, bf16[512,1,512]{2,0,1:T(8,128)(2,1)S(1)}, u32[]{:S(2)}, u32[]{:S(2)}) collective-permute-start(bf16[512,1,512]{2,0,1:T(8,128)(2,1)} %param.9), channel_id=1, source_target_pairs={{0,4},{4,8},{8,12},{1,5},{5,9},{9,13},{2,6},{6,10},{10,14},{3,7},{... | collective-permute-start | bytes 1572872 | tf_op jit(solution)/shard_map/ppermute | solution.py:22
  8.0 9.6 %collective-permute-start = (bf16[32,512]{1,0:T(8,128)(2,1)S(1)}, bf16[32,512]{1,0:T(8,128)(2,1)S(1)}, u32[]{:S(2)}, u32[]{:S(2)}) collective-permute-start(bf16[32,512]{1,0:T(8,128)(2,1)S(1)} %get-tuple-element.25), channel_id=1, source_target_pairs={{0,4},{4,8},{8,12},{12,0},{1,5},{5,9},{9,13},{13,1},{2,6},{6,10},{... | collective-permute-start | bytes 98312 | tf_op jit(solution)/shard_map/ppermute | solution.py:436
  9.6 8.0 %collective-permute-start.1 = (bf16[32,512]{1,0:T(8,128)(2,1)S(1)}, bf16[32,512]{1,0:T(8,128)(2,1)S(1)}, u32[]{:S(2)}, u32[]{:S(2)}) collective-permute-start(bf16[32,512]{1,0:T(8,128)(2,1)S(1)} %get-tuple-element.26), channel_id=1, source_target_pairs={{4,0},{8,4},{12,8},{5,1},{9,5},{13,9},{6,2},{10,6},{14,10},{7,3},{... | collective-permute-start | bytes 98312 | tf_op jit(solution)/shard_map/ppermute | solution.py:22
  10.9 10.1 %collective-permute-start.4 = (bf16[256,512]{1,0:T(8,128)(2,1)S(1)}, bf16[256,512]{1,0:T(8,128)(2,1)S(1)}, u32[]{:S(2)}, u32[]{:S(2)}) collective-permute-start(bf16[256,512]{1,0:T(8,128)(2,1)S(1)} %get-tuple-element.43), channel_id=1, source_target_pairs={{4,0},{8,4},{12,8},{5,1},{9,5},{13,9},{6,2},{10,6},{14,10},{7,3},{... | collective-permute-start | bytes 786440 | tf_op jit(solution)/shard_map/ppermute | solution.py:22
  19.8 1.6 %collective-permute-start.3 = (bf16[272,512]{1,0:T(8,128)(2,1)S(1)}, bf16[272,512]{1,0:T(8,128)(2,1)S(1)}, u32[]{:S(2)}, u32[]{:S(2)}) collective-permute-start(bf16[272,512]{1,0:T(8,128)(2,1)S(1)} %get-tuple-element.39), channel_id=1, source_target_pairs={{0,1},{1,0},{2,3},{3,2},{4,5},{5,4},{6,7},{7,6},{8,9},{9,8},{10,11... | collective-permute-start | bytes 835592 | tf_op jit(solution)/shard_map/ppermute | solution.py:31
  21.1 2.5 %collective-permute-start.5 = (bf16[256,512]{1,0:T(8,128)(2,1)S(1)}, bf16[256,512]{1,0:T(8,128)(2,1)S(1)}, u32[]{:S(2)}, u32[]{:S(2)}) collective-permute-start(bf16[256,512]{1,0:T(8,128)(2,1)S(1)} %collective-permute-done.4.rest_0_), channel_id=1, source_target_pairs={{0,1},{1,0},{2,3},{3,2},{4,5},{5,4},{6,7},{7,6},{8,9},{9,8},{10,11... | collective-permute-start | bytes 786440 | tf_op jit(solution)/shard_map/ppermute | solution.py:31
  21.4 5.7 %collective-permute-start.7 = (bf16[128,512]{1,0:T(8,128)(2,1)S(1)}, bf16[128,512]{1,0:T(8,128)(2,1)S(1)}, u32[]{:S(2)}, u32[]{:S(2)}) collective-permute-start(bf16[128,512]{1,0:T(8,128)(2,1)S(1)} %get-tuple-element.45), channel_id=1, source_target_pairs={{0,2},{2,0},{1,3},{3,1},{4,6},{6,4},{5,7},{7,5},{8,10},{10,8},{9,1... | collective-permute-start | bytes 393224 | tf_op jit(solution)/shard_map/ppermute | solution.py:31
  23.0 4.2 %collective-permute-start.6 = (bf16[16,128]{1,0:T(8,128)(2,1)S(1)}, bf16[16,128]{1,0:T(8,128)(2,1)S(1)}, u32[]{:S(2)}, u32[]{:S(2)}) collective-permute-start(bf16[16,128]{1,0:T(8,128)(2,1)S(1)} %get-tuple-element.40.mark_ref.refs_0_), channel_id=1, source_target_pairs={{0,2},{2,0},{1,3},{3,1},{4,6},{6,4},{5,7},{7,5},{8,10},{10,8},{9,1... | collective-permute-start | bytes 12296 | tf_op jit(solution)/shard_map/ppermute | solution.py:31
